TPU v7x, 256 devices: a whole 4x4x8 slice. The times are simulated.
256 devices in a mesh: east: 16 (over x, z_hi), north: 16 (over y, z_lo, core).
Axes of the slice: x: 4, y: 4, z: 8 (z_hi: 4, z_lo: 2; z = z_hi * 2 + z_lo), core: 2. Of those that a mesh axis runs over, the one named last changes fastest.
Arguments:
- features: bfloat16 [96, 128, 2048], P(None, 'east', 'north'), may hold values from -6 to 6
- occupancy: int32 [16, 16, 2], P('east', 'north'), may hold values from 0 to 1, as said below
- weight_first: bfloat16 [27, 96, 96], replicated, may hold values from -0.125 to 0.125
- weight_second: bfloat16 [27, 96, 96], replicated, may hold values from -0.125 to 0.125
- cotangent: bfloat16 [96, 128, 2048], P(None, 'east', 'north'), may hold values from -6 to 6
Outputs:
- activated: bfloat16 [96, 128, 2048], P(None, 'east', 'north')
- feature_grad: bfloat16 [96, 128, 2048], P(None, 'east', 'north')
- grad_first: float32 [248832], P(('east', 'north'))
- grad_second: float32 [248832], P(('east', 'north'))
Inputs may be any that keep to these rules, and one draw needn't show every extreme that they name: `occupancy`: every ground cell's column holds at least one occupied block; occupied blocks of a column lie in one run of consecutive heights.
All inputs are finite; a program needn't handle non-finite values.
Results may differ from a plain program's by a relative error of at most 0.0085.
Values may be sent and summed in bfloat16 or wider, within the bound.
No kernel may reach another device: no remote copies, remote signals or barrier semaphores. Data moves between devices by JAX's collectives and lax.ppermute only.
A program may use at most 64 MiB of HBM per device.

v0:
```python
import math

import jax
import jax.numpy as jnp
from jax import lax
from jax.sharding import PartitionSpec as P


def padded_2(block, sides, width):
    for axis, dim in sides:
        count = lax.axis_size(axis)
        forward = [(i, i + 1) for i in range(count - 1)]
        backward = [(target, source) for source, target in forward]
        low = lax.ppermute(
            lax.slice_in_dim(block, block.shape[dim] - width, None, axis=dim), axis, forward
        )
        high = lax.ppermute(lax.slice_in_dim(block, 0, width, axis=dim), axis, backward)
        block = jnp.concatenate([low, block, high], axis=dim)
    return block


def shifted(window, offset, transposed, width_x, width_y, depth):
    start_x = offset // 9
    start_y = offset // 3 % 3
    start_z = offset % 3
    if transposed:
        start_x, start_y, start_z = (2 - start_x, 2 - start_y, 2 - start_z)
    piece = window[
        :, start_x : start_x + width_x, start_y : start_y + width_y, start_z : start_z + depth
    ]
    return piece.reshape(piece.shape[0], -1)


def conv_window(window, weight, transposed):
    width_x = window.shape[1] - 2
    width_y = window.shape[2] - 2
    depth = window.shape[3] - 2
    total = jnp.zeros((weight.shape[2], width_x * width_y * depth), jnp.float32)
    for offset in range(27):
        matrix = weight[offset] if transposed else weight[offset].T
        total = total + jnp.dot(
            matrix,
            shifted(window, offset, transposed, width_x, width_y, depth),
            preferred_element_type=jnp.float32,
        )
    return total.reshape(weight.shape[2], width_x, width_y, depth)


def grad_window(window, cotan):
    flat = cotan.reshape(cotan.shape[0], -1)
    parts = []
    for offset in range(27):
        piece = shifted(window, offset, False, cotan.shape[1], cotan.shape[2], cotan.shape[3])
        parts.append(
            lax.dot_general(
                piece, flat, (((1,), (1,)), ((), ())), preferred_element_type=jnp.float32
            )
        )
    return jnp.stack(parts)


def silu_slope(value):
    sigma = jax.nn.sigmoid(value)
    return sigma * (1.0 + value * (1.0 - sigma))


def extend(field):
    wider = padded_2(field, (("east", 1), ("north", 2)), 1)
    return jnp.pad(wider, ((0, 0), (0, 0), (0, 0), (1, 1)))


def convolve(padded, weight, transposed):
    return conv_window(padded, weight, transposed)


def kernel_grad(padded, cotan):
    return grad_window(padded, cotan)


def local(features, occupancy, weight_first, weight_second, cotangent):
    channels = features.shape[0]
    width_x = features.shape[1]
    width_y = 8
    depth = features.shape[2] // width_y
    grid = features.reshape(channels, width_x, width_y, depth)
    blocks = occupancy.reshape(-1)
    voxel_mask = jnp.repeat(blocks, 8).astype(jnp.float32)[None, None, None, :]
    masked = (grid * voxel_mask).astype(jnp.bfloat16)
    masked_wide = extend(masked)
    first = voxel_mask * convolve(masked_wide, weight_first, False)
    hidden = jax.nn.silu(first).astype(jnp.bfloat16)
    hidden_wide = extend(hidden)
    second = voxel_mask * convolve(hidden_wide, weight_second, False)
    activated = jax.nn.silu(second).astype(jnp.bfloat16)
    upstream = cotangent.reshape(channels, width_x, width_y, depth).astype(jnp.float32)
    grad_two = (upstream * silu_slope(second) * voxel_mask).astype(jnp.bfloat16)
    voxel_total = lax.axis_size("east") * width_x * lax.axis_size("north") * width_y * depth
    factor = 1.0 / math.sqrt(voxel_total)
    term_second = (kernel_grad(hidden_wide, grad_two) * factor).reshape(-1)
    grad_second = lax.psum_scatter(term_second, ("east", "north"), scatter_dimension=0, tiled=True)
    back_hidden = convolve(extend(grad_two), weight_second, True)
    grad_one = (back_hidden * silu_slope(first) * voxel_mask).astype(jnp.bfloat16)
    term_first = (kernel_grad(masked_wide, grad_one) * factor).reshape(-1)
    grad_first = lax.psum_scatter(term_first, ("east", "north"), scatter_dimension=0, tiled=True)
    feature_grad = (voxel_mask * convolve(extend(grad_one), weight_first, True)).astype(
        jnp.bfloat16
    )
    return (
        activated.reshape(channels, width_x, width_y * depth),
        feature_grad.reshape(channels, width_x, width_y * depth),
        grad_first,
        grad_second,
    )


def solution(mesh):
    return jax.shard_map(
        local,
        mesh=mesh,
        in_specs=(
            P(None, "east", "north"),
            P("east", "north", None),
            P(),
            P(),
            P(None, "east", "north"),
        ),
        out_specs=(
            P(None, "east", "north"),
            P(None, "east", "north"),
            P(("east", "north")),
            P(("east", "north")),
        ),
        check_vma=False,
    )
```

profile of v0, /device:TPU:2, one launch (start us, length us, event | category | flops | bytes accessed | tf_op | source)
XLA Modules:
  0.0 453.8 jit_solution(2061140184804513067)
XLA Ops:
  8.0 1.1 copy.30
  9.3 8.2 %collective-permute-start.1 = (bf16[96,1,8,16]{0,3,2,1:T(8,128)(2,1)S(1)}, bf16[96,1,8,16]{0,3,2,1:T(8,128)(2,1)S(1)}, u32[]{:S(2)}, u32[]{:S(2)}) collective-permute-start(bf16[96,1,8,16]{0,3,2,1:T(8,128)(2,1)S(1)} %get-tuple-element.143), channel_id=1, source_target_pairs={{16,0},{32,16},{48,32},{64,48},{80,64},{96,80},{112,96},{128,112},... | collective-permute-start | bytes 73736 | tf_op jit(solution)/shard_map/ppermute | solution.py:17
  17.5 1.9 collective-permute-start
  19.8 6.5 %collective-permute-done = bf16[96,1,8,16]{0,3,2,1:T(8,128)(2,1)S(1)} collective-permute-done((bf16[96,1,8,16]{0,3,2,1:T(8,128)(2,1)S(1)}, bf16[96,1,8,16]{0,3,2,1:T(8,128)(2,1)S(1)}, u32[]{:S(2)}, u32[]{:S(2)}) %collective-permute-start) | collective-permute-done | bytes 24608 | tf_op jit(solution)/shard_map/ppermute | solution.py:14
  26.3 1.3 collective-permute-start.3
  27.6 3.0 collective-permute-start.2
  41.1 1.9 collective-permute-start.5
  43.0 4.8 %collective-permute-start.4 = (bf16[96,1,8,16]{0,3,2,1:T(8,128)(2,1)S(1)}, bf16[96,1,8,16]{0,3,2,1:T(8,128)(2,1)S(1)}, u32[]{:S(2)}, u32[]{:S(2)}) collective-permute-start(bf16[96,1,8,16]{0,3,2,1:T(8,128)(2,1)S(1)} %get-tuple-element.138), channel_id=1, source_target_pairs={{0,16},{16,32},{32,48},{48,64},{64,80},{80,96},{96,112},{112,128},... | collective-permute-start | bytes 73736 | tf_op jit(solution)/shard_map/ppermute | solution.py:14
  50.0 2.6 collective-permute-done.4
  52.6 1.3 collective-permute-start.7
  53.9 3.2 collective-permute-start.6
  58.1 1.0 fusion.398
  67.7 1.3 multiply_convert_fusion.3
  69.9 1.9 collective-permute-start.9
  71.9 4.8 %collective-permute-start.8 = (bf16[96,1,8,16]{0,3,2,1:T(8,128)(2,1)S(1)}, bf16[96,1,8,16]{0,3,2,1:T(8,128)(2,1)S(1)}, u32[]{:S(2)}, u32[]{:S(2)}) collective-permute-start(bf16[96,1,8,16]{0,3,2,1:T(8,128)(2,1)S(1)} %get-tuple-element.134), channel_id=1, source_target_pairs={{0,16},{16,32},{32,48},{48,64},{64,80},{80,96},{96,112},{112,128},... | collective-permute-start | bytes 73736 | tf_op jit(solution)/shard_map/ppermute | solution.py:14
  87.2 1.3 collective-permute-start.11
  88.5 4.5 collective-permute-start.10
  93.9 1.0 fusion.397
  102.6 1.0 multiply_convert_fusion.8
  103.7 1.2 copy.36
  106.7 4.3 collective-permute-start.13
  111.0 2.4 collective-permute-start.12
  136.4 1.4 broadcast_multiply_fusion.1
  137.9 1.8 mul.188
  140.4 1.3 collective-permute-start.15
  141.7 5.3 %collective-permute-start.14 = (bf16[96,10,1,16]{0,3,2,1:T(8,128)(2,1)S(1)}, bf16[96,10,1,16]{0,3,2,1:T(8,128)(2,1)S(1)}, u32[]{:S(2)}, u32[]{:S(2)}) collective-permute-start(bf16[96,10,1,16]{0,3,2,1:T(8,128)(2,1)S(1)} %get-tuple-element.114), channel_id=1, source_target_pairs={{0,1},{1,2},{2,3},{3,4},{4,5},{5,6},{6,7},{7,8},{8,9},{9,10},{10,1... | collective-permute-start | bytes 92168 | tf_op jit(solution)/shard_map/ppermute | solution.py:14
  147.9 1.1 select_maximum_fusion
  170.7 1.4 broadcast_multiply_fusion
  172.1 1.8 mul.194
  175.6 268.6 %all-reduce.9.cloned.1.call-done = (f32[248832]{0:T(1024)}, f32[248832]{0:T(1024)}) async-done(((f32[248832]{0:T(1024)}, f32[248832]{0:T(1024)}), (f32[248832]{0:T(1024)}, f32[248832]{0:T(1024)})) %all-reduce.9.cloned.1.call-update) | async-done | bytes 1990672
  444.2 1.4 dynamic-slice
  445.5 1.4 dynamic-slice.1
  (323 shorter events, 92.5 us)
Async XLA Ops:
  7.2 437.0 %all-reduce.9.cloned.1.call-start = ((), (), s32[]{:S(2)}) async-start(), calls=%async_computation | async-start | bytes 3981312
  8.0 32.8 %copy-start.41 = (f32[16]{0:T(128)}, f32[16]{0:T(128)S(1)}, u32[]{:S(2)}) copy-start(f32[16]{0:T(128)S(1)} %convert_element_type.96) | copy-start | bytes 196
  9.3 10.4 %collective-permute-start.1 = (bf16[96,1,8,16]{0,3,2,1:T(8,128)(2,1)S(1)}, bf16[96,1,8,16]{0,3,2,1:T(8,128)(2,1)S(1)}, u32[]{:S(2)}, u32[]{:S(2)}) collective-permute-start(bf16[96,1,8,16]{0,3,2,1:T(8,128)(2,1)S(1)} %get-tuple-element.143), channel_id=1, source_target_pairs={{16,0},{32,16},{48,32},{64,48},{80,64},{96,80},{112,96},{128,112},... | collective-permute-start | bytes 73736 | tf_op jit(solution)/shard_map/ppermute | solution.py:17
  17.5 8.8 %collective-permute-start = (bf16[96,1,8,16]{0,3,2,1:T(8,128)(2,1)S(1)}, bf16[96,1,8,16]{0,3,2,1:T(8,128)(2,1)S(1)}, u32[]{:S(2)}, u32[]{:S(2)}) collective-permute-start(bf16[96,1,8,16]{0,3,2,1:T(8,128)(2,1)S(1)} %get-tuple-element.142), channel_id=1, source_target_pairs={{0,16},{16,32},{32,48},{48,64},{64,80},{80,96},{96,112},{112,128},... | collective-permute-start | bytes 73736 | tf_op jit(solution)/shard_map/ppermute | solution.py:14
  19.5 12.3 %copy-start.44 = (f32[128]{0:T(128)}, f32[128]{0:T(128)S(1)}, u32[]{:S(2)}) copy-start(f32[128]{0:T(128)S(1)} %mul.154) | copy-start | bytes 1540
  19.6 17.2 %copy-start.11 = (bf16[96,8,128]{0,2,1:T(8,128)(2,1)}, bf16[96,8,128]{0,2,1:T(8,128)(2,1)S(1)}, u32[]{:S(2)}) copy-start(bf16[96,8,128]{0,2,1:T(8,128)(2,1)S(1)} %multiply_convert_fusion.6) | copy-start | bytes 589828
  19.7 20.6 %copy-start.46 = (f32[1024]{0:T(1024)}, f32[1024]{0:T(1024)S(1)}, u32[]{:S(2)}) copy-start(f32[1024]{0:T(1024)S(1)} %mul.162) | copy-start | bytes 12292
  19.7 13.7 %copy-start.19 = (bf16[96,1,8,16]{0,3,2,1:T(8,128)(2,1)}, bf16[96,1,8,16]{0,3,2,1:T(8,128)(2,1)S(1)}, u32[]{:S(2)}) copy-start(bf16[96,1,8,16]{0,3,2,1:T(8,128)(2,1)S(1)} %collective-permute-done.1) | copy-start | bytes 73732
  26.3 7.2 %copy-start.22 = (bf16[96,1,8,16]{0,3,2,1:T(8,128)(2,1)}, bf16[96,1,8,16]{0,3,2,1:T(8,128)(2,1)S(1)}, u32[]{:S(2)}) copy-start(bf16[96,1,8,16]{0,3,2,1:T(8,128)(2,1)S(1)} %collective-permute-done) | copy-start | bytes 73732
  26.3 4.4 collective-permute-start.3
  27.6 3.9 collective-permute-start.2
  40.6 7.2 %copy-start.29 = (bf16[96,8,128]{2,1,0:T(8,128)(2,1)S(1)}, bf16[96,8,128]{2,1,0:T(8,128)(2,1)}, u32[]{:S(2)}) copy-start(bf16[96,8,128]{2,1,0:T(8,128)(2,1)} %param.9) | copy-start | bytes 589828
  41.1 8.9 %collective-permute-start.5 = (bf16[96,1,8,16]{0,3,2,1:T(8,128)(2,1)S(1)}, bf16[96,1,8,16]{0,3,2,1:T(8,128)(2,1)S(1)}, u32[]{:S(2)}, u32[]{:S(2)}) collective-permute-start(bf16[96,1,8,16]{0,3,2,1:T(8,128)(2,1)S(1)} %get-tuple-element.139), channel_id=1, source_target_pairs={{16,0},{32,16},{48,32},{64,48},{80,64},{96,80},{112,96},{128,112},... | collective-permute-start | bytes 73736 | tf_op jit(solution)/shard_map/ppermute | solution.py:17
  43.0 9.6 %collective-permute-start.4 = (bf16[96,1,8,16]{0,3,2,1:T(8,128)(2,1)S(1)}, bf16[96,1,8,16]{0,3,2,1:T(8,128)(2,1)S(1)}, u32[]{:S(2)}, u32[]{:S(2)}) collective-permute-start(bf16[96,1,8,16]{0,3,2,1:T(8,128)(2,1)S(1)} %get-tuple-element.138), channel_id=1, source_target_pairs={{0,16},{16,32},{32,48},{48,64},{64,80},{80,96},{96,112},{112,128},... | collective-permute-start | bytes 73736 | tf_op jit(solution)/shard_map/ppermute | solution.py:14
  48.1 9.1 %copy-start.7 = (bf16[96,8,128]{0,2,1:T(8,128)(2,1)}, bf16[96,8,128]{0,2,1:T(8,128)(2,1)S(1)}, u32[]{:S(2)}) copy-start(bf16[96,8,128]{0,2,1:T(8,128)(2,1)S(1)} %copy.33) | copy-start | bytes 589828
  48.1 11.0 %copy-start.2 = (f32[96,8,128]{0,2,1:T(8,128)}, f32[96,8,128]{0,2,1:T(8,128)S(1)}, u32[]{:S(2)}) copy-start(f32[96,8,128]{0,2,1:T(8,128)S(1)} %convert_element_type.122) | copy-start | bytes 1179652
  50.0 34.6 %copy-start.13 = (bf16[96,1,8,16]{0,3,2,1:T(8,128)(2,1)}, bf16[96,1,8,16]{0,3,2,1:T(8,128)(2,1)S(1)}, u32[]{:S(2)}) copy-start(bf16[96,1,8,16]{0,3,2,1:T(8,128)(2,1)S(1)} %collective-permute-done.5) | copy-start | bytes 73732
  52.6 4.6 %collective-permute-start.7 = (bf16[96,10,1,16]{0,3,2,1:T(8,128)(2,1)S(1)}, bf16[96,10,1,16]{0,3,2,1:T(8,128)(2,1)S(1)}, u32[]{:S(2)}, u32[]{:S(2)}) collective-permute-start(bf16[96,10,1,16]{0,3,2,1:T(8,128)(2,1)S(1)} %get-tuple-element.123), channel_id=1, source_target_pairs={{1,0},{2,1},{3,2},{4,3},{5,4},{6,5},{7,6},{8,7},{9,8},{10,9},{11,1... | collective-permute-start | bytes 92168 | tf_op jit(solution)/shard_map/ppermute | solution.py:17
  53.9 3.9 collective-permute-start.6
  67.7 9.0 %copy-start.17 = (bf16[96,1,8,16]{0,3,2,1:T(8,128)(2,1)S(1)}, bf16[96,1,8,16]{0,3,2,1:T(8,128)(2,1)}, u32[]{:S(2)}) copy-start(bf16[96,1,8,16]{0,3,2,1:T(8,128)(2,1)} %copy-done.15) | copy-start | bytes 73732
  67.7 9.0 %copy-start.34 = (bf16[96,10,1,16]{0,3,2,1:T(8,128)(2,1)S(1)}, bf16[96,10,1,16]{0,3,2,1:T(8,128)(2,1)}, u32[]{:S(2)}) copy-start(bf16[96,10,1,16]{0,3,2,1:T(8,128)(2,1)} %copy-done.33) | copy-start | bytes 92164
  69.9 17.2 %collective-permute-start.9 = (bf16[96,1,8,16]{0,3,2,1:T(8,128)(2,1)S(1)}, bf16[96,1,8,16]{0,3,2,1:T(8,128)(2,1)S(1)}, u32[]{:S(2)}, u32[]{:S(2)}) collective-permute-start(bf16[96,1,8,16]{0,3,2,1:T(8,128)(2,1)S(1)} %get-tuple-element.135), channel_id=1, source_target_pairs={{16,0},{32,16},{48,32},{64,48},{80,64},{96,80},{112,96},{128,112},... | collective-permute-start | bytes 73736 | tf_op jit(solution)/shard_map/ppermute | solution.py:17
  71.9 15.3 %collective-permute-start.8 = (bf16[96,1,8,16]{0,3,2,1:T(8,128)(2,1)S(1)}, bf16[96,1,8,16]{0,3,2,1:T(8,128)(2,1)S(1)}, u32[]{:S(2)}, u32[]{:S(2)}) collective-permute-start(bf16[96,1,8,16]{0,3,2,1:T(8,128)(2,1)S(1)} %get-tuple-element.134), channel_id=1, source_target_pairs={{0,16},{16,32},{32,48},{48,64},{64,80},{80,96},{96,112},{112,128},... | collective-permute-start | bytes 73736 | tf_op jit(solution)/shard_map/ppermute | solution.py:14
  87.2 5.9 %collective-permute-start.11 = (bf16[96,10,1,16]{0,3,2,1:T(8,128)(2,1)S(1)}, bf16[96,10,1,16]{0,3,2,1:T(8,128)(2,1)S(1)}, u32[]{:S(2)}, u32[]{:S(2)}) collective-permute-start(bf16[96,10,1,16]{0,3,2,1:T(8,128)(2,1)S(1)} %get-tuple-element.119), channel_id=1, source_target_pairs={{1,0},{2,1},{3,2},{4,3},{5,4},{6,5},{7,6},{8,7},{9,8},{10,9},{11,1... | collective-permute-start | bytes 92168 | tf_op jit(solution)/shard_map/ppermute | solution.py:17
  88.5 5.1 %collective-permute-start.10 = (bf16[96,10,1,16]{0,3,2,1:T(8,128)(2,1)S(1)}, bf16[96,10,1,16]{0,3,2,1:T(8,128)(2,1)S(1)}, u32[]{:S(2)}, u32[]{:S(2)}) collective-permute-start(bf16[96,10,1,16]{0,3,2,1:T(8,128)(2,1)S(1)} %get-tuple-element.118), channel_id=1, source_target_pairs={{0,1},{1,2},{2,3},{3,4},{4,5},{5,6},{6,7},{7,8},{8,9},{9,10},{10,1... | collective-permute-start | bytes 92168 | tf_op jit(solution)/shard_map/ppermute | solution.py:14
  104.9 8.6 %copy-start.20 = (bf16[96,1,8,16]{0,3,2,1:T(8,128)(2,1)S(1)}, bf16[96,1,8,16]{0,3,2,1:T(8,128)(2,1)}, u32[]{:S(2)}) copy-start(bf16[96,1,8,16]{0,3,2,1:T(8,128)(2,1)} %copy-done.19) | copy-start | bytes 73732
  104.9 8.6 %copy-start.23 = (bf16[96,1,8,16]{0,3,2,1:T(8,128)(2,1)S(1)}, bf16[96,1,8,16]{0,3,2,1:T(8,128)(2,1)}, u32[]{:S(2)}) copy-start(bf16[96,1,8,16]{0,3,2,1:T(8,128)(2,1)} %copy-done.22) | copy-start | bytes 73732
  104.9 8.6 %copy-start.39 = (bf16[96,10,1,16]{0,3,2,1:T(8,128)(2,1)S(1)}, bf16[96,10,1,16]{0,3,2,1:T(8,128)(2,1)}, u32[]{:S(2)}) copy-start(bf16[96,10,1,16]{0,3,2,1:T(8,128)(2,1)} %copy-done.38) | copy-start | bytes 92164
  106.7 33.0 %collective-permute-start.13 = (bf16[96,1,8,16]{0,3,2,1:T(8,128)(2,1)}, bf16[96,1,8,16]{0,3,2,1:T(8,128)(2,1)}, u32[]{:S(2)}, u32[]{:S(2)}) collective-permute-start(bf16[96,1,8,16]{0,3,2,1:T(8,128)(2,1)} %get-tuple-element.131), channel_id=1, source_target_pairs={{16,0},{32,16},{48,32},{64,48},{80,64},{96,80},{112,96},{128,112},... | collective-permute-start | bytes 73736 | tf_op jit(solution)/shard_map/ppermute | solution.py:17
  111.0 28.7 %collective-permute-start.12 = (bf16[96,1,8,16]{0,3,2,1:T(8,128)(2,1)}, bf16[96,1,8,16]{0,3,2,1:T(8,128)(2,1)}, u32[]{:S(2)}, u32[]{:S(2)}) collective-permute-start(bf16[96,1,8,16]{0,3,2,1:T(8,128)(2,1)} %get-tuple-element.130), channel_id=1, source_target_pairs={{0,16},{16,32},{32,48},{48,64},{64,80},{80,96},{96,112},{112,128},... | collective-permute-start | bytes 73736 | tf_op jit(solution)/shard_map/ppermute | solution.py:14
  140.4 7.5 %collective-permute-start.15 = (bf16[96,10,1,16]{0,3,2,1:T(8,128)(2,1)S(1)}, bf16[96,10,1,16]{0,3,2,1:T(8,128)(2,1)S(1)}, u32[]{:S(2)}, u32[]{:S(2)}) collective-permute-start(bf16[96,10,1,16]{0,3,2,1:T(8,128)(2,1)S(1)} %get-tuple-element.115), channel_id=1, source_target_pairs={{1,0},{2,1},{3,2},{4,3},{5,4},{6,5},{7,6},{8,7},{9,8},{10,9},{11,1... | collective-permute-start | bytes 92168 | tf_op jit(solution)/shard_map/ppermute | solution.py:17
  141.7 6.2 %collective-permute-start.14 = (bf16[96,10,1,16]{0,3,2,1:T(8,128)(2,1)S(1)}, bf16[96,10,1,16]{0,3,2,1:T(8,128)(2,1)S(1)}, u32[]{:S(2)}, u32[]{:S(2)}) collective-permute-start(bf16[96,10,1,16]{0,3,2,1:T(8,128)(2,1)S(1)} %get-tuple-element.114), channel_id=1, source_target_pairs={{0,1},{1,2},{2,3},{3,4},{4,5},{5,6},{6,7},{7,8},{8,9},{9,10},{10,1... | collective-permute-start | bytes 92168 | tf_op jit(solution)/shard_map/ppermute | solution.py:14
  (33 other events, 54.2 us)
Sparse Core Ops, SparseCore 0:
  174.0 270.1 all-reduce.8
where the time goes:
time: 455 us; the launch traced here: 454 us
  waiting for transfers between devices  280 us (62%)
  matrix products  74.2 us (16%)
  starting transfers between devices  51.6 us (11%)
  local copies, waits for them, and re-layouts  22 us (5%)
  between operations  15.2 us (3%)
  other arithmetic  11.1 us (2%)
    unnamed x2, waiting for transfers between devices  269 us
    dot_general x54, matrix products, grad_window(): lax.dot_general(piece, flat, (((1,), (1,)), ((), ())), preferred_element_...  47.2 us
    ppermute x8, starting transfers between devices, padded_2(): lax.ppermute(lax.slice_in_dim(block, block.shape[dim] - width, None, axis...  30.1 us
    dot_general x108, matrix products, conv_window(): jnp.dot(matrix, shifted(window, offset, transposed, width_x, width_y, dep...  27.1 us
    ppermute x8, starting transfers between devices, padded_2(): lax.ppermute(lax.slice_in_dim(block, 0, width, axis=dim), axis, backward)  21.5 us
    ppermute x8, waiting for transfers between devices, padded_2(): lax.ppermute(lax.slice_in_dim(block, block.shape[dim] - width, None, axis...  11 us
  transfers between devices with their start and end apart: 17, of which 6 were waited for; matrix products, arithmetic and copies ran while one was open for 9% of the time, Pallas kernels for 0%

commit v1 on v0

v1 whole, which is shorter than its diff:
```python
import math

import jax
import jax.numpy as jnp
from jax import lax
from jax.experimental import pallas as pl
from jax.experimental.pallas import tpu as pltpu
from jax.sharding import PartitionSpec as P

BOTH = ("east", "north")
F32 = jnp.float32
BF16 = jnp.bfloat16
CH = 96
LN = 128
TAPS = 9 * LN


def flip_pad(value):
    wide = jnp.concatenate(
        [value.astype(F32), jnp.zeros((LN - value.shape[0], value.shape[1]), F32)], axis=0
    )
    return wide.T


def weights_kernel(first, second, fwd_one, fwd_two, back_two, back_one):
    for out in (fwd_one, fwd_two, back_two, back_one):
        out[...] = jnp.zeros_like(out)

    def body(tap, carry):
        plane = tap // 9
        row = pl.multiple_of((tap % 9) * LN, LN)
        for source, ahead, back in ((first, fwd_one, back_one), (second, fwd_two, back_two)):
            ahead[plane + 1, pl.ds(row, CH), 0:CH] = source[tap]
            turned = jnp.pad(source[26 - tap].astype(F32), ((0, LN - CH), (0, LN - CH))).T
            back[plane + 1, pl.ds(row, LN), :] = turned.astype(BF16)
        return carry

    lax.fori_loop(0, 27, body, 0)


def spread(taps, plane_hi, plane_lo, value, rows):
    count = rows + 32
    level = lax.broadcasted_iota(jnp.int32, (count, LN), 0) & 15
    below = jnp.where(level == 0, 0.0, pltpu.roll(value, 1, 0))
    above = jnp.where(level == 15, 0.0, pltpu.roll(value, count - 1, 0))
    for c, moved in enumerate((below, value, above)):
        short = moved.astype(BF16)
        for b in range(3):
            lane = (3 * b + c) * LN
            taps[plane_hi, plane_lo, 0:rows, lane : lane + LN] = short[16 * b : 16 * b + rows]


def convolve(taps, weight, total, pairs, rows):
    size = pairs * rows
    for j in range(4):
        left = taps[j // 2 : j // 2 + pairs, j % 2, 0:rows, :].reshape(size, TAPS)
        right = jnp.concatenate([weight[j + 1], weight[j]], axis=1)
        part = jnp.dot(left, right, preferred_element_type=F32)
        if j == 0:
            total[0:size, :] = part
        else:
            total[0:size, :] += part


def kernel_grad(turned, planes, shift, scale, result):
    def piece(k):
        a, b = k // 3, k % 3
        start = (shift + 1 - b) * 16
        return planes[shift + 1 - a : shift + 9 - a, start : start + 128, :].reshape(1024, LN)

    for k in range(0, 9, 2):
        right = jnp.concatenate([piece(k), piece(min(k + 1, 8))], axis=1)
        part = jnp.dot(turned[...], right, preferred_element_type=F32) * scale
        result[k * 288 : k * 288 + 288, :] = part[:, 0:LN]
        if k < 8:
            result[(k + 1) * 288 : (k + 1) * 288 + 288, :] = part[:, LN : 2 * LN]


def turn_own(taps, first_plane, first_row, turned):
    for x in range(8):
        p = first_plane + x
        for c in range(3):
            lane = (3 + c) * LN
            block = taps[p // 2, p % 2, first_row : first_row + 128, lane : lane + LN]
            turned[c * CH : (c + 1) * CH, x * 128 : x * 128 + 128] = (
                block.astype(F32).T[0:CH].astype(BF16)
            )


def main_kernel(
    scale,
    place,
    feat,
    cot,
    west,
    east,
    south,
    north,
    own_mask,
    fwd_one,
    fwd_two,
    back_two,
    back_one,
    activated,
    feature_grad,
    keep,
    send,
    taps,
    grid,
    upstream,
    total,
    slope_one,
    planes,
    turned_one,
    turned_two,
    masks,
    grad_one_sum,
    grad_two_sum,
):
    has = [place[k].astype(F32) for k in range(4)]

    def mask_rows(ref, row):
        tile = ref[row : row + 16, :].astype(F32)
        return jnp.concatenate([tile] * 8, axis=0).T

    middle = [mask_rows(west, 576) * has[0], mask_rows(own_mask, 0), mask_rows(east, 576) * has[1]]
    for bx in range(3):
        side = 1.0 if bx == 1 else has[0] if bx == 0 else has[1]
        masks[bx, 0:64, :] = mask_rows(south, 1056 + 16 * bx)[0:64] * (has[2] * side)
        masks[bx, 64:192, :] = middle[bx]
        masks[bx, 192:256, :] = mask_rows(north, 1056 + 16 * bx)[0:64] * (has[3] * side)

    for p in range(16):
        if p < 4:
            block = west[p * CH : (p + 1) * CH, :]
        elif p < 12:
            block = feat[p - 4]
        else:
            block = east[(p - 12) * CH : (p - 11) * CH, :]
        grid[p, 64:192, :] = flip_pad(block)
    for k in range(8):
        for ref, row in ((south, 0), (north, 192)):
            both = flip_pad(ref[k * CH : (k + 1) * CH, :])
            grid[k, row : row + 64, :] = both[0:64]
            grid[k + 8, row : row + 64, :] = both[64:128]
    for p in range(12):
        if p < 2:
            block = west[384 + p * CH : 384 + (p + 1) * CH, :]
        elif p < 10:
            block = cot[p - 2]
        else:
            block = east[384 + (p - 10) * CH : 384 + (p - 9) * CH, :]
        upstream[p, 32:160, :] = flip_pad(block)
    for k in range(3):
        for ref, row in ((south, 0), (north, 160)):
            four = flip_pad(ref[768 + k * CH : 768 + (k + 1) * CH, :])
            for q in range(4):
                upstream[k + 3 * q, row : row + 32, :] = four[32 * q : 32 * q + 32]

    def band(p, low, high):
        return (p >= low).astype(jnp.int32) + (p >= high).astype(jnp.int32)

    def start(p, carry):
        spread(taps, p // 2, p % 2, grid[p] * masks[band(p, 4, 12)], 224)
        return carry

    lax.fori_loop(0, 16, start, 0)
    turn_own(taps, 4, 48, turned_one)
    convolve(taps, fwd_one, total, 7, 224)

    def after_one(i, carry):
        for half in range(2):
            p = 2 * i + half
            value = total[pl.ds(pl.multiple_of(i * 224, 16), 224), half * LN : half * LN + LN]
            value = value * masks[band(p, 3, 11), 16:240, :]
            sigma = jax.nn.sigmoid(value)
            slope_one[p] = (sigma * (1.0 + value * (1.0 - sigma)))[32:192]
            spread(taps, i, half, value * sigma, 192)
        return carry

    lax.fori_loop(0, 7, after_one, 0)
    turn_own(taps, 3, 32, turned_two)
    convolve(taps, fwd_two, total, 6, 192)

    def after_two(i, carry):
        for half in range(2):
            p = 2 * i + half
            value = total[pl.ds(pl.multiple_of(i * 192, 16), 192), half * LN : half * LN + LN]
            mask = masks[band(p, 2, 10), 32:224, :]
            value = value * mask
            sigma = jax.nn.sigmoid(value)

            @pl.when((p >= 2) & (p < 10))
            def _():
                activated[p - 2] = (value * sigma)[32:160].T[0:CH].astype(BF16)

            slope = sigma * (1.0 + value * (1.0 - sigma))
            grad = upstream[p] * slope * mask
            planes[p] = grad.astype(BF16)
            spread(taps, i, half, grad, 160)
        return carry

    lax.fori_loop(0, 6, after_two, 0)
    kernel_grad(turned_two, planes, 2, scale, grad_two_sum)
    convolve(taps, back_two, total, 5, 160)

    def after_three(i, carry):
        for half in range(2):
            p = 2 * i + half
            value = total[pl.ds(pl.multiple_of(i * 160, 16), 160), half * LN : half * LN + LN]
            grad = value * slope_one[p + 2] * masks[band(p, 1, 9), 48:208, :]
            planes[p, 0:160, :] = grad.astype(BF16)
            spread(taps, i, half, grad, 128)
        return carry

    lax.fori_loop(0, 5, after_three, 0)
    kernel_grad(turned_one, planes, 1, scale, grad_one_sum)
    convolve(taps, back_one, total, 4, 128)
    for p in range(8):
        i, half = p // 2, p % 2
        value = total[i * 128 : i * 128 + 128, half * LN : half * LN + LN] * masks[1, 64:192, :]
        feature_grad[p] = value.T[0:CH].astype(BF16)

    me = place[4]
    for out, low in ((keep, 0), (send, 1)):
        for e in range(4):
            j = jnp.bitwise_xor(me, 2 * e + low)

            def pack(g, carry):
                row = 81 * g + 10 * j
                one = grad_one_sum[pl.ds(row, 16), 0:CH]
                two = grad_two_sum[pl.ds(row, 16), 0:CH]
                out[e, g, 0:16, :] = one.astype(BF16)
                out[e, g, 16:32, :] = two.astype(BF16)
                return carry

            lax.fori_loop(0, 32, pack, 0)


def shift_by(step, axis):
    count = lax.axis_size(axis)
    return [(i, (i + step) % count) for i in range(count)]


def swap(value, bits):
    count = lax.axis_size("east") * lax.axis_size("north")
    return lax.ppermute(value, BOTH, [(i, i ^ bits) for i in range(count)])


def local(features, occupancy, weight_first, weight_second, cotangent):
    column = lax.axis_index("east")
    row = lax.axis_index("north")
    position = column * 16 + row
    voxel_total = 16 * 8 * 16 * 8 * 16
    scale = 1.0 / math.sqrt(voxel_total)

    feat = jnp.transpose(features, (1, 0, 2))
    cot = jnp.transpose(cotangent, (1, 0, 2))
    levels = jnp.repeat(occupancy.reshape(-1), 8).astype(BF16)
    own_mask = jnp.broadcast_to(jnp.tile(levels, 8)[None, :], (16, LN))

    def strip(f, c):
        return jnp.concatenate([f.reshape(-1, LN), c.reshape(-1, LN), own_mask], axis=0)

    west = lax.ppermute(strip(feat[4:8], cot[6:8]), "east", shift_by(1, "east"))
    east = lax.ppermute(strip(feat[0:4], cot[0:2]), "east", shift_by(-1, "east"))

    vmem = pl.BlockSpec(memory_space=pltpu.VMEM)
    packed = jax.ShapeDtypeStruct((5, TAPS, LN), BF16)
    weights = pl.pallas_call(
        weights_kernel,
        out_shape=[packed] * 4,
        in_specs=[vmem] * 2,
        out_specs=[vmem] * 4,
        compiler_params=pltpu.CompilerParams(vmem_limit_bytes=32 << 20),
        cost_estimate=pl.CostEstimate(flops=1 << 20, bytes_accessed=8 << 20, transcendentals=0),
        name="weights",
    )(weight_first, weight_second)

    all_feat = jnp.concatenate(
        [west[0:384].reshape(4, CH, LN), feat, east[0:384].reshape(4, CH, LN)], axis=0
    )
    all_cot = jnp.concatenate(
        [west[384:576].reshape(2, CH, LN), cot, east[384:576].reshape(2, CH, LN)], axis=0
    )
    all_mask = [west[576:592], own_mask, east[576:592]]

    def edge(at_feat, at_cot):
        f = all_feat[:, :, at_feat : at_feat + 64]
        f = jnp.concatenate([f[0:8], f[8:16]], axis=2)
        c = all_cot[:, :, at_cot : at_cot + 32]
        c = jnp.concatenate([c[0:3], c[3:6], c[6:9], c[9:12]], axis=2)
        return jnp.concatenate([f.reshape(-1, LN), c.reshape(-1, LN)] + all_mask, axis=0)

    south = lax.ppermute(edge(64, 96), "north", shift_by(1, "north"))
    north = lax.ppermute(edge(0, 0), "north", shift_by(-1, "north"))

    place = jnp.stack(
        [column > 0, column < 15, row > 0, row < 15, position % 8]
    ).astype(jnp.int32)
    image = jax.ShapeDtypeStruct((8, CH, LN), BF16)
    pieces = jax.ShapeDtypeStruct((4, 32, 32, CH), BF16)
    activated, feature_grad, keep, send = pl.pallas_call(
        lambda *refs: main_kernel(scale, *refs),
        out_shape=[image, image, pieces, pieces],
        in_specs=[pl.BlockSpec(memory_space=pltpu.SMEM)] + [vmem] * 11,
        out_specs=[vmem] * 4,
        scratch_shapes=[
            pltpu.VMEM((8, 2, 224, TAPS), BF16),
            pltpu.VMEM((16, 256, LN), F32),
            pltpu.VMEM((12, 192, LN), F32),
            pltpu.VMEM((7 * 224, 2 * LN), F32),
            pltpu.VMEM((14, 160, LN), F32),
            pltpu.VMEM((12, 192, LN), BF16),
            pltpu.VMEM((288, 1024), BF16),
            pltpu.VMEM((288, 1024), BF16),
            pltpu.VMEM((3, 256, LN), F32),
            pltpu.VMEM((2592 + 16, LN), F32),
            pltpu.VMEM((2592 + 16, LN), F32),
        ],
        compiler_params=pltpu.CompilerParams(vmem_limit_bytes=56 << 20),
        name="level",
    )(place, feat, cot, west, east, south, north, own_mask, *weights)

    def add(*terms):
        return sum(t.astype(F32) for t in terms).astype(BF16)

    part = add(keep, swap(send, 1))
    others = [swap(part[k], 2 * k) for k in (1, 2, 3)]
    part = add(part[0], *others)
    block = position // 8
    for bit in (1, 8, 16, 2, 4):
        count = part.shape[0]
        inner = {1: 1, 8: 4, 16: 4, 2: 1, 4: 1}[bit]
        half = part.reshape((count // (2 * inner), 2, inner) + part.shape[1:])
        mine = (block // bit) % 2
        held = lax.dynamic_index_in_dim(half, mine, 1, keepdims=False)
        given = lax.dynamic_index_in_dim(half, 1 - mine, 1, keepdims=False)
        part = add(held, swap(given, 8 * bit)).reshape((count // 2,) + part.shape[1:])
    flat = part[0].astype(F32)

    def own_share(rows):
        return lax.dynamic_slice_in_dim(rows[0:12].reshape(-1), 12 * (position % 8), 972)

    return (
        jnp.transpose(activated, (1, 0, 2)).reshape(CH, 8, LN),
        jnp.transpose(feature_grad, (1, 0, 2)).reshape(CH, 8, LN),
        own_share(flat[0:16]),
        own_share(flat[16:32]),
    )


def solution(mesh):
    return jax.shard_map(
        local,
        mesh=mesh,
        in_specs=(
            P(None, "east", "north"),
            P("east", "north", None),
            P(),
            P(),
            P(None, "east", "north"),
        ),
        out_specs=(
            P(None, "east", "north"),
            P(None, "east", "north"),
            P(BOTH),
            P(BOTH),
        ),
        check_vma=False,
    )
```

time: 455 us -> 120 us (0.26)
  waiting for transfers between devices: 280 us -> 36.6 us
  matrix products: 74.2 us -> 0 us
  Pallas kernels: 0 us -> 40.3 us
  starting transfers between devices: 51.6 us -> 27.1 us
  between operations: 15.2 us -> 0.96 us
  local copies, waits for them, and re-layouts: 22 us -> 11.6 us
  other arithmetic: 11.1 us -> 3.07 us
    unnamed x2 -> x0, waiting for transfers between devices: 269 us -> none
    dot_general x162 -> x0, matrix products: 74.2 us -> none  [the longest x54 47.2 us: grad_window(): lax.dot_general(piece, flat, (((1,), (1,)), ((), ())), preferred_element_...]
    pallas_call x0 -> x2, Pallas kernels: none -> 40.3 us  [the longest x1 36.5 us: local(): pl.pallas_call(lambda *refs: main_kernel(scale, *refs), out_shape=[image,...]
    ppermute x16 -> x13, waiting for transfers between devices: 11 us -> 36.6 us  [the longest x9 28.4 us: swap(): return lax.ppermute(value, BOTH, [(i, i ^ bits) for i in range(count)])]
    ppermute x16 -> x13, starting transfers between devices: 51.5 us -> 27.1 us  [the longest x9 16.7 us: swap(): return lax.ppermute(value, BOTH, [(i, i ^ bits) for i in range(count)])]
    slice x15 -> x8, local copies, waits for them, and re-layouts: 5.81 us -> 0.16 us  [the longest x1 0.11 us: edge(): c = jnp.concatenate([c[0:3], c[3:6], c[6:9], c[9:12]], axis=2)]
  transfers between devices with their start and end apart: 17 -> 13, of which waited for: 6 -> 10; matrix products, arithmetic and copies ran while one was open for 9% -> 2% of each run, Pallas kernels for 0% -> 3%
where the time goes in v1:
time: 120 us
  Pallas kernels  40.3 us (34%)
  waiting for transfers between devices  36.6 us (30%)
  starting transfers between devices  27.1 us (23%)
  local copies, waits for them, and re-layouts  11.6 us (10%)
  other arithmetic  3.07 us (3%)
    pallas_call x1, Pallas kernels, local(): pl.pallas_call(lambda *refs: main_kernel(scale, *refs), out_shape=[image,...  36.5 us
    ppermute x9, waiting for transfers between devices, swap(): return lax.ppermute(value, BOTH, [(i, i ^ bits) for i in range(count)])  28.4 us
    ppermute x9, starting transfers between devices, swap(): return lax.ppermute(value, BOTH, [(i, i ^ bits) for i in range(count)])  16.7 us
    unnamed x39, local copies, waits for them, and re-layouts  9.02 us
    ppermute x1, waiting for transfers between devices, local(): west = lax.ppermute(strip(feat[4:8], cot[6:8]), 'east', shift_by(1, 'east'))  4.32 us
    ppermute x1, waiting for transfers between devices, local(): lax.ppermute(strip(feat[0:4], cot[0:2]), 'east', shift_by(-1, 'east'))  3.85 us
    ppermute x1, starting transfers between devices, local(): north = lax.ppermute(edge(0, 0), 'north', shift_by(-1, 'north'))  3.84 us
    pallas_call x1, Pallas kernels, local(): pl.pallas_call(weights_kernel, out_shape=[packed] * 4, in_specs=[vmem] *...  3.8 us
  transfers between devices with their start and end apart: 13, of which 10 were waited for; matrix products, arithmetic and copies ran while one was open for 2% of the time, Pallas kernels for 3%

profile of v1, /device:TPU:2, one launch (start us, length us, event | category | flops | bytes accessed | tf_op | source)
XLA Modules:
  0.0 119.7 jit_solution(14213172216752892635)
XLA Ops:
  0.6 1.0 copy.30
  1.6 1.0 copy.29
  2.6 0.7 convert_bitcast_fusion
  3.7 3.3 %collective-permute-start = (bf16[592,128]{1,0:T(8,128)(2,1)S(1)}, bf16[592,128]{1,0:T(8,128)(2,1)S(1)}, u32[]{:S(2)}, u32[]{:S(2)}) collective-permute-start(bf16[592,128]{1,0:T(8,128)(2,1)S(1)} %get-tuple-element.58), channel_id=1, source_target_pairs={{0,16},{16,32},{32,48},{48,64},{64,80},{80,96},{96,112},{112,128},... | collective-permute-start | bytes 454664 | tf_op jit(solution)/shard_map/ppermute | solution.py:265
  7.0 3.1 %collective-permute-start.1 = (bf16[592,128]{1,0:T(8,128)(2,1)S(1)}, bf16[592,128]{1,0:T(8,128)(2,1)S(1)}, u32[]{:S(2)}, u32[]{:S(2)}) collective-permute-start(bf16[592,128]{1,0:T(8,128)(2,1)S(1)} %get-tuple-element.57), channel_id=1, source_target_pairs={{0,240},{16,0},{32,16},{48,32},{64,48},{80,64},{96,80},{112,96},{1... | collective-permute-start | bytes 454664 | tf_op jit(solution)/shard_map/ppermute | solution.py:266
  10.2 4.3 %collective-permute-done.refs_3_ = bf16[592,128]{1,0:T(8,128)(2,1)S(1)} collective-permute-done((bf16[592,128]{1,0:T(8,128)(2,1)S(1)}, bf16[592,128]{1,0:T(8,128)(2,1)S(1)}, u32[]{:S(2)}, u32[]{:S(2)}) %collective-permute-start) | collective-permute-done | bytes 151584 | tf_op jit(solution)/shard_map/ppermute | solution.py:265
  14.6 3.8 %collective-permute-done.1.refs_4_ = bf16[592,128]{1,0:T(8,128)(2,1)S(1)} collective-permute-done((bf16[592,128]{1,0:T(8,128)(2,1)S(1)}, bf16[592,128]{1,0:T(8,128)(2,1)S(1)}, u32[]{:S(2)}, u32[]{:S(2)}) %collective-permute-start.1) | collective-permute-done | bytes 151584 | tf_op jit(solution)/shard_map/ppermute | solution.py:266
  19.4 3.8 %collective-permute-start.3 = (bf16[1104,128]{1,0:T(8,128)(2,1)S(1)}, bf16[1104,128]{1,0:T(8,128)(2,1)S(1)}, u32[]{:S(2)}, u32[]{:S(2)}) collective-permute-start(bf16[1104,128]{1,0:T(8,128)(2,1)S(1)} %get-tuple-element.51), channel_id=1, source_target_pairs={{0,15},{1,0},{2,1},{3,2},{4,3},{5,4},{6,5},{7,6},{8,7},{9,8},{10,9... | collective-permute-start | bytes 847880 | tf_op jit(solution)/shard_map/ppermute | solution.py:296
  23.8 3.8 %weights.1 = (bf16[5,1152,128]{2,1,0:T(8,128)(2,1)S(1)}, bf16[5,1152,128]{2,1,0:T(8,128)(2,1)S(1)}, bf16[5,1152,128]{2,1,0:T(8,128)(2,1)S(1)}, bf16[5,1152,128]{2,1,0:T(8,128)(2,1)S(1)}) custom-call(bf16[27,96,96]{2,1,0:T(8,128)(2,1)S(1)} %copy-done.4, bf16[27,96,96]{2,1,0:T(8,128)(2,1)S(1)} %copy-done.5), custom_call_target="tpu_custom_call" | custom-call | flops 1048576 | bytes 8388608 | tf_op jit(solution)/shard_map/weights/pallas_call | solution.py:270
  27.6 1.1 copy-done
  28.8 1.1 copy-done.1
  29.9 1.1 copy-done.2
  31.0 1.2 copy-done.3
  32.2 0.7 copy-done.10
  33.1 36.5 %level.1 = (bf16[8,96,128]{2,1,0:T(8,128)(2,1)}, bf16[8,96,128]{2,1,0:T(8,128)(2,1)}, bf16[4,32,32,96]{3,2,1,0:T(8,128)(2,1)}, bf16[4,32,32,96]{3,2,1,0:T(8,128)(2,1)}) custom-call(s32[5]{0:T(128)} %stack.39.refs_0_, bf16[8,96,128]{2,1,0:T(8,128)(2,1)} %bitcast.65, bf16[8,96,128]{2,1,0:T(8,128)(2,1)} %bitcast.69, bf16[592,128]{1,0:T(8,128)(2,1)} %copy-done.8, ...), custom_call_target="tpu_custom_call" | custom-call | tf_op jit(solution)/shard_map/level/pallas_call | solution.py:303
  69.6 2.9 %collective-permute-done.4 = bf16[4,32,32,96]{3,2,1,0:T(8,128)(2,1)S(1)} collective-permute-done((bf16[4,32,32,96]{3,2,1,0:T(8,128)(2,1)}, bf16[4,32,32,96]{3,2,1,0:T(8,128)(2,1)S(1)}, u32[]{:S(2)}, u32[]{:S(2)}) %collective-permute-start.4) | collective-permute-done | bytes 786464 | tf_op jit(solution)/shard_map/ppermute | solution.py:247
  72.5 1.5 %add_convert_fusion = bf16[4,32,32,96]{3,2,1,0:T(8,128)(2,1)S(1)} fusion(bf16[4,32,32,96]{3,2,1,0:T(8,128)(2,1)S(1)} %collective-permute-done.4, bf16[4,32,32,96]{3,2,1,0:T(8,128)(2,1)} %get-tuple-element.18), kind=kLoop, calls=%fused_computation | loop fusion | flops 1572864 | bytes 2359296 | tf_op jit(solution)/shard_map/convert_element_type | solution.py:326
  74.6 3.0 %collective-permute-start.5 = (bf16[32,32,96]{2,1,0:T(8,128)(2,1)S(1)}, bf16[32,32,96]{2,1,0:T(8,128)(2,1)S(1)}, u32[]{:S(2)}, u32[]{:S(2)}) collective-permute-start(bf16[32,32,96]{2,1,0:T(8,128)(2,1)S(1)} %get-tuple-element.36), channel_id=1, source_target_pairs={{0,2},{1,3},{2,0},{3,1},{4,6},{5,7},{6,4},{7,5},{8,10},{9,11},{10,... | collective-permute-start | bytes 589832 | tf_op jit(solution)/shard_map/ppermute | solution.py:247
  77.6 6.6 %collective-permute-done.7 = bf16[32,32,96]{2,1,0:T(8,128)(2,1)S(1)} collective-permute-done((bf16[32,32,96]{2,1,0:T(8,128)(2,1)S(1)}, bf16[32,32,96]{2,1,0:T(8,128)(2,1)S(1)}, u32[]{:S(2)}, u32[]{:S(2)}) %collective-permute-start.7) | collective-permute-done | bytes 196640 | tf_op jit(solution)/shard_map/ppermute | solution.py:247
  84.2 4.0 %collective-permute-done.6 = bf16[32,32,96]{2,1,0:T(8,128)(2,1)S(1)} collective-permute-done((bf16[32,32,96]{2,1,0:T(8,128)(2,1)S(1)}, bf16[32,32,96]{2,1,0:T(8,128)(2,1)S(1)}, u32[]{:S(2)}, u32[]{:S(2)}) %collective-permute-start.6) | collective-permute-done | bytes 196640 | tf_op jit(solution)/shard_map/ppermute | solution.py:247
  88.4 2.7 %collective-permute-start.8 = (bf16[16,1,32,96]{3,2,0,1:T(8,128)(2,1)S(1)}, bf16[16,1,32,96]{3,2,0,1:T(8,128)(2,1)S(1)}, u32[]{:S(2)}, u32[]{:S(2)}) collective-permute-start(bf16[16,1,32,96]{3,2,0,1:T(8,128)(2,1)S(1)} %dynamic-slice_bitcast_fusion), channel_id=1, source_target_pairs={{0,8},{1,9},{2,10},{3,11},{4,12},{5,13},{6,14},{7,15},{8,0},{9,1},... | collective-permute-start | bytes 294920 | tf_op jit(solution)/shard_map/ppermute | solution.py:247
  91.1 3.8 %collective-permute-done.8 = bf16[16,1,32,96]{3,2,0,1:T(8,128)(2,1)S(1)} collective-permute-done((bf16[16,1,32,96]{3,2,0,1:T(8,128)(2,1)S(1)}, bf16[16,1,32,96]{3,2,0,1:T(8,128)(2,1)S(1)}, u32[]{:S(2)}, u32[]{:S(2)}) %collective-permute-start.8) | collective-permute-done | bytes 98336 | tf_op jit(solution)/shard_map/ppermute | solution.py:247
  95.0 1.5 %collective-permute-start.9 = (bf16[2,4,32,96]{3,2,1,0:T(8,128)(2,1)S(1)}, bf16[2,4,32,96]{3,2,1,0:T(8,128)(2,1)S(1)}, u32[]{:S(2)}, u32[]{:S(2)}) collective-permute-start(bf16[2,4,32,96]{3,2,1,0:T(8,128)(2,1)S(1)} %dynamic-slice_bitcast_fusion.1), channel_id=1, source_target_pairs={{0,64},{1,65},{2,66},{3,67},{4,68},{5,69},{6,70},{7,71},{8,72},{9,... | collective-permute-start | bytes 147464 | tf_op jit(solution)/shard_map/ppermute | solution.py:247
  96.5 2.9 %collective-permute-done.9 = bf16[2,4,32,96]{3,2,1,0:T(8,128)(2,1)S(1)} collective-permute-done((bf16[2,4,32,96]{3,2,1,0:T(8,128)(2,1)S(1)}, bf16[2,4,32,96]{3,2,1,0:T(8,128)(2,1)S(1)}, u32[]{:S(2)}, u32[]{:S(2)}) %collective-permute-start.9) | collective-permute-done | bytes 49184 | tf_op jit(solution)/shard_map/ppermute | solution.py:247
  99.4 2.2 %collective-permute-start.10 = (bf16[1,4,32,96]{3,2,1,0:T(8,128)(2,1)S(1)}, bf16[1,4,32,96]{3,2,1,0:T(8,128)(2,1)S(1)}, u32[]{:S(2)}, u32[]{:S(2)}) collective-permute-start(bf16[1,4,32,96]{3,2,1,0:T(8,128)(2,1)S(1)} %constant_dynamic-slice_fusion.1), channel_id=1, source_target_pairs={{0,128},{1,129},{2,130},{3,131},{4,132},{5,133},{6,134},{7,135},{8... | collective-permute-start | bytes 73736 | tf_op jit(solution)/shard_map/ppermute | solution.py:247
  101.6 3.3 %collective-permute-done.10 = bf16[1,4,32,96]{3,2,1,0:T(8,128)(2,1)S(1)} collective-permute-done((bf16[1,4,32,96]{3,2,1,0:T(8,128)(2,1)S(1)}, bf16[1,4,32,96]{3,2,1,0:T(8,128)(2,1)S(1)}, u32[]{:S(2)}, u32[]{:S(2)}) %collective-permute-start.10) | collective-permute-done | bytes 24608 | tf_op jit(solution)/shard_map/ppermute | solution.py:247
  104.9 3.8 %collective-permute-start.11 = (bf16[2,1,32,96]{3,2,0,1:T(8,128)(2,1)S(1)}, bf16[2,1,32,96]{3,2,0,1:T(8,128)(2,1)S(1)}, u32[]{:S(2)}, u32[]{:S(2)}) collective-permute-start(bf16[2,1,32,96]{3,2,0,1:T(8,128)(2,1)S(1)} %dynamic-slice_bitcast_fusion.2), channel_id=1, source_target_pairs={{0,16},{1,17},{2,18},{3,19},{4,20},{5,21},{6,22},{7,23},{8,24},{9,... | collective-permute-start | bytes 36872 | tf_op jit(solution)/shard_map/ppermute | solution.py:247
  108.8 1.8 %collective-permute-done.11 = bf16[2,1,32,96]{3,2,0,1:T(8,128)(2,1)S(1)} collective-permute-done((bf16[2,1,32,96]{3,2,0,1:T(8,128)(2,1)S(1)}, bf16[2,1,32,96]{3,2,0,1:T(8,128)(2,1)S(1)}, u32[]{:S(2)}, u32[]{:S(2)}) %collective-permute-start.11) | collective-permute-done | bytes 12320 | tf_op jit(solution)/shard_map/ppermute | solution.py:247
  110.6 2.9 %collective-permute-start.12 = (bf16[1,1,32,96]{3,2,0,1:T(8,128)(2,1)S(1)}, bf16[1,1,32,96]{3,2,0,1:T(8,128)(2,1)S(1)}, u32[]{:S(2)}, u32[]{:S(2)}) collective-permute-start(bf16[1,1,32,96]{3,2,0,1:T(8,128)(2,1)S(1)} %constant_dynamic-slice_fusion), channel_id=1, source_target_pairs={{0,32},{1,33},{2,34},{3,35},{4,36},{5,37},{6,38},{7,39},{8,40},{9,... | collective-permute-start | bytes 18440 | tf_op jit(solution)/shard_map/ppermute | solution.py:247
  113.5 0.8 copy.24
  114.2 0.8 copy.25
  115.0 3.2 %collective-permute-done.12 = bf16[1,1,32,96]{3,2,0,1:T(8,128)(2,1)S(1)} collective-permute-done((bf16[1,1,32,96]{3,2,0,1:T(8,128)(2,1)S(1)}, bf16[1,1,32,96]{3,2,0,1:T(8,128)(2,1)S(1)}, u32[]{:S(2)}, u32[]{:S(2)}) %collective-permute-start.12) | collective-permute-done | bytes 6176 | tf_op jit(solution)/shard_map/ppermute | solution.py:247
  (73 shorter events, 4.4 us)
Async XLA Ops:
  1.6 17.0 %copy-start.6 = (bf16[96,8,128]{2,0,1:T(8,128)(2,1)}, bf16[96,8,128]{2,0,1:T(8,128)(2,1)S(1)}, u32[]{:S(2)}) copy-start(bf16[96,8,128]{2,0,1:T(8,128)(2,1)S(1)} %copy.30) | copy-start | bytes 589828
  2.6 16.3 %copy-start.7 = (bf16[96,8,128]{2,0,1:T(8,128)(2,1)}, bf16[96,8,128]{2,0,1:T(8,128)(2,1)S(1)}, u32[]{:S(2)}) copy-start(bf16[96,8,128]{2,0,1:T(8,128)(2,1)S(1)} %copy.29) | copy-start | bytes 589828
  3.6 15.1 %copy-start.14 = (bf16[16,128]{1,0:T(8,128)(2,1)}, bf16[16,128]{1,0:T(8,128)(2,1)S(1)}, u32[]{:S(2)}) copy-start(bf16[16,128]{1,0:T(8,128)(2,1)S(1)} %broadcast_in_dim.12.refs_7_) | copy-start | bytes 12292
  3.7 10.9 %collective-permute-start = (bf16[592,128]{1,0:T(8,128)(2,1)S(1)}, bf16[592,128]{1,0:T(8,128)(2,1)S(1)}, u32[]{:S(2)}, u32[]{:S(2)}) collective-permute-start(bf16[592,128]{1,0:T(8,128)(2,1)S(1)} %get-tuple-element.58), channel_id=1, source_target_pairs={{0,16},{16,32},{32,48},{48,64},{64,80},{80,96},{96,112},{112,128},... | collective-permute-start | bytes 454664 | tf_op jit(solution)/shard_map/ppermute | solution.py:265
  7.0 11.4 %collective-permute-start.1 = (bf16[592,128]{1,0:T(8,128)(2,1)S(1)}, bf16[592,128]{1,0:T(8,128)(2,1)S(1)}, u32[]{:S(2)}, u32[]{:S(2)}) collective-permute-start(bf16[592,128]{1,0:T(8,128)(2,1)S(1)} %get-tuple-element.57), channel_id=1, source_target_pairs={{0,240},{16,0},{32,16},{48,32},{64,48},{80,64},{96,80},{112,96},{1... | collective-permute-start | bytes 454664 | tf_op jit(solution)/shard_map/ppermute | solution.py:266
  14.5 4.7 %copy-start.8 = (bf16[592,128]{1,0:T(8,128)(2,1)}, bf16[592,128]{1,0:T(8,128)(2,1)S(1)}, u32[]{:S(2)}) copy-start(bf16[592,128]{1,0:T(8,128)(2,1)S(1)} %collective-permute-done.refs_3_) | copy-start | bytes 454660
  18.4 0.9 copy-start.9
  18.7 5.1 %copy-start.4 = (bf16[27,96,96]{2,1,0:T(8,128)(2,1)S(1)}, bf16[27,96,96]{2,1,0:T(8,128)(2,1)}, u32[]{:S(2)}) copy-start(bf16[27,96,96]{2,1,0:T(8,128)(2,1)} %first.1) | copy-start | bytes 1492996
  18.8 5.1 %copy-start.5 = (bf16[27,96,96]{2,1,0:T(8,128)(2,1)S(1)}, bf16[27,96,96]{2,1,0:T(8,128)(2,1)}, u32[]{:S(2)}) copy-start(bf16[27,96,96]{2,1,0:T(8,128)(2,1)} %second.1) | copy-start | bytes 1492996
  19.3 12.9 %collective-permute-start.2 = (bf16[1104,128]{1,0:T(8,128)(2,1)S(1)}, bf16[1104,128]{1,0:T(8,128)(2,1)S(1)}, u32[]{:S(2)}, u32[]{:S(2)}) collective-permute-start(bf16[1104,128]{1,0:T(8,128)(2,1)S(1)} %get-tuple-element.52), channel_id=1, source_target_pairs={{0,1},{1,2},{2,3},{3,4},{4,5},{5,6},{6,7},{7,8},{8,9},{9,10},{10,1... | collective-permute-start | bytes 847880 | tf_op jit(solution)/shard_map/ppermute | solution.py:295
  19.4 12.8 %collective-permute-start.3 = (bf16[1104,128]{1,0:T(8,128)(2,1)S(1)}, bf16[1104,128]{1,0:T(8,128)(2,1)S(1)}, u32[]{:S(2)}, u32[]{:S(2)}) collective-permute-start(bf16[1104,128]{1,0:T(8,128)(2,1)S(1)} %get-tuple-element.51), channel_id=1, source_target_pairs={{0,15},{1,0},{2,1},{3,2},{4,3},{5,4},{6,5},{7,6},{8,7},{9,8},{10,9... | collective-permute-start | bytes 847880 | tf_op jit(solution)/shard_map/ppermute | solution.py:296
  27.6 1.1 copy-start
  28.8 1.1 copy-start.1
  29.9 1.1 copy-start.2
  31.0 1.2 copy-start.3
  32.2 0.7 copy-start.10
  32.2 0.9 copy-start.11
  69.6 2.9 %collective-permute-start.4 = (bf16[4,32,32,96]{3,2,1,0:T(8,128)(2,1)}, bf16[4,32,32,96]{3,2,1,0:T(8,128)(2,1)S(1)}, u32[]{:S(2)}, u32[]{:S(2)}) collective-permute-start(bf16[4,32,32,96]{3,2,1,0:T(8,128)(2,1)} %get-tuple-element.19), channel_id=1, source_target_pairs={{0,1},{1,0},{2,3},{3,2},{4,5},{5,4},{6,7},{7,6},{8,9},{9,8},{10,11... | collective-permute-start | bytes 2359304 | tf_op jit(solution)/shard_map/ppermute | solution.py:247
  74.0 39.5 %copy-start.13 = (bf16[8,96,128]{2,1,0:T(8,128)(2,1)S(1)}, bf16[8,96,128]{2,1,0:T(8,128)(2,1)}, u32[]{:S(2)}) copy-start(bf16[8,96,128]{2,1,0:T(8,128)(2,1)} %get-tuple-element.16) | copy-start | bytes 589828
  74.0 10.2 %collective-permute-start.7 = (bf16[32,32,96]{2,1,0:T(8,128)(2,1)S(1)}, bf16[32,32,96]{2,1,0:T(8,128)(2,1)S(1)}, u32[]{:S(2)}, u32[]{:S(2)}) collective-permute-start(bf16[32,32,96]{2,1,0:T(8,128)(2,1)S(1)} %get-tuple-element.37), channel_id=1, source_target_pairs={{0,6},{1,7},{2,4},{3,5},{4,2},{5,3},{6,0},{7,1},{8,14},{9,15},{10,... | collective-permute-start | bytes 589832 | tf_op jit(solution)/shard_map/ppermute | solution.py:247
  74.1 14.1 %collective-permute-start.6 = (bf16[32,32,96]{2,1,0:T(8,128)(2,1)S(1)}, bf16[32,32,96]{2,1,0:T(8,128)(2,1)S(1)}, u32[]{:S(2)}, u32[]{:S(2)}) collective-permute-start(bf16[32,32,96]{2,1,0:T(8,128)(2,1)S(1)} %get-tuple-element.38), channel_id=1, source_target_pairs={{0,4},{1,5},{2,6},{3,7},{4,0},{5,1},{6,2},{7,3},{8,12},{9,13},{10,... | collective-permute-start | bytes 589832 | tf_op jit(solution)/shard_map/ppermute | solution.py:247
  74.6 13.6 %collective-permute-start.5 = (bf16[32,32,96]{2,1,0:T(8,128)(2,1)S(1)}, bf16[32,32,96]{2,1,0:T(8,128)(2,1)S(1)}, u32[]{:S(2)}, u32[]{:S(2)}) collective-permute-start(bf16[32,32,96]{2,1,0:T(8,128)(2,1)S(1)} %get-tuple-element.36), channel_id=1, source_target_pairs={{0,2},{1,3},{2,0},{3,1},{4,6},{5,7},{6,4},{7,5},{8,10},{9,11},{10,... | collective-permute-start | bytes 589832 | tf_op jit(solution)/shard_map/ppermute | solution.py:247
  77.6 36.6 %copy-start.12 = (bf16[8,96,128]{2,1,0:T(8,128)(2,1)S(1)}, bf16[8,96,128]{2,1,0:T(8,128)(2,1)}, u32[]{:S(2)}) copy-start(bf16[8,96,128]{2,1,0:T(8,128)(2,1)} %get-tuple-element.17) | copy-start | bytes 589828
  88.4 6.6 %collective-permute-start.8 = (bf16[16,1,32,96]{3,2,0,1:T(8,128)(2,1)S(1)}, bf16[16,1,32,96]{3,2,0,1:T(8,128)(2,1)S(1)}, u32[]{:S(2)}, u32[]{:S(2)}) collective-permute-start(bf16[16,1,32,96]{3,2,0,1:T(8,128)(2,1)S(1)} %dynamic-slice_bitcast_fusion), channel_id=1, source_target_pairs={{0,8},{1,9},{2,10},{3,11},{4,12},{5,13},{6,14},{7,15},{8,0},{9,1},... | collective-permute-start | bytes 294920 | tf_op jit(solution)/shard_map/ppermute | solution.py:247
  95.0 4.4 %collective-permute-start.9 = (bf16[2,4,32,96]{3,2,1,0:T(8,128)(2,1)S(1)}, bf16[2,4,32,96]{3,2,1,0:T(8,128)(2,1)S(1)}, u32[]{:S(2)}, u32[]{:S(2)}) collective-permute-start(bf16[2,4,32,96]{3,2,1,0:T(8,128)(2,1)S(1)} %dynamic-slice_bitcast_fusion.1), channel_id=1, source_target_pairs={{0,64},{1,65},{2,66},{3,67},{4,68},{5,69},{6,70},{7,71},{8,72},{9,... | collective-permute-start | bytes 147464 | tf_op jit(solution)/shard_map/ppermute | solution.py:247
  99.4 5.5 %collective-permute-start.10 = (bf16[1,4,32,96]{3,2,1,0:T(8,128)(2,1)S(1)}, bf16[1,4,32,96]{3,2,1,0:T(8,128)(2,1)S(1)}, u32[]{:S(2)}, u32[]{:S(2)}) collective-permute-start(bf16[1,4,32,96]{3,2,1,0:T(8,128)(2,1)S(1)} %constant_dynamic-slice_fusion.1), channel_id=1, source_target_pairs={{0,128},{1,129},{2,130},{3,131},{4,132},{5,133},{6,134},{7,135},{8... | collective-permute-start | bytes 73736 | tf_op jit(solution)/shard_map/ppermute | solution.py:247
  104.9 5.6 %collective-permute-start.11 = (bf16[2,1,32,96]{3,2,0,1:T(8,128)(2,1)S(1)}, bf16[2,1,32,96]{3,2,0,1:T(8,128)(2,1)S(1)}, u32[]{:S(2)}, u32[]{:S(2)}) collective-permute-start(bf16[2,1,32,96]{3,2,0,1:T(8,128)(2,1)S(1)} %dynamic-slice_bitcast_fusion.2), channel_id=1, source_target_pairs={{0,16},{1,17},{2,18},{3,19},{4,20},{5,21},{6,22},{7,23},{8,24},{9,... | collective-permute-start | bytes 36872 | tf_op jit(solution)/shard_map/ppermute | solution.py:247
  110.6 7.6 %collective-permute-start.12 = (bf16[1,1,32,96]{3,2,0,1:T(8,128)(2,1)S(1)}, bf16[1,1,32,96]{3,2,0,1:T(8,128)(2,1)S(1)}, u32[]{:S(2)}, u32[]{:S(2)}) collective-permute-start(bf16[1,1,32,96]{3,2,0,1:T(8,128)(2,1)S(1)} %constant_dynamic-slice_fusion), channel_id=1, source_target_pairs={{0,32},{1,33},{2,34},{3,35},{4,36},{5,37},{6,38},{7,39},{8,40},{9,... | collective-permute-start | bytes 18440 | tf_op jit(solution)/shard_map/ppermute | solution.py:247

commit v2 on v1

v2 whole, which is shorter than its diff:
```python
import math

import jax
import jax.numpy as jnp
from jax import lax
from jax.experimental import pallas as pl
from jax.experimental.pallas import tpu as pltpu
from jax.sharding import PartitionSpec as P

BOTH = ("east", "north")
F32 = jnp.float32
BF16 = jnp.bfloat16
CH = 96
LN = 128
TAPS = 9 * LN
STRIP = 6 * CH + 16
VMEM = pl.BlockSpec(memory_space=pltpu.VMEM)
SMEM = pl.BlockSpec(memory_space=pltpu.SMEM)


def lanes(rows):
    return lax.broadcasted_iota(jnp.int32, (rows, LN), 1)


def flip_pad(value):
    wide = jnp.concatenate(
        [value.astype(F32), jnp.zeros((LN - value.shape[0], value.shape[1]), F32)], axis=0
    )
    return wide.T


def mask_column(ref, row):
    tile = ref[row : row + 16, :].astype(F32)
    return jnp.concatenate([tile] * 8, axis=0).T


def strips_kernel(
    occupied, features, cotangent, feat, cot, to_west, to_east, own_mask, wide_feat, wide_cot
):
    wide_feat[...] = features[...].astype(F32).reshape(CH * 8, LN)
    wide_cot[...] = cotangent[...].astype(F32).reshape(CH * 8, LN)
    for x in range(8):
        feat[x] = wide_feat[pl.ds(x, CH, stride=8), :].astype(BF16)
        cot[x] = wide_cot[pl.ds(x, CH, stride=8), :].astype(BF16)
    low = occupied[0, 0].astype(F32)
    high = occupied[0, 1].astype(F32)
    own_mask[...] = jnp.where((lanes(16) & 15) < 8, low, high).astype(BF16)
    for out, first, second in ((to_west, 0, 0), (to_east, 4, 6)):
        for k in range(4):
            out[k * CH : (k + 1) * CH, :] = feat[first + k]
        for k in range(2):
            out[(4 + k) * CH : (5 + k) * CH, :] = cot[second + k]
        out[6 * CH : STRIP, :] = own_mask[...]


def turn_levels(value, x, turned):
    lane = lanes(CH) & 15
    below = jnp.where(lane == 0, 0.0, pltpu.roll(value, 1, 1))
    above = jnp.where(lane == 15, 0.0, pltpu.roll(value, LN - 1, 1))
    start = x * LN if isinstance(x, int) else pl.multiple_of(x * LN, LN)
    for c, moved in enumerate((below, value, above)):
        turned[c * CH : (c + 1) * CH, pl.ds(start, LN)] = moved.astype(BF16)


def prepare_kernel(
    first,
    second,
    feat,
    cot,
    own_mask,
    fwd_one,
    fwd_two,
    back_two,
    back_one,
    turned_one,
    own_grid,
    own_cot,
):
    for out in (fwd_one, fwd_two, back_two, back_one):
        out[...] = jnp.zeros_like(out)

    def body(tap, carry):
        plane = tap // 9
        row = pl.multiple_of((tap % 9) * LN, LN)
        for source, ahead, back in ((first, fwd_one, back_one), (second, fwd_two, back_two)):
            ahead[plane + 1, pl.ds(row, CH), 0:CH] = source[tap]
            turned = jnp.pad(source[26 - tap].astype(F32), ((0, LN - CH), (0, LN - CH))).T
            back[plane + 1, pl.ds(row, LN), :] = turned.astype(BF16)
        return carry

    lax.fori_loop(0, 27, body, 0)
    mask = jnp.concatenate([own_mask[...].astype(F32)] * 6, axis=0)
    for x in range(8):
        value = feat[x].astype(F32) * mask
        turn_levels(value, x, turned_one)
        own_grid[x] = flip_pad(value).astype(BF16)
        own_cot[x] = flip_pad(cot[x]).astype(BF16)


def sides_kernel(place, own_mask, west, east, side_grid, side_cot, middle):
    middle[0] = mask_column(west, 6 * CH) * place[0].astype(F32)
    middle[1] = mask_column(own_mask, 0)
    middle[2] = mask_column(east, 6 * CH) * place[1].astype(F32)
    for side, ref in ((0, west), (1, east)):
        for k in range(4):
            block = flip_pad(ref[k * CH : (k + 1) * CH, :]) * middle[2 * side]
            side_grid[4 * side + k] = block.astype(BF16)
        for k in range(2):
            side_cot[2 * side + k] = flip_pad(ref[(4 + k) * CH : (5 + k) * CH, :]).astype(BF16)


def spread(taps, plane_hi, plane_lo, value, rows):
    count = rows + 32
    level = lax.broadcasted_iota(jnp.int32, (count, LN), 0) & 15
    below = jnp.where(level == 0, 0.0, pltpu.roll(value, 1, 0))
    above = jnp.where(level == 15, 0.0, pltpu.roll(value, count - 1, 0))
    for c, moved in enumerate((below, value, above)):
        short = moved.astype(BF16)
        for b in range(3):
            lane = (3 * b + c) * LN
            taps[plane_hi, plane_lo, 0:rows, lane : lane + LN] = short[16 * b : 16 * b + rows]


def convolve(taps, weight, total, pairs, rows):
    size = pairs * rows
    left = jnp.concatenate(
        [
            taps[j // 2 : j // 2 + pairs, j % 2, 0:rows, :].reshape(size, TAPS)
            for j in range(4)
        ],
        axis=1,
    )
    right = jnp.concatenate(
        [jnp.concatenate([weight[j + 1], weight[j]], axis=1) for j in range(4)], axis=0
    )
    total[0:size, :] = jnp.dot(left, right, preferred_element_type=F32)


def kernel_grad(turned, planes, shift, scale, result):
    def piece(k):
        a, b = k // 3, k % 3
        start = (shift + 1 - b) * 16
        return planes[shift + 1 - a : shift + 9 - a, start : start + 128, :].reshape(1024, LN)

    for k in range(0, 9, 2):
        right = jnp.concatenate([piece(k), piece(min(k + 1, 8))], axis=1)
        part = jnp.dot(turned[...], right, preferred_element_type=F32) * scale
        result[k * 288 : k * 288 + 288, :] = part[:, 0:LN]
        if k < 8:
            result[(k + 1) * 288 : (k + 1) * 288 + 288, :] = part[:, LN : 2 * LN]


def band(p, low, high):
    return (p >= low).astype(jnp.int32) + (p >= high).astype(jnp.int32)


def level_kernel(
    scale,
    place,
    own_grid,
    side_grid,
    own_cot,
    side_cot,
    middle,
    south,
    north,
    fwd_one,
    fwd_two,
    back_two,
    turned_one,
    activated,
    grad_one,
    masks,
    keep,
    send,
    taps,
    edge,
    upstream,
    total,
    slope_one,
    grad_two,
    turned_two,
    grad_one_sum,
    grad_two_sum,
    packed,
):
    for ref, flag, row in ((south, place[2], 0), (north, place[3], 192)):
        tile = ref[11 * CH : 11 * CH + 48, :].astype(F32) * flag.astype(F32)
        turned = jnp.concatenate([tile, jnp.zeros((80, LN), F32)], axis=0).T[0:64]
        for bx in range(3):
            side = place[bx // 2].astype(F32) if bx != 1 else 1.0
            column = turned[:, 16 * bx : 16 * bx + 1] * side
            masks[bx, row : row + 64, :] = jnp.broadcast_to(column, (64, LN))
    masks[:, 64:192, :] = middle[...]

    for k in range(8):
        for ref, row in ((south, 0), (north, 64)):
            both = flip_pad(ref[k * CH : (k + 1) * CH, :])
            edge[k, row : row + 64, :] = both[0:64]
            edge[k + 8, row : row + 64, :] = both[64:128]
    for k in range(3):
        for ref, row in ((south, 0), (north, 160)):
            four = flip_pad(ref[(8 + k) * CH : (9 + k) * CH, :])
            for q in range(4):
                upstream[k + 3 * q, row : row + 32, :] = four[32 * q : 32 * q + 32]
    for k in range(2):
        upstream[k, 32:160, :] = side_cot[k].astype(F32)
        upstream[10 + k, 32:160, :] = side_cot[2 + k].astype(F32)
    for k in range(8):
        upstream[2 + k, 32:160, :] = own_cot[k].astype(F32)

    def begin(p, value, bx):
        low = edge[p, 0:64, :] * masks[bx, 0:64, :]
        high = edge[p, 64:128, :] * masks[bx, 192:256, :]
        whole = jnp.concatenate([low, value.astype(F32), high], axis=0)
        spread(taps, p // 2, p % 2, whole, 224)

    def begin_west(p, carry):
        begin(p, side_grid[p], 0)
        return carry

    def begin_own(p, carry):
        begin(p + 4, own_grid[p], 1)
        return carry

    def begin_east(p, carry):
        begin(p + 12, side_grid[p + 4], 2)
        return carry

    lax.fori_loop(0, 4, begin_west, 0)
    lax.fori_loop(0, 8, begin_own, 0)
    lax.fori_loop(0, 4, begin_east, 0)
    convolve(taps, fwd_one, total, 7, 224)

    def after_one(i, carry):
        for half in range(2):
            p = 2 * i + half
            value = total[pl.ds(pl.multiple_of(i * 224, 16), 224), half * LN : half * LN + LN]
            value = value * masks[band(p, 3, 11), 16:240, :]
            sigma = jax.nn.sigmoid(value)
            slope_one[p] = (sigma * (1.0 + value * (1.0 - sigma)))[32:192]
            hidden = (value * sigma).astype(BF16).astype(F32)
            spread(taps, i, half, hidden, 192)

            @pl.when((p >= 3) & (p < 11))
            def _():
                turn_levels(hidden[48:176].T[0:CH], p - 3, turned_two)

        return carry

    lax.fori_loop(0, 7, after_one, 0)
    convolve(taps, fwd_two, total, 6, 192)

    def after_two(i, carry):
        for half in range(2):
            p = 2 * i + half
            value = total[pl.ds(pl.multiple_of(i * 192, 16), 192), half * LN : half * LN + LN]
            mask = masks[band(p, 2, 10), 32:224, :]
            value = value * mask
            sigma = jax.nn.sigmoid(value)

            @pl.when((p >= 2) & (p < 10))
            def _():
                activated[p - 2] = (value * sigma)[32:160].T[0:CH].astype(BF16)

            slope = sigma * (1.0 + value * (1.0 - sigma))
            grad = upstream[p] * slope * mask
            grad_two[p] = grad.astype(BF16)
            spread(taps, i, half, grad, 160)
        return carry

    lax.fori_loop(0, 6, after_two, 0)
    kernel_grad(turned_two, grad_two, 2, scale, grad_two_sum)
    convolve(taps, back_two, total, 5, 160)

    def after_three(i, carry):
        for half in range(2):
            p = 2 * i + half
            value = total[pl.ds(pl.multiple_of(i * 160, 16), 160), half * LN : half * LN + LN]
            grad = value * slope_one[p + 2] * masks[band(p, 1, 9), 48:208, :]
            grad_one[p] = grad.astype(BF16)
        return carry

    lax.fori_loop(0, 5, after_three, 0)
    kernel_grad(turned_one, grad_one, 1, scale, grad_one_sum)

    me = place[4]
    tail = lanes(CH) < CH
    for out, low in ((keep, 0), (send, 1)):
        for e in range(4):
            j = jnp.bitwise_xor(me, 2 * e + low)
            for grad, source in ((0, grad_one_sum), (1, grad_two_sum)):

                def gather(g, carry):
                    packed[pl.ds(12 * g, 16), :] = source[pl.ds(81 * g + 10 * j, 16), :]
                    return carry

                lax.fori_loop(0, 32, gather, 0, unroll=8)
                last = packed[288:384, :]
                for k in range(3):
                    block = jnp.where(
                        tail, packed[CH * k : CH * k + CH, :], pltpu.roll(last, CH - 32 * k, 1)
                    )
                    start = 288 * grad + CH * k
                    out[e, start : start + CH, :] = block.astype(BF16)


def final_kernel(grad_one, masks, back_one, feature_grad, taps, total):
    def begin(i, carry):
        for half in range(2):
            spread(taps, i, half, grad_one[2 * i + half].astype(F32), 128)
        return carry

    lax.fori_loop(0, 5, begin, 0)
    convolve(taps, back_one, total, 4, 128)
    for p in range(8):
        i, half = p // 2, p % 2
        value = total[i * 128 : i * 128 + 128, half * LN : half * LN + LN] * masks[1, 64:192, :]
        feature_grad[p] = value.T[0:CH].astype(BF16)


def combine_kernel(place, a0, a1, a2, a3, hold, give, rows, ordered):
    bit = place[5]
    lane = lanes(CH)
    for grad in range(2):
        blocks = []
        for k in range(3):
            start = 288 * grad + CH * k
            blocks.append(
                sum(ref[start : start + CH, :].astype(F32) for ref in (a0, a1, a2, a3))
            )
        a, b, c = blocks
        last = jnp.where(
            lane < 32,
            pltpu.roll(a, 32, 1),
            jnp.where(lane < 64, pltpu.roll(b, 64, 1), pltpu.roll(c, 96, 1)),
        )
        for k, block in enumerate((a, b, c, last)):
            rows[grad, CH * k : CH * k + CH, :] = block
    for out, want in ((hold, bit), (give, 1 - bit)):
        for m in range(16):
            for grad in range(2):
                start = 24 * m + 12 * grad
                ordered[start : start + 12, :] = rows[grad, pl.ds(24 * m + 12 * want, 12), :]
        out[...] = ordered[...].astype(BF16)


def finish_kernel(place, held, got, out_one, out_two):
    j = place[4]
    lane = lanes(1)
    value = held[...] + got[...]
    for grad, out in ((0, out_one), (1, out_two)):
        flat = []
        for m in range(3):
            r = [value[12 * grad + 4 * m + q : 12 * grad + 4 * m + q + 1] for q in range(4)]
            flat.append(jnp.where(lane < 96, r[0], pltpu.roll(r[1], 96, 1)))
            flat.append(jnp.where(lane < 64, pltpu.roll(r[1], 96, 1), pltpu.roll(r[2], 64, 1)))
            flat.append(jnp.where(lane < 32, pltpu.roll(r[2], 64, 1), pltpu.roll(r[3], 32, 1)))
        low = jnp.concatenate(flat[0:8], axis=0)
        high = jnp.concatenate(flat[1:9], axis=0)
        turn = lax.rem(LN - 12 * j, LN)
        out[...] = jnp.where(
            lanes(8) < LN - 12 * j, pltpu.roll(low, turn, 1), pltpu.roll(high, turn, 1)
        )


def call(kernel, name, outs, scratch, limit, flops, specs, *args):
    return pl.pallas_call(
        kernel,
        out_shape=outs,
        in_specs=specs,
        out_specs=[VMEM] * len(outs),
        scratch_shapes=scratch,
        compiler_params=pltpu.CompilerParams(vmem_limit_bytes=limit << 20),
        cost_estimate=pl.CostEstimate(flops=flops, bytes_accessed=1 << 20, transcendentals=0),
        name=name,
    )(*args)


def shape(*dims, dtype=BF16):
    return jax.ShapeDtypeStruct(dims, dtype)


def shift_by(step, axis):
    count = lax.axis_size(axis)
    return [(i, (i + step) % count) for i in range(count)]


def swap(value, bits):
    count = lax.axis_size("east") * lax.axis_size("north")
    return lax.ppermute(value, BOTH, [(i, i ^ bits) for i in range(count)])


def local(features, occupancy, weight_first, weight_second, cotangent):
    column = lax.axis_index("east")
    row = lax.axis_index("north")
    position = column * 16 + row
    block = position // 8
    scale = 1.0 / math.sqrt(128 * 128 * 16)
    place = jnp.stack(
        [column > 0, column < 15, row > 0, row < 15, position % 8, block % 2]
    ).astype(jnp.int32)

    feat, cot, to_west, to_east, own_mask = call(
        strips_kernel,
        "strips",
        [shape(8, CH, LN), shape(8, CH, LN), shape(STRIP, LN), shape(STRIP, LN), shape(16, LN)],
        [pltpu.VMEM((CH * 8, LN), F32), pltpu.VMEM((CH * 8, LN), F32)],
        8,
        1 << 20,
        [SMEM, VMEM, VMEM],
        occupancy.reshape(1, 2),
        features,
        cotangent,
    )
    west = lax.ppermute(to_east, "east", shift_by(1, "east"))
    east = lax.ppermute(to_west, "east", shift_by(-1, "east"))

    weight = shape(5, TAPS, LN)
    tile = shape(8, LN, LN)
    prepared = call(
        prepare_kernel,
        "prepare",
        [weight, weight, weight, weight, shape(288, 1024), tile, tile],
        [],
        16,
        1 << 33,
        [VMEM] * 5,
        weight_first,
        weight_second,
        feat,
        cot,
        own_mask,
    )
    (west, east), prepared = lax.optimization_barrier(((west, east), prepared))
    fwd_one, fwd_two, back_two, back_one, turned_one, own_grid, own_cot = prepared

    all_feat = jnp.concatenate(
        [west[0:384].reshape(4, CH, LN), feat, east[0:384].reshape(4, CH, LN)], axis=0
    )
    all_cot = jnp.concatenate(
        [west[384:576].reshape(2, CH, LN), cot, east[384:576].reshape(2, CH, LN)], axis=0
    )
    all_mask = [west[576:592], own_mask, east[576:592]]

    def rim(at_feat, at_cot):
        f = all_feat[:, :, at_feat : at_feat + 64]
        f = jnp.concatenate([f[0:8], f[8:16]], axis=2)
        c = all_cot[:, :, at_cot : at_cot + 32]
        c = jnp.concatenate([c[0:3], c[3:6], c[6:9], c[9:12]], axis=2)
        return jnp.concatenate([f.reshape(-1, LN), c.reshape(-1, LN)] + all_mask, axis=0)

    south = lax.ppermute(rim(64, 96), "north", shift_by(1, "north"))
    north = lax.ppermute(rim(0, 0), "north", shift_by(-1, "north"))
    sides = call(
        sides_kernel,
        "sides",
        [tile, shape(4, LN, LN), shape(3, LN, LN, dtype=F32)],
        [],
        8,
        1 << 31,
        [SMEM] + [VMEM] * 3,
        place,
        own_mask,
        west,
        east,
    )
    (south, north), sides = lax.optimization_barrier(((south, north), sides))
    side_grid, side_cot, middle = sides

    activated, grad_one, masks, keep, send = call(
        lambda *refs: level_kernel(scale, *refs),
        "level",
        [
            shape(8, CH, LN),
            shape(10, 160, LN),
            shape(3, 256, LN, dtype=F32),
            shape(4, 576, LN),
            shape(4, 576, LN),
        ],
        [
            pltpu.VMEM((8, 2, 224, TAPS), BF16),
            pltpu.VMEM((16, 128, LN), F32),
            pltpu.VMEM((12, 192, LN), F32),
            pltpu.VMEM((7 * 224, 2 * LN), F32),
            pltpu.VMEM((14, 160, LN), F32),
            pltpu.VMEM((12, 192, LN), BF16),
            pltpu.VMEM((288, 1024), BF16),
            pltpu.VMEM((2592 + 16, LN), F32),
            pltpu.VMEM((2592 + 16, LN), F32),
            pltpu.VMEM((400, LN), F32),
        ],
        36,
        1 << 34,
        [SMEM] + [VMEM] * 11,
        place,
        own_grid,
        side_grid,
        own_cot,
        side_cot,
        middle,
        south,
        north,
        fwd_one,
        fwd_two,
        back_two,
        turned_one,
    )

    def add(*terms):
        return sum(t.astype(F32) for t in terms)

    part = add(keep, swap(send, 1)).astype(BF16)
    others = [swap(part[k], 2 * k) for k in (1, 2, 3)]
    (feature_grad,) = call(
        final_kernel,
        "final",
        [shape(8, CH, LN)],
        [pltpu.VMEM((5, 2, 128, TAPS), BF16), pltpu.VMEM((512, 2 * LN), F32)],
        16,
        1 << 32,
        [VMEM] * 3,
        grad_one,
        masks,
        back_one,
    )
    others, feature_grad = lax.optimization_barrier((others, feature_grad))
    hold, give = call(
        combine_kernel,
        "combine",
        [shape(384, LN), shape(384, LN)],
        [pltpu.VMEM((2, 384, LN), F32), pltpu.VMEM((384, LN), F32)],
        8,
        1 << 20,
        [SMEM] + [VMEM] * 4,
        place,
        part[0],
        *others,
    )
    part = add(hold, swap(give, 8)).reshape(16, 24, LN)
    for bit, kind in ((8, BF16), (4, F32), (2, F32)):
        half = part.reshape((2, -1, 24, LN)).astype(kind)
        mine = (block // (2 * bit)) % 2
        held = lax.dynamic_index_in_dim(half, mine, 0, keepdims=False)
        given = lax.dynamic_index_in_dim(half, 1 - mine, 0, keepdims=False)
        part = add(held, swap(given, 16 * bit))
    mine = (block // 2) % 2
    held = lax.dynamic_index_in_dim(part, mine, 0, keepdims=False)
    given = lax.dynamic_index_in_dim(part, 1 - mine, 0, keepdims=False)
    one, two = call(
        finish_kernel,
        "finish",
        [shape(8, LN, dtype=F32), shape(8, LN, dtype=F32)],
        [],
        8,
        1 << 20,
        [SMEM] + [VMEM] * 2,
        place,
        held,
        swap(given, 16),
    )

    return (
        jnp.transpose(activated, (1, 0, 2)),
        jnp.transpose(feature_grad, (1, 0, 2)),
        one.reshape(-1)[0:972],
        two.reshape(-1)[0:972],
    )


def solution(mesh):
    return jax.shard_map(
        local,
        mesh=mesh,
        in_specs=(
            P(None, "east", "north"),
            P("east", "north", None),
            P(),
            P(),
            P(None, "east", "north"),
        ),
        out_specs=(
            P(None, "east", "north"),
            P(None, "east", "north"),
            P(BOTH),
            P(BOTH),
        ),
        check_vma=False,
    )
```

time: 120 us -> 108 us (0.900); the launches traced: 120 us -> 106 us
  waiting for transfers between devices: 36.6 us -> 24.1 us
  starting transfers between devices: 27.1 us -> 30 us
  Pallas kernels: 40.3 us -> 37.5 us
  other arithmetic: 3.07 us -> 0.84 us
    ppermute x9, waiting for transfers between devices: 28.4 us -> 19 us  [swap(): return lax.ppermute(value, BOTH, [(i, i ^ bits) for i in range(count)])]
    ppermute x4, waiting for transfers between devices: 8.17 us -> 5.1 us  [the longest x1 4.93 us: local(): south = lax.ppermute(rim(64, 96), 'north', shift_by(1, 'north'))]
    ppermute x9, starting transfers between devices: 16.7 us -> 19.7 us  [swap(): return lax.ppermute(value, BOTH, [(i, i ^ bits) for i in range(count)])]
    pallas_call x2 -> x7, Pallas kernels: 40.3 us -> 37.5 us  [call(): pl.pallas_call(kernel, out_shape=outs, in_specs=specs, out_specs=[VMEM] *...]
    unnamed x39 -> x33, local copies, waits for them, and re-layouts: 9.02 us -> 11.7 us
    convert_element_type x8 -> x2, other arithmetic: 2.41 us -> 0.18 us  [the longest x1 0.16 us: local(): part = add(keep, swap(send, 1)).astype(BF16)]
    dynamic_slice x2 -> x0, local copies, waits for them, and re-layouts: 1.33 us -> none  [own_share(): lax.dynamic_slice_in_dim(rows[0:12].reshape(-1), 12 * (position % 8), 972)]
  transfers between devices with their start and end apart: 13 -> 13, of which waited for: 10 -> 11; matrix products, arithmetic and copies ran while one was open for 2% -> 2% of each run, Pallas kernels for 3% -> 6%
where the time goes in v2:
time: 108 us; the launch traced here: 106 us
  Pallas kernels  37.5 us (35%)
  starting transfers between devices  30 us (28%)
  waiting for transfers between devices  24.1 us (22%)
  local copies, waits for them, and re-layouts  12.6 us (12%)
    pallas_call x7, Pallas kernels, call(): pl.pallas_call(kernel, out_shape=outs, in_specs=specs, out_specs=[VMEM] *...  37.5 us
    ppermute x9, starting transfers between devices, swap(): return lax.ppermute(value, BOTH, [(i, i ^ bits) for i in range(count)])  19.7 us
    ppermute x9, waiting for transfers between devices, swap(): return lax.ppermute(value, BOTH, [(i, i ^ bits) for i in range(count)])  19 us
    unnamed x33, local copies, waits for them, and re-layouts  11.7 us
    ppermute x1, waiting for transfers between devices, local(): south = lax.ppermute(rim(64, 96), 'north', shift_by(1, 'north'))  4.93 us
    ppermute x1, starting transfers between devices, local(): north = lax.ppermute(rim(0, 0), 'north', shift_by(-1, 'north'))  3.85 us
    ppermute x1, starting transfers between devices, local(): west = lax.ppermute(to_east, 'east', shift_by(1, 'east'))  3.35 us
    ppermute x1, starting transfers between devices, local(): east = lax.ppermute(to_west, 'east', shift_by(-1, 'east'))  3.09 us
  transfers between devices with their start and end apart: 13, of which 11 were waited for; matrix products, arithmetic and copies ran while one was open for 2% of the time, Pallas kernels for 6%

profile of v2, /device:TPU:2, one launch (start us, length us, event | category | flops | bytes accessed | tf_op | source)
XLA Modules:
  0.0 105.9 jit_solution(2821525024587876581)
XLA Ops:
  0.6 0.9 copy-done
  1.6 0.9 copy-done.1
  3.9 3.3 %collective-permute-start = (bf16[592,128]{1,0:T(8,128)(2,1)S(1)}, bf16[592,128]{1,0:T(8,128)(2,1)S(1)}, u32[]{:S(2)}, u32[]{:S(2)}) collective-permute-start(bf16[592,128]{1,0:T(8,128)(2,1)S(1)} %get-tuple-element.46), channel_id=1, source_target_pairs={{0,16},{16,32},{32,48},{48,64},{64,80},{80,96},{96,112},{112,128},... | collective-permute-start | bytes 454664 | tf_op jit(solution)/shard_map/ppermute | solution.py:416
  7.2 3.1 %collective-permute-start.1 = (bf16[592,128]{1,0:T(8,128)(2,1)S(1)}, bf16[592,128]{1,0:T(8,128)(2,1)S(1)}, u32[]{:S(2)}, u32[]{:S(2)}) collective-permute-start(bf16[592,128]{1,0:T(8,128)(2,1)S(1)} %get-tuple-element.47), channel_id=1, source_target_pairs={{0,240},{16,0},{32,16},{48,32},{64,48},{80,64},{96,80},{112,96},{1... | collective-permute-start | bytes 454664 | tf_op jit(solution)/shard_map/ppermute | solution.py:417
  10.3 1.1 %copy-done.3 = bf16[27,96,96]{2,1,0:T(8,128)(2,1)S(1)} copy-done((bf16[27,96,96]{2,1,0:T(8,128)(2,1)S(1)}, bf16[27,96,96]{2,1,0:T(8,128)(2,1)}, u32[]{:S(2)}) %copy-start.3) | copy-done | bytes 497688
  11.4 1.1 %copy-done.4 = bf16[27,96,96]{2,1,0:T(8,128)(2,1)S(1)} copy-done((bf16[27,96,96]{2,1,0:T(8,128)(2,1)S(1)}, bf16[27,96,96]{2,1,0:T(8,128)(2,1)}, u32[]{:S(2)}) %copy-start.4) | copy-done | bytes 497688
  12.5 4.0 %prepare.1 = (bf16[5,1152,128]{2,1,0:T(8,128)(2,1)S(1)}, bf16[5,1152,128]{2,1,0:T(8,128)(2,1)S(1)}, bf16[5,1152,128]{2,1,0:T(8,128)(2,1)S(1)}, bf16[5,1152,128]{...) custom-call(bf16[27,96,96]{2,1,0:T(8,128)(2,1)S(1)} %copy-done.3, ...), custom_call_target="tpu_custom_call" | custom-call | flops 8589934592 | bytes 1048576 | tf_op jit(solution)/shard_map/prepare/pallas_call | solution.py:368
  16.5 1.1 %copy-done.9 = bf16[5,1152,128]{2,1,0:T(8,128)(2,1)} copy-done((bf16[5,1152,128]{2,1,0:T(8,128)(2,1)}, bf16[5,1152,128]{2,1,0:T(8,128)(2,1)S(1)}, u32[]{:S(2)}) %copy-start.9) | copy-done | bytes 1474584
  19.0 1.0 constant_dynamic-update-slice_fusion.9
  23.5 3.9 %collective-permute-start.3 = (bf16[1104,128]{1,0:T(8,128)(2,1)}, bf16[1104,128]{1,0:T(8,128)(2,1)S(1)}, u32[]{:S(2)}, u32[]{:S(2)}) collective-permute-start(bf16[1104,128]{1,0:T(8,128)(2,1)} %get-tuple-element.104), channel_id=1, source_target_pairs={{0,15},{1,0},{2,1},{3,2},{4,3},{5,4},{6,5},{7,6},{8,7},{9,8},{10,9... | collective-permute-start | bytes 847880 | tf_op jit(solution)/shard_map/ppermute | solution.py:454
  28.3 4.9 %collective-permute-done.2.refs_6_ = bf16[1104,128]{1,0:T(8,128)(2,1)S(1)} collective-permute-done((bf16[1104,128]{1,0:T(8,128)(2,1)}, bf16[1104,128]{1,0:T(8,128)(2,1)S(1)}, u32[]{:S(2)}, u32[]{:S(2)}) %collective-permute-start.2) | collective-permute-done | bytes 282656 | tf_op jit(solution)/shard_map/ppermute | solution.py:453
  33.2 28.2 %level.1 = (bf16[8,96,128]{2,1,0:T(8,128)(2,1)S(1)}, bf16[10,160,128]{2,1,0:T(8,128)(2,1)S(1)}, f32[3,256,128]{2,1,0:T(8,128)S(1)}, bf16[4,576,128]{2,1,0:T(8,128)(2,1)S(1)}, bf16[4,576,128]{2,1,0:T(8,128)(2,1)S(1)}) custom-call(s32[6]{0:T(128)S(1)} %stack.43.place.refs_0_, bf16[8,128,128]{2,1,0:T(8,128)(2,1)S(1)} %get-tuple-element.58.refs_1_, ...), custom_call_target="tpu_custom_call" | custom-call | flops 17179869184 | bytes 1048576 | tf_op jit(solution)/shard_map/level/pallas_call | solution.py:368
  62.2 1.6 %collective-permute-done.4 = bf16[4,576,128]{2,1,0:T(8,128)(2,1)S(1)} collective-permute-done((bf16[4,576,128]{2,1,0:T(8,128)(2,1)S(1)}, bf16[4,576,128]{2,1,0:T(8,128)(2,1)S(1)}, u32[]{:S(2)}, u32[]{:S(2)}) %collective-permute-start.4) | collective-permute-done | bytes 589856 | tf_op jit(solution)/shard_map/ppermute | solution.py:391
  64.0 1.1 %collective-permute-start.5 = (bf16[576,128]{1,0:T(8,128)(2,1)S(1)}, bf16[576,128]{1,0:T(8,128)(2,1)S(1)}, u32[]{:S(2)}, u32[]{:S(2)}) collective-permute-start(bf16[576,128]{1,0:T(8,128)(2,1)S(1)} %get-tuple-element.95), channel_id=1, source_target_pairs={{0,2},{1,3},{2,0},{3,1},{4,6},{5,7},{6,4},{7,5},{8,10},{9,11},{10,... | collective-permute-start | bytes 442376 | tf_op jit(solution)/shard_map/ppermute | solution.py:391
  65.1 1.6 %collective-permute-start.6 = (bf16[576,128]{1,0:T(8,128)(2,1)S(1)}, bf16[576,128]{1,0:T(8,128)(2,1)S(1)}, u32[]{:S(2)}, u32[]{:S(2)}) collective-permute-start(bf16[576,128]{1,0:T(8,128)(2,1)S(1)} %get-tuple-element.94), channel_id=1, source_target_pairs={{0,4},{1,5},{2,6},{3,7},{4,0},{5,1},{6,2},{7,3},{8,12},{9,13},{10,... | collective-permute-start | bytes 442376 | tf_op jit(solution)/shard_map/ppermute | solution.py:391
  66.7 0.9 collective-permute-start.7
  67.6 1.9 %final.1 = bf16[8,96,128]{2,1,0:T(8,128)(2,1)S(1)} custom-call(bf16[10,160,128]{2,1,0:T(8,128)(2,1)S(1)} %get-tuple-element.77.grad_one, f32[3,256,128]{2,1,0:T(8,128)S(1)} %get-tuple-element.78.masks, bf16[5,1152,128]{2,1,0:T(8,128)(2,1)S(1)} %get-tuple-element.79.back_one), custom_call_target="tpu_custom_call" | custom-call | flops 4294967296 | bytes 1048576 | tf_op jit(solution)/shard_map/final/pallas_call | solution.py:368
  69.5 1.3 %collective-permute-done.5.a1 = bf16[576,128]{1,0:T(8,128)(2,1)S(1)} collective-permute-done((bf16[576,128]{1,0:T(8,128)(2,1)S(1)}, bf16[576,128]{1,0:T(8,128)(2,1)S(1)}, u32[]{:S(2)}, u32[]{:S(2)}) %collective-permute-start.5) | collective-permute-done | bytes 147488 | tf_op jit(solution)/shard_map/ppermute | solution.py:391
  70.8 2.4 %collective-permute-done.6.a2 = bf16[576,128]{1,0:T(8,128)(2,1)S(1)} collective-permute-done((bf16[576,128]{1,0:T(8,128)(2,1)S(1)}, bf16[576,128]{1,0:T(8,128)(2,1)S(1)}, u32[]{:S(2)}, u32[]{:S(2)}) %collective-permute-start.6) | collective-permute-done | bytes 147488 | tf_op jit(solution)/shard_map/ppermute | solution.py:391
  73.2 1.2 %collective-permute-done.7.a3 = bf16[576,128]{1,0:T(8,128)(2,1)S(1)} collective-permute-done((bf16[576,128]{1,0:T(8,128)(2,1)S(1)}, bf16[576,128]{1,0:T(8,128)(2,1)S(1)}, u32[]{:S(2)}, u32[]{:S(2)}) %collective-permute-start.7) | collective-permute-done | bytes 147488 | tf_op jit(solution)/shard_map/ppermute | solution.py:391
  75.1 2.7 %collective-permute-start.8 = (bf16[384,128]{1,0:T(8,128)(2,1)S(1)}, bf16[384,128]{1,0:T(8,128)(2,1)S(1)}, u32[]{:S(2)}, u32[]{:S(2)}) collective-permute-start(bf16[384,128]{1,0:T(8,128)(2,1)S(1)} %get-tuple-element.85), channel_id=1, source_target_pairs={{0,8},{1,9},{2,10},{3,11},{4,12},{5,13},{6,14},{7,15},{8,0},{9,1},... | collective-permute-start | bytes 294920 | tf_op jit(solution)/shard_map/ppermute | solution.py:391
  77.8 3.5 %collective-permute-done.8 = bf16[384,128]{1,0:T(8,128)(2,1)S(1)} collective-permute-done((bf16[384,128]{1,0:T(8,128)(2,1)S(1)}, bf16[384,128]{1,0:T(8,128)(2,1)S(1)}, u32[]{:S(2)}, u32[]{:S(2)}) %collective-permute-start.8) | collective-permute-done | bytes 98336 | tf_op jit(solution)/shard_map/ppermute | solution.py:391
  81.4 2.5 %collective-permute-start.9 = (bf16[8,24,128]{2,1,0:T(8,128)(2,1)S(1)}, bf16[8,24,128]{2,1,0:T(8,128)(2,1)S(1)}, u32[]{:S(2)}, u32[]{:S(2)}) collective-permute-start(bf16[8,24,128]{2,1,0:T(8,128)(2,1)S(1)} %dynamic-slice_bitcast_fusion.1), channel_id=1, source_target_pairs={{0,128},{1,129},{2,130},{3,131},{4,132},{5,133},{6,134},{7,135},{8... | collective-permute-start | bytes 147464 | tf_op jit(solution)/shard_map/ppermute | solution.py:391
  83.9 3.2 %collective-permute-done.9 = bf16[8,24,128]{2,1,0:T(8,128)(2,1)S(1)} collective-permute-done((bf16[8,24,128]{2,1,0:T(8,128)(2,1)S(1)}, bf16[8,24,128]{2,1,0:T(8,128)(2,1)S(1)}, u32[]{:S(2)}, u32[]{:S(2)}) %collective-permute-start.9) | collective-permute-done | bytes 49184 | tf_op jit(solution)/shard_map/ppermute | solution.py:391
  87.1 2.8 %collective-permute-start.10 = (f32[4,24,128]{2,1,0:T(8,128)S(1)}, f32[4,24,128]{2,1,0:T(8,128)S(1)}, u32[]{:S(2)}, u32[]{:S(2)}) collective-permute-start(f32[4,24,128]{2,1,0:T(8,128)S(1)} %dynamic-slice_bitcast_fusion), channel_id=1, source_target_pairs={{0,64},{1,65},{2,66},{3,67},{4,68},{5,69},{6,70},{7,71},{8,72},{9,... | collective-permute-start | bytes 147464 | tf_op jit(solution)/shard_map/ppermute | solution.py:391
  89.9 2.1 %collective-permute-done.10 = f32[4,24,128]{2,1,0:T(8,128)S(1)} collective-permute-done((f32[4,24,128]{2,1,0:T(8,128)S(1)}, f32[4,24,128]{2,1,0:T(8,128)S(1)}, u32[]{:S(2)}, u32[]{:S(2)}) %collective-permute-start.10) | collective-permute-done | bytes 49184 | tf_op jit(solution)/shard_map/ppermute | solution.py:391
  92.0 4.3 %collective-permute-start.11 = (f32[2,24,128]{2,1,0:T(8,128)S(1)}, f32[2,24,128]{2,1,0:T(8,128)S(1)}, u32[]{:S(2)}, u32[]{:S(2)}) collective-permute-start(f32[2,24,128]{2,1,0:T(8,128)S(1)} %dynamic-slice_bitcast_fusion.2), channel_id=1, source_target_pairs={{0,32},{1,33},{2,34},{3,35},{4,36},{5,37},{6,38},{7,39},{8,40},{9,... | collective-permute-start | bytes 73736 | tf_op jit(solution)/shard_map/ppermute | solution.py:391
  96.4 3.5 %collective-permute-done.11 = f32[2,24,128]{2,1,0:T(8,128)S(1)} collective-permute-done((f32[2,24,128]{2,1,0:T(8,128)S(1)}, f32[2,24,128]{2,1,0:T(8,128)S(1)}, u32[]{:S(2)}, u32[]{:S(2)}) %collective-permute-start.11) | collective-permute-done | bytes 24608 | tf_op jit(solution)/shard_map/ppermute | solution.py:391
  99.9 3.0 %collective-permute-start.12 = (f32[24,128]{1,0:T(8,128)S(1)}, f32[24,128]{1,0:T(8,128)S(1)}, u32[]{:S(2)}, u32[]{:S(2)}) collective-permute-start(f32[24,128]{1,0:T(8,128)S(1)} %get-tuple-element.108), channel_id=1, source_target_pairs={{0,16},{1,17},{2,18},{3,19},{4,20},{5,21},{6,22},{7,23},{8,24},{9,... | collective-permute-start | bytes 36872 | tf_op jit(solution)/shard_map/ppermute | solution.py:391
  102.9 0.8 copy.9
  103.7 0.8 copy.10
  104.6 1.3 %finish.1 = (f32[8,128]{1,0:T(8,128)}, f32[8,128]{1,0:T(8,128)}) custom-call(s32[6]{0:T(128)S(1)} %stack.43.place.refs_0_, f32[24,128]{1,0:T(8,128)S(1)} %get-tuple-element.109.held, f32[24,128]{1,0:T(8,128)S(1)} %collective-permute-done.12.got), custom_call_target="tpu_custom_call" | custom-call | flops 1048576 | bytes 1048576 | tf_op jit(solution)/shard_map/finish/pallas_call | solution.py:368
  (55 shorter events, 9.0 us)
Async XLA Ops:
  0.6 0.9 copy-start
  1.6 0.9 copy-start.1
  2.5 0.7 copy-start.2
  3.9 14.6 %collective-permute-start = (bf16[592,128]{1,0:T(8,128)(2,1)S(1)}, bf16[592,128]{1,0:T(8,128)(2,1)S(1)}, u32[]{:S(2)}, u32[]{:S(2)}) collective-permute-start(bf16[592,128]{1,0:T(8,128)(2,1)S(1)} %get-tuple-element.46), channel_id=1, source_target_pairs={{0,16},{16,32},{32,48},{48,64},{64,80},{80,96},{96,112},{112,128},... | collective-permute-start | bytes 454664 | tf_op jit(solution)/shard_map/ppermute | solution.py:416
  7.2 11.4 %collective-permute-start.1 = (bf16[592,128]{1,0:T(8,128)(2,1)S(1)}, bf16[592,128]{1,0:T(8,128)(2,1)S(1)}, u32[]{:S(2)}, u32[]{:S(2)}) collective-permute-start(bf16[592,128]{1,0:T(8,128)(2,1)S(1)} %get-tuple-element.47), channel_id=1, source_target_pairs={{0,240},{16,0},{32,16},{48,32},{64,48},{80,64},{96,80},{112,96},{1... | collective-permute-start | bytes 454664 | tf_op jit(solution)/shard_map/ppermute | solution.py:417
  10.3 1.1 %copy-start.3 = (bf16[27,96,96]{2,1,0:T(8,128)(2,1)S(1)}, bf16[27,96,96]{2,1,0:T(8,128)(2,1)}, u32[]{:S(2)}) copy-start(bf16[27,96,96]{2,1,0:T(8,128)(2,1)} %first.1) | copy-start | bytes 1492996
  11.4 1.1 %copy-start.4 = (bf16[27,96,96]{2,1,0:T(8,128)(2,1)S(1)}, bf16[27,96,96]{2,1,0:T(8,128)(2,1)}, u32[]{:S(2)}) copy-start(bf16[27,96,96]{2,1,0:T(8,128)(2,1)} %second.1) | copy-start | bytes 1492996
  16.5 1.2 %copy-start.9 = (bf16[5,1152,128]{2,1,0:T(8,128)(2,1)}, bf16[5,1152,128]{2,1,0:T(8,128)(2,1)S(1)}, u32[]{:S(2)}) copy-start(bf16[5,1152,128]{2,1,0:T(8,128)(2,1)S(1)} %get-tuple-element.72.refs_10_) | copy-start | bytes 4423684
  17.6 0.7 copy-start.11
  18.3 1.7 %copy-start.5 = (bf16[5,1152,128]{2,1,0:T(8,128)(2,1)}, bf16[5,1152,128]{2,1,0:T(8,128)(2,1)S(1)}, u32[]{:S(2)}) copy-start(bf16[5,1152,128]{2,1,0:T(8,128)(2,1)S(1)} %get-tuple-element.70.refs_8_) | copy-start | bytes 4423684
  18.3 1.7 %copy-start.7 = (bf16[5,1152,128]{2,1,0:T(8,128)(2,1)}, bf16[5,1152,128]{2,1,0:T(8,128)(2,1)S(1)}, u32[]{:S(2)}) copy-start(bf16[5,1152,128]{2,1,0:T(8,128)(2,1)S(1)} %get-tuple-element.71.refs_9_) | copy-start | bytes 4423684
  23.5 9.6 %collective-permute-start.2 = (bf16[1104,128]{1,0:T(8,128)(2,1)}, bf16[1104,128]{1,0:T(8,128)(2,1)S(1)}, u32[]{:S(2)}, u32[]{:S(2)}) collective-permute-start(bf16[1104,128]{1,0:T(8,128)(2,1)} %get-tuple-element.105), channel_id=1, source_target_pairs={{0,1},{1,2},{2,3},{3,4},{4,5},{5,6},{6,7},{7,8},{8,9},{9,10},{10,1... | collective-permute-start | bytes 847880 | tf_op jit(solution)/shard_map/ppermute | solution.py:453
  23.5 9.6 %collective-permute-start.3 = (bf16[1104,128]{1,0:T(8,128)(2,1)}, bf16[1104,128]{1,0:T(8,128)(2,1)S(1)}, u32[]{:S(2)}, u32[]{:S(2)}) collective-permute-start(bf16[1104,128]{1,0:T(8,128)(2,1)} %get-tuple-element.104), channel_id=1, source_target_pairs={{0,15},{1,0},{2,1},{3,2},{4,3},{5,4},{6,5},{7,6},{8,7},{9,8},{10,9... | collective-permute-start | bytes 847880 | tf_op jit(solution)/shard_map/ppermute | solution.py:454
  27.5 5.7 %copy-start.6 = (bf16[5,1152,128]{2,1,0:T(8,128)(2,1)S(1)}, bf16[5,1152,128]{2,1,0:T(8,128)(2,1)}, u32[]{:S(2)}) copy-start(bf16[5,1152,128]{2,1,0:T(8,128)(2,1)} %copy-done.5) | copy-start | bytes 4423684
  27.5 5.7 %copy-start.8 = (bf16[5,1152,128]{2,1,0:T(8,128)(2,1)S(1)}, bf16[5,1152,128]{2,1,0:T(8,128)(2,1)}, u32[]{:S(2)}) copy-start(bf16[5,1152,128]{2,1,0:T(8,128)(2,1)} %copy-done.7) | copy-start | bytes 4423684
  27.5 5.7 %copy-start.10 = (bf16[5,1152,128]{2,1,0:T(8,128)(2,1)S(1)}, bf16[5,1152,128]{2,1,0:T(8,128)(2,1)}, u32[]{:S(2)}) copy-start(bf16[5,1152,128]{2,1,0:T(8,128)(2,1)} %copy-done.9) | copy-start | bytes 4423684
  27.5 5.7 %copy-start.12 = (bf16[8,128,128]{2,1,0:T(8,128)(2,1)S(1)}, bf16[8,128,128]{2,1,0:T(8,128)(2,1)}, u32[]{:S(2)}) copy-start(bf16[8,128,128]{2,1,0:T(8,128)(2,1)} %copy-done.11) | copy-start | bytes 786436
  61.4 2.4 %collective-permute-start.4 = (bf16[4,576,128]{2,1,0:T(8,128)(2,1)S(1)}, bf16[4,576,128]{2,1,0:T(8,128)(2,1)S(1)}, u32[]{:S(2)}, u32[]{:S(2)}) collective-permute-start(bf16[4,576,128]{2,1,0:T(8,128)(2,1)S(1)} %get-tuple-element.76), channel_id=1, source_target_pairs={{0,1},{1,0},{2,3},{3,2},{4,5},{5,4},{6,7},{7,6},{8,9},{9,8},{10,11... | collective-permute-start | bytes 1769480 | tf_op jit(solution)/shard_map/ppermute | solution.py:391
  64.0 6.8 %collective-permute-start.5 = (bf16[576,128]{1,0:T(8,128)(2,1)S(1)}, bf16[576,128]{1,0:T(8,128)(2,1)S(1)}, u32[]{:S(2)}, u32[]{:S(2)}) collective-permute-start(bf16[576,128]{1,0:T(8,128)(2,1)S(1)} %get-tuple-element.95), channel_id=1, source_target_pairs={{0,2},{1,3},{2,0},{3,1},{4,6},{5,7},{6,4},{7,5},{8,10},{9,11},{10,... | collective-permute-start | bytes 442376 | tf_op jit(solution)/shard_map/ppermute | solution.py:391
  65.1 8.1 %collective-permute-start.6 = (bf16[576,128]{1,0:T(8,128)(2,1)S(1)}, bf16[576,128]{1,0:T(8,128)(2,1)S(1)}, u32[]{:S(2)}, u32[]{:S(2)}) collective-permute-start(bf16[576,128]{1,0:T(8,128)(2,1)S(1)} %get-tuple-element.94), channel_id=1, source_target_pairs={{0,4},{1,5},{2,6},{3,7},{4,0},{5,1},{6,2},{7,3},{8,12},{9,13},{10,... | collective-permute-start | bytes 442376 | tf_op jit(solution)/shard_map/ppermute | solution.py:391
  66.7 7.7 %collective-permute-start.7 = (bf16[576,128]{1,0:T(8,128)(2,1)S(1)}, bf16[576,128]{1,0:T(8,128)(2,1)S(1)}, u32[]{:S(2)}, u32[]{:S(2)}) collective-permute-start(bf16[576,128]{1,0:T(8,128)(2,1)S(1)} %get-tuple-element.93), channel_id=1, source_target_pairs={{0,6},{1,7},{2,4},{3,5},{4,2},{5,3},{6,0},{7,1},{8,14},{9,15},{10,... | collective-permute-start | bytes 442376 | tf_op jit(solution)/shard_map/ppermute | solution.py:391
  75.1 6.2 %collective-permute-start.8 = (bf16[384,128]{1,0:T(8,128)(2,1)S(1)}, bf16[384,128]{1,0:T(8,128)(2,1)S(1)}, u32[]{:S(2)}, u32[]{:S(2)}) collective-permute-start(bf16[384,128]{1,0:T(8,128)(2,1)S(1)} %get-tuple-element.85), channel_id=1, source_target_pairs={{0,8},{1,9},{2,10},{3,11},{4,12},{5,13},{6,14},{7,15},{8,0},{9,1},... | collective-permute-start | bytes 294920 | tf_op jit(solution)/shard_map/ppermute | solution.py:391
  81.4 5.7 %collective-permute-start.9 = (bf16[8,24,128]{2,1,0:T(8,128)(2,1)S(1)}, bf16[8,24,128]{2,1,0:T(8,128)(2,1)S(1)}, u32[]{:S(2)}, u32[]{:S(2)}) collective-permute-start(bf16[8,24,128]{2,1,0:T(8,128)(2,1)S(1)} %dynamic-slice_bitcast_fusion.1), channel_id=1, source_target_pairs={{0,128},{1,129},{2,130},{3,131},{4,132},{5,133},{6,134},{7,135},{8... | collective-permute-start | bytes 147464 | tf_op jit(solution)/shard_map/ppermute | solution.py:391
  87.1 4.9 %collective-permute-start.10 = (f32[4,24,128]{2,1,0:T(8,128)S(1)}, f32[4,24,128]{2,1,0:T(8,128)S(1)}, u32[]{:S(2)}, u32[]{:S(2)}) collective-permute-start(f32[4,24,128]{2,1,0:T(8,128)S(1)} %dynamic-slice_bitcast_fusion), channel_id=1, source_target_pairs={{0,64},{1,65},{2,66},{3,67},{4,68},{5,69},{6,70},{7,71},{8,72},{9,... | collective-permute-start | bytes 147464 | tf_op jit(solution)/shard_map/ppermute | solution.py:391
  92.0 7.8 %collective-permute-start.11 = (f32[2,24,128]{2,1,0:T(8,128)S(1)}, f32[2,24,128]{2,1,0:T(8,128)S(1)}, u32[]{:S(2)}, u32[]{:S(2)}) collective-permute-start(f32[2,24,128]{2,1,0:T(8,128)S(1)} %dynamic-slice_bitcast_fusion.2), channel_id=1, source_target_pairs={{0,32},{1,33},{2,34},{3,35},{4,36},{5,37},{6,38},{7,39},{8,40},{9,... | collective-permute-start | bytes 73736 | tf_op jit(solution)/shard_map/ppermute | solution.py:391
  99.9 4.7 %collective-permute-start.12 = (f32[24,128]{1,0:T(8,128)S(1)}, f32[24,128]{1,0:T(8,128)S(1)}, u32[]{:S(2)}, u32[]{:S(2)}) collective-permute-start(f32[24,128]{1,0:T(8,128)S(1)} %get-tuple-element.108), channel_id=1, source_target_pairs={{0,16},{1,17},{2,18},{3,19},{4,20},{5,21},{6,22},{7,23},{8,24},{9,... | collective-permute-start | bytes 36872 | tf_op jit(solution)/shard_map/ppermute | solution.py:391

commit v3 on v2

v3 whole, which is shorter than its diff:
```python
import math

import jax
import jax.numpy as jnp
from jax import lax
from jax.experimental import pallas as pl
from jax.experimental.pallas import tpu as pltpu
from jax.sharding import PartitionSpec as P

BOTH = ("east", "north")
F32 = jnp.float32
BF16 = jnp.bfloat16
CH = 96
LN = 128
TAPS = 7 * LN
WHOLE = (0, 2, 3, 5, 6, 7, 8)
SPLIT = (1, 1, 1, 4, 4, 4)
STRIP = 6 * CH + 16
RIM = 11 * CH + 48
VMEM = pl.BlockSpec(memory_space=pltpu.VMEM)
SMEM = pl.BlockSpec(memory_space=pltpu.SMEM)


def lanes(rows):
    return lax.broadcasted_iota(jnp.int32, (rows, LN), 1)


def flip_pad(value):
    wide = jnp.concatenate(
        [value.astype(F32), jnp.zeros((LN - value.shape[0], value.shape[1]), F32)], axis=0
    )
    return wide.T


def mask_column(ref, row):
    tile = ref[row : row + 16, :].astype(F32)
    return jnp.concatenate([tile] * 8, axis=0).T


def strips_kernel(
    occupied,
    features,
    cotangent,
    feat,
    cot,
    to_west,
    to_east,
    own_mask,
    near_feat,
    near_cot,
    near_occupied,
    wide_feat,
    wide_cot,
    sems,
):
    copies = [
        pltpu.make_async_copy(features, near_feat, sems.at[0]),
        pltpu.make_async_copy(cotangent, near_cot, sems.at[1]),
        pltpu.make_async_copy(occupied, near_occupied, sems.at[2]),
    ]
    for copy in copies:
        copy.start()
    for copy, near, wide, out in (
        (copies[0], near_feat, wide_feat, feat),
        (copies[1], near_cot, wide_cot, cot),
    ):
        copy.wait()
        wide[...] = near[...].astype(F32).reshape(CH * 8, LN)
        for x in range(8):
            out[x] = wide[pl.ds(x, CH, stride=8), :].astype(BF16)
    copies[2].wait()
    levels = near_occupied[...].astype(F32)
    own_mask[...] = jnp.where((lanes(16) & 15) < 8, levels[:, 0:1], levels[:, 1:2]).astype(BF16)
    for out, first, second in ((to_west, 0, 0), (to_east, 4, 6)):
        for k in range(4):
            out[k * CH : (k + 1) * CH, :] = feat[first + k]
        for k in range(2):
            out[(4 + k) * CH : (5 + k) * CH, :] = cot[second + k]
        out[6 * CH : STRIP, :] = own_mask[...]


def turn_levels(value, x, turned):
    lane = lanes(CH) & 15
    below = jnp.where(lane == 0, 0.0, pltpu.roll(value, 1, 1))
    above = jnp.where(lane == 15, 0.0, pltpu.roll(value, LN - 1, 1))
    start = x * LN if isinstance(x, int) else pl.multiple_of(x * LN, LN)
    for c, moved in enumerate((below, value, above)):
        turned[c * CH : (c + 1) * CH, pl.ds(start, LN)] = moved.astype(BF16)


def prepare_kernel(
    first,
    second,
    feat,
    cot,
    own_mask,
    fwd_one,
    fwd_two,
    back_two,
    back_one,
    turned_one,
    own_grid,
    own_cot,
    token,
):
    token[...] = jnp.zeros_like(token)
    for out in (fwd_one, fwd_two, back_two, back_one):
        out[...] = jnp.zeros_like(out)

    def body(plane, carry):
        for source, ahead, back in ((first, fwd_one, back_one), (second, fwd_two, back_two)):
            for k in range(9):
                straight = source[9 * plane + k]
                turned = jnp.pad(
                    source[26 - 9 * plane - k].astype(F32), ((0, LN - CH), (0, LN - CH))
                ).T.astype(BF16)
                if k in WHOLE:
                    row = WHOLE.index(k) * LN
                    ahead[plane + 1, row : row + CH, 0:CH] = straight
                    back[plane + 1, row : row + CH, :] = turned[0:CH]
                else:
                    for q in range(3):
                        row = (SPLIT.index(k) + q) * LN + CH
                        ahead[plane + 1, row : row + 32, 0:CH] = straight[32 * q : 32 * q + 32]
                        back[plane + 1, row : row + 32, :] = turned[32 * q : 32 * q + 32]
        return carry

    lax.fori_loop(0, 3, body, 0)
    mask = jnp.concatenate([own_mask[...].astype(F32)] * 6, axis=0)
    for x in range(8):
        value = feat[x].astype(F32) * mask
        turn_levels(value, x, turned_one)
        own_grid[x] = flip_pad(value).astype(BF16)
        own_cot[x] = flip_pad(cot[x]).astype(BF16)


def rims_kernel(west, east, feat, cot, own_mask, to_south, to_north):
    half = lanes(CH) < 64
    quarter = lanes(CH) // 32

    def feat_plane(p):
        if p < 4:
            return west[p * CH : (p + 1) * CH, :].astype(F32)
        if p < 12:
            return feat[p - 4].astype(F32)
        return east[(p - 12) * CH : (p - 11) * CH, :].astype(F32)

    def cot_plane(p):
        if p < 2:
            return west[(4 + p) * CH : (5 + p) * CH, :].astype(F32)
        if p < 10:
            return cot[p - 2].astype(F32)
        return east[(p - 6) * CH : (p - 5) * CH, :].astype(F32)

    for k in range(8):
        one, two = feat_plane(k), feat_plane(k + 8)
        rows = slice(k * CH, (k + 1) * CH)
        to_south[rows, :] = jnp.where(half, one, pltpu.roll(two, 64, 1)).astype(BF16)
        to_north[rows, :] = jnp.where(half, pltpu.roll(one, 64, 1), two).astype(BF16)
    for k in range(3):
        four = [cot_plane(k + 3 * q) for q in range(4)]
        rows = slice((8 + k) * CH, (9 + k) * CH)
        for out, shift in ((to_south, 0), (to_north, 32)):
            moved = [
                pltpu.roll(four[q], (32 * q + shift) % LN, 1) if (32 * q + shift) % LN else four[q]
                for q in range(4)
            ]
            packed = jnp.where(
                quarter < 2,
                jnp.where(quarter == 0, moved[0], moved[1]),
                jnp.where(quarter == 2, moved[2], moved[3]),
            )
            out[rows, :] = packed.astype(BF16)
    for out in (to_south, to_north):
        out[11 * CH : 11 * CH + 16, :] = west[6 * CH : STRIP, :]
        out[11 * CH + 16 : 11 * CH + 32, :] = own_mask[...]
        out[11 * CH + 32 : RIM, :] = east[6 * CH : STRIP, :]


def sides_kernel(place, own_mask, west, east, side_grid, side_cot, middle, token):
    token[...] = jnp.zeros_like(token)
    middle[0] = mask_column(west, 6 * CH) * place[0].astype(F32)
    middle[1] = mask_column(own_mask, 0)
    middle[2] = mask_column(east, 6 * CH) * place[1].astype(F32)
    for side, ref in ((0, west), (1, east)):
        for k in range(4):
            block = flip_pad(ref[k * CH : (k + 1) * CH, :]) * middle[2 * side]
            side_grid[4 * side + k] = block.astype(BF16)
        for k in range(2):
            side_cot[2 * side + k] = flip_pad(ref[(4 + k) * CH : (5 + k) * CH, :]).astype(BF16)


def spread(taps, plane, value, rows):
    count = rows + 32
    level = lax.broadcasted_iota(jnp.int32, (count, LN), 0) & 15
    below = jnp.where(level == 0, 0.0, pltpu.roll(value, 1, 0))
    above = jnp.where(level == 15, 0.0, pltpu.roll(value, count - 1, 0))
    spare = lanes(count) >= CH
    short = [moved.astype(BF16) for moved in (below, value, above)]
    rest = [
        jnp.where(spare, pltpu.roll(value, CH - 32 * q, 1), 0.0).astype(BF16) for q in range(3)
    ]
    for n, k in enumerate(WHOLE):
        start = 16 * (k // 3)
        block = short[k % 3][start : start + rows]
        if n < 6:
            start = 16 * (SPLIT[n] // 3)
            block = block + rest[n % 3][start : start + rows]
        taps[plane // 2, plane % 2, 0:rows, n * LN : (n + 1) * LN] = block


def convolve(taps, weight, pair, rows):
    left = jnp.concatenate(
        [taps[pair + j // 2, j % 2, 0:rows, :] for j in range(4)], axis=1
    )
    right = jnp.concatenate(
        [jnp.concatenate([weight[j + 1], weight[j]], axis=1) for j in range(4)], axis=0
    )
    return jnp.dot(left, right, preferred_element_type=F32)


def pipeline(taps, weight, total, pairs, rows, after):
    for i in range(pairs + 1):
        if i < pairs:
            total[i * rows : (i + 1) * rows, :] = convolve(taps, weight, i, rows)
        if i > 0:
            for half in range(2):
                value = total[(i - 1) * rows : i * rows, half * LN : half * LN + LN]
                after(2 * (i - 1) + half, value)


def kernel_grad(turned, planes, shift, scale, result):
    def piece(k):
        a, b = k // 3, k % 3
        start = (shift + 1 - b) * 16
        return planes[shift + 1 - a : shift + 9 - a, start : start + 128, :].reshape(1024, LN)

    for k in range(0, 9, 2):
        right = jnp.concatenate([piece(k), piece(min(k + 1, 8))], axis=1)
        part = jnp.dot(turned[...], right, preferred_element_type=F32) * scale
        result[k * 288 : k * 288 + 288, :] = part[:, 0:LN]
        if k < 8:
            result[(k + 1) * 288 : (k + 1) * 288 + 288, :] = part[:, LN : 2 * LN]


def band(p, low, high):
    return int(p >= low) + int(p >= high)


def level_kernel(
    scale,
    place,
    own_grid,
    side_grid,
    own_cot,
    side_cot,
    middle,
    south,
    north,
    fwd_one,
    fwd_two,
    back_two,
    turned_one,
    activated,
    grad_one,
    masks,
    keep,
    send,
    taps,
    more_taps,
    edge,
    upstream,
    total,
    slope_one,
    grad_two,
    turned_two,
    grad_one_sum,
    grad_two_sum,
    packed,
):
    for ref, flag, row in ((south, place[2], 0), (north, place[3], 192)):
        tile = ref[11 * CH : 11 * CH + 48, :].astype(F32) * flag.astype(F32)
        turned = jnp.concatenate([tile, jnp.zeros((80, LN), F32)], axis=0).T[0:64]
        for bx in range(3):
            side = place[bx // 2].astype(F32) if bx != 1 else 1.0
            column = turned[:, 16 * bx : 16 * bx + 1] * side
            masks[bx, row : row + 64, :] = jnp.broadcast_to(column, (64, LN))
    masks[:, 64:192, :] = middle[...]

    for k in range(8):
        for ref, row in ((south, 0), (north, 64)):
            both = flip_pad(ref[k * CH : (k + 1) * CH, :])
            edge[k, row : row + 64, :] = both[0:64]
            edge[k + 8, row : row + 64, :] = both[64:128]
    for k in range(3):
        for ref, row in ((south, 0), (north, 160)):
            four = flip_pad(ref[(8 + k) * CH : (9 + k) * CH, :])
            for q in range(4):
                upstream[k + 3 * q, row : row + 32, :] = four[32 * q : 32 * q + 32]
    for k in range(2):
        upstream[k, 32:160, :] = side_cot[k].astype(F32)
        upstream[10 + k, 32:160, :] = side_cot[2 + k].astype(F32)
    for k in range(8):
        upstream[2 + k, 32:160, :] = own_cot[k].astype(F32)

    for p in range(16):
        bx = band(p, 4, 12)
        value = own_grid[p - 4] if bx == 1 else side_grid[p % 8]
        low = edge[p, 0:64, :] * masks[bx, 0:64, :]
        high = edge[p, 64:128, :] * masks[bx, 192:256, :]
        spread(taps, p, jnp.concatenate([low, value.astype(F32), high], axis=0), 224)

    def after_one(p, value):
        value = value * masks[band(p, 3, 11), 16:240, :]
        sigma = jax.nn.sigmoid(value)
        if 2 <= p < 12:
            slope_one[p - 2] = (sigma * (1.0 + value * (1.0 - sigma)))[32:192]
        hidden = (value * sigma).astype(BF16).astype(F32)
        spread(more_taps, p, hidden, 192)
        if 3 <= p < 11:
            turn_levels(hidden[48:176].T[0:CH], p - 3, turned_two)

    pipeline(taps, fwd_one, total, 7, 224, after_one)

    def after_two(p, value):
        mask = masks[band(p, 2, 10), 32:224, :]
        value = value * mask
        sigma = jax.nn.sigmoid(value)
        if 2 <= p < 10:
            activated[p - 2] = (value * sigma)[32:160].T[0:CH].astype(BF16)
        slope = sigma * (1.0 + value * (1.0 - sigma))
        grad = upstream[p] * slope * mask
        grad_two[p] = grad.astype(BF16)
        spread(taps, p, grad, 160)

    pipeline(more_taps, fwd_two, total, 6, 192, after_two)
    kernel_grad(turned_two, grad_two, 2, scale, grad_two_sum)

    def after_three(p, value):
        grad = value * slope_one[p] * masks[band(p, 1, 9), 48:208, :]
        grad_one[p] = grad.astype(BF16)

    pipeline(taps, back_two, total, 5, 160, after_three)
    kernel_grad(turned_one, grad_one, 1, scale, grad_one_sum)

    me = place[4]
    bit = place[5]
    tail = lanes(CH) < CH
    for out, low in ((keep, 0), (send, 1)):
        for e in range(4):
            near, far = e % 2, e // 2
            for grad, source in ((0, grad_one_sum), (1, grad_two_sum)):
                for turn in range(2):
                    j = jnp.bitwise_xor(me, 4 * (turn ^ far) + 2 * near + low)
                    first = 10 * j + 81 * jnp.bitwise_xor(bit, far)

                    def gather(m, carry):
                        packed[pl.ds(192 * turn + 12 * m, 16), :] = source[
                            pl.ds(first + 162 * m, 16), :
                        ]
                        return carry

                    lax.fori_loop(0, 16, gather, 0, unroll=8)
                last = packed[288:384, :]
                for k in range(3):
                    block = jnp.where(
                        tail, packed[CH * k : CH * k + CH, :], pltpu.roll(last, CH - 32 * k, 1)
                    )
                    start = 288 * grad + CH * k
                    out[e, start : start + CH, :] = block.astype(BF16)


def final_kernel(grad_one, masks, back_one, feature_grad, token, taps, total):
    token[...] = jnp.zeros_like(token)
    for p in range(10):
        spread(taps, p, grad_one[p].astype(F32), 128)

    def after_four(p, value):
        feature_grad[p] = (value * masks[1, 64:192, :]).T[0:CH].astype(BF16)

    pipeline(taps, back_one, total, 4, 128, after_four)


def combine_kernel(a0, a1, a2, a3, hold, give, ordered):
    lane = lanes(CH)
    for grad in range(2):
        blocks = []
        for k in range(3):
            start = 288 * grad + CH * k
            blocks.append(
                sum(ref[start : start + CH, :].astype(F32) for ref in (a0, a1, a2, a3))
            )
        a, b, c = blocks
        last = jnp.where(
            lane < 32,
            pltpu.roll(a, 32, 1),
            jnp.where(lane < 64, pltpu.roll(b, 64, 1), pltpu.roll(c, 96, 1)),
        )
        for k, block in enumerate((a, b, c, last)):
            for m in range(8):
                start = 192 * k + 24 * m + 12 * grad
                ordered[start : start + 12, :] = block[12 * m : 12 * m + 12]
    hold[...] = ordered[0:384, :].astype(BF16)
    give[...] = ordered[384:768, :].astype(BF16)


def finish_kernel(place, held, got, out_one, out_two):
    j = place[4]
    lane = lanes(1)
    value = held[...] + got[...]
    for grad, out in ((0, out_one), (1, out_two)):
        flat = []
        for m in range(3):
            r = [value[12 * grad + 4 * m + q : 12 * grad + 4 * m + q + 1] for q in range(4)]
            flat.append(jnp.where(lane < 96, r[0], pltpu.roll(r[1], 96, 1)))
            flat.append(jnp.where(lane < 64, pltpu.roll(r[1], 96, 1), pltpu.roll(r[2], 64, 1)))
            flat.append(jnp.where(lane < 32, pltpu.roll(r[2], 64, 1), pltpu.roll(r[3], 32, 1)))
        low = jnp.concatenate(flat[0:8], axis=0)
        high = jnp.concatenate(flat[1:9], axis=0)
        turn = lax.rem(LN - 12 * j, LN)
        out[...] = jnp.where(
            lanes(8) < LN - 12 * j, pltpu.roll(low, turn, 1), pltpu.roll(high, turn, 1)
        )


def call(kernel, name, outs, scratch, limit, flops, specs, *args):
    return pl.pallas_call(
        kernel,
        out_shape=outs,
        in_specs=specs,
        out_specs=[VMEM] * len(outs),
        scratch_shapes=scratch,
        compiler_params=pltpu.CompilerParams(vmem_limit_bytes=limit << 20),
        cost_estimate=pl.CostEstimate(flops=flops, bytes_accessed=1 << 20, transcendentals=0),
        name=name,
    )(*args)


def shape(*dims, dtype=BF16):
    return jax.ShapeDtypeStruct(dims, dtype)


def shift_by(step, axis):
    count = lax.axis_size(axis)
    return [(i, (i + step) % count) for i in range(count)]


def swap(value, bits):
    count = lax.axis_size("east") * lax.axis_size("north")
    return lax.ppermute(value, BOTH, [(i, i ^ bits) for i in range(count)])


def local(features, occupancy, weight_first, weight_second, cotangent):
    column = lax.axis_index("east")
    row = lax.axis_index("north")
    position = column * 16 + row
    block = position // 8
    scale = 1.0 / math.sqrt(128 * 128 * 16)
    place = jnp.stack(
        [column > 0, column < 15, row > 0, row < 15, position % 8, block % 2]
    ).astype(jnp.int32)

    feat, cot, to_west, to_east, own_mask = call(
        strips_kernel,
        "strips",
        [shape(8, CH, LN), shape(8, CH, LN), shape(STRIP, LN), shape(STRIP, LN), shape(16, LN)],
        [
            pltpu.VMEM((CH, 8, LN), BF16),
            pltpu.VMEM((CH, 8, LN), BF16),
            pltpu.VMEM((1, 2), jnp.int32),
            pltpu.VMEM((CH * 8, LN), F32),
            pltpu.VMEM((CH * 8, LN), F32),
            pltpu.SemaphoreType.DMA((3,)),
        ],
        60,
        1 << 20,
        [pl.BlockSpec(memory_space=pltpu.HBM)] * 3,
        occupancy.reshape(1, 2),
        features,
        cotangent,
    )
    west = lax.ppermute(to_east, "east", shift_by(1, "east"))
    east = lax.ppermute(to_west, "east", shift_by(-1, "east"))

    weight = shape(5, TAPS, LN)
    tile = shape(8, LN, LN)
    mark = shape(8, LN, dtype=F32)
    prepared = call(
        prepare_kernel,
        "prepare",
        [weight, weight, weight, weight, shape(288, 1024), tile, tile, mark],
        [],
        16,
        1 << 33,
        [VMEM] * 5,
        weight_first,
        weight_second,
        feat,
        cot,
        own_mask,
    )
    fwd_one, fwd_two, back_two, back_one, turned_one, own_grid, own_cot, token = prepared
    west, east, token = lax.optimization_barrier((west, east, token))
    to_south, to_north = call(
        rims_kernel,
        "rims",
        [shape(RIM, LN), shape(RIM, LN)],
        [],
        8,
        1 << 20,
        [VMEM] * 5,
        west,
        east,
        feat,
        cot,
        own_mask,
    )
    south = lax.ppermute(to_north, "north", shift_by(1, "north"))
    north = lax.ppermute(to_south, "north", shift_by(-1, "north"))
    side_grid, side_cot, middle, token = call(
        sides_kernel,
        "sides",
        [tile, shape(4, LN, LN), shape(3, LN, LN, dtype=F32), mark],
        [],
        8,
        1 << 31,
        [SMEM] + [VMEM] * 3,
        place,
        own_mask,
        west,
        east,
    )
    south, north, token = lax.optimization_barrier((south, north, token))

    activated, grad_one, masks, keep, send = call(
        lambda *refs: level_kernel(scale, *refs),
        "level",
        [
            shape(8, CH, LN),
            shape(10, 160, LN),
            shape(3, 256, LN, dtype=F32),
            shape(4, 576, LN),
            shape(4, 576, LN),
        ],
        [
            pltpu.VMEM((8, 2, 224, TAPS), BF16),
            pltpu.VMEM((7, 2, 192, TAPS), BF16),
            pltpu.VMEM((16, 128, LN), F32),
            pltpu.VMEM((12, 192, LN), F32),
            pltpu.VMEM((7 * 224, 2 * LN), F32),
            pltpu.VMEM((10, 160, LN), F32),
            pltpu.VMEM((12, 192, LN), BF16),
            pltpu.VMEM((288, 1024), BF16),
            pltpu.VMEM((2592 + 16, LN), F32),
            pltpu.VMEM((2592 + 16, LN), F32),
            pltpu.VMEM((400, LN), F32),
        ],
        36,
        1 << 34,
        [SMEM] + [VMEM] * 11,
        place,
        own_grid,
        side_grid,
        own_cot,
        side_cot,
        middle,
        south,
        north,
        fwd_one,
        fwd_two,
        back_two,
        turned_one,
    )

    def add(*terms):
        return sum(t.astype(F32) for t in terms)

    part = add(keep, swap(send, 1)).astype(BF16)
    others = [swap(part[k], bits) for k, bits in ((1, 2), (2, 12), (3, 14))]
    feature_grad, token = call(
        final_kernel,
        "final",
        [shape(8, CH, LN), mark],
        [pltpu.VMEM((5, 2, 128, TAPS), BF16), pltpu.VMEM((512, 2 * LN), F32)],
        16,
        1 << 32,
        [VMEM] * 3,
        grad_one,
        masks,
        back_one,
    )
    others, token = lax.optimization_barrier((others, token))
    hold, give = call(
        combine_kernel,
        "combine",
        [shape(384, LN), shape(384, LN)],
        [pltpu.VMEM((768, LN), F32)],
        8,
        1 << 20,
        [VMEM] * 4,
        part[0],
        *others,
    )
    part = add(hold, swap(give, 4)).reshape(16, 24, LN)
    for bit, kind, partner in ((8, BF16, 192), (4, F32, 64), (2, F32, 48)):
        half = part.reshape((2, -1, 24, LN)).astype(kind)
        mine = (block // (2 * bit)) % 2
        held = lax.dynamic_index_in_dim(half, mine, 0, keepdims=False)
        given = lax.dynamic_index_in_dim(half, 1 - mine, 0, keepdims=False)
        part = add(held, swap(given, partner))
    mine = (block // 2) % 2
    held = lax.dynamic_index_in_dim(part, mine, 0, keepdims=False)
    given = lax.dynamic_index_in_dim(part, 1 - mine, 0, keepdims=False)
    one, two = call(
        finish_kernel,
        "finish",
        [shape(8, LN, dtype=F32), shape(8, LN, dtype=F32)],
        [],
        8,
        1 << 20,
        [SMEM] + [VMEM] * 2,
        place,
        held,
        swap(given, 16),
    )

    return (
        jnp.transpose(activated, (1, 0, 2)),
        jnp.transpose(feature_grad, (1, 0, 2)),
        one.reshape(-1)[0:972],
        two.reshape(-1)[0:972],
    )


def solution(mesh):
    return jax.shard_map(
        local,
        mesh=mesh,
        in_specs=(
            P(None, "east", "north"),
            P("east", "north", None),
            P(),
            P(),
            P(None, "east", "north"),
        ),
        out_specs=(
            P(None, "east", "north"),
            P(None, "east", "north"),
            P(BOTH),
            P(BOTH),
        ),
        check_vma=False,
    )
```

time: 108 us -> 93.4 us (0.86)
  Pallas kernels: 37.5 us -> 22.7 us
  waiting for transfers between devices: 24.1 us -> 27.9 us
  starting transfers between devices: 30 us -> 26.6 us
    pallas_call x7 -> x8, Pallas kernels: 37.5 us -> 22.7 us  [call(): pl.pallas_call(kernel, out_shape=outs, in_specs=specs, out_specs=[VMEM] *...]
    ppermute x2, waiting for transfers between devices: 4.94 us -> 0.01 us  [the longest x1 0.01 us: local(): south = lax.ppermute(to_north, 'north', shift_by(1, 'north'))]
    ppermute x1, waiting for transfers between devices: 0.01 us -> 4.64 us  [local(): west = lax.ppermute(to_east, 'east', shift_by(1, 'east'))]
    ppermute x1, waiting for transfers between devices: 0.16 us -> 3.86 us  [local(): east = lax.ppermute(to_west, 'east', shift_by(-1, 'east'))]
    ppermute x9, starting transfers between devices: 19.7 us -> 16.3 us  [swap(): return lax.ppermute(value, BOTH, [(i, i ^ bits) for i in range(count)])]
    unnamed x33 -> x36, local copies, waits for them, and re-layouts: 11.7 us -> 13.4 us
  transfers between devices with their start and end apart: 13 -> 13, of which waited for: 11 -> 10; matrix products, arithmetic and copies ran while one was open for 2% -> 2% of each run, Pallas kernels for 6% -> 6%
where the time goes in v3:
time: 93.4 us; the launch traced here: 91.8 us
  waiting for transfers between devices  27.9 us (30%)
  starting transfers between devices  26.6 us (28%)
  Pallas kernels  22.7 us (24%)
  local copies, waits for them, and re-layouts  13.6 us (15%)
    pallas_call x8, Pallas kernels, call(): pl.pallas_call(kernel, out_shape=outs, in_specs=specs, out_specs=[VMEM] *...  22.7 us
    ppermute x9, waiting for transfers between devices, swap(): return lax.ppermute(value, BOTH, [(i, i ^ bits) for i in range(count)])  19.4 us
    ppermute x9, starting transfers between devices, swap(): return lax.ppermute(value, BOTH, [(i, i ^ bits) for i in range(count)])  16.3 us
    unnamed x36, local copies, waits for them, and re-layouts  13.4 us
    ppermute x1, waiting for transfers between devices, local(): west = lax.ppermute(to_east, 'east', shift_by(1, 'east'))  4.64 us
    ppermute x1, waiting for transfers between devices, local(): east = lax.ppermute(to_west, 'east', shift_by(-1, 'east'))  3.86 us
    ppermute x1, starting transfers between devices, local(): north = lax.ppermute(to_south, 'north', shift_by(-1, 'north'))  3.84 us
    ppermute x1, starting transfers between devices, local(): west = lax.ppermute(to_east, 'east', shift_by(1, 'east'))  3.35 us
  transfers between devices with their start and end apart: 13, of which 10 were waited for; matrix products, arithmetic and copies ran while one was open for 2% of the time, Pallas kernels for 6%

profile of v3, /device:TPU:2, one launch (start us, length us, event | category | flops | bytes accessed | tf_op | source)
XLA Modules:
  0.0 91.8 jit_solution(11964507079448806529)
XLA Ops:
  0.6 2.0 %strips.1 = (bf16[8,96,128]{2,1,0:T(8,128)(2,1)}, bf16[8,96,128]{2,1,0:T(8,128)(2,1)}, bf16[592,128]{1,0:T(8,128)(2,1)}, bf16[592,128]{1,0:T(8,128)(2,1)}, bf16[16,128]{1,0:T(8,128)(2,1)}) custom-call(s32[1,2]{1,0:T(1,128)} %bitcast.49, bf16[96,8,128]{2,1,0:T(8,128)(2,1)} %features.1, bf16[96,8,128]{2,1,0:T(8,128)(2,1)} %cotangent.1), custom_call_target="tpu_custom_call" | custom-call | flops 1048576 | bytes 1048576 | tf_op jit(solution)/shard_map/strips/pallas_call | solution.py:427
  2.6 3.3 %collective-permute-start = (bf16[592,128]{1,0:T(8,128)(2,1)}, bf16[592,128]{1,0:T(8,128)(2,1)S(1)}, u32[]{:S(2)}, u32[]{:S(2)}) collective-permute-start(bf16[592,128]{1,0:T(8,128)(2,1)} %get-tuple-element.42), channel_id=1, source_target_pairs={{0,16},{16,32},{32,48},{48,64},{64,80},{80,96},{96,112},{112,128},... | collective-permute-start | bytes 454664 | tf_op jit(solution)/shard_map/ppermute | solution.py:482
  6.0 3.1 %collective-permute-start.1 = (bf16[592,128]{1,0:T(8,128)(2,1)}, bf16[592,128]{1,0:T(8,128)(2,1)S(1)}, u32[]{:S(2)}, u32[]{:S(2)}) collective-permute-start(bf16[592,128]{1,0:T(8,128)(2,1)} %get-tuple-element.43), channel_id=1, source_target_pairs={{0,240},{16,0},{32,16},{48,32},{64,48},{80,64},{96,80},{112,96},{1... | collective-permute-start | bytes 454664 | tf_op jit(solution)/shard_map/ppermute | solution.py:483
  9.1 4.6 %collective-permute-done.west = bf16[592,128]{1,0:T(8,128)(2,1)S(1)} collective-permute-done((bf16[592,128]{1,0:T(8,128)(2,1)}, bf16[592,128]{1,0:T(8,128)(2,1)S(1)}, u32[]{:S(2)}, u32[]{:S(2)}) %collective-permute-start) | collective-permute-done | bytes 151584 | tf_op jit(solution)/shard_map/ppermute | solution.py:482
  13.7 3.9 %collective-permute-done.1.east = bf16[592,128]{1,0:T(8,128)(2,1)S(1)} collective-permute-done((bf16[592,128]{1,0:T(8,128)(2,1)}, bf16[592,128]{1,0:T(8,128)(2,1)S(1)}, u32[]{:S(2)}, u32[]{:S(2)}) %collective-permute-start.1) | collective-permute-done | bytes 151584 | tf_op jit(solution)/shard_map/ppermute | solution.py:483
  17.6 0.9 %copy-done = bf16[8,96,128]{2,1,0:T(8,128)(2,1)S(1)} copy-done((bf16[8,96,128]{2,1,0:T(8,128)(2,1)S(1)}, bf16[8,96,128]{2,1,0:T(8,128)(2,1)}, u32[]{:S(2)}) %copy-start) | copy-done | bytes 196632
  18.5 0.9 %copy-done.2 = bf16[8,96,128]{2,1,0:T(8,128)(2,1)S(1)} copy-done((bf16[8,96,128]{2,1,0:T(8,128)(2,1)S(1)}, bf16[8,96,128]{2,1,0:T(8,128)(2,1)}, u32[]{:S(2)}) %copy-start.2) | copy-done | bytes 196632
  20.5 3.8 %collective-permute-start.3 = (bf16[1104,128]{1,0:T(8,128)(2,1)S(1)}, bf16[1104,128]{1,0:T(8,128)(2,1)S(1)}, u32[]{:S(2)}, u32[]{:S(2)}) collective-permute-start(bf16[1104,128]{1,0:T(8,128)(2,1)S(1)} %get-tuple-element.51), channel_id=1, source_target_pairs={{0,15},{1,0},{2,1},{3,2},{4,3},{5,4},{6,5},{7,6},{8,7},{9,8},{10,9... | collective-permute-start | bytes 847880 | tf_op jit(solution)/shard_map/ppermute | solution.py:519
  26.9 1.1 %copy-done.7 = bf16[27,96,96]{2,1,0:T(8,128)(2,1)S(1)} copy-done((bf16[27,96,96]{2,1,0:T(8,128)(2,1)S(1)}, bf16[27,96,96]{2,1,0:T(8,128)(2,1)}, u32[]{:S(2)}) %copy-start.7) | copy-done | bytes 497688
  28.0 1.1 %copy-done.8 = bf16[27,96,96]{2,1,0:T(8,128)(2,1)S(1)} copy-done((bf16[27,96,96]{2,1,0:T(8,128)(2,1)S(1)}, bf16[27,96,96]{2,1,0:T(8,128)(2,1)}, u32[]{:S(2)}) %copy-start.8) | copy-done | bytes 497688
  29.1 2.2 %prepare.1 = (bf16[5,896,128]{2,1,0:T(8,128)(2,1)S(1)}, bf16[5,896,128]{2,1,0:T(8,128)(2,1)S(1)}, bf16[5,896,128]{2,1,0:T(8,128)(2,1)S(1)}, bf16[5,896,128]{2,1,...) custom-call(bf16[27,96,96]{2,1,0:T(8,128)(2,1)S(1)} %copy-done.7, ...), custom_call_target="tpu_custom_call" | custom-call | flops 8589934592 | bytes 1048576 | tf_op jit(solution)/shard_map/prepare/pallas_call | solution.py:427
  31.3 1.0 %copy-done.9 = bf16[5,896,128]{2,1,0:T(8,128)(2,1)} copy-done((bf16[5,896,128]{2,1,0:T(8,128)(2,1)}, bf16[5,896,128]{2,1,0:T(8,128)(2,1)S(1)}, u32[]{:S(2)}) %copy-start.9) | copy-done | bytes 1146904
  32.3 1.0 %copy-done.11 = bf16[5,896,128]{2,1,0:T(8,128)(2,1)} copy-done((bf16[5,896,128]{2,1,0:T(8,128)(2,1)}, bf16[5,896,128]{2,1,0:T(8,128)(2,1)S(1)}, u32[]{:S(2)}) %copy-start.11) | copy-done | bytes 1146904
  33.3 1.0 %copy-done.13 = bf16[5,896,128]{2,1,0:T(8,128)(2,1)} copy-done((bf16[5,896,128]{2,1,0:T(8,128)(2,1)}, bf16[5,896,128]{2,1,0:T(8,128)(2,1)S(1)}, u32[]{:S(2)}) %copy-start.13) | copy-done | bytes 1146904
  35.2 1.3 %sides.1 = (bf16[8,128,128]{2,1,0:T(8,128)(2,1)S(1)}, bf16[4,128,128]{2,1,0:T(8,128)(2,1)S(1)}, f32[3,128,128]{2,1,0:T(8,128)S(1)}, f32[8,128]{1,0:T(8,128)}) custom-call(s32[6]{0:T(128)S(1)} %stack.43.place.refs_0_, bf16[16,128]{1,0:T(8,128)(2,1)S(1)} %copy-done.6, bf16[592,128]{1,0:T(8,128)(2,1)S(1)} %collective-permute-done.west, ...), custom_call_target="tpu_custom_call" | custom-call | flops 2147483648 | bytes 1048576 | tf_op jit(solution)/shard_map/sides/pallas_call | solution.py:427
  37.3 13.6 %level.1 = (bf16[8,96,128]{2,1,0:T(8,128)(2,1)S(1)}, bf16[10,160,128]{2,1,0:T(8,128)(2,1)S(1)}, f32[3,256,128]{2,1,0:T(8,128)S(1)}, bf16[4,576,128]{2,1,0:T(8,128)(2,1)S(1)}, bf16[4,576,128]{2,1,0:T(8,128)(2,1)S(1)}) custom-call(s32[6]{0:T(128)S(1)} %stack.43.place.refs_0_, bf16[8,128,128]{2,1,0:T(8,128)(2,1)S(1)} %get-tuple-element.41.refs_1_, ...), custom_call_target="tpu_custom_call" | custom-call | flops 17179869184 | bytes 1048576 | tf_op jit(solution)/shard_map/level/pallas_call | solution.py:427
  51.3 2.0 %collective-permute-done.4 = bf16[4,576,128]{2,1,0:T(8,128)(2,1)S(1)} collective-permute-done((bf16[4,576,128]{2,1,0:T(8,128)(2,1)S(1)}, bf16[4,576,128]{2,1,0:T(8,128)(2,1)S(1)}, u32[]{:S(2)}, u32[]{:S(2)}) %collective-permute-start.4) | collective-permute-done | bytes 589856 | tf_op jit(solution)/shard_map/ppermute | solution.py:450
  53.6 1.9 %collective-permute-start.6 = (bf16[576,128]{1,0:T(8,128)(2,1)S(1)}, bf16[576,128]{1,0:T(8,128)(2,1)S(1)}, u32[]{:S(2)}, u32[]{:S(2)}) collective-permute-start(bf16[576,128]{1,0:T(8,128)(2,1)S(1)} %get-tuple-element.77), channel_id=1, source_target_pairs={{0,12},{1,13},{2,14},{3,15},{4,8},{5,9},{6,10},{7,11},{8,4},{9,5},... | collective-permute-start | bytes 442376 | tf_op jit(solution)/shard_map/ppermute | solution.py:450
  55.5 2.8 %collective-permute-start.7 = (bf16[576,128]{1,0:T(8,128)(2,1)S(1)}, bf16[576,128]{1,0:T(8,128)(2,1)S(1)}, u32[]{:S(2)}, u32[]{:S(2)}) collective-permute-start(bf16[576,128]{1,0:T(8,128)(2,1)S(1)} %get-tuple-element.76), channel_id=1, source_target_pairs={{0,14},{1,15},{2,12},{3,13},{4,10},{5,11},{6,8},{7,9},{8,6},{9,7},... | collective-permute-start | bytes 442376 | tf_op jit(solution)/shard_map/ppermute | solution.py:450
  58.3 1.8 %collective-permute-done.5.a1 = bf16[576,128]{1,0:T(8,128)(2,1)S(1)} collective-permute-done((bf16[576,128]{1,0:T(8,128)(2,1)S(1)}, bf16[576,128]{1,0:T(8,128)(2,1)S(1)}, u32[]{:S(2)}, u32[]{:S(2)}) %collective-permute-start.5) | collective-permute-done | bytes 147488 | tf_op jit(solution)/shard_map/ppermute | solution.py:450
  60.1 2.0 %collective-permute-done.6.a2 = bf16[576,128]{1,0:T(8,128)(2,1)S(1)} collective-permute-done((bf16[576,128]{1,0:T(8,128)(2,1)S(1)}, bf16[576,128]{1,0:T(8,128)(2,1)S(1)}, u32[]{:S(2)}, u32[]{:S(2)}) %collective-permute-start.6) | collective-permute-done | bytes 147488 | tf_op jit(solution)/shard_map/ppermute | solution.py:450
  62.1 1.9 %collective-permute-done.7.a3 = bf16[576,128]{1,0:T(8,128)(2,1)S(1)} collective-permute-done((bf16[576,128]{1,0:T(8,128)(2,1)S(1)}, bf16[576,128]{1,0:T(8,128)(2,1)S(1)}, u32[]{:S(2)}, u32[]{:S(2)}) %collective-permute-start.7) | collective-permute-done | bytes 147488 | tf_op jit(solution)/shard_map/ppermute | solution.py:450
  64.2 4.6 %collective-permute-done.8 = bf16[384,128]{1,0:T(8,128)(2,1)S(1)} collective-permute-done((bf16[384,128]{1,0:T(8,128)(2,1)S(1)}, bf16[384,128]{1,0:T(8,128)(2,1)S(1)}, u32[]{:S(2)}, u32[]{:S(2)}) %collective-permute-start.8) | collective-permute-done | bytes 98336 | tf_op jit(solution)/shard_map/ppermute | solution.py:450
  68.9 1.6 %collective-permute-start.9 = (bf16[8,24,128]{2,1,0:T(8,128)(2,1)S(1)}, bf16[8,24,128]{2,1,0:T(8,128)(2,1)S(1)}, u32[]{:S(2)}, u32[]{:S(2)}) collective-permute-start(bf16[8,24,128]{2,1,0:T(8,128)(2,1)S(1)} %dynamic-slice_bitcast_fusion.1), channel_id=1, source_target_pairs={{0,192},{1,193},{2,194},{3,195},{4,196},{5,197},{6,198},{7,199},{8... | collective-permute-start | bytes 147464 | tf_op jit(solution)/shard_map/ppermute | solution.py:450
  70.4 2.6 %collective-permute-done.9 = bf16[8,24,128]{2,1,0:T(8,128)(2,1)S(1)} collective-permute-done((bf16[8,24,128]{2,1,0:T(8,128)(2,1)S(1)}, bf16[8,24,128]{2,1,0:T(8,128)(2,1)S(1)}, u32[]{:S(2)}, u32[]{:S(2)}) %collective-permute-start.9) | collective-permute-done | bytes 49184 | tf_op jit(solution)/shard_map/ppermute | solution.py:450
  73.1 1.9 %collective-permute-start.10 = (f32[4,24,128]{2,1,0:T(8,128)S(1)}, f32[4,24,128]{2,1,0:T(8,128)S(1)}, u32[]{:S(2)}, u32[]{:S(2)}) collective-permute-start(f32[4,24,128]{2,1,0:T(8,128)S(1)} %dynamic-slice_bitcast_fusion), channel_id=1, source_target_pairs={{0,64},{1,65},{2,66},{3,67},{4,68},{5,69},{6,70},{7,71},{8,72},{9,... | collective-permute-start | bytes 147464 | tf_op jit(solution)/shard_map/ppermute | solution.py:450
  74.9 2.3 %collective-permute-done.10 = f32[4,24,128]{2,1,0:T(8,128)S(1)} collective-permute-done((f32[4,24,128]{2,1,0:T(8,128)S(1)}, f32[4,24,128]{2,1,0:T(8,128)S(1)}, u32[]{:S(2)}, u32[]{:S(2)}) %collective-permute-start.10) | collective-permute-done | bytes 49184 | tf_op jit(solution)/shard_map/ppermute | solution.py:450
  77.3 3.8 %collective-permute-start.11 = (f32[2,24,128]{2,1,0:T(8,128)S(1)}, f32[2,24,128]{2,1,0:T(8,128)S(1)}, u32[]{:S(2)}, u32[]{:S(2)}) collective-permute-start(f32[2,24,128]{2,1,0:T(8,128)S(1)} %dynamic-slice_bitcast_fusion.2), channel_id=1, source_target_pairs={{0,48},{1,49},{2,50},{3,51},{4,52},{5,53},{6,54},{7,55},{8,56},{9,... | collective-permute-start | bytes 73736 | tf_op jit(solution)/shard_map/ppermute | solution.py:450
  81.0 2.3 %collective-permute-done.11 = f32[2,24,128]{2,1,0:T(8,128)S(1)} collective-permute-done((f32[2,24,128]{2,1,0:T(8,128)S(1)}, f32[2,24,128]{2,1,0:T(8,128)S(1)}, u32[]{:S(2)}, u32[]{:S(2)}) %collective-permute-start.11) | collective-permute-done | bytes 24608 | tf_op jit(solution)/shard_map/ppermute | solution.py:450
  83.3 3.8 %collective-permute-start.12 = (f32[24,128]{1,0:T(8,128)S(1)}, f32[24,128]{1,0:T(8,128)S(1)}, u32[]{:S(2)}, u32[]{:S(2)}) collective-permute-start(f32[24,128]{1,0:T(8,128)S(1)} %get-tuple-element.80), channel_id=1, source_target_pairs={{0,16},{1,17},{2,18},{3,19},{4,20},{5,21},{6,22},{7,23},{8,24},{9,... | collective-permute-start | bytes 36872 | tf_op jit(solution)/shard_map/ppermute | solution.py:450
  87.2 1.9 %final.1 = (bf16[8,96,128]{2,1,0:T(8,128)(2,1)S(1)}, f32[8,128]{1,0:T(8,128)}) custom-call(bf16[10,160,128]{2,1,0:T(8,128)(2,1)S(1)} %get-tuple-element.59.grad_one, f32[3,256,128]{2,1,0:T(8,128)S(1)} %get-tuple-element.60.masks, bf16[5,896,128]{2,1,0:T(8,128)(2,1)S(1)} %get-tuple-element.61.back_one), custom_call_target="tpu_custom_call" | custom-call | flops 4294967296 | bytes 1048576 | tf_op jit(solution)/shard_map/final/pallas_call | solution.py:427
  90.5 1.3 %finish.1 = (f32[8,128]{1,0:T(8,128)}, f32[8,128]{1,0:T(8,128)}) custom-call(s32[6]{0:T(128)S(1)} %stack.43.place.refs_0_, f32[24,128]{1,0:T(8,128)S(1)} %get-tuple-element.81.held, f32[24,128]{1,0:T(8,128)S(1)} %collective-permute-done.12.got), custom_call_target="tpu_custom_call" | custom-call | flops 1048576 | bytes 1048576 | tf_op jit(solution)/shard_map/finish/pallas_call | solution.py:427
  (49 shorter events, 7.9 us)
Async XLA Ops:
  2.6 11.1 %collective-permute-start = (bf16[592,128]{1,0:T(8,128)(2,1)}, bf16[592,128]{1,0:T(8,128)(2,1)S(1)}, u32[]{:S(2)}, u32[]{:S(2)}) collective-permute-start(bf16[592,128]{1,0:T(8,128)(2,1)} %get-tuple-element.42), channel_id=1, source_target_pairs={{0,16},{16,32},{32,48},{48,64},{64,80},{80,96},{96,112},{112,128},... | collective-permute-start | bytes 454664 | tf_op jit(solution)/shard_map/ppermute | solution.py:482
  6.0 11.6 %collective-permute-start.1 = (bf16[592,128]{1,0:T(8,128)(2,1)}, bf16[592,128]{1,0:T(8,128)(2,1)S(1)}, u32[]{:S(2)}, u32[]{:S(2)}) collective-permute-start(bf16[592,128]{1,0:T(8,128)(2,1)} %get-tuple-element.43), channel_id=1, source_target_pairs={{0,240},{16,0},{32,16},{48,32},{64,48},{80,64},{96,80},{112,96},{1... | collective-permute-start | bytes 454664 | tf_op jit(solution)/shard_map/ppermute | solution.py:483
  17.6 0.9 %copy-start = (bf16[8,96,128]{2,1,0:T(8,128)(2,1)S(1)}, bf16[8,96,128]{2,1,0:T(8,128)(2,1)}, u32[]{:S(2)}) copy-start(bf16[8,96,128]{2,1,0:T(8,128)(2,1)} %get-tuple-element.38.feat) | copy-start | bytes 589828
  18.5 0.9 %copy-start.2 = (bf16[8,96,128]{2,1,0:T(8,128)(2,1)S(1)}, bf16[8,96,128]{2,1,0:T(8,128)(2,1)}, u32[]{:S(2)}) copy-start(bf16[8,96,128]{2,1,0:T(8,128)(2,1)} %get-tuple-element.39.cot) | copy-start | bytes 589828
  19.4 0.7 copy-start.4
  20.4 16.1 %collective-permute-start.2 = (bf16[1104,128]{1,0:T(8,128)(2,1)S(1)}, bf16[1104,128]{1,0:T(8,128)(2,1)S(1)}, u32[]{:S(2)}, u32[]{:S(2)}) collective-permute-start(bf16[1104,128]{1,0:T(8,128)(2,1)S(1)} %get-tuple-element.50), channel_id=1, source_target_pairs={{0,1},{1,2},{2,3},{3,4},{4,5},{5,6},{6,7},{7,8},{8,9},{9,10},{10,1... | collective-permute-start | bytes 847880 | tf_op jit(solution)/shard_map/ppermute | solution.py:518
  20.5 16.0 %collective-permute-start.3 = (bf16[1104,128]{1,0:T(8,128)(2,1)S(1)}, bf16[1104,128]{1,0:T(8,128)(2,1)S(1)}, u32[]{:S(2)}, u32[]{:S(2)}) collective-permute-start(bf16[1104,128]{1,0:T(8,128)(2,1)S(1)} %get-tuple-element.51), channel_id=1, source_target_pairs={{0,15},{1,0},{2,1},{3,2},{4,3},{5,4},{6,5},{7,6},{8,7},{9,8},{10,9... | collective-permute-start | bytes 847880 | tf_op jit(solution)/shard_map/ppermute | solution.py:519
  24.4 0.9 %copy-start.1 = (bf16[8,96,128]{2,1,0:T(8,128)(2,1)S(1)}, bf16[8,96,128]{2,1,0:T(8,128)(2,1)}, u32[]{:S(2)}) copy-start(bf16[8,96,128]{2,1,0:T(8,128)(2,1)} %get-tuple-element.38.feat) | copy-start | bytes 589828
  25.3 0.9 %copy-start.3 = (bf16[8,96,128]{2,1,0:T(8,128)(2,1)S(1)}, bf16[8,96,128]{2,1,0:T(8,128)(2,1)}, u32[]{:S(2)}) copy-start(bf16[8,96,128]{2,1,0:T(8,128)(2,1)} %get-tuple-element.39.cot) | copy-start | bytes 589828
  26.2 0.7 copy-start.5
  26.9 1.1 %copy-start.7 = (bf16[27,96,96]{2,1,0:T(8,128)(2,1)S(1)}, bf16[27,96,96]{2,1,0:T(8,128)(2,1)}, u32[]{:S(2)}) copy-start(bf16[27,96,96]{2,1,0:T(8,128)(2,1)} %first.1) | copy-start | bytes 1492996
  28.0 1.1 %copy-start.8 = (bf16[27,96,96]{2,1,0:T(8,128)(2,1)S(1)}, bf16[27,96,96]{2,1,0:T(8,128)(2,1)}, u32[]{:S(2)}) copy-start(bf16[27,96,96]{2,1,0:T(8,128)(2,1)} %second.1) | copy-start | bytes 1492996
  29.1 6.1 %copy-start.6 = (bf16[16,128]{1,0:T(8,128)(2,1)S(1)}, bf16[16,128]{1,0:T(8,128)(2,1)}, u32[]{:S(2)}) copy-start(bf16[16,128]{1,0:T(8,128)(2,1)} %get-tuple-element.40.own_mask) | copy-start | bytes 12292
  31.3 1.0 %copy-start.9 = (bf16[5,896,128]{2,1,0:T(8,128)(2,1)}, bf16[5,896,128]{2,1,0:T(8,128)(2,1)S(1)}, u32[]{:S(2)}) copy-start(bf16[5,896,128]{2,1,0:T(8,128)(2,1)S(1)} %get-tuple-element.54.refs_8_) | copy-start | bytes 3440644
  32.3 1.0 %copy-start.11 = (bf16[5,896,128]{2,1,0:T(8,128)(2,1)}, bf16[5,896,128]{2,1,0:T(8,128)(2,1)S(1)}, u32[]{:S(2)}) copy-start(bf16[5,896,128]{2,1,0:T(8,128)(2,1)S(1)} %get-tuple-element.55.refs_9_) | copy-start | bytes 3440644
  33.3 1.0 %copy-start.13 = (bf16[5,896,128]{2,1,0:T(8,128)(2,1)}, bf16[5,896,128]{2,1,0:T(8,128)(2,1)S(1)}, u32[]{:S(2)}) copy-start(bf16[5,896,128]{2,1,0:T(8,128)(2,1)S(1)} %get-tuple-element.56.refs_10_) | copy-start | bytes 3440644
  34.3 0.8 copy-start.15
  35.2 1.3 %copy-start.10 = (bf16[5,896,128]{2,1,0:T(8,128)(2,1)S(1)}, bf16[5,896,128]{2,1,0:T(8,128)(2,1)}, u32[]{:S(2)}) copy-start(bf16[5,896,128]{2,1,0:T(8,128)(2,1)} %copy-done.9) | copy-start | bytes 3440644
  35.2 1.6 %copy-start.12 = (bf16[5,896,128]{2,1,0:T(8,128)(2,1)S(1)}, bf16[5,896,128]{2,1,0:T(8,128)(2,1)}, u32[]{:S(2)}) copy-start(bf16[5,896,128]{2,1,0:T(8,128)(2,1)} %copy-done.11) | copy-start | bytes 3440644
  35.2 1.9 %copy-start.14 = (bf16[5,896,128]{2,1,0:T(8,128)(2,1)S(1)}, bf16[5,896,128]{2,1,0:T(8,128)(2,1)}, u32[]{:S(2)}) copy-start(bf16[5,896,128]{2,1,0:T(8,128)(2,1)} %copy-done.13) | copy-start | bytes 3440644
  35.2 2.1 %copy-start.16 = (bf16[288,1024]{1,0:T(8,128)(2,1)S(1)}, bf16[288,1024]{1,0:T(8,128)(2,1)}, u32[]{:S(2)}) copy-start(bf16[288,1024]{1,0:T(8,128)(2,1)} %copy-done.15) | copy-start | bytes 1769476
  51.0 2.3 %collective-permute-start.4 = (bf16[4,576,128]{2,1,0:T(8,128)(2,1)S(1)}, bf16[4,576,128]{2,1,0:T(8,128)(2,1)S(1)}, u32[]{:S(2)}, u32[]{:S(2)}) collective-permute-start(bf16[4,576,128]{2,1,0:T(8,128)(2,1)S(1)} %get-tuple-element.64), channel_id=1, source_target_pairs={{0,1},{1,0},{2,3},{3,2},{4,5},{5,4},{6,7},{7,6},{8,9},{9,8},{10,11... | collective-permute-start | bytes 1769480 | tf_op jit(solution)/shard_map/ppermute | solution.py:450
  53.5 6.6 %collective-permute-start.5 = (bf16[576,128]{1,0:T(8,128)(2,1)S(1)}, bf16[576,128]{1,0:T(8,128)(2,1)S(1)}, u32[]{:S(2)}, u32[]{:S(2)}) collective-permute-start(bf16[576,128]{1,0:T(8,128)(2,1)S(1)} %get-tuple-element.78), channel_id=1, source_target_pairs={{0,2},{1,3},{2,0},{3,1},{4,6},{5,7},{6,4},{7,5},{8,10},{9,11},{10,... | collective-permute-start | bytes 442376 | tf_op jit(solution)/shard_map/ppermute | solution.py:450
  53.6 8.5 %collective-permute-start.6 = (bf16[576,128]{1,0:T(8,128)(2,1)S(1)}, bf16[576,128]{1,0:T(8,128)(2,1)S(1)}, u32[]{:S(2)}, u32[]{:S(2)}) collective-permute-start(bf16[576,128]{1,0:T(8,128)(2,1)S(1)} %get-tuple-element.77), channel_id=1, source_target_pairs={{0,12},{1,13},{2,14},{3,15},{4,8},{5,9},{6,10},{7,11},{8,4},{9,5},... | collective-permute-start | bytes 442376 | tf_op jit(solution)/shard_map/ppermute | solution.py:450
  55.5 8.5 %collective-permute-start.7 = (bf16[576,128]{1,0:T(8,128)(2,1)S(1)}, bf16[576,128]{1,0:T(8,128)(2,1)S(1)}, u32[]{:S(2)}, u32[]{:S(2)}) collective-permute-start(bf16[576,128]{1,0:T(8,128)(2,1)S(1)} %get-tuple-element.76), channel_id=1, source_target_pairs={{0,14},{1,15},{2,12},{3,13},{4,10},{5,11},{6,8},{7,9},{8,6},{9,7},... | collective-permute-start | bytes 442376 | tf_op jit(solution)/shard_map/ppermute | solution.py:450
  64.1 4.7 %collective-permute-start.8 = (bf16[384,128]{1,0:T(8,128)(2,1)S(1)}, bf16[384,128]{1,0:T(8,128)(2,1)S(1)}, u32[]{:S(2)}, u32[]{:S(2)}) collective-permute-start(bf16[384,128]{1,0:T(8,128)(2,1)S(1)} %get-tuple-element.69), channel_id=1, source_target_pairs={{0,4},{1,5},{2,6},{3,7},{4,0},{5,1},{6,2},{7,3},{8,12},{9,13},{10,... | collective-permute-start | bytes 294920 | tf_op jit(solution)/shard_map/ppermute | solution.py:450
  68.9 4.2 %collective-permute-start.9 = (bf16[8,24,128]{2,1,0:T(8,128)(2,1)S(1)}, bf16[8,24,128]{2,1,0:T(8,128)(2,1)S(1)}, u32[]{:S(2)}, u32[]{:S(2)}) collective-permute-start(bf16[8,24,128]{2,1,0:T(8,128)(2,1)S(1)} %dynamic-slice_bitcast_fusion.1), channel_id=1, source_target_pairs={{0,192},{1,193},{2,194},{3,195},{4,196},{5,197},{6,198},{7,199},{8... | collective-permute-start | bytes 147464 | tf_op jit(solution)/shard_map/ppermute | solution.py:450
  73.1 4.2 %collective-permute-start.10 = (f32[4,24,128]{2,1,0:T(8,128)S(1)}, f32[4,24,128]{2,1,0:T(8,128)S(1)}, u32[]{:S(2)}, u32[]{:S(2)}) collective-permute-start(f32[4,24,128]{2,1,0:T(8,128)S(1)} %dynamic-slice_bitcast_fusion), channel_id=1, source_target_pairs={{0,64},{1,65},{2,66},{3,67},{4,68},{5,69},{6,70},{7,71},{8,72},{9,... | collective-permute-start | bytes 147464 | tf_op jit(solution)/shard_map/ppermute | solution.py:450
  77.3 6.0 %collective-permute-start.11 = (f32[2,24,128]{2,1,0:T(8,128)S(1)}, f32[2,24,128]{2,1,0:T(8,128)S(1)}, u32[]{:S(2)}, u32[]{:S(2)}) collective-permute-start(f32[2,24,128]{2,1,0:T(8,128)S(1)} %dynamic-slice_bitcast_fusion.2), channel_id=1, source_target_pairs={{0,48},{1,49},{2,50},{3,51},{4,52},{5,53},{6,54},{7,55},{8,56},{9,... | collective-permute-start | bytes 73736 | tf_op jit(solution)/shard_map/ppermute | solution.py:450
  83.3 7.2 %collective-permute-start.12 = (f32[24,128]{1,0:T(8,128)S(1)}, f32[24,128]{1,0:T(8,128)S(1)}, u32[]{:S(2)}, u32[]{:S(2)}) collective-permute-start(f32[24,128]{1,0:T(8,128)S(1)} %get-tuple-element.80), channel_id=1, source_target_pairs={{0,16},{1,17},{2,18},{3,19},{4,20},{5,21},{6,22},{7,23},{8,24},{9,... | collective-permute-start | bytes 36872 | tf_op jit(solution)/shard_map/ppermute | solution.py:450

commit v4 on v3

--- a/solution.py
+++ b/solution.py
@@ -37,15 +37,32 @@
     return jnp.concatenate([tile] * 8, axis=0).T
 
 
+def here():
+    return lax.axis_index("east"), lax.axis_index("north")
+
+
+def as_float(flag):
+    return flag.astype(jnp.int32).astype(F32)
+
+
+def neighbours():
+    column, row = here()
+    last_column, last_row = lax.axis_size("east") - 1, lax.axis_size("north") - 1
+    flags = (column > 0, column < last_column, row > 0, row < last_row)
+    return [as_float(flag) for flag in flags]
+
+
+def mask_tile(occupied):
+    levels = occupied[...].astype(F32)
+    return jnp.where((lanes(16) & 15) < 8, levels[:, 0:1], levels[:, 1:2]).astype(BF16)
+
+
 def strips_kernel(
     occupied,
     features,
     cotangent,
-    feat,
-    cot,
     to_west,
     to_east,
-    own_mask,
     near_feat,
     near_cot,
     near_occupied,
@@ -60,23 +77,20 @@
     ]
     for copy in copies:
         copy.start()
-    for copy, near, wide, out in (
-        (copies[0], near_feat, wide_feat, feat),
-        (copies[1], near_cot, wide_cot, cot),
+    for copy, near, wide, start, count in (
+        (copies[0], near_feat, wide_feat, 0, 4),
+        (copies[1], near_cot, wide_cot, 4, 2),
     ):
         copy.wait()
         wide[...] = near[...].astype(F32).reshape(CH * 8, LN)
-        for x in range(8):
-            out[x] = wide[pl.ds(x, CH, stride=8), :].astype(BF16)
+        for k in range(count):
+            rows = slice((start + k) * CH, (start + k + 1) * CH)
+            to_west[rows, :] = wide[pl.ds(k, CH, stride=8), :].astype(BF16)
+            to_east[rows, :] = wide[pl.ds(8 - count + k, CH, stride=8), :].astype(BF16)
     copies[2].wait()
-    levels = near_occupied[...].astype(F32)
-    own_mask[...] = jnp.where((lanes(16) & 15) < 8, levels[:, 0:1], levels[:, 1:2]).astype(BF16)
-    for out, first, second in ((to_west, 0, 0), (to_east, 4, 6)):
-        for k in range(4):
-            out[k * CH : (k + 1) * CH, :] = feat[first + k]
-        for k in range(2):
-            out[(4 + k) * CH : (5 + k) * CH, :] = cot[second + k]
-        out[6 * CH : STRIP, :] = own_mask[...]
+    mask = mask_tile(near_occupied)
+    to_west[6 * CH : STRIP, :] = mask
+    to_east[6 * CH : STRIP, :] = mask
 
 
 def turn_levels(value, x, turned):
@@ -91,9 +105,9 @@
 def prepare_kernel(
     first,
     second,
-    feat,
-    cot,
-    own_mask,
+    features,
+    cotangent,
+    occupied,
     fwd_one,
     fwd_two,
     back_two,
@@ -101,9 +115,15 @@
     turned_one,
     own_grid,
     own_cot,
-    token,
+    feat,
+    cot,
+    own_mask,
+    wide_feat,
+    wide_cot,
 ):
-    token[...] = jnp.zeros_like(token)
+    wide_feat[...] = features[...].astype(F32).reshape(CH * 8, LN)
+    wide_cot[...] = cotangent[...].astype(F32).reshape(CH * 8, LN)
+    own_mask[...] = mask_tile(occupied)
     for out in (fwd_one, fwd_two, back_two, back_one):
         out[...] = jnp.zeros_like(out)
 
@@ -128,10 +148,14 @@
     lax.fori_loop(0, 3, body, 0)
     mask = jnp.concatenate([own_mask[...].astype(F32)] * 6, axis=0)
     for x in range(8):
-        value = feat[x].astype(F32) * mask
+        plain = wide_feat[pl.ds(x, CH, stride=8), :]
+        feat[x] = plain.astype(BF16)
+        value = plain * mask
         turn_levels(value, x, turned_one)
         own_grid[x] = flip_pad(value).astype(BF16)
-        own_cot[x] = flip_pad(cot[x]).astype(BF16)
+        plain = wide_cot[pl.ds(x, CH, stride=8), :]
+        cot[x] = plain.astype(BF16)
+        own_cot[x] = flip_pad(plain).astype(BF16)
 
 
 def rims_kernel(west, east, feat, cot, own_mask, to_south, to_north):
@@ -177,11 +201,11 @@
         out[11 * CH + 32 : RIM, :] = east[6 * CH : STRIP, :]
 
 
-def sides_kernel(place, own_mask, west, east, side_grid, side_cot, middle, token):
-    token[...] = jnp.zeros_like(token)
-    middle[0] = mask_column(west, 6 * CH) * place[0].astype(F32)
+def sides_kernel(own_mask, west, east, side_grid, side_cot, middle):
+    has = neighbours()
+    middle[0] = mask_column(west, 6 * CH) * has[0]
     middle[1] = mask_column(own_mask, 0)
-    middle[2] = mask_column(east, 6 * CH) * place[1].astype(F32)
+    middle[2] = mask_column(east, 6 * CH) * has[1]
     for side, ref in ((0, west), (1, east)):
         for k in range(4):
             block = flip_pad(ref[k * CH : (k + 1) * CH, :]) * middle[2 * side]
@@ -249,7 +273,6 @@
 
 def level_kernel(
     scale,
-    place,
     own_grid,
     side_grid,
     own_cot,
@@ -277,12 +300,14 @@
     grad_one_sum,
     grad_two_sum,
     packed,
+    rows,
 ):
-    for ref, flag, row in ((south, place[2], 0), (north, place[3], 192)):
-        tile = ref[11 * CH : 11 * CH + 48, :].astype(F32) * flag.astype(F32)
+    has = neighbours()
+    for ref, flag, row in ((south, has[2], 0), (north, has[3], 192)):
+        tile = ref[11 * CH : 11 * CH + 48, :].astype(F32) * flag
         turned = jnp.concatenate([tile, jnp.zeros((80, LN), F32)], axis=0).T[0:64]
         for bx in range(3):
-            side = place[bx // 2].astype(F32) if bx != 1 else 1.0
+            side = has[bx // 2] if bx != 1 else 1.0
             column = turned[:, 16 * bx : 16 * bx + 1] * side
             masks[bx, row : row + 64, :] = jnp.broadcast_to(column, (64, LN))
     masks[:, 64:192, :] = middle[...]
@@ -327,13 +352,14 @@
         value = value * mask
         sigma = jax.nn.sigmoid(value)
         if 2 <= p < 10:
-            activated[p - 2] = (value * sigma)[32:160].T[0:CH].astype(BF16)
+            rows[pl.ds(p - 2, CH, stride=8), :] = (value * sigma)[32:160].T[0:CH]
         slope = sigma * (1.0 + value * (1.0 - sigma))
         grad = upstream[p] * slope * mask
         grad_two[p] = grad.astype(BF16)
         spread(taps, p, grad, 160)
 
     pipeline(more_taps, fwd_two, total, 6, 192, after_two)
+    activated[...] = rows[...].reshape(CH, 8, LN).astype(BF16)
     kernel_grad(turned_two, grad_two, 2, scale, grad_two_sum)
 
     def after_three(p, value):
@@ -343,8 +369,9 @@
     pipeline(taps, back_two, total, 5, 160, after_three)
     kernel_grad(turned_one, grad_one, 1, scale, grad_one_sum)
 
-    me = place[4]
-    bit = place[5]
+    row = lax.axis_index("north")
+    me = row & 7
+    bit = row >> 3
     tail = lanes(CH) < CH
     for out, low in ((keep, 0), (send, 1)):
         for e in range(4):
@@ -370,18 +397,19 @@
                     out[e, start : start + CH, :] = block.astype(BF16)
 
 
-def final_kernel(grad_one, masks, back_one, feature_grad, token, taps, total):
+def final_kernel(grad_one, masks, back_one, feature_grad, token, taps, total, rows):
     token[...] = jnp.zeros_like(token)
     for p in range(10):
         spread(taps, p, grad_one[p].astype(F32), 128)
 
     def after_four(p, value):
-        feature_grad[p] = (value * masks[1, 64:192, :]).T[0:CH].astype(BF16)
+        rows[pl.ds(p, CH, stride=8), :] = (value * masks[1, 64:192, :]).T[0:CH]
 
     pipeline(taps, back_one, total, 4, 128, after_four)
-
-
-def combine_kernel(a0, a1, a2, a3, hold, give, ordered):
+    feature_grad[...] = rows[...].reshape(CH, 8, LN).astype(BF16)
+
+
+def combine_kernel(a0, a1, a2, a3, token, hold, give, ordered):
     lane = lanes(CH)
     for grad in range(2):
         blocks = []
@@ -404,8 +432,14 @@
     give[...] = ordered[384:768, :].astype(BF16)
 
 
-def finish_kernel(place, held, got, out_one, out_two):
-    j = place[4]
+def step_kernel(shift, held, got, hold, give):
+    bit = (lax.axis_index("east") >> shift) & 1
+    for out, want in ((hold, bit), (give, 1 - bit)):
+        out[...] = (held[want].astype(F32) + got[want].astype(F32)).astype(out.dtype)
+
+
+def finish_kernel(held, got, out_one, out_two):
+    j = lax.axis_index("north") & 7
     lane = lanes(1)
     value = held[...] + got[...]
     for grad, out in ((0, out_one), (1, out_two)):
@@ -451,31 +485,20 @@
 
 
 def local(features, occupancy, weight_first, weight_second, cotangent):
-    column = lax.axis_index("east")
-    row = lax.axis_index("north")
-    position = column * 16 + row
-    block = position // 8
     scale = 1.0 / math.sqrt(128 * 128 * 16)
-    place = jnp.stack(
-        [column > 0, column < 15, row > 0, row < 15, position % 8, block % 2]
-    ).astype(jnp.int32)
-
-    feat, cot, to_west, to_east, own_mask = call(
+    occupied = occupancy.reshape(1, 2)
+    wide = pltpu.VMEM((CH * 8, LN), F32)
+    near = pltpu.VMEM((CH, 8, LN), BF16)
+
+    to_west, to_east = call(
         strips_kernel,
         "strips",
-        [shape(8, CH, LN), shape(8, CH, LN), shape(STRIP, LN), shape(STRIP, LN), shape(16, LN)],
-        [
-            pltpu.VMEM((CH, 8, LN), BF16),
-            pltpu.VMEM((CH, 8, LN), BF16),
-            pltpu.VMEM((1, 2), jnp.int32),
-            pltpu.VMEM((CH * 8, LN), F32),
-            pltpu.VMEM((CH * 8, LN), F32),
-            pltpu.SemaphoreType.DMA((3,)),
-        ],
+        [shape(STRIP, LN), shape(STRIP, LN)],
+        [near, near, pltpu.VMEM((1, 2), jnp.int32), wide, wide, pltpu.SemaphoreType.DMA((3,))],
         60,
         1 << 20,
         [pl.BlockSpec(memory_space=pltpu.HBM)] * 3,
-        occupancy.reshape(1, 2),
+        occupied,
         features,
         cotangent,
     )
@@ -484,23 +507,22 @@
 
     weight = shape(5, TAPS, LN)
     tile = shape(8, LN, LN)
-    mark = shape(8, LN, dtype=F32)
-    prepared = call(
+    image = shape(CH, 8, LN)
+    planes = shape(8, CH, LN)
+    fwd_one, fwd_two, back_two, back_one, turned_one, own_grid, own_cot, feat, cot, own_mask = call(
         prepare_kernel,
         "prepare",
-        [weight, weight, weight, weight, shape(288, 1024), tile, tile, mark],
-        [],
-        16,
+        [weight] * 4 + [shape(288, 1024), tile, tile, planes, planes, shape(16, LN)],
+        [wide, wide],
+        12,
         1 << 33,
         [VMEM] * 5,
         weight_first,
         weight_second,
-        feat,
-        cot,
-        own_mask,
-    )
-    fwd_one, fwd_two, back_two, back_one, turned_one, own_grid, own_cot, token = prepared
-    west, east, token = lax.optimization_barrier((west, east, token))
+        features,
+        cotangent,
+        occupied,
+    )
     to_south, to_north = call(
         rims_kernel,
         "rims",
@@ -517,26 +539,24 @@
     )
     south = lax.ppermute(to_north, "north", shift_by(1, "north"))
     north = lax.ppermute(to_south, "north", shift_by(-1, "north"))
-    side_grid, side_cot, middle, token = call(
+    side_grid, side_cot, middle = call(
         sides_kernel,
         "sides",
-        [tile, shape(4, LN, LN), shape(3, LN, LN, dtype=F32), mark],
+        [tile, shape(4, LN, LN), shape(3, LN, LN, dtype=F32)],
         [],
         8,
         1 << 31,
-        [SMEM] + [VMEM] * 3,
-        place,
+        [VMEM] * 3,
         own_mask,
         west,
         east,
     )
-    south, north, token = lax.optimization_barrier((south, north, token))
 
     activated, grad_one, masks, keep, send = call(
         lambda *refs: level_kernel(scale, *refs),
         "level",
         [
-            shape(8, CH, LN),
+            image,
             shape(10, 160, LN),
             shape(3, 256, LN, dtype=F32),
             shape(4, 576, LN),
@@ -554,11 +574,11 @@
             pltpu.VMEM((2592 + 16, LN), F32),
             pltpu.VMEM((2592 + 16, LN), F32),
             pltpu.VMEM((400, LN), F32),
+            wide,
         ],
-        36,
+        32,
         1 << 34,
-        [SMEM] + [VMEM] * 11,
-        place,
+        [VMEM] * 11,
         own_grid,
         side_grid,
         own_cot,
@@ -572,45 +592,47 @@
         turned_one,
     )
 
-    def add(*terms):
-        return sum(t.astype(F32) for t in terms)
-
-    part = add(keep, swap(send, 1)).astype(BF16)
+    part = (keep.astype(F32) + swap(send, 1).astype(F32)).astype(BF16)
     others = [swap(part[k], bits) for k, bits in ((1, 2), (2, 12), (3, 14))]
     feature_grad, token = call(
         final_kernel,
         "final",
-        [shape(8, CH, LN), mark],
-        [pltpu.VMEM((5, 2, 128, TAPS), BF16), pltpu.VMEM((512, 2 * LN), F32)],
-        16,
+        [image, shape(8, LN, dtype=F32)],
+        [pltpu.VMEM((5, 2, 128, TAPS), BF16), pltpu.VMEM((512, 2 * LN), F32), wide],
+        12,
         1 << 32,
         [VMEM] * 3,
         grad_one,
         masks,
         back_one,
     )
-    others, token = lax.optimization_barrier((others, token))
-    hold, give = call(
+    held, given = call(
         combine_kernel,
         "combine",
         [shape(384, LN), shape(384, LN)],
         [pltpu.VMEM((768, LN), F32)],
         8,
         1 << 20,
-        [VMEM] * 4,
+        [VMEM] * 5,
         part[0],
         *others,
-    )
-    part = add(hold, swap(give, 4)).reshape(16, 24, LN)
-    for bit, kind, partner in ((8, BF16, 192), (4, F32, 64), (2, F32, 48)):
-        half = part.reshape((2, -1, 24, LN)).astype(kind)
-        mine = (block // (2 * bit)) % 2
-        held = lax.dynamic_index_in_dim(half, mine, 0, keepdims=False)
-        given = lax.dynamic_index_in_dim(half, 1 - mine, 0, keepdims=False)
-        part = add(held, swap(given, partner))
-    mine = (block // 2) % 2
-    held = lax.dynamic_index_in_dim(part, mine, 0, keepdims=False)
-    given = lax.dynamic_index_in_dim(part, 1 - mine, 0, keepdims=False)
+        token,
+    )
+    partner, size = 4, 384
+    for shift, after, kind in ((3, 192, BF16), (2, 64, BF16), (1, 48, F32), (0, 16, F32)):
+        got = swap(given, partner)
+        partner, size = after, size // 2
+        held, given = call(
+            lambda *refs: step_kernel(shift, *refs),
+            "step",
+            [shape(size, LN, dtype=kind)] * 2,
+            [],
+            8,
+            1 << 20,
+            [VMEM] * 2,
+            held.reshape(2, size, LN),
+            got.reshape(2, size, LN),
+        )
     one, two = call(
         finish_kernel,
         "finish",
@@ -618,18 +640,11 @@
         [],
         8,
         1 << 20,
-        [SMEM] + [VMEM] * 2,
-        place,
+        [VMEM] * 2,
         held,
-        swap(given, 16),
-    )
-
-    return (
-        jnp.transpose(activated, (1, 0, 2)),
-        jnp.transpose(feature_grad, (1, 0, 2)),
-        one.reshape(-1)[0:972],
-        two.reshape(-1)[0:972],
-    )
+        swap(given, partner),
+    )
+    return activated, feature_grad, one.reshape(-1)[0:972], two.reshape(-1)[0:972]
 
 
 def solution(mesh):

time: 93.4 us -> 81.9 us (0.88)
  local copies, waits for them, and re-layouts: 13.6 us -> 4.73 us
  starting transfers between devices: 26.6 us -> 24.7 us
  Pallas kernels: 22.7 us -> 21.1 us
  waiting for transfers between devices: 27.9 us -> 29 us
    unnamed x36 -> x10, local copies, waits for them, and re-layouts: 13.4 us -> 4.69 us
    ppermute x1, waiting for transfers between devices: 0.01 us -> 6.7 us  [local(): south = lax.ppermute(to_north, 'north', shift_by(1, 'north'))]
    ppermute x1, waiting for transfers between devices: 4.64 us -> 0.01 us  [local(): west = lax.ppermute(to_east, 'east', shift_by(1, 'east'))]
    ppermute x9, starting transfers between devices: 16.3 us -> 14.4 us  [swap(): return lax.ppermute(value, BOTH, [(i, i ^ bits) for i in range(count)])]
    ppermute x1, waiting for transfers between devices: 3.86 us -> 1.98 us  [local(): east = lax.ppermute(to_west, 'east', shift_by(-1, 'east'))]
    pallas_call x8 -> x12, Pallas kernels: 22.7 us -> 21.1 us  [call(): pl.pallas_call(kernel, out_shape=outs, in_specs=specs, out_specs=[VMEM] *...]
  transfers between devices with their start and end apart: 13 -> 13, of which waited for: 10 -> 10; matrix products, arithmetic and copies ran while one was open for 2% -> 0% of each run, Pallas kernels for 6% -> 5%
where the time goes in v4:
time: 81.9 us; the launch traced here: 80.5 us
  waiting for transfers between devices  29 us (35%)
  starting transfers between devices  24.7 us (30%)
  Pallas kernels  21.1 us (26%)
  local copies, waits for them, and re-layouts  4.73 us (6%)
    pallas_call x12, Pallas kernels, call(): pl.pallas_call(kernel, out_shape=outs, in_specs=specs, out_specs=[VMEM] *...  21.1 us
    ppermute x9, waiting for transfers between devices, swap(): return lax.ppermute(value, BOTH, [(i, i ^ bits) for i in range(count)])  20.3 us
    ppermute x9, starting transfers between devices, swap(): return lax.ppermute(value, BOTH, [(i, i ^ bits) for i in range(count)])  14.4 us
    ppermute x1, waiting for transfers between devices, local(): south = lax.ppermute(to_north, 'north', shift_by(1, 'north'))  6.7 us
    unnamed x10, local copies, waits for them, and re-layouts  4.69 us
    ppermute x1, starting transfers between devices, local(): north = lax.ppermute(to_south, 'north', shift_by(-1, 'north'))  3.84 us
    ppermute x1, starting transfers between devices, local(): west = lax.ppermute(to_east, 'east', shift_by(1, 'east'))  3.35 us
    ppermute x1, starting transfers between devices, local(): east = lax.ppermute(to_west, 'east', shift_by(-1, 'east'))  3.09 us
  transfers between devices with their start and end apart: 13, of which 10 were waited for; matrix products, arithmetic and copies ran while one was open for 0% of the time, Pallas kernels for 5%

profile of v4, /device:TPU:2, one launch (start us, length us, event | category | flops | bytes accessed | tf_op | source)
XLA Modules:
  0.0 80.5 jit_solution(3091594297942057202)
XLA Ops:
  0.6 1.9 %strips.1 = (bf16[592,128]{1,0:T(8,128)(2,1)}, bf16[592,128]{1,0:T(8,128)(2,1)}) custom-call(s32[1,2]{1,0:T(1,128)} %bitcast.29, bf16[96,8,128]{2,1,0:T(8,128)(2,1)} %features.3, bf16[96,8,128]{2,1,0:T(8,128)(2,1)} %cotangent.3), custom_call_target="tpu_custom_call" | custom-call | flops 1048576 | bytes 1048576 | tf_op jit(solution)/shard_map/strips/pallas_call | solution.py:461
  2.5 3.3 %collective-permute-start = (bf16[592,128]{1,0:T(8,128)(2,1)}, bf16[592,128]{1,0:T(8,128)(2,1)S(1)}, u32[]{:S(2)}, u32[]{:S(2)}) collective-permute-start(bf16[592,128]{1,0:T(8,128)(2,1)} %get-tuple-element.42), channel_id=1, source_target_pairs={{0,16},{16,32},{32,48},{48,64},{64,80},{80,96},{96,112},{112,128},... | collective-permute-start | bytes 454664 | tf_op jit(solution)/shard_map/ppermute | solution.py:505
  5.9 3.1 %collective-permute-start.1 = (bf16[592,128]{1,0:T(8,128)(2,1)}, bf16[592,128]{1,0:T(8,128)(2,1)S(1)}, u32[]{:S(2)}, u32[]{:S(2)}) collective-permute-start(bf16[592,128]{1,0:T(8,128)(2,1)} %get-tuple-element.43), channel_id=1, source_target_pairs={{0,240},{16,0},{32,16},{48,32},{64,48},{80,64},{96,80},{112,96},{1... | collective-permute-start | bytes 454664 | tf_op jit(solution)/shard_map/ppermute | solution.py:506
  9.0 0.9 %copy-done = bf16[96,8,128]{2,1,0:T(8,128)(2,1)S(1)} copy-done((bf16[96,8,128]{2,1,0:T(8,128)(2,1)S(1)}, bf16[96,8,128]{2,1,0:T(8,128)(2,1)}, u32[]{:S(2)}) %copy-start) | copy-done | bytes 196632
  9.9 0.9 %copy-done.1 = bf16[96,8,128]{2,1,0:T(8,128)(2,1)S(1)} copy-done((bf16[96,8,128]{2,1,0:T(8,128)(2,1)S(1)}, bf16[96,8,128]{2,1,0:T(8,128)(2,1)}, u32[]{:S(2)}) %copy-start.1) | copy-done | bytes 196632
  10.8 0.7 copy-done.2
  11.5 1.1 %copy-done.3 = bf16[27,96,96]{2,1,0:T(8,128)(2,1)S(1)} copy-done((bf16[27,96,96]{2,1,0:T(8,128)(2,1)S(1)}, bf16[27,96,96]{2,1,0:T(8,128)(2,1)}, u32[]{:S(2)}) %copy-start.3) | copy-done | bytes 497688
  12.6 1.1 %copy-done.4 = bf16[27,96,96]{2,1,0:T(8,128)(2,1)S(1)} copy-done((bf16[27,96,96]{2,1,0:T(8,128)(2,1)S(1)}, bf16[27,96,96]{2,1,0:T(8,128)(2,1)}, u32[]{:S(2)}) %copy-start.4) | copy-done | bytes 497688
  13.7 1.8 %prepare.1 = (bf16[5,896,128]{2,1,0:T(8,128)(2,1)S(1)}, bf16[5,896,128]{2,1,0:T(8,128)(2,1)S(1)}, bf16[5,896,128]{2,1,0:T(8,128)(2,1)S(1)}, bf16[5,896,128]{2,1,...) custom-call(bf16[27,96,96]{2,1,0:T(8,128)(2,1)S(1)} %copy-done.3, ...), custom_call_target="tpu_custom_call" | custom-call | flops 8589934592 | bytes 1048576 | tf_op jit(solution)/shard_map/prepare/pallas_call | solution.py:461
  15.5 2.0 %collective-permute-done.1.east = bf16[592,128]{1,0:T(8,128)(2,1)S(1)} collective-permute-done((bf16[592,128]{1,0:T(8,128)(2,1)}, bf16[592,128]{1,0:T(8,128)(2,1)S(1)}, u32[]{:S(2)}, u32[]{:S(2)}) %collective-permute-start.1) | collective-permute-done | bytes 151584 | tf_op jit(solution)/shard_map/ppermute | solution.py:506
  17.5 0.3 rims.1
  17.9 3.8 %collective-permute-start.3 = (bf16[1104,128]{1,0:T(8,128)(2,1)S(1)}, bf16[1104,128]{1,0:T(8,128)(2,1)S(1)}, u32[]{:S(2)}, u32[]{:S(2)}) collective-permute-start(bf16[1104,128]{1,0:T(8,128)(2,1)S(1)} %get-tuple-element.51), channel_id=1, source_target_pairs={{0,15},{1,0},{2,1},{3,2},{4,3},{5,4},{6,5},{7,6},{8,7},{9,8},{10,9... | collective-permute-start | bytes 847880 | tf_op jit(solution)/shard_map/ppermute | solution.py:541
  21.7 0.2 sides.1
  21.9 6.7 %collective-permute-done.2.refs_5_ = bf16[1104,128]{1,0:T(8,128)(2,1)S(1)} collective-permute-done((bf16[1104,128]{1,0:T(8,128)(2,1)S(1)}, bf16[1104,128]{1,0:T(8,128)(2,1)S(1)}, u32[]{:S(2)}, u32[]{:S(2)}) %collective-permute-start.2) | collective-permute-done | bytes 282656 | tf_op jit(solution)/shard_map/ppermute | solution.py:540
  28.6 13.8 %level.1 = (bf16[96,8,128]{2,1,0:T(8,128)(2,1)}, bf16[10,160,128]{2,1,0:T(8,128)(2,1)S(1)}, f32[3,256,128]{2,1,0:T(8,128)S(1)}, bf16[4,576,128]{2,1,0:T(8,128)(2,1)S(1)}, bf16[4,576,128]{2,1,0:T(8,128)(2,1)S(1)}) custom-call(bf16[8,128,128]{2,1,0:T(8,128)(2,1)S(1)} %get-tuple-element.40.refs_0_, bf16[8,128,128]{2,1,0:T(8,128)(2,1)S(1)} %get-tuple-element.44.refs_1_, ...), custom_call_target="tpu_custom_call" | custom-call | flops 17179869184 | bytes 1048576 | tf_op jit(solution)/shard_map/level/pallas_call | solution.py:461
  42.4 2.0 %collective-permute-done.4 = bf16[4,576,128]{2,1,0:T(8,128)(2,1)S(1)} collective-permute-done((bf16[4,576,128]{2,1,0:T(8,128)(2,1)S(1)}, bf16[4,576,128]{2,1,0:T(8,128)(2,1)S(1)}, u32[]{:S(2)}, u32[]{:S(2)}) %collective-permute-start.4) | collective-permute-done | bytes 589856 | tf_op jit(solution)/shard_map/ppermute | solution.py:484
  44.6 1.3 %collective-permute-start.7 = (bf16[576,128]{1,0:T(8,128)(2,1)S(1)}, bf16[576,128]{1,0:T(8,128)(2,1)S(1)}, u32[]{:S(2)}, u32[]{:S(2)}) collective-permute-start(bf16[576,128]{1,0:T(8,128)(2,1)S(1)} %get-tuple-element.76), channel_id=1, source_target_pairs={{0,14},{1,15},{2,12},{3,13},{4,10},{5,11},{6,8},{7,9},{8,6},{9,7},... | collective-permute-start | bytes 442376 | tf_op jit(solution)/shard_map/ppermute | solution.py:484
  46.0 0.4 collective-permute-start.6
  46.4 3.0 %collective-permute-start.5 = (bf16[576,128]{1,0:T(8,128)(2,1)S(1)}, bf16[576,128]{1,0:T(8,128)(2,1)S(1)}, u32[]{:S(2)}, u32[]{:S(2)}) collective-permute-start(bf16[576,128]{1,0:T(8,128)(2,1)S(1)} %get-tuple-element.78), channel_id=1, source_target_pairs={{0,2},{1,3},{2,0},{3,1},{4,6},{5,7},{6,4},{7,5},{8,10},{9,11},{10,... | collective-permute-start | bytes 442376 | tf_op jit(solution)/shard_map/ppermute | solution.py:484
  49.4 2.1 %final.1 = (bf16[96,8,128]{2,1,0:T(8,128)(2,1)}, f32[8,128]{1,0:T(8,128)S(1)}) custom-call(bf16[10,160,128]{2,1,0:T(8,128)(2,1)S(1)} %get-tuple-element.57.grad_one, f32[3,256,128]{2,1,0:T(8,128)S(1)} %get-tuple-element.58.masks, bf16[5,896,128]{2,1,0:T(8,128)(2,1)S(1)} %get-tuple-element.59.back_one), custom_call_target="tpu_custom_call" | custom-call | flops 4294967296 | bytes 1048576 | tf_op jit(solution)/shard_map/final/pallas_call | solution.py:461
  51.6 2.0 %collective-permute-done.7.a3 = bf16[576,128]{1,0:T(8,128)(2,1)S(1)} collective-permute-done((bf16[576,128]{1,0:T(8,128)(2,1)S(1)}, bf16[576,128]{1,0:T(8,128)(2,1)S(1)}, u32[]{:S(2)}, u32[]{:S(2)}) %collective-permute-start.7) | collective-permute-done | bytes 147488 | tf_op jit(solution)/shard_map/ppermute | solution.py:484
  53.6 2.3 %collective-permute-done.6.a2 = bf16[576,128]{1,0:T(8,128)(2,1)S(1)} collective-permute-done((bf16[576,128]{1,0:T(8,128)(2,1)S(1)}, bf16[576,128]{1,0:T(8,128)(2,1)S(1)}, u32[]{:S(2)}, u32[]{:S(2)}) %collective-permute-start.6) | collective-permute-done | bytes 147488 | tf_op jit(solution)/shard_map/ppermute | solution.py:484
  56.2 4.7 %collective-permute-done.8 = bf16[384,128]{1,0:T(8,128)(2,1)S(1)} collective-permute-done((bf16[384,128]{1,0:T(8,128)(2,1)S(1)}, bf16[384,128]{1,0:T(8,128)(2,1)S(1)}, u32[]{:S(2)}, u32[]{:S(2)}) %collective-permute-start.8) | collective-permute-done | bytes 98336 | tf_op jit(solution)/shard_map/ppermute | solution.py:484
  60.9 1.6 %collective-permute-start.9 = (bf16[192,128]{1,0:T(8,128)(2,1)S(1)}, bf16[192,128]{1,0:T(8,128)(2,1)S(1)}, u32[]{:S(2)}, u32[]{:S(2)}) collective-permute-start(bf16[192,128]{1,0:T(8,128)(2,1)S(1)} %get-tuple-element.67), channel_id=1, source_target_pairs={{0,192},{1,193},{2,194},{3,195},{4,196},{5,197},{6,198},{7,199},{8... | collective-permute-start | bytes 147464 | tf_op jit(solution)/shard_map/ppermute | solution.py:484
  62.5 2.6 %collective-permute-done.9 = bf16[192,128]{1,0:T(8,128)(2,1)S(1)} collective-permute-done((bf16[192,128]{1,0:T(8,128)(2,1)S(1)}, bf16[192,128]{1,0:T(8,128)(2,1)S(1)}, u32[]{:S(2)}, u32[]{:S(2)}) %collective-permute-start.9) | collective-permute-done | bytes 49184 | tf_op jit(solution)/shard_map/ppermute | solution.py:484
  65.1 1.1 %collective-permute-start.10 = (bf16[96,128]{1,0:T(8,128)(2,1)S(1)}, bf16[96,128]{1,0:T(8,128)(2,1)S(1)}, u32[]{:S(2)}, u32[]{:S(2)}) collective-permute-start(bf16[96,128]{1,0:T(8,128)(2,1)S(1)} %get-tuple-element.69), channel_id=1, source_target_pairs={{0,64},{1,65},{2,66},{3,67},{4,68},{5,69},{6,70},{7,71},{8,72},{9,... | collective-permute-start | bytes 73736 | tf_op jit(solution)/shard_map/ppermute | solution.py:484
  66.2 2.9 %collective-permute-done.10 = bf16[96,128]{1,0:T(8,128)(2,1)S(1)} collective-permute-done((bf16[96,128]{1,0:T(8,128)(2,1)S(1)}, bf16[96,128]{1,0:T(8,128)(2,1)S(1)}, u32[]{:S(2)}, u32[]{:S(2)}) %collective-permute-start.10) | collective-permute-done | bytes 24608 | tf_op jit(solution)/shard_map/ppermute | solution.py:484
  69.0 3.9 %collective-permute-start.11 = (f32[48,128]{1,0:T(8,128)S(1)}, f32[48,128]{1,0:T(8,128)S(1)}, u32[]{:S(2)}, u32[]{:S(2)}) collective-permute-start(f32[48,128]{1,0:T(8,128)S(1)} %get-tuple-element.71), channel_id=1, source_target_pairs={{0,48},{1,49},{2,50},{3,51},{4,52},{5,53},{6,54},{7,55},{8,56},{9,... | collective-permute-start | bytes 73736 | tf_op jit(solution)/shard_map/ppermute | solution.py:484
  72.9 2.1 %collective-permute-done.11 = f32[48,128]{1,0:T(8,128)S(1)} collective-permute-done((f32[48,128]{1,0:T(8,128)S(1)}, f32[48,128]{1,0:T(8,128)S(1)}, u32[]{:S(2)}, u32[]{:S(2)}) %collective-permute-start.11) | collective-permute-done | bytes 24608 | tf_op jit(solution)/shard_map/ppermute | solution.py:484
  75.1 3.0 %collective-permute-start.12 = (f32[24,128]{1,0:T(8,128)S(1)}, f32[24,128]{1,0:T(8,128)S(1)}, u32[]{:S(2)}, u32[]{:S(2)}) collective-permute-start(f32[24,128]{1,0:T(8,128)S(1)} %get-tuple-element.73), channel_id=1, source_target_pairs={{0,16},{1,17},{2,18},{3,19},{4,20},{5,21},{6,22},{7,23},{8,24},{9,... | collective-permute-start | bytes 36872 | tf_op jit(solution)/shard_map/ppermute | solution.py:484
  78.0 1.7 %collective-permute-done.12.got = f32[24,128]{1,0:T(8,128)S(1)} collective-permute-done((f32[24,128]{1,0:T(8,128)S(1)}, f32[24,128]{1,0:T(8,128)S(1)}, u32[]{:S(2)}, u32[]{:S(2)}) %collective-permute-start.12) | collective-permute-done | bytes 12320 | tf_op jit(solution)/shard_map/ppermute | solution.py:484
  79.7 0.8 finish.1
  (18 shorter events, 0.6 us)
Async XLA Ops:
  2.5 13.0 %collective-permute-start = (bf16[592,128]{1,0:T(8,128)(2,1)}, bf16[592,128]{1,0:T(8,128)(2,1)S(1)}, u32[]{:S(2)}, u32[]{:S(2)}) collective-permute-start(bf16[592,128]{1,0:T(8,128)(2,1)} %get-tuple-element.42), channel_id=1, source_target_pairs={{0,16},{16,32},{32,48},{48,64},{64,80},{80,96},{96,112},{112,128},... | collective-permute-start | bytes 454664 | tf_op jit(solution)/shard_map/ppermute | solution.py:505
  5.9 11.6 %collective-permute-start.1 = (bf16[592,128]{1,0:T(8,128)(2,1)}, bf16[592,128]{1,0:T(8,128)(2,1)S(1)}, u32[]{:S(2)}, u32[]{:S(2)}) collective-permute-start(bf16[592,128]{1,0:T(8,128)(2,1)} %get-tuple-element.43), channel_id=1, source_target_pairs={{0,240},{16,0},{32,16},{48,32},{64,48},{80,64},{96,80},{112,96},{1... | collective-permute-start | bytes 454664 | tf_op jit(solution)/shard_map/ppermute | solution.py:506
  9.0 0.9 %copy-start = (bf16[96,8,128]{2,1,0:T(8,128)(2,1)S(1)}, bf16[96,8,128]{2,1,0:T(8,128)(2,1)}, u32[]{:S(2)}) copy-start(bf16[96,8,128]{2,1,0:T(8,128)(2,1)} %features.3) | copy-start | bytes 589828
  9.9 0.9 %copy-start.1 = (bf16[96,8,128]{2,1,0:T(8,128)(2,1)S(1)}, bf16[96,8,128]{2,1,0:T(8,128)(2,1)}, u32[]{:S(2)}) copy-start(bf16[96,8,128]{2,1,0:T(8,128)(2,1)} %cotangent.3) | copy-start | bytes 589828
  10.8 0.7 copy-start.2
  11.5 1.1 %copy-start.3 = (bf16[27,96,96]{2,1,0:T(8,128)(2,1)S(1)}, bf16[27,96,96]{2,1,0:T(8,128)(2,1)}, u32[]{:S(2)}) copy-start(bf16[27,96,96]{2,1,0:T(8,128)(2,1)} %first.1) | copy-start | bytes 1492996
  12.6 1.1 %copy-start.4 = (bf16[27,96,96]{2,1,0:T(8,128)(2,1)S(1)}, bf16[27,96,96]{2,1,0:T(8,128)(2,1)}, u32[]{:S(2)}) copy-start(bf16[27,96,96]{2,1,0:T(8,128)(2,1)} %second.1) | copy-start | bytes 1492996
  17.8 10.8 %collective-permute-start.2 = (bf16[1104,128]{1,0:T(8,128)(2,1)S(1)}, bf16[1104,128]{1,0:T(8,128)(2,1)S(1)}, u32[]{:S(2)}, u32[]{:S(2)}) collective-permute-start(bf16[1104,128]{1,0:T(8,128)(2,1)S(1)} %get-tuple-element.50), channel_id=1, source_target_pairs={{0,1},{1,2},{2,3},{3,4},{4,5},{5,6},{6,7},{7,8},{8,9},{9,10},{10,1... | collective-permute-start | bytes 847880 | tf_op jit(solution)/shard_map/ppermute | solution.py:540
  17.9 10.8 %collective-permute-start.3 = (bf16[1104,128]{1,0:T(8,128)(2,1)S(1)}, bf16[1104,128]{1,0:T(8,128)(2,1)S(1)}, u32[]{:S(2)}, u32[]{:S(2)}) collective-permute-start(bf16[1104,128]{1,0:T(8,128)(2,1)S(1)} %get-tuple-element.51), channel_id=1, source_target_pairs={{0,15},{1,0},{2,1},{3,2},{4,3},{5,4},{6,5},{7,6},{8,7},{9,8},{10,9... | collective-permute-start | bytes 847880 | tf_op jit(solution)/shard_map/ppermute | solution.py:541
  42.4 2.0 %collective-permute-start.4 = (bf16[4,576,128]{2,1,0:T(8,128)(2,1)S(1)}, bf16[4,576,128]{2,1,0:T(8,128)(2,1)S(1)}, u32[]{:S(2)}, u32[]{:S(2)}) collective-permute-start(bf16[4,576,128]{2,1,0:T(8,128)(2,1)S(1)} %get-tuple-element.62), channel_id=1, source_target_pairs={{0,1},{1,0},{2,3},{3,2},{4,5},{5,4},{6,7},{7,6},{8,9},{9,8},{10,11... | collective-permute-start | bytes 1769480 | tf_op jit(solution)/shard_map/ppermute | solution.py:484
  44.6 8.9 %collective-permute-start.7 = (bf16[576,128]{1,0:T(8,128)(2,1)S(1)}, bf16[576,128]{1,0:T(8,128)(2,1)S(1)}, u32[]{:S(2)}, u32[]{:S(2)}) collective-permute-start(bf16[576,128]{1,0:T(8,128)(2,1)S(1)} %get-tuple-element.76), channel_id=1, source_target_pairs={{0,14},{1,15},{2,12},{3,13},{4,10},{5,11},{6,8},{7,9},{8,6},{9,7},... | collective-permute-start | bytes 442376 | tf_op jit(solution)/shard_map/ppermute | solution.py:484
  46.0 9.9 %collective-permute-start.6 = (bf16[576,128]{1,0:T(8,128)(2,1)S(1)}, bf16[576,128]{1,0:T(8,128)(2,1)S(1)}, u32[]{:S(2)}, u32[]{:S(2)}) collective-permute-start(bf16[576,128]{1,0:T(8,128)(2,1)S(1)} %get-tuple-element.77), channel_id=1, source_target_pairs={{0,12},{1,13},{2,14},{3,15},{4,8},{5,9},{6,10},{7,11},{8,4},{9,5},... | collective-permute-start | bytes 442376 | tf_op jit(solution)/shard_map/ppermute | solution.py:484
  46.4 9.5 %collective-permute-start.5 = (bf16[576,128]{1,0:T(8,128)(2,1)S(1)}, bf16[576,128]{1,0:T(8,128)(2,1)S(1)}, u32[]{:S(2)}, u32[]{:S(2)}) collective-permute-start(bf16[576,128]{1,0:T(8,128)(2,1)S(1)} %get-tuple-element.78), channel_id=1, source_target_pairs={{0,2},{1,3},{2,0},{3,1},{4,6},{5,7},{6,4},{7,5},{8,10},{9,11},{10,... | collective-permute-start | bytes 442376 | tf_op jit(solution)/shard_map/ppermute | solution.py:484
  56.1 4.8 %collective-permute-start.8 = (bf16[384,128]{1,0:T(8,128)(2,1)S(1)}, bf16[384,128]{1,0:T(8,128)(2,1)S(1)}, u32[]{:S(2)}, u32[]{:S(2)}) collective-permute-start(bf16[384,128]{1,0:T(8,128)(2,1)S(1)} %get-tuple-element.65), channel_id=1, source_target_pairs={{0,4},{1,5},{2,6},{3,7},{4,0},{5,1},{6,2},{7,3},{8,12},{9,13},{10,... | collective-permute-start | bytes 294920 | tf_op jit(solution)/shard_map/ppermute | solution.py:484
  60.9 4.2 %collective-permute-start.9 = (bf16[192,128]{1,0:T(8,128)(2,1)S(1)}, bf16[192,128]{1,0:T(8,128)(2,1)S(1)}, u32[]{:S(2)}, u32[]{:S(2)}) collective-permute-start(bf16[192,128]{1,0:T(8,128)(2,1)S(1)} %get-tuple-element.67), channel_id=1, source_target_pairs={{0,192},{1,193},{2,194},{3,195},{4,196},{5,197},{6,198},{7,199},{8... | collective-permute-start | bytes 147464 | tf_op jit(solution)/shard_map/ppermute | solution.py:484
  65.1 3.9 %collective-permute-start.10 = (bf16[96,128]{1,0:T(8,128)(2,1)S(1)}, bf16[96,128]{1,0:T(8,128)(2,1)S(1)}, u32[]{:S(2)}, u32[]{:S(2)}) collective-permute-start(bf16[96,128]{1,0:T(8,128)(2,1)S(1)} %get-tuple-element.69), channel_id=1, source_target_pairs={{0,64},{1,65},{2,66},{3,67},{4,68},{5,69},{6,70},{7,71},{8,72},{9,... | collective-permute-start | bytes 73736 | tf_op jit(solution)/shard_map/ppermute | solution.py:484
  69.0 6.0 %collective-permute-start.11 = (f32[48,128]{1,0:T(8,128)S(1)}, f32[48,128]{1,0:T(8,128)S(1)}, u32[]{:S(2)}, u32[]{:S(2)}) collective-permute-start(f32[48,128]{1,0:T(8,128)S(1)} %get-tuple-element.71), channel_id=1, source_target_pairs={{0,48},{1,49},{2,50},{3,51},{4,52},{5,53},{6,54},{7,55},{8,56},{9,... | collective-permute-start | bytes 73736 | tf_op jit(solution)/shard_map/ppermute | solution.py:484
  75.1 4.7 %collective-permute-start.12 = (f32[24,128]{1,0:T(8,128)S(1)}, f32[24,128]{1,0:T(8,128)S(1)}, u32[]{:S(2)}, u32[]{:S(2)}) collective-permute-start(f32[24,128]{1,0:T(8,128)S(1)} %get-tuple-element.73), channel_id=1, source_target_pairs={{0,16},{1,17},{2,18},{3,19},{4,20},{5,21},{6,22},{7,23},{8,24},{9,... | collective-permute-start | bytes 36872 | tf_op jit(solution)/shard_map/ppermute | solution.py:484

commit v5 on v4

--- a/solution.py
+++ b/solution.py
@@ -233,24 +233,30 @@
         taps[plane // 2, plane % 2, 0:rows, n * LN : (n + 1) * LN] = block
 
 
-def convolve(taps, weight, pair, rows):
+def convolve(taps, weight, total, pair, rows):
     left = jnp.concatenate(
         [taps[pair + j // 2, j % 2, 0:rows, :] for j in range(4)], axis=1
     )
     right = jnp.concatenate(
         [jnp.concatenate([weight[j + 1], weight[j]], axis=1) for j in range(4)], axis=0
     )
-    return jnp.dot(left, right, preferred_element_type=F32)
-
-
-def pipeline(taps, weight, total, pairs, rows, after):
-    for i in range(pairs + 1):
-        if i < pairs:
-            total[i * rows : (i + 1) * rows, :] = convolve(taps, weight, i, rows)
-        if i > 0:
-            for half in range(2):
-                value = total[(i - 1) * rows : i * rows, half * LN : half * LN + LN]
-                after(2 * (i - 1) + half, value)
+    total[pair * rows : (pair + 1) * rows, :] = jnp.dot(left, right, preferred_element_type=F32)
+
+
+def half_of(total, p, rows):
+    start = p % 2 * LN
+    return total[p // 2 * rows : (p // 2 + 1) * rows, start : start + LN]
+
+
+HOPS = (1, 12, 192, 64, 4, 48, 16, 2)
+
+
+def path(code):
+    mask = 0
+    for k, hop in enumerate(HOPS):
+        if code >> (7 - k) & 1:
+            mask ^= hop
+    return mask
 
 
 def kernel_grad(turned, planes, shift, scale, result):
@@ -289,11 +295,14 @@
     masks,
     keep,
     send,
-    taps,
-    more_taps,
+    taps_one,
+    taps_two,
+    taps_three,
+    total_one,
+    total_two,
+    total_three,
     edge,
     upstream,
-    total,
     slope_one,
     grad_two,
     turned_two,
@@ -328,73 +337,81 @@
     for k in range(8):
         upstream[2 + k, 32:160, :] = own_cot[k].astype(F32)
 
-    for p in range(16):
+    def begin(p):
         bx = band(p, 4, 12)
         value = own_grid[p - 4] if bx == 1 else side_grid[p % 8]
         low = edge[p, 0:64, :] * masks[bx, 0:64, :]
         high = edge[p, 64:128, :] * masks[bx, 192:256, :]
-        spread(taps, p, jnp.concatenate([low, value.astype(F32), high], axis=0), 224)
-
-    def after_one(p, value):
-        value = value * masks[band(p, 3, 11), 16:240, :]
+        spread(taps_one, p, jnp.concatenate([low, value.astype(F32), high], axis=0), 224)
+
+    def after_one(p):
+        value = half_of(total_one, p, 224) * masks[band(p, 3, 11), 16:240, :]
         sigma = jax.nn.sigmoid(value)
         if 2 <= p < 12:
             slope_one[p - 2] = (sigma * (1.0 + value * (1.0 - sigma)))[32:192]
         hidden = (value * sigma).astype(BF16).astype(F32)
-        spread(more_taps, p, hidden, 192)
+        spread(taps_two, p, hidden, 192)
         if 3 <= p < 11:
             turn_levels(hidden[48:176].T[0:CH], p - 3, turned_two)
 
-    pipeline(taps, fwd_one, total, 7, 224, after_one)
-
-    def after_two(p, value):
+    def after_two(p):
         mask = masks[band(p, 2, 10), 32:224, :]
-        value = value * mask
+        value = half_of(total_two, p, 192) * mask
         sigma = jax.nn.sigmoid(value)
         if 2 <= p < 10:
             rows[pl.ds(p - 2, CH, stride=8), :] = (value * sigma)[32:160].T[0:CH]
         slope = sigma * (1.0 + value * (1.0 - sigma))
         grad = upstream[p] * slope * mask
         grad_two[p] = grad.astype(BF16)
-        spread(taps, p, grad, 160)
-
-    pipeline(more_taps, fwd_two, total, 6, 192, after_two)
+        spread(taps_three, p, grad, 160)
+
+    def after_three(p):
+        grad = half_of(total_three, p, 160) * slope_one[p] * masks[band(p, 1, 9), 48:208, :]
+        grad_one[p] = grad.astype(BF16)
+
+    for p in range(4):
+        begin(p)
+    for t in range(12):
+        if t < 7:
+            convolve(taps_one, fwd_one, total_one, t, 224)
+        if t < 6:
+            begin(2 * t + 4)
+            begin(2 * t + 5)
+        if 1 <= t < 8:
+            after_one(2 * t - 2)
+            after_one(2 * t - 1)
+        if 3 <= t < 9:
+            convolve(taps_two, fwd_two, total_two, t - 3, 192)
+        if 4 <= t < 10:
+            after_two(2 * t - 8)
+            after_two(2 * t - 7)
+        if 6 <= t < 11:
+            convolve(taps_three, back_two, total_three, t - 6, 160)
+        if 7 <= t < 12:
+            after_three(2 * t - 14)
+            after_three(2 * t - 13)
+        if t == 10:
+            kernel_grad(turned_two, grad_two, 2, scale, grad_two_sum)
     activated[...] = rows[...].reshape(CH, 8, LN).astype(BF16)
-    kernel_grad(turned_two, grad_two, 2, scale, grad_two_sum)
-
-    def after_three(p, value):
-        grad = value * slope_one[p] * masks[band(p, 1, 9), 48:208, :]
-        grad_one[p] = grad.astype(BF16)
-
-    pipeline(taps, back_two, total, 5, 160, after_three)
     kernel_grad(turned_one, grad_one, 1, scale, grad_one_sum)
 
-    row = lax.axis_index("north")
-    me = row & 7
-    bit = row >> 3
-    tail = lanes(CH) < CH
-    for out, low in ((keep, 0), (send, 1)):
-        for e in range(4):
-            near, far = e % 2, e // 2
-            for grad, source in ((0, grad_one_sum), (1, grad_two_sum)):
-                for turn in range(2):
-                    j = jnp.bitwise_xor(me, 4 * (turn ^ far) + 2 * near + low)
-                    first = 10 * j + 81 * jnp.bitwise_xor(bit, far)
-
-                    def gather(m, carry):
-                        packed[pl.ds(192 * turn + 12 * m, 16), :] = source[
-                            pl.ds(first + 162 * m, 16), :
-                        ]
-                        return carry
-
-                    lax.fori_loop(0, 16, gather, 0, unroll=8)
-                last = packed[288:384, :]
-                for k in range(3):
-                    block = jnp.where(
-                        tail, packed[CH * k : CH * k + CH, :], pltpu.roll(last, CH - 32 * k, 1)
-                    )
-                    start = 288 * grad + CH * k
-                    out[e, start : start + CH, :] = block.astype(BF16)
+    column, row = here()
+    position = column * 16 + row
+    spare = lanes(48) >= CH
+    for grad, source in ((1, grad_two_sum), (0, grad_one_sum)):
+        for code in range(256):
+            owner = jnp.bitwise_xor(position, path(code))
+            start = 81 * (owner >> 3) + 10 * (owner & 7)
+            packed[24 * code + 12 * grad : 24 * code + 12 * grad + 12, :] = source[
+                pl.ds(start, 12), :
+            ]
+    for code in range(0, 256, 8):
+        block = [packed[24 * code + 48 * k : 24 * code + 48 * k + 48, :] for k in range(4)]
+        out = keep if code < 128 else send
+        first = 144 * (code // 8 % 4)
+        for k in range(3):
+            mixed = jnp.where(spare, pltpu.roll(block[3], CH - 32 * k, 1), block[k])
+            out[code // 32 % 4, first + 48 * k : first + 48 * k + 48, :] = mixed.astype(BF16)
 
 
 def final_kernel(grad_one, masks, back_one, feature_grad, token, taps, total, rows):
@@ -402,40 +419,45 @@
     for p in range(10):
         spread(taps, p, grad_one[p].astype(F32), 128)
 
-    def after_four(p, value):
+    def after_four(p):
+        value = half_of(total, p, 128)
         rows[pl.ds(p, CH, stride=8), :] = (value * masks[1, 64:192, :]).T[0:CH]
 
-    pipeline(taps, back_one, total, 4, 128, after_four)
+    for t in range(5):
+        if t < 4:
+            convolve(taps, back_one, total, t, 128)
+        if t > 0:
+            after_four(2 * t - 2)
+            after_four(2 * t - 1)
     feature_grad[...] = rows[...].reshape(CH, 8, LN).astype(BF16)
 
 
-def combine_kernel(a0, a1, a2, a3, token, hold, give, ordered):
-    lane = lanes(CH)
-    for grad in range(2):
-        blocks = []
-        for k in range(3):
-            start = 288 * grad + CH * k
-            blocks.append(
-                sum(ref[start : start + CH, :].astype(F32) for ref in (a0, a1, a2, a3))
-            )
-        a, b, c = blocks
-        last = jnp.where(
-            lane < 32,
-            pltpu.roll(a, 32, 1),
-            jnp.where(lane < 64, pltpu.roll(b, 64, 1), pltpu.roll(c, 96, 1)),
-        )
-        for k, block in enumerate((a, b, c, last)):
-            for m in range(8):
-                start = 192 * k + 24 * m + 12 * grad
-                ordered[start : start + 12, :] = block[12 * m : 12 * m + 12]
-    hold[...] = ordered[0:384, :].astype(BF16)
-    give[...] = ordered[384:768, :].astype(BF16)
-
-
-def step_kernel(shift, held, got, hold, give):
-    bit = (lax.axis_index("east") >> shift) & 1
-    for out, want in ((hold, bit), (give, 1 - bit)):
-        out[...] = (held[want].astype(F32) + got[want].astype(F32)).astype(out.dtype)
+def gather_kernel(a0, a1, a2, a3, token, *outs):
+    for k, out in enumerate(outs):
+        piece = slice(144 * k, 144 * k + 144)
+        out[...] = sum(ref[piece, :].astype(F32) for ref in (a0, a1, a2, a3)).astype(BF16)
+
+
+def unpack_kernel(a0, a1, a2, a3, hold, give):
+    lane = lanes(48)
+    a, b, c = (
+        sum(ref[48 * k : 48 * k + 48, :].astype(F32) for ref in (a0, a1, a2, a3))
+        for k in range(3)
+    )
+    last = jnp.where(
+        lane < 32,
+        pltpu.roll(a, 32, 1),
+        jnp.where(lane < 64, pltpu.roll(b, 64, 1), pltpu.roll(c, 96, 1)),
+    )
+    for out, pair in ((hold, (a, b)), (give, (c, last))):
+        out[...] = jnp.concatenate(pair, axis=0).astype(BF16)
+
+
+def step_kernel(held, got, hold, give):
+    size = hold.shape[0]
+    total = held[...].astype(F32) + got[...].astype(F32)
+    hold[...] = total[0:size].astype(hold.dtype)
+    give[...] = total[size : 2 * size].astype(give.dtype)
 
 
 def finish_kernel(held, got, out_one, out_two):
@@ -565,18 +587,21 @@
         [
             pltpu.VMEM((8, 2, 224, TAPS), BF16),
             pltpu.VMEM((7, 2, 192, TAPS), BF16),
+            pltpu.VMEM((6, 2, 160, TAPS), BF16),
+            pltpu.VMEM((7 * 224, 2 * LN), F32),
+            pltpu.VMEM((6 * 192, 2 * LN), F32),
+            pltpu.VMEM((5 * 160, 2 * LN), F32),
             pltpu.VMEM((16, 128, LN), F32),
             pltpu.VMEM((12, 192, LN), F32),
-            pltpu.VMEM((7 * 224, 2 * LN), F32),
             pltpu.VMEM((10, 160, LN), F32),
             pltpu.VMEM((12, 192, LN), BF16),
             pltpu.VMEM((288, 1024), BF16),
             pltpu.VMEM((2592 + 16, LN), F32),
             pltpu.VMEM((2592 + 16, LN), F32),
-            pltpu.VMEM((400, LN), F32),
+            pltpu.VMEM((256 * 24, LN), F32),
             wide,
         ],
-        32,
+        40,
         1 << 34,
         [VMEM] * 11,
         own_grid,
@@ -593,7 +618,7 @@
     )
 
     part = (keep.astype(F32) + swap(send, 1).astype(F32)).astype(BF16)
-    others = [swap(part[k], bits) for k, bits in ((1, 2), (2, 12), (3, 14))]
+    others = [swap(part[k], bits) for k, bits in ((2, 12), (1, 192), (3, 204))]
     feature_grad, token = call(
         final_kernel,
         "final",
@@ -606,11 +631,11 @@
         masks,
         back_one,
     )
-    held, given = call(
-        combine_kernel,
-        "combine",
-        [shape(384, LN), shape(384, LN)],
-        [pltpu.VMEM((768, LN), F32)],
+    pieces = call(
+        gather_kernel,
+        "gather",
+        [shape(144, LN)] * 4,
+        [],
         8,
         1 << 20,
         [VMEM] * 5,
@@ -618,20 +643,29 @@
         *others,
         token,
     )
-    partner, size = 4, 384
-    for shift, after, kind in ((3, 192, BF16), (2, 64, BF16), (1, 48, F32), (0, 16, F32)):
-        got = swap(given, partner)
-        partner, size = after, size // 2
+    others = [swap(pieces[k], bits) for k, bits in ((2, 64), (1, 4), (3, 68))]
+    held, given = call(
+        unpack_kernel,
+        "unpack",
+        [shape(96, LN), shape(96, LN)],
+        [],
+        8,
+        1 << 20,
+        [VMEM] * 4,
+        pieces[0],
+        *others,
+    )
+    for partner, size, kind in ((48, 48, BF16), (16, 24, F32)):
         held, given = call(
-            lambda *refs: step_kernel(shift, *refs),
+            step_kernel,
             "step",
             [shape(size, LN, dtype=kind)] * 2,
             [],
             8,
             1 << 20,
             [VMEM] * 2,
-            held.reshape(2, size, LN),
-            got.reshape(2, size, LN),
+            held,
+            swap(given, partner),
         )
     one, two = call(
         finish_kernel,
@@ -642,7 +676,7 @@
         1 << 20,
         [VMEM] * 2,
         held,
-        swap(given, partner),
+        swap(given, 2),
     )
     return activated, feature_grad, one.reshape(-1)[0:972], two.reshape(-1)[0:972]
 

time: 81.9 us -> 77.5 us (0.946)
  waiting for transfers between devices: 29 us -> 24 us
  starting transfers between devices: 24.7 us -> 27.8 us
  Pallas kernels: 21.1 us -> 18.6 us
    ppermute x9 -> x10, waiting for transfers between devices: 20.3 us -> 15.3 us  [swap(): return lax.ppermute(value, BOTH, [(i, i ^ bits) for i in range(count)])]
    ppermute x9 -> x10, starting transfers between devices: 14.4 us -> 17.4 us  [swap(): return lax.ppermute(value, BOTH, [(i, i ^ bits) for i in range(count)])]
    pallas_call x12 -> x11, Pallas kernels: 21.1 us -> 18.6 us  [call(): pl.pallas_call(kernel, out_shape=outs, in_specs=specs, out_specs=[VMEM] *...]
  transfers between devices with their start and end apart: 13 -> 14, of which waited for: 10 -> 12; matrix products, arithmetic and copies ran while one was open for 0% -> 0% of each run, Pallas kernels for 5% -> 5%
where the time goes in v5:
time: 77.5 us; the launch traced here: 76 us
  starting transfers between devices  27.8 us (36%)
  waiting for transfers between devices  24 us (31%)
  Pallas kernels  18.6 us (24%)
  local copies, waits for them, and re-layouts  4.73 us (6%)
    pallas_call x11, Pallas kernels, call(): pl.pallas_call(kernel, out_shape=outs, in_specs=specs, out_specs=[VMEM] *...  18.6 us
    ppermute x10, starting transfers between devices, swap(): return lax.ppermute(value, BOTH, [(i, i ^ bits) for i in range(count)])  17.4 us
    ppermute x10, waiting for transfers between devices, swap(): return lax.ppermute(value, BOTH, [(i, i ^ bits) for i in range(count)])  15.3 us
    ppermute x1, waiting for transfers between devices, local(): south = lax.ppermute(to_north, 'north', shift_by(1, 'north'))  6.7 us
    unnamed x10, local copies, waits for them, and re-layouts  4.69 us
    ppermute x1, starting transfers between devices, local(): north = lax.ppermute(to_south, 'north', shift_by(-1, 'north'))  3.84 us
    ppermute x1, starting transfers between devices, local(): west = lax.ppermute(to_east, 'east', shift_by(1, 'east'))  3.35 us
    ppermute x1, starting transfers between devices, local(): east = lax.ppermute(to_west, 'east', shift_by(-1, 'east'))  3.09 us
  transfers between devices with their start and end apart: 14, of which 12 were waited for; matrix products, arithmetic and copies ran while one was open for 0% of the time, Pallas kernels for 5%

profile of v5, /device:TPU:2, one launch (start us, length us, event | category | flops | bytes accessed | tf_op | source)
XLA Modules:
  0.0 76.0 jit_solution(15398748332372836759)
XLA Ops:
  0.6 1.9 %strips.1 = (bf16[592,128]{1,0:T(8,128)(2,1)}, bf16[592,128]{1,0:T(8,128)(2,1)}) custom-call(s32[1,2]{1,0:T(1,128)} %bitcast.13, bf16[96,8,128]{2,1,0:T(8,128)(2,1)} %features.3, bf16[96,8,128]{2,1,0:T(8,128)(2,1)} %cotangent.3), custom_call_target="tpu_custom_call" | custom-call | flops 1048576 | bytes 1048576 | tf_op jit(solution)/shard_map/strips/pallas_call | solution.py:483
  2.5 3.3 %collective-permute-start = (bf16[592,128]{1,0:T(8,128)(2,1)}, bf16[592,128]{1,0:T(8,128)(2,1)S(1)}, u32[]{:S(2)}, u32[]{:S(2)}) collective-permute-start(bf16[592,128]{1,0:T(8,128)(2,1)} %get-tuple-element.42), channel_id=1, source_target_pairs={{0,16},{16,32},{32,48},{48,64},{64,80},{80,96},{96,112},{112,128},... | collective-permute-start | bytes 454664 | tf_op jit(solution)/shard_map/ppermute | solution.py:527
  5.9 3.1 %collective-permute-start.1 = (bf16[592,128]{1,0:T(8,128)(2,1)}, bf16[592,128]{1,0:T(8,128)(2,1)S(1)}, u32[]{:S(2)}, u32[]{:S(2)}) collective-permute-start(bf16[592,128]{1,0:T(8,128)(2,1)} %get-tuple-element.43), channel_id=1, source_target_pairs={{0,240},{16,0},{32,16},{48,32},{64,48},{80,64},{96,80},{112,96},{1... | collective-permute-start | bytes 454664 | tf_op jit(solution)/shard_map/ppermute | solution.py:528
  9.0 0.9 %copy-done = bf16[96,8,128]{2,1,0:T(8,128)(2,1)S(1)} copy-done((bf16[96,8,128]{2,1,0:T(8,128)(2,1)S(1)}, bf16[96,8,128]{2,1,0:T(8,128)(2,1)}, u32[]{:S(2)}) %copy-start) | copy-done | bytes 196632
  9.9 0.9 %copy-done.1 = bf16[96,8,128]{2,1,0:T(8,128)(2,1)S(1)} copy-done((bf16[96,8,128]{2,1,0:T(8,128)(2,1)S(1)}, bf16[96,8,128]{2,1,0:T(8,128)(2,1)}, u32[]{:S(2)}) %copy-start.1) | copy-done | bytes 196632
  10.8 0.7 copy-done.2
  11.5 1.1 %copy-done.3 = bf16[27,96,96]{2,1,0:T(8,128)(2,1)S(1)} copy-done((bf16[27,96,96]{2,1,0:T(8,128)(2,1)S(1)}, bf16[27,96,96]{2,1,0:T(8,128)(2,1)}, u32[]{:S(2)}) %copy-start.3) | copy-done | bytes 497688
  12.6 1.1 %copy-done.4 = bf16[27,96,96]{2,1,0:T(8,128)(2,1)S(1)} copy-done((bf16[27,96,96]{2,1,0:T(8,128)(2,1)S(1)}, bf16[27,96,96]{2,1,0:T(8,128)(2,1)}, u32[]{:S(2)}) %copy-start.4) | copy-done | bytes 497688
  13.7 1.8 %prepare.1 = (bf16[5,896,128]{2,1,0:T(8,128)(2,1)S(1)}, bf16[5,896,128]{2,1,0:T(8,128)(2,1)S(1)}, bf16[5,896,128]{2,1,0:T(8,128)(2,1)S(1)}, bf16[5,896,128]{2,1,...) custom-call(bf16[27,96,96]{2,1,0:T(8,128)(2,1)S(1)} %copy-done.3, ...), custom_call_target="tpu_custom_call" | custom-call | flops 8589934592 | bytes 1048576 | tf_op jit(solution)/shard_map/prepare/pallas_call | solution.py:483
  15.5 2.0 %collective-permute-done.1.east = bf16[592,128]{1,0:T(8,128)(2,1)S(1)} collective-permute-done((bf16[592,128]{1,0:T(8,128)(2,1)}, bf16[592,128]{1,0:T(8,128)(2,1)S(1)}, u32[]{:S(2)}, u32[]{:S(2)}) %collective-permute-start.1) | collective-permute-done | bytes 151584 | tf_op jit(solution)/shard_map/ppermute | solution.py:528
  17.9 3.8 %collective-permute-start.3 = (bf16[1104,128]{1,0:T(8,128)(2,1)S(1)}, bf16[1104,128]{1,0:T(8,128)(2,1)S(1)}, u32[]{:S(2)}, u32[]{:S(2)}) collective-permute-start(bf16[1104,128]{1,0:T(8,128)(2,1)S(1)} %get-tuple-element.51), channel_id=1, source_target_pairs={{0,15},{1,0},{2,1},{3,2},{4,3},{5,4},{6,5},{7,6},{8,7},{9,8},{10,9... | collective-permute-start | bytes 847880 | tf_op jit(solution)/shard_map/ppermute | solution.py:563
  21.9 6.7 %collective-permute-done.2.refs_5_ = bf16[1104,128]{1,0:T(8,128)(2,1)S(1)} collective-permute-done((bf16[1104,128]{1,0:T(8,128)(2,1)S(1)}, bf16[1104,128]{1,0:T(8,128)(2,1)S(1)}, u32[]{:S(2)}, u32[]{:S(2)}) %collective-permute-start.2) | collective-permute-done | bytes 282656 | tf_op jit(solution)/shard_map/ppermute | solution.py:562
  28.6 11.3 %level.1 = (bf16[96,8,128]{2,1,0:T(8,128)(2,1)}, bf16[10,160,128]{2,1,0:T(8,128)(2,1)S(1)}, f32[3,256,128]{2,1,0:T(8,128)S(1)}, bf16[4,576,128]{2,1,0:T(8,128)(2,1)S(1)}, bf16[4,576,128]{2,1,0:T(8,128)(2,1)S(1)}) custom-call(bf16[8,128,128]{2,1,0:T(8,128)(2,1)S(1)} %get-tuple-element.40.refs_0_, bf16[8,128,128]{2,1,0:T(8,128)(2,1)S(1)} %get-tuple-element.44.refs_1_, ...), custom_call_target="tpu_custom_call" | custom-call | flops 17179869184 | bytes 1048576 | tf_op jit(solution)/shard_map/level/pallas_call | solution.py:483
  40.0 2.0 %collective-permute-done.4 = bf16[4,576,128]{2,1,0:T(8,128)(2,1)S(1)} collective-permute-done((bf16[4,576,128]{2,1,0:T(8,128)(2,1)S(1)}, bf16[4,576,128]{2,1,0:T(8,128)(2,1)S(1)}, u32[]{:S(2)}, u32[]{:S(2)}) %collective-permute-start.4) | collective-permute-done | bytes 589856 | tf_op jit(solution)/shard_map/ppermute | solution.py:506
  42.2 2.6 %collective-permute-start.7 = (bf16[576,128]{1,0:T(8,128)(2,1)S(1)}, bf16[576,128]{1,0:T(8,128)(2,1)S(1)}, u32[]{:S(2)}, u32[]{:S(2)}) collective-permute-start(bf16[576,128]{1,0:T(8,128)(2,1)S(1)} %get-tuple-element.76), channel_id=1, source_target_pairs={{0,204},{1,205},{2,206},{3,207},{4,200},{5,201},{6,202},{7,203},{8... | collective-permute-start | bytes 442376 | tf_op jit(solution)/shard_map/ppermute | solution.py:506
  44.8 0.5 collective-permute-start.6
  45.3 1.6 %collective-permute-start.5 = (bf16[576,128]{1,0:T(8,128)(2,1)S(1)}, bf16[576,128]{1,0:T(8,128)(2,1)S(1)}, u32[]{:S(2)}, u32[]{:S(2)}) collective-permute-start(bf16[576,128]{1,0:T(8,128)(2,1)S(1)} %get-tuple-element.78), channel_id=1, source_target_pairs={{0,12},{1,13},{2,14},{3,15},{4,8},{5,9},{6,10},{7,11},{8,4},{9,5},... | collective-permute-start | bytes 442376 | tf_op jit(solution)/shard_map/ppermute | solution.py:506
  47.0 2.1 %final.1 = (bf16[96,8,128]{2,1,0:T(8,128)(2,1)}, f32[8,128]{1,0:T(8,128)S(1)}) custom-call(bf16[10,160,128]{2,1,0:T(8,128)(2,1)S(1)} %get-tuple-element.57.grad_one, f32[3,256,128]{2,1,0:T(8,128)S(1)} %get-tuple-element.58.masks, bf16[5,896,128]{2,1,0:T(8,128)(2,1)S(1)} %get-tuple-element.59.back_one), custom_call_target="tpu_custom_call" | custom-call | flops 4294967296 | bytes 1048576 | tf_op jit(solution)/shard_map/final/pallas_call | solution.py:483
  49.1 2.0 %collective-permute-done.7.a3 = bf16[576,128]{1,0:T(8,128)(2,1)S(1)} collective-permute-done((bf16[576,128]{1,0:T(8,128)(2,1)S(1)}, bf16[576,128]{1,0:T(8,128)(2,1)S(1)}, u32[]{:S(2)}, u32[]{:S(2)}) %collective-permute-start.7) | collective-permute-done | bytes 147488 | tf_op jit(solution)/shard_map/ppermute | solution.py:506
  51.1 1.3 %collective-permute-done.6.a2 = bf16[576,128]{1,0:T(8,128)(2,1)S(1)} collective-permute-done((bf16[576,128]{1,0:T(8,128)(2,1)S(1)}, bf16[576,128]{1,0:T(8,128)(2,1)S(1)}, u32[]{:S(2)}, u32[]{:S(2)}) %collective-permute-start.6) | collective-permute-done | bytes 147488 | tf_op jit(solution)/shard_map/ppermute | solution.py:506
  52.4 1.1 %collective-permute-done.5.a1 = bf16[576,128]{1,0:T(8,128)(2,1)S(1)} collective-permute-done((bf16[576,128]{1,0:T(8,128)(2,1)S(1)}, bf16[576,128]{1,0:T(8,128)(2,1)S(1)}, u32[]{:S(2)}, u32[]{:S(2)}) %collective-permute-start.5) | collective-permute-done | bytes 147488 | tf_op jit(solution)/shard_map/ppermute | solution.py:506
  53.5 1.1 %collective-permute-start.8 = (bf16[144,128]{1,0:T(8,128)(2,1)S(1)}, bf16[144,128]{1,0:T(8,128)(2,1)S(1)}, u32[]{:S(2)}, u32[]{:S(2)}) collective-permute-start(bf16[144,128]{1,0:T(8,128)(2,1)S(1)} %get-tuple-element.65), channel_id=1, source_target_pairs={{0,64},{1,65},{2,66},{3,67},{4,68},{5,69},{6,70},{7,71},{8,72},{9,... | collective-permute-start | bytes 110600 | tf_op jit(solution)/shard_map/ppermute | solution.py:506
  54.9 2.1 %collective-permute-start.10 = (bf16[144,128]{1,0:T(8,128)(2,1)S(1)}, bf16[144,128]{1,0:T(8,128)(2,1)S(1)}, u32[]{:S(2)}, u32[]{:S(2)}) collective-permute-start(bf16[144,128]{1,0:T(8,128)(2,1)S(1)} %get-tuple-element.67), channel_id=1, source_target_pairs={{0,68},{1,69},{2,70},{3,71},{4,64},{5,65},{6,66},{7,67},{8,76},{9,... | collective-permute-start | bytes 110600 | tf_op jit(solution)/shard_map/ppermute | solution.py:506
  57.6 1.1 %collective-permute-done.9.a2 = bf16[144,128]{1,0:T(8,128)(2,1)S(1)} collective-permute-done((bf16[144,128]{1,0:T(8,128)(2,1)S(1)}, bf16[144,128]{1,0:T(8,128)(2,1)S(1)}, u32[]{:S(2)}, u32[]{:S(2)}) %collective-permute-start.9) | collective-permute-done | bytes 36896 | tf_op jit(solution)/shard_map/ppermute | solution.py:506
  58.7 1.1 %collective-permute-done.10.a3 = bf16[144,128]{1,0:T(8,128)(2,1)S(1)} collective-permute-done((bf16[144,128]{1,0:T(8,128)(2,1)S(1)}, bf16[144,128]{1,0:T(8,128)(2,1)S(1)}, u32[]{:S(2)}, u32[]{:S(2)}) %collective-permute-start.10) | collective-permute-done | bytes 36896 | tf_op jit(solution)/shard_map/ppermute | solution.py:506
  59.9 4.3 %collective-permute-start.11 = (bf16[96,128]{1,0:T(8,128)(2,1)S(1)}, bf16[96,128]{1,0:T(8,128)(2,1)S(1)}, u32[]{:S(2)}, u32[]{:S(2)}) collective-permute-start(bf16[96,128]{1,0:T(8,128)(2,1)S(1)} %get-tuple-element.69), channel_id=1, source_target_pairs={{0,48},{1,49},{2,50},{3,51},{4,52},{5,53},{6,54},{7,55},{8,56},{9,... | collective-permute-start | bytes 73736 | tf_op jit(solution)/shard_map/ppermute | solution.py:506
  64.2 1.8 %collective-permute-done.11.got = bf16[96,128]{1,0:T(8,128)(2,1)S(1)} collective-permute-done((bf16[96,128]{1,0:T(8,128)(2,1)S(1)}, bf16[96,128]{1,0:T(8,128)(2,1)S(1)}, u32[]{:S(2)}, u32[]{:S(2)}) %collective-permute-start.11) | collective-permute-done | bytes 24608 | tf_op jit(solution)/shard_map/ppermute | solution.py:506
  66.0 3.8 %collective-permute-start.12 = (bf16[48,128]{1,0:T(8,128)(2,1)S(1)}, bf16[48,128]{1,0:T(8,128)(2,1)S(1)}, u32[]{:S(2)}, u32[]{:S(2)}) collective-permute-start(bf16[48,128]{1,0:T(8,128)(2,1)S(1)} %get-tuple-element.71), channel_id=1, source_target_pairs={{0,16},{1,17},{2,18},{3,19},{4,20},{5,21},{6,22},{7,23},{8,24},{9,... | collective-permute-start | bytes 36872 | tf_op jit(solution)/shard_map/ppermute | solution.py:506
  69.9 1.7 %collective-permute-done.12.got = bf16[48,128]{1,0:T(8,128)(2,1)S(1)} collective-permute-done((bf16[48,128]{1,0:T(8,128)(2,1)S(1)}, bf16[48,128]{1,0:T(8,128)(2,1)S(1)}, u32[]{:S(2)}, u32[]{:S(2)}) %collective-permute-start.12) | collective-permute-done | bytes 12320 | tf_op jit(solution)/shard_map/ppermute | solution.py:506
  71.6 0.9 %collective-permute-start.13 = (f32[24,128]{1,0:T(8,128)S(1)}, f32[24,128]{1,0:T(8,128)S(1)}, u32[]{:S(2)}, u32[]{:S(2)}) collective-permute-start(f32[24,128]{1,0:T(8,128)S(1)} %get-tuple-element.73), channel_id=1, source_target_pairs={{0,2},{1,3},{2,0},{3,1},{4,6},{5,7},{6,4},{7,5},{8,10},{9,11},{10,... | collective-permute-start | bytes 36872 | tf_op jit(solution)/shard_map/ppermute | solution.py:506
  72.4 2.8 %collective-permute-done.13.got = f32[24,128]{1,0:T(8,128)S(1)} collective-permute-done((f32[24,128]{1,0:T(8,128)S(1)}, f32[24,128]{1,0:T(8,128)S(1)}, u32[]{:S(2)}, u32[]{:S(2)}) %collective-permute-start.13) | collective-permute-done | bytes 12320 | tf_op jit(solution)/shard_map/ppermute | solution.py:506
  75.3 0.8 finish.1
  (19 shorter events, 1.8 us)
Async XLA Ops:
  2.5 13.0 %collective-permute-start = (bf16[592,128]{1,0:T(8,128)(2,1)}, bf16[592,128]{1,0:T(8,128)(2,1)S(1)}, u32[]{:S(2)}, u32[]{:S(2)}) collective-permute-start(bf16[592,128]{1,0:T(8,128)(2,1)} %get-tuple-element.42), channel_id=1, source_target_pairs={{0,16},{16,32},{32,48},{48,64},{64,80},{80,96},{96,112},{112,128},... | collective-permute-start | bytes 454664 | tf_op jit(solution)/shard_map/ppermute | solution.py:527
  5.9 11.6 %collective-permute-start.1 = (bf16[592,128]{1,0:T(8,128)(2,1)}, bf16[592,128]{1,0:T(8,128)(2,1)S(1)}, u32[]{:S(2)}, u32[]{:S(2)}) collective-permute-start(bf16[592,128]{1,0:T(8,128)(2,1)} %get-tuple-element.43), channel_id=1, source_target_pairs={{0,240},{16,0},{32,16},{48,32},{64,48},{80,64},{96,80},{112,96},{1... | collective-permute-start | bytes 454664 | tf_op jit(solution)/shard_map/ppermute | solution.py:528
  9.0 0.9 %copy-start = (bf16[96,8,128]{2,1,0:T(8,128)(2,1)S(1)}, bf16[96,8,128]{2,1,0:T(8,128)(2,1)}, u32[]{:S(2)}) copy-start(bf16[96,8,128]{2,1,0:T(8,128)(2,1)} %features.3) | copy-start | bytes 589828
  9.9 0.9 %copy-start.1 = (bf16[96,8,128]{2,1,0:T(8,128)(2,1)S(1)}, bf16[96,8,128]{2,1,0:T(8,128)(2,1)}, u32[]{:S(2)}) copy-start(bf16[96,8,128]{2,1,0:T(8,128)(2,1)} %cotangent.3) | copy-start | bytes 589828
  10.8 0.7 copy-start.2
  11.5 1.1 %copy-start.3 = (bf16[27,96,96]{2,1,0:T(8,128)(2,1)S(1)}, bf16[27,96,96]{2,1,0:T(8,128)(2,1)}, u32[]{:S(2)}) copy-start(bf16[27,96,96]{2,1,0:T(8,128)(2,1)} %first.1) | copy-start | bytes 1492996
  12.6 1.1 %copy-start.4 = (bf16[27,96,96]{2,1,0:T(8,128)(2,1)S(1)}, bf16[27,96,96]{2,1,0:T(8,128)(2,1)}, u32[]{:S(2)}) copy-start(bf16[27,96,96]{2,1,0:T(8,128)(2,1)} %second.1) | copy-start | bytes 1492996
  17.8 10.8 %collective-permute-start.2 = (bf16[1104,128]{1,0:T(8,128)(2,1)S(1)}, bf16[1104,128]{1,0:T(8,128)(2,1)S(1)}, u32[]{:S(2)}, u32[]{:S(2)}) collective-permute-start(bf16[1104,128]{1,0:T(8,128)(2,1)S(1)} %get-tuple-element.50), channel_id=1, source_target_pairs={{0,1},{1,2},{2,3},{3,4},{4,5},{5,6},{6,7},{7,8},{8,9},{9,10},{10,1... | collective-permute-start | bytes 847880 | tf_op jit(solution)/shard_map/ppermute | solution.py:562
  17.9 10.8 %collective-permute-start.3 = (bf16[1104,128]{1,0:T(8,128)(2,1)S(1)}, bf16[1104,128]{1,0:T(8,128)(2,1)S(1)}, u32[]{:S(2)}, u32[]{:S(2)}) collective-permute-start(bf16[1104,128]{1,0:T(8,128)(2,1)S(1)} %get-tuple-element.51), channel_id=1, source_target_pairs={{0,15},{1,0},{2,1},{3,2},{4,3},{5,4},{6,5},{7,6},{8,7},{9,8},{10,9... | collective-permute-start | bytes 847880 | tf_op jit(solution)/shard_map/ppermute | solution.py:563
  40.0 2.0 %collective-permute-start.4 = (bf16[4,576,128]{2,1,0:T(8,128)(2,1)S(1)}, bf16[4,576,128]{2,1,0:T(8,128)(2,1)S(1)}, u32[]{:S(2)}, u32[]{:S(2)}) collective-permute-start(bf16[4,576,128]{2,1,0:T(8,128)(2,1)S(1)} %get-tuple-element.62), channel_id=1, source_target_pairs={{0,1},{1,0},{2,3},{3,2},{4,5},{5,4},{6,7},{7,6},{8,9},{9,8},{10,11... | collective-permute-start | bytes 1769480 | tf_op jit(solution)/shard_map/ppermute | solution.py:506
  42.2 8.9 %collective-permute-start.7 = (bf16[576,128]{1,0:T(8,128)(2,1)S(1)}, bf16[576,128]{1,0:T(8,128)(2,1)S(1)}, u32[]{:S(2)}, u32[]{:S(2)}) collective-permute-start(bf16[576,128]{1,0:T(8,128)(2,1)S(1)} %get-tuple-element.76), channel_id=1, source_target_pairs={{0,204},{1,205},{2,206},{3,207},{4,200},{5,201},{6,202},{7,203},{8... | collective-permute-start | bytes 442376 | tf_op jit(solution)/shard_map/ppermute | solution.py:506
  44.8 7.6 %collective-permute-start.6 = (bf16[576,128]{1,0:T(8,128)(2,1)S(1)}, bf16[576,128]{1,0:T(8,128)(2,1)S(1)}, u32[]{:S(2)}, u32[]{:S(2)}) collective-permute-start(bf16[576,128]{1,0:T(8,128)(2,1)S(1)} %get-tuple-element.77), channel_id=1, source_target_pairs={{0,192},{1,193},{2,194},{3,195},{4,196},{5,197},{6,198},{7,199},{8... | collective-permute-start | bytes 442376 | tf_op jit(solution)/shard_map/ppermute | solution.py:506
  45.3 8.1 %collective-permute-start.5 = (bf16[576,128]{1,0:T(8,128)(2,1)S(1)}, bf16[576,128]{1,0:T(8,128)(2,1)S(1)}, u32[]{:S(2)}, u32[]{:S(2)}) collective-permute-start(bf16[576,128]{1,0:T(8,128)(2,1)S(1)} %get-tuple-element.78), channel_id=1, source_target_pairs={{0,12},{1,13},{2,14},{3,15},{4,8},{5,9},{6,10},{7,11},{8,4},{9,5},... | collective-permute-start | bytes 442376 | tf_op jit(solution)/shard_map/ppermute | solution.py:506
  53.5 4.0 %collective-permute-start.8 = (bf16[144,128]{1,0:T(8,128)(2,1)S(1)}, bf16[144,128]{1,0:T(8,128)(2,1)S(1)}, u32[]{:S(2)}, u32[]{:S(2)}) collective-permute-start(bf16[144,128]{1,0:T(8,128)(2,1)S(1)} %get-tuple-element.65), channel_id=1, source_target_pairs={{0,64},{1,65},{2,66},{3,67},{4,68},{5,69},{6,70},{7,71},{8,72},{9,... | collective-permute-start | bytes 110600 | tf_op jit(solution)/shard_map/ppermute | solution.py:506
  54.6 4.1 %collective-permute-start.9 = (bf16[144,128]{1,0:T(8,128)(2,1)S(1)}, bf16[144,128]{1,0:T(8,128)(2,1)S(1)}, u32[]{:S(2)}, u32[]{:S(2)}) collective-permute-start(bf16[144,128]{1,0:T(8,128)(2,1)S(1)} %get-tuple-element.66), channel_id=1, source_target_pairs={{0,4},{1,5},{2,6},{3,7},{4,0},{5,1},{6,2},{7,3},{8,12},{9,13},{10,... | collective-permute-start | bytes 110600 | tf_op jit(solution)/shard_map/ppermute | solution.py:506
  54.9 4.9 %collective-permute-start.10 = (bf16[144,128]{1,0:T(8,128)(2,1)S(1)}, bf16[144,128]{1,0:T(8,128)(2,1)S(1)}, u32[]{:S(2)}, u32[]{:S(2)}) collective-permute-start(bf16[144,128]{1,0:T(8,128)(2,1)S(1)} %get-tuple-element.67), channel_id=1, source_target_pairs={{0,68},{1,69},{2,70},{3,71},{4,64},{5,65},{6,66},{7,67},{8,76},{9,... | collective-permute-start | bytes 110600 | tf_op jit(solution)/shard_map/ppermute | solution.py:506
  59.9 6.1 %collective-permute-start.11 = (bf16[96,128]{1,0:T(8,128)(2,1)S(1)}, bf16[96,128]{1,0:T(8,128)(2,1)S(1)}, u32[]{:S(2)}, u32[]{:S(2)}) collective-permute-start(bf16[96,128]{1,0:T(8,128)(2,1)S(1)} %get-tuple-element.69), channel_id=1, source_target_pairs={{0,48},{1,49},{2,50},{3,51},{4,52},{5,53},{6,54},{7,55},{8,56},{9,... | collective-permute-start | bytes 73736 | tf_op jit(solution)/shard_map/ppermute | solution.py:506
  66.0 5.5 %collective-permute-start.12 = (bf16[48,128]{1,0:T(8,128)(2,1)S(1)}, bf16[48,128]{1,0:T(8,128)(2,1)S(1)}, u32[]{:S(2)}, u32[]{:S(2)}) collective-permute-start(bf16[48,128]{1,0:T(8,128)(2,1)S(1)} %get-tuple-element.71), channel_id=1, source_target_pairs={{0,16},{1,17},{2,18},{3,19},{4,20},{5,21},{6,22},{7,23},{8,24},{9,... | collective-permute-start | bytes 36872 | tf_op jit(solution)/shard_map/ppermute | solution.py:506
  71.6 3.7 %collective-permute-start.13 = (f32[24,128]{1,0:T(8,128)S(1)}, f32[24,128]{1,0:T(8,128)S(1)}, u32[]{:S(2)}, u32[]{:S(2)}) collective-permute-start(f32[24,128]{1,0:T(8,128)S(1)} %get-tuple-element.73), channel_id=1, source_target_pairs={{0,2},{1,3},{2,0},{3,1},{4,6},{5,7},{6,4},{7,5},{8,10},{9,11},{10,... | collective-permute-start | bytes 36872 | tf_op jit(solution)/shard_map/ppermute | solution.py:506

commit v6 on v5

--- a/solution.py
+++ b/solution.py
@@ -158,7 +158,12 @@
         own_cot[x] = flip_pad(plain).astype(BF16)
 
 
-def rims_kernel(west, east, feat, cot, own_mask, to_south, to_north):
+def northern(row):
+    return (row & 1) == 0
+
+
+def rims_kernel(west, east, feat, cot, own_mask, first, second):
+    even = northern(lax.axis_index("north"))
     half = lanes(CH) < 64
     quarter = lanes(CH) // 32
 
@@ -179,12 +184,15 @@
     for k in range(8):
         one, two = feat_plane(k), feat_plane(k + 8)
         rows = slice(k * CH, (k + 1) * CH)
-        to_south[rows, :] = jnp.where(half, one, pltpu.roll(two, 64, 1)).astype(BF16)
-        to_north[rows, :] = jnp.where(half, pltpu.roll(one, 64, 1), two).astype(BF16)
+        low = jnp.where(half, one, pltpu.roll(two, 64, 1))
+        high = jnp.where(half, pltpu.roll(one, 64, 1), two)
+        first[rows, :] = jnp.where(even, high, low).astype(BF16)
+        second[rows, :] = jnp.where(even, low, high).astype(BF16)
     for k in range(3):
         four = [cot_plane(k + 3 * q) for q in range(4)]
         rows = slice((8 + k) * CH, (9 + k) * CH)
-        for out, shift in ((to_south, 0), (to_north, 32)):
+        packs = []
+        for shift in (0, 32):
             moved = [
                 pltpu.roll(four[q], (32 * q + shift) % LN, 1) if (32 * q + shift) % LN else four[q]
                 for q in range(4)
@@ -194,8 +202,11 @@
                 jnp.where(quarter == 0, moved[0], moved[1]),
                 jnp.where(quarter == 2, moved[2], moved[3]),
             )
-            out[rows, :] = packed.astype(BF16)
-    for out in (to_south, to_north):
+            packs.append(packed)
+        low, high = packs
+        first[rows, :] = jnp.where(even, high, low).astype(BF16)
+        second[rows, :] = jnp.where(even, low, high).astype(BF16)
+    for out in (first, second):
         out[11 * CH : 11 * CH + 16, :] = west[6 * CH : STRIP, :]
         out[11 * CH + 16 : 11 * CH + 32, :] = own_mask[...]
         out[11 * CH + 32 : RIM, :] = east[6 * CH : STRIP, :]
@@ -259,18 +270,22 @@
     return mask
 
 
-def kernel_grad(turned, planes, shift, scale, result):
+def kernel_grad(turned, planes, shift, scale, result, part):
     def piece(k):
-        a, b = k // 3, k % 3
-        start = (shift + 1 - b) * 16
-        return planes[shift + 1 - a : shift + 9 - a, start : start + 128, :].reshape(1024, LN)
-
+        first = shift + 1 - k // 3 + 4 * part
+        start = (shift + 1 - k % 3) * 16
+        return planes[first : first + 4, start : start + 128, :].reshape(512, LN)
+
+    left = turned[:, 512 * part : 512 * part + 512]
     for k in range(0, 9, 2):
         right = jnp.concatenate([piece(k), piece(min(k + 1, 8))], axis=1)
-        part = jnp.dot(turned[...], right, preferred_element_type=F32) * scale
-        result[k * 288 : k * 288 + 288, :] = part[:, 0:LN]
-        if k < 8:
-            result[(k + 1) * 288 : (k + 1) * 288 + 288, :] = part[:, LN : 2 * LN]
+        value = jnp.dot(left, right, preferred_element_type=F32) * scale
+        for q in range(min(2, 9 - k)):
+            rows = slice((k + q) * 288, (k + q + 1) * 288)
+            if part:
+                result[rows, :] += value[:, q * LN : (q + 1) * LN]
+            else:
+                result[rows, :] = value[:, q * LN : (q + 1) * LN]
 
 
 def band(p, low, high):
@@ -284,8 +299,8 @@
     own_cot,
     side_cot,
     middle,
-    south,
-    north,
+    first,
+    second,
     fwd_one,
     fwd_two,
     back_two,
@@ -312,9 +327,15 @@
     rows,
 ):
     has = neighbours()
-    for ref, flag, row in ((south, has[2], 0), (north, has[3], 192)):
-        tile = ref[11 * CH : 11 * CH + 48, :].astype(F32) * flag
-        turned = jnp.concatenate([tile, jnp.zeros((80, LN), F32)], axis=0).T[0:64]
+    even = northern(lax.axis_index("north"))
+
+    def halos(start, count):
+        a = first[start : start + count, :].astype(F32)
+        b = second[start : start + count, :].astype(F32)
+        return jnp.where(even, b, a), jnp.where(even, a, b)
+
+    for tile, flag, row in zip(halos(11 * CH, 48), has[2:], (0, 192)):
+        turned = jnp.concatenate([tile * flag, jnp.zeros((80, LN), F32)], axis=0).T[0:64]
         for bx in range(3):
             side = has[bx // 2] if bx != 1 else 1.0
             column = turned[:, 16 * bx : 16 * bx + 1] * side
@@ -322,13 +343,13 @@
     masks[:, 64:192, :] = middle[...]
 
     for k in range(8):
-        for ref, row in ((south, 0), (north, 64)):
-            both = flip_pad(ref[k * CH : (k + 1) * CH, :])
+        for block, row in zip(halos(k * CH, CH), (0, 64)):
+            both = flip_pad(block)
             edge[k, row : row + 64, :] = both[0:64]
             edge[k + 8, row : row + 64, :] = both[64:128]
     for k in range(3):
-        for ref, row in ((south, 0), (north, 160)):
-            four = flip_pad(ref[(8 + k) * CH : (9 + k) * CH, :])
+        for block, row in zip(halos((8 + k) * CH, CH), (0, 160)):
+            four = flip_pad(block)
             for q in range(4):
                 upstream[k + 3 * q, row : row + 32, :] = four[32 * q : 32 * q + 32]
     for k in range(2):
@@ -390,10 +411,14 @@
         if 7 <= t < 12:
             after_three(2 * t - 14)
             after_three(2 * t - 13)
+        if t == 8:
+            kernel_grad(turned_two, grad_two, 2, scale, grad_two_sum, 0)
+        if t == 9:
+            activated[...] = rows[...].reshape(CH, 8, LN).astype(BF16)
+            kernel_grad(turned_two, grad_two, 2, scale, grad_two_sum, 1)
         if t == 10:
-            kernel_grad(turned_two, grad_two, 2, scale, grad_two_sum)
-    activated[...] = rows[...].reshape(CH, 8, LN).astype(BF16)
-    kernel_grad(turned_one, grad_one, 1, scale, grad_one_sum)
+            kernel_grad(turned_one, grad_one, 1, scale, grad_one_sum, 0)
+    kernel_grad(turned_one, grad_one, 1, scale, grad_one_sum, 1)
 
     column, row = here()
     position = column * 16 + row
@@ -501,6 +526,11 @@
     return [(i, (i + step) % count) for i in range(count)]
 
 
+def mirror(phase, axis):
+    count = lax.axis_size(axis)
+    return [(i, (i + (1 if i % 2 == phase else -1)) % count) for i in range(count)]
+
+
 def swap(value, bits):
     count = lax.axis_size("east") * lax.axis_size("north")
     return lax.ppermute(value, BOTH, [(i, i ^ bits) for i in range(count)])
@@ -545,7 +575,7 @@
         cotangent,
         occupied,
     )
-    to_south, to_north = call(
+    first, second = call(
         rims_kernel,
         "rims",
         [shape(RIM, LN), shape(RIM, LN)],
@@ -559,8 +589,8 @@
         cot,
         own_mask,
     )
-    south = lax.ppermute(to_north, "north", shift_by(1, "north"))
-    north = lax.ppermute(to_south, "north", shift_by(-1, "north"))
+    first = lax.ppermute(first, "north", mirror(0, "north"))
+    second = lax.ppermute(second, "north", mirror(1, "north"))
     side_grid, side_cot, middle = call(
         sides_kernel,
         "sides",
@@ -609,8 +639,8 @@
         own_cot,
         side_cot,
         middle,
-        south,
-        north,
+        first,
+        second,
         fwd_one,
         fwd_two,
         back_two,

time: 77.5 us -> 77.9 us (level)
  waiting for transfers between devices: 24 us -> 27.2 us
  starting transfers between devices: 27.8 us -> 24.9 us
    ppermute x10, waiting for transfers between devices: 15.3 us -> 17.1 us  [swap(): return lax.ppermute(value, BOTH, [(i, i ^ bits) for i in range(count)])]
    ppermute x10, starting transfers between devices: 17.4 us -> 15.9 us  [swap(): return lax.ppermute(value, BOTH, [(i, i ^ bits) for i in range(count)])]
    ppermute x2, starting transfers between devices: 3.93 us -> 2.47 us  [the longest x1 2.38 us: local(): second = lax.ppermute(second, 'north', mirror(1, 'north'))]
    ppermute x2, waiting for transfers between devices: 6.7 us -> 8.11 us  [the longest x1 8.11 us: local(): second = lax.ppermute(second, 'north', mirror(1, 'north'))]
where the time goes in v6:
time: 77.9 us; the launch traced here: 76.5 us
  waiting for transfers between devices  27.2 us (35%)
  starting transfers between devices  24.9 us (32%)
  Pallas kernels  18.9 us (24%)
  local copies, waits for them, and re-layouts  4.73 us (6%)
    pallas_call x11, Pallas kernels, call(): pl.pallas_call(kernel, out_shape=outs, in_specs=specs, out_specs=[VMEM] *...  18.9 us
    ppermute x10, waiting for transfers between devices, swap(): return lax.ppermute(value, BOTH, [(i, i ^ bits) for i in range(count)])  17.1 us
    ppermute x10, starting transfers between devices, swap(): return lax.ppermute(value, BOTH, [(i, i ^ bits) for i in range(count)])  15.9 us
    ppermute x1, waiting for transfers between devices, local(): second = lax.ppermute(second, 'north', mirror(1, 'north'))  8.11 us
    unnamed x10, local copies, waits for them, and re-layouts  4.69 us
    ppermute x1, starting transfers between devices, local(): west = lax.ppermute(to_east, 'east', shift_by(1, 'east'))  3.35 us
    ppermute x1, starting transfers between devices, local(): east = lax.ppermute(to_west, 'east', shift_by(-1, 'east'))  3.09 us
    ppermute x1, starting transfers between devices, local(): second = lax.ppermute(second, 'north', mirror(1, 'north'))  2.38 us
  transfers between devices with their start and end apart: 14, of which 12 were waited for; matrix products, arithmetic and copies ran while one was open for 0% of the time, Pallas kernels for 5%

profile of v6, /device:TPU:2, one launch (start us, length us, event | category | flops | bytes accessed | tf_op | source)
XLA Modules:
  0.0 76.5 jit_solution(1594846054555198007)
XLA Ops:
  0.6 1.9 %strips.1 = (bf16[592,128]{1,0:T(8,128)(2,1)}, bf16[592,128]{1,0:T(8,128)(2,1)}) custom-call(s32[1,2]{1,0:T(1,128)} %bitcast.13, bf16[96,8,128]{2,1,0:T(8,128)(2,1)} %features.3, bf16[96,8,128]{2,1,0:T(8,128)(2,1)} %cotangent.3), custom_call_target="tpu_custom_call" | custom-call | flops 1048576 | bytes 1048576 | tf_op jit(solution)/shard_map/strips/pallas_call | solution.py:508
  2.5 3.3 %collective-permute-start = (bf16[592,128]{1,0:T(8,128)(2,1)}, bf16[592,128]{1,0:T(8,128)(2,1)S(1)}, u32[]{:S(2)}, u32[]{:S(2)}) collective-permute-start(bf16[592,128]{1,0:T(8,128)(2,1)} %get-tuple-element.42), channel_id=1, source_target_pairs={{0,16},{16,32},{32,48},{48,64},{64,80},{80,96},{96,112},{112,128},... | collective-permute-start | bytes 454664 | tf_op jit(solution)/shard_map/ppermute | solution.py:557
  5.9 3.1 %collective-permute-start.1 = (bf16[592,128]{1,0:T(8,128)(2,1)}, bf16[592,128]{1,0:T(8,128)(2,1)S(1)}, u32[]{:S(2)}, u32[]{:S(2)}) collective-permute-start(bf16[592,128]{1,0:T(8,128)(2,1)} %get-tuple-element.43), channel_id=1, source_target_pairs={{0,240},{16,0},{32,16},{48,32},{64,48},{80,64},{96,80},{112,96},{1... | collective-permute-start | bytes 454664 | tf_op jit(solution)/shard_map/ppermute | solution.py:558
  9.0 0.9 %copy-done = bf16[96,8,128]{2,1,0:T(8,128)(2,1)S(1)} copy-done((bf16[96,8,128]{2,1,0:T(8,128)(2,1)S(1)}, bf16[96,8,128]{2,1,0:T(8,128)(2,1)}, u32[]{:S(2)}) %copy-start) | copy-done | bytes 196632
  9.9 0.9 %copy-done.1 = bf16[96,8,128]{2,1,0:T(8,128)(2,1)S(1)} copy-done((bf16[96,8,128]{2,1,0:T(8,128)(2,1)S(1)}, bf16[96,8,128]{2,1,0:T(8,128)(2,1)}, u32[]{:S(2)}) %copy-start.1) | copy-done | bytes 196632
  10.8 0.7 copy-done.2
  11.5 1.1 %copy-done.3 = bf16[27,96,96]{2,1,0:T(8,128)(2,1)S(1)} copy-done((bf16[27,96,96]{2,1,0:T(8,128)(2,1)S(1)}, bf16[27,96,96]{2,1,0:T(8,128)(2,1)}, u32[]{:S(2)}) %copy-start.3) | copy-done | bytes 497688
  12.6 1.1 %copy-done.4 = bf16[27,96,96]{2,1,0:T(8,128)(2,1)S(1)} copy-done((bf16[27,96,96]{2,1,0:T(8,128)(2,1)S(1)}, bf16[27,96,96]{2,1,0:T(8,128)(2,1)}, u32[]{:S(2)}) %copy-start.4) | copy-done | bytes 497688
  13.7 1.8 %prepare.1 = (bf16[5,896,128]{2,1,0:T(8,128)(2,1)S(1)}, bf16[5,896,128]{2,1,0:T(8,128)(2,1)S(1)}, bf16[5,896,128]{2,1,0:T(8,128)(2,1)S(1)}, bf16[5,896,128]{2,1,...) custom-call(bf16[27,96,96]{2,1,0:T(8,128)(2,1)S(1)} %copy-done.3, ...), custom_call_target="tpu_custom_call" | custom-call | flops 8589934592 | bytes 1048576 | tf_op jit(solution)/shard_map/prepare/pallas_call | solution.py:508
  15.5 2.0 %collective-permute-done.1.east = bf16[592,128]{1,0:T(8,128)(2,1)S(1)} collective-permute-done((bf16[592,128]{1,0:T(8,128)(2,1)}, bf16[592,128]{1,0:T(8,128)(2,1)S(1)}, u32[]{:S(2)}, u32[]{:S(2)}) %collective-permute-start.1) | collective-permute-done | bytes 151584 | tf_op jit(solution)/shard_map/ppermute | solution.py:558
  17.9 2.4 %collective-permute-start.3 = (bf16[1104,128]{1,0:T(8,128)(2,1)S(1)}, bf16[1104,128]{1,0:T(8,128)(2,1)S(1)}, u32[]{:S(2)}, u32[]{:S(2)}) collective-permute-start(bf16[1104,128]{1,0:T(8,128)(2,1)S(1)} %get-tuple-element.51), channel_id=1, source_target_pairs={{0,15},{1,2},{2,1},{3,4},{4,3},{5,6},{6,5},{7,8},{8,7},{9,10},{10,... | collective-permute-start | bytes 847880 | tf_op jit(solution)/shard_map/ppermute | solution.py:593
  20.5 8.1 %collective-permute-done.3.refs_6_ = bf16[1104,128]{1,0:T(8,128)(2,1)S(1)} collective-permute-done((bf16[1104,128]{1,0:T(8,128)(2,1)S(1)}, bf16[1104,128]{1,0:T(8,128)(2,1)S(1)}, u32[]{:S(2)}, u32[]{:S(2)}) %collective-permute-start.3) | collective-permute-done | bytes 282656 | tf_op jit(solution)/shard_map/ppermute | solution.py:593
  28.6 11.6 %level.1 = (bf16[96,8,128]{2,1,0:T(8,128)(2,1)}, bf16[10,160,128]{2,1,0:T(8,128)(2,1)S(1)}, f32[3,256,128]{2,1,0:T(8,128)S(1)}, bf16[4,576,128]{2,1,0:T(8,128)(2,1)S(1)}, bf16[4,576,128]{2,1,0:T(8,128)(2,1)S(1)}) custom-call(bf16[8,128,128]{2,1,0:T(8,128)(2,1)S(1)} %get-tuple-element.40.refs_0_, bf16[8,128,128]{2,1,0:T(8,128)(2,1)S(1)} %get-tuple-element.44.refs_1_, ...), custom_call_target="tpu_custom_call" | custom-call | flops 17179869184 | bytes 1048576 | tf_op jit(solution)/shard_map/level/pallas_call | solution.py:508
  40.2 2.0 %collective-permute-done.4 = bf16[4,576,128]{2,1,0:T(8,128)(2,1)S(1)} collective-permute-done((bf16[4,576,128]{2,1,0:T(8,128)(2,1)S(1)}, bf16[4,576,128]{2,1,0:T(8,128)(2,1)S(1)}, u32[]{:S(2)}, u32[]{:S(2)}) %collective-permute-start.4) | collective-permute-done | bytes 589856 | tf_op jit(solution)/shard_map/ppermute | solution.py:536
  42.4 3.2 %collective-permute-start.7 = (bf16[576,128]{1,0:T(8,128)(2,1)S(1)}, bf16[576,128]{1,0:T(8,128)(2,1)S(1)}, u32[]{:S(2)}, u32[]{:S(2)}) collective-permute-start(bf16[576,128]{1,0:T(8,128)(2,1)S(1)} %get-tuple-element.76), channel_id=1, source_target_pairs={{0,204},{1,205},{2,206},{3,207},{4,200},{5,201},{6,202},{7,203},{8... | collective-permute-start | bytes 442376 | tf_op jit(solution)/shard_map/ppermute | solution.py:536
  45.6 0.5 collective-permute-start.6
  46.2 1.0 %collective-permute-start.5 = (bf16[576,128]{1,0:T(8,128)(2,1)S(1)}, bf16[576,128]{1,0:T(8,128)(2,1)S(1)}, u32[]{:S(2)}, u32[]{:S(2)}) collective-permute-start(bf16[576,128]{1,0:T(8,128)(2,1)S(1)} %get-tuple-element.78), channel_id=1, source_target_pairs={{0,12},{1,13},{2,14},{3,15},{4,8},{5,9},{6,10},{7,11},{8,4},{9,5},... | collective-permute-start | bytes 442376 | tf_op jit(solution)/shard_map/ppermute | solution.py:536
  47.2 2.1 %final.1 = (bf16[96,8,128]{2,1,0:T(8,128)(2,1)}, f32[8,128]{1,0:T(8,128)S(1)}) custom-call(bf16[10,160,128]{2,1,0:T(8,128)(2,1)S(1)} %get-tuple-element.57.grad_one, f32[3,256,128]{2,1,0:T(8,128)S(1)} %get-tuple-element.58.masks, bf16[5,896,128]{2,1,0:T(8,128)(2,1)S(1)} %get-tuple-element.59.back_one), custom_call_target="tpu_custom_call" | custom-call | flops 4294967296 | bytes 1048576 | tf_op jit(solution)/shard_map/final/pallas_call | solution.py:508
  49.3 2.0 %collective-permute-done.7.a3 = bf16[576,128]{1,0:T(8,128)(2,1)S(1)} collective-permute-done((bf16[576,128]{1,0:T(8,128)(2,1)S(1)}, bf16[576,128]{1,0:T(8,128)(2,1)S(1)}, u32[]{:S(2)}, u32[]{:S(2)}) %collective-permute-start.7) | collective-permute-done | bytes 147488 | tf_op jit(solution)/shard_map/ppermute | solution.py:536
  51.3 1.9 %collective-permute-done.6.a2 = bf16[576,128]{1,0:T(8,128)(2,1)S(1)} collective-permute-done((bf16[576,128]{1,0:T(8,128)(2,1)S(1)}, bf16[576,128]{1,0:T(8,128)(2,1)S(1)}, u32[]{:S(2)}, u32[]{:S(2)}) %collective-permute-start.6) | collective-permute-done | bytes 147488 | tf_op jit(solution)/shard_map/ppermute | solution.py:536
  53.2 0.5 collective-permute-done.5.a1
  53.7 2.6 %collective-permute-start.8 = (bf16[144,128]{1,0:T(8,128)(2,1)S(1)}, bf16[144,128]{1,0:T(8,128)(2,1)S(1)}, u32[]{:S(2)}, u32[]{:S(2)}) collective-permute-start(bf16[144,128]{1,0:T(8,128)(2,1)S(1)} %get-tuple-element.65), channel_id=1, source_target_pairs={{0,64},{1,65},{2,66},{3,67},{4,68},{5,69},{6,70},{7,71},{8,72},{9,... | collective-permute-start | bytes 110600 | tf_op jit(solution)/shard_map/ppermute | solution.py:536
  56.3 1.6 %collective-permute-start.10 = (bf16[144,128]{1,0:T(8,128)(2,1)S(1)}, bf16[144,128]{1,0:T(8,128)(2,1)S(1)}, u32[]{:S(2)}, u32[]{:S(2)}) collective-permute-start(bf16[144,128]{1,0:T(8,128)(2,1)S(1)} %get-tuple-element.67), channel_id=1, source_target_pairs={{0,68},{1,69},{2,70},{3,71},{4,64},{5,65},{6,66},{7,67},{8,76},{9,... | collective-permute-start | bytes 110600 | tf_op jit(solution)/shard_map/ppermute | solution.py:536
  58.2 2.0 %collective-permute-done.9.a2 = bf16[144,128]{1,0:T(8,128)(2,1)S(1)} collective-permute-done((bf16[144,128]{1,0:T(8,128)(2,1)S(1)}, bf16[144,128]{1,0:T(8,128)(2,1)S(1)}, u32[]{:S(2)}, u32[]{:S(2)}) %collective-permute-start.9) | collective-permute-done | bytes 36896 | tf_op jit(solution)/shard_map/ppermute | solution.py:536
  60.2 0.9 %collective-permute-done.10.a3 = bf16[144,128]{1,0:T(8,128)(2,1)S(1)} collective-permute-done((bf16[144,128]{1,0:T(8,128)(2,1)S(1)}, bf16[144,128]{1,0:T(8,128)(2,1)S(1)}, u32[]{:S(2)}, u32[]{:S(2)}) %collective-permute-start.10) | collective-permute-done | bytes 36896 | tf_op jit(solution)/shard_map/ppermute | solution.py:536
  61.2 3.0 %collective-permute-start.11 = (bf16[96,128]{1,0:T(8,128)(2,1)S(1)}, bf16[96,128]{1,0:T(8,128)(2,1)S(1)}, u32[]{:S(2)}, u32[]{:S(2)}) collective-permute-start(bf16[96,128]{1,0:T(8,128)(2,1)S(1)} %get-tuple-element.69), channel_id=1, source_target_pairs={{0,48},{1,49},{2,50},{3,51},{4,52},{5,53},{6,54},{7,55},{8,56},{9,... | collective-permute-start | bytes 73736 | tf_op jit(solution)/shard_map/ppermute | solution.py:536
  64.3 3.0 %collective-permute-done.11.got = bf16[96,128]{1,0:T(8,128)(2,1)S(1)} collective-permute-done((bf16[96,128]{1,0:T(8,128)(2,1)S(1)}, bf16[96,128]{1,0:T(8,128)(2,1)S(1)}, u32[]{:S(2)}, u32[]{:S(2)}) %collective-permute-start.11) | collective-permute-done | bytes 24608 | tf_op jit(solution)/shard_map/ppermute | solution.py:536
  67.3 3.1 %collective-permute-start.12 = (bf16[48,128]{1,0:T(8,128)(2,1)S(1)}, bf16[48,128]{1,0:T(8,128)(2,1)S(1)}, u32[]{:S(2)}, u32[]{:S(2)}) collective-permute-start(bf16[48,128]{1,0:T(8,128)(2,1)S(1)} %get-tuple-element.71), channel_id=1, source_target_pairs={{0,16},{1,17},{2,18},{3,19},{4,20},{5,21},{6,22},{7,23},{8,24},{9,... | collective-permute-start | bytes 36872 | tf_op jit(solution)/shard_map/ppermute | solution.py:536
  70.4 1.7 %collective-permute-done.12.got = bf16[48,128]{1,0:T(8,128)(2,1)S(1)} collective-permute-done((bf16[48,128]{1,0:T(8,128)(2,1)S(1)}, bf16[48,128]{1,0:T(8,128)(2,1)S(1)}, u32[]{:S(2)}, u32[]{:S(2)}) %collective-permute-start.12) | collective-permute-done | bytes 12320 | tf_op jit(solution)/shard_map/ppermute | solution.py:536
  72.1 0.9 %collective-permute-start.13 = (f32[24,128]{1,0:T(8,128)S(1)}, f32[24,128]{1,0:T(8,128)S(1)}, u32[]{:S(2)}, u32[]{:S(2)}) collective-permute-start(f32[24,128]{1,0:T(8,128)S(1)} %get-tuple-element.73), channel_id=1, source_target_pairs={{0,2},{1,3},{2,0},{3,1},{4,6},{5,7},{6,4},{7,5},{8,10},{9,11},{10,... | collective-permute-start | bytes 36872 | tf_op jit(solution)/shard_map/ppermute | solution.py:536
  72.9 2.8 %collective-permute-done.13.got = f32[24,128]{1,0:T(8,128)S(1)} collective-permute-done((f32[24,128]{1,0:T(8,128)S(1)}, f32[24,128]{1,0:T(8,128)S(1)}, u32[]{:S(2)}, u32[]{:S(2)}) %collective-permute-start.13) | collective-permute-done | bytes 12320 | tf_op jit(solution)/shard_map/ppermute | solution.py:536
  75.8 0.8 finish.1
  (19 shorter events, 1.4 us)
Async XLA Ops:
  2.5 13.0 %collective-permute-start = (bf16[592,128]{1,0:T(8,128)(2,1)}, bf16[592,128]{1,0:T(8,128)(2,1)S(1)}, u32[]{:S(2)}, u32[]{:S(2)}) collective-permute-start(bf16[592,128]{1,0:T(8,128)(2,1)} %get-tuple-element.42), channel_id=1, source_target_pairs={{0,16},{16,32},{32,48},{48,64},{64,80},{80,96},{96,112},{112,128},... | collective-permute-start | bytes 454664 | tf_op jit(solution)/shard_map/ppermute | solution.py:557
  5.9 11.6 %collective-permute-start.1 = (bf16[592,128]{1,0:T(8,128)(2,1)}, bf16[592,128]{1,0:T(8,128)(2,1)S(1)}, u32[]{:S(2)}, u32[]{:S(2)}) collective-permute-start(bf16[592,128]{1,0:T(8,128)(2,1)} %get-tuple-element.43), channel_id=1, source_target_pairs={{0,240},{16,0},{32,16},{48,32},{64,48},{80,64},{96,80},{112,96},{1... | collective-permute-start | bytes 454664 | tf_op jit(solution)/shard_map/ppermute | solution.py:558
  9.0 0.9 %copy-start = (bf16[96,8,128]{2,1,0:T(8,128)(2,1)S(1)}, bf16[96,8,128]{2,1,0:T(8,128)(2,1)}, u32[]{:S(2)}) copy-start(bf16[96,8,128]{2,1,0:T(8,128)(2,1)} %features.3) | copy-start | bytes 589828
  9.9 0.9 %copy-start.1 = (bf16[96,8,128]{2,1,0:T(8,128)(2,1)S(1)}, bf16[96,8,128]{2,1,0:T(8,128)(2,1)}, u32[]{:S(2)}) copy-start(bf16[96,8,128]{2,1,0:T(8,128)(2,1)} %cotangent.3) | copy-start | bytes 589828
  10.8 0.7 copy-start.2
  11.5 1.1 %copy-start.3 = (bf16[27,96,96]{2,1,0:T(8,128)(2,1)S(1)}, bf16[27,96,96]{2,1,0:T(8,128)(2,1)}, u32[]{:S(2)}) copy-start(bf16[27,96,96]{2,1,0:T(8,128)(2,1)} %first.1) | copy-start | bytes 1492996
  12.6 1.1 %copy-start.4 = (bf16[27,96,96]{2,1,0:T(8,128)(2,1)S(1)}, bf16[27,96,96]{2,1,0:T(8,128)(2,1)}, u32[]{:S(2)}) copy-start(bf16[27,96,96]{2,1,0:T(8,128)(2,1)} %second.1) | copy-start | bytes 1492996
  17.8 2.7 %collective-permute-start.2 = (bf16[1104,128]{1,0:T(8,128)(2,1)S(1)}, bf16[1104,128]{1,0:T(8,128)(2,1)S(1)}, u32[]{:S(2)}, u32[]{:S(2)}) collective-permute-start(bf16[1104,128]{1,0:T(8,128)(2,1)S(1)} %get-tuple-element.50), channel_id=1, source_target_pairs={{0,1},{1,0},{2,3},{3,2},{4,5},{5,4},{6,7},{7,6},{8,9},{9,8},{10,11... | collective-permute-start | bytes 847880 | tf_op jit(solution)/shard_map/ppermute | solution.py:592
  17.9 10.7 %collective-permute-start.3 = (bf16[1104,128]{1,0:T(8,128)(2,1)S(1)}, bf16[1104,128]{1,0:T(8,128)(2,1)S(1)}, u32[]{:S(2)}, u32[]{:S(2)}) collective-permute-start(bf16[1104,128]{1,0:T(8,128)(2,1)S(1)} %get-tuple-element.51), channel_id=1, source_target_pairs={{0,15},{1,2},{2,1},{3,4},{4,3},{5,6},{6,5},{7,8},{8,7},{9,10},{10,... | collective-permute-start | bytes 847880 | tf_op jit(solution)/shard_map/ppermute | solution.py:593
  40.2 2.0 %collective-permute-start.4 = (bf16[4,576,128]{2,1,0:T(8,128)(2,1)S(1)}, bf16[4,576,128]{2,1,0:T(8,128)(2,1)S(1)}, u32[]{:S(2)}, u32[]{:S(2)}) collective-permute-start(bf16[4,576,128]{2,1,0:T(8,128)(2,1)S(1)} %get-tuple-element.62), channel_id=1, source_target_pairs={{0,1},{1,0},{2,3},{3,2},{4,5},{5,4},{6,7},{7,6},{8,9},{9,8},{10,11... | collective-permute-start | bytes 1769480 | tf_op jit(solution)/shard_map/ppermute | solution.py:536
  42.4 8.9 %collective-permute-start.7 = (bf16[576,128]{1,0:T(8,128)(2,1)S(1)}, bf16[576,128]{1,0:T(8,128)(2,1)S(1)}, u32[]{:S(2)}, u32[]{:S(2)}) collective-permute-start(bf16[576,128]{1,0:T(8,128)(2,1)S(1)} %get-tuple-element.76), channel_id=1, source_target_pairs={{0,204},{1,205},{2,206},{3,207},{4,200},{5,201},{6,202},{7,203},{8... | collective-permute-start | bytes 442376 | tf_op jit(solution)/shard_map/ppermute | solution.py:536
  45.6 7.6 %collective-permute-start.6 = (bf16[576,128]{1,0:T(8,128)(2,1)S(1)}, bf16[576,128]{1,0:T(8,128)(2,1)S(1)}, u32[]{:S(2)}, u32[]{:S(2)}) collective-permute-start(bf16[576,128]{1,0:T(8,128)(2,1)S(1)} %get-tuple-element.77), channel_id=1, source_target_pairs={{0,192},{1,193},{2,194},{3,195},{4,196},{5,197},{6,198},{7,199},{8... | collective-permute-start | bytes 442376 | tf_op jit(solution)/shard_map/ppermute | solution.py:536
  46.2 7.5 %collective-permute-start.5 = (bf16[576,128]{1,0:T(8,128)(2,1)S(1)}, bf16[576,128]{1,0:T(8,128)(2,1)S(1)}, u32[]{:S(2)}, u32[]{:S(2)}) collective-permute-start(bf16[576,128]{1,0:T(8,128)(2,1)S(1)} %get-tuple-element.78), channel_id=1, source_target_pairs={{0,12},{1,13},{2,14},{3,15},{4,8},{5,9},{6,10},{7,11},{8,4},{9,5},... | collective-permute-start | bytes 442376 | tf_op jit(solution)/shard_map/ppermute | solution.py:536
  53.7 4.5 %collective-permute-start.8 = (bf16[144,128]{1,0:T(8,128)(2,1)S(1)}, bf16[144,128]{1,0:T(8,128)(2,1)S(1)}, u32[]{:S(2)}, u32[]{:S(2)}) collective-permute-start(bf16[144,128]{1,0:T(8,128)(2,1)S(1)} %get-tuple-element.65), channel_id=1, source_target_pairs={{0,64},{1,65},{2,66},{3,67},{4,68},{5,69},{6,70},{7,71},{8,72},{9,... | collective-permute-start | bytes 110600 | tf_op jit(solution)/shard_map/ppermute | solution.py:536
  56.3 4.0 %collective-permute-start.9 = (bf16[144,128]{1,0:T(8,128)(2,1)S(1)}, bf16[144,128]{1,0:T(8,128)(2,1)S(1)}, u32[]{:S(2)}, u32[]{:S(2)}) collective-permute-start(bf16[144,128]{1,0:T(8,128)(2,1)S(1)} %get-tuple-element.66), channel_id=1, source_target_pairs={{0,4},{1,5},{2,6},{3,7},{4,0},{5,1},{6,2},{7,3},{8,12},{9,13},{10,... | collective-permute-start | bytes 110600 | tf_op jit(solution)/shard_map/ppermute | solution.py:536
  56.3 4.9 %collective-permute-start.10 = (bf16[144,128]{1,0:T(8,128)(2,1)S(1)}, bf16[144,128]{1,0:T(8,128)(2,1)S(1)}, u32[]{:S(2)}, u32[]{:S(2)}) collective-permute-start(bf16[144,128]{1,0:T(8,128)(2,1)S(1)} %get-tuple-element.67), channel_id=1, source_target_pairs={{0,68},{1,69},{2,70},{3,71},{4,64},{5,65},{6,66},{7,67},{8,76},{9,... | collective-permute-start | bytes 110600 | tf_op jit(solution)/shard_map/ppermute | solution.py:536
  61.2 6.0 %collective-permute-start.11 = (bf16[96,128]{1,0:T(8,128)(2,1)S(1)}, bf16[96,128]{1,0:T(8,128)(2,1)S(1)}, u32[]{:S(2)}, u32[]{:S(2)}) collective-permute-start(bf16[96,128]{1,0:T(8,128)(2,1)S(1)} %get-tuple-element.69), channel_id=1, source_target_pairs={{0,48},{1,49},{2,50},{3,51},{4,52},{5,53},{6,54},{7,55},{8,56},{9,... | collective-permute-start | bytes 73736 | tf_op jit(solution)/shard_map/ppermute | solution.py:536
  67.3 4.8 %collective-permute-start.12 = (bf16[48,128]{1,0:T(8,128)(2,1)S(1)}, bf16[48,128]{1,0:T(8,128)(2,1)S(1)}, u32[]{:S(2)}, u32[]{:S(2)}) collective-permute-start(bf16[48,128]{1,0:T(8,128)(2,1)S(1)} %get-tuple-element.71), channel_id=1, source_target_pairs={{0,16},{1,17},{2,18},{3,19},{4,20},{5,21},{6,22},{7,23},{8,24},{9,... | collective-permute-start | bytes 36872 | tf_op jit(solution)/shard_map/ppermute | solution.py:536
  72.1 3.7 %collective-permute-start.13 = (f32[24,128]{1,0:T(8,128)S(1)}, f32[24,128]{1,0:T(8,128)S(1)}, u32[]{:S(2)}, u32[]{:S(2)}) collective-permute-start(f32[24,128]{1,0:T(8,128)S(1)} %get-tuple-element.73), channel_id=1, source_target_pairs={{0,2},{1,3},{2,0},{3,1},{4,6},{5,7},{6,4},{7,5},{8,10},{9,11},{10,... | collective-permute-start | bytes 36872 | tf_op jit(solution)/shard_map/ppermute | solution.py:536

commit v7 on v5

--- a/solution.py
+++ b/solution.py
@@ -214,7 +214,7 @@
             side_cot[2 * side + k] = flip_pad(ref[(4 + k) * CH : (5 + k) * CH, :]).astype(BF16)
 
 
-def spread(taps, plane, value, rows):
+def spread(taps, plane, value, rows, first=0):
     count = rows + 32
     level = lax.broadcasted_iota(jnp.int32, (count, LN), 0) & 15
     below = jnp.where(level == 0, 0.0, pltpu.roll(value, 1, 0))
@@ -222,7 +222,7 @@
     spare = lanes(count) >= CH
     short = [moved.astype(BF16) for moved in (below, value, above)]
     rest = [
-        jnp.where(spare, pltpu.roll(value, CH - 32 * q, 1), 0.0).astype(BF16) for q in range(3)
+        jnp.where(spare, pltpu.roll(short[1], CH - 32 * q, 1), jnp.bfloat16(0)) for q in range(3)
     ]
     for n, k in enumerate(WHOLE):
         start = 16 * (k // 3)
@@ -230,7 +230,7 @@
         if n < 6:
             start = 16 * (SPLIT[n] // 3)
             block = block + rest[n % 3][start : start + rows]
-        taps[plane // 2, plane % 2, 0:rows, n * LN : (n + 1) * LN] = block
+        taps[plane // 2, plane % 2, first : first + rows, n * LN : (n + 1) * LN] = block
 
 
 def convolve(taps, weight, total, pair, rows):
@@ -275,6 +275,29 @@
 
 def band(p, low, high):
     return int(p >= low) + int(p >= high)
+
+
+def silu_parts(value):
+    sigma = jax.nn.sigmoid(value)
+    return (value * sigma).astype(BF16), sigma * (1.0 + value * (1.0 - sigma))
+
+
+def inner_kernel(own_grid, side_grid, middle, fwd_one, hidden, slope, taps, total):
+    for p in range(16):
+        value = own_grid[p - 4] if 4 <= p < 12 else side_grid[p % 8]
+        spread(taps, p, value.astype(F32), 96)
+    left = jnp.concatenate(
+        [taps[j // 2 : j // 2 + 7, j % 2, :, :].reshape(672, TAPS) for j in range(4)], axis=1
+    )
+    right = jnp.concatenate(
+        [jnp.concatenate([fwd_one[j + 1], fwd_one[j]], axis=1) for j in range(4)], axis=0
+    )
+    total[...] = jnp.dot(left, right, preferred_element_type=F32)
+    for p in range(14):
+        parts = silu_parts(half_of(total, p, 96) * middle[band(p, 3, 11), 16:112, :])
+        hidden[p] = parts[0]
+        if 2 <= p < 12:
+            slope[p - 2] = parts[1]
 
 
 def level_kernel(
@@ -290,6 +313,8 @@
     fwd_two,
     back_two,
     turned_one,
+    inner_hidden,
+    inner_slope,
     activated,
     grad_one,
     masks,
@@ -342,14 +367,20 @@
         value = own_grid[p - 4] if bx == 1 else side_grid[p % 8]
         low = edge[p, 0:64, :] * masks[bx, 0:64, :]
         high = edge[p, 64:128, :] * masks[bx, 192:256, :]
-        spread(taps_one, p, jnp.concatenate([low, value.astype(F32), high], axis=0), 224)
+        value = value.astype(F32)
+        spread(taps_one, p, jnp.concatenate([low, value[0:32]], axis=0), 64)
+        spread(taps_one, p, jnp.concatenate([value[96:128], high], axis=0), 64, 64)
 
     def after_one(p):
-        value = half_of(total_one, p, 224) * masks[band(p, 3, 11), 16:240, :]
-        sigma = jax.nn.sigmoid(value)
+        bx = band(p, 3, 11)
+        mask = jnp.concatenate([masks[bx, 16:80, :], masks[bx, 176:240, :]], axis=0)
+        hidden, slope = silu_parts(half_of(total_one, p, 128) * mask)
         if 2 <= p < 12:
-            slope_one[p - 2] = (sigma * (1.0 + value * (1.0 - sigma)))[32:192]
-        hidden = (value * sigma).astype(BF16).astype(F32)
+            slope_one[p - 2, 0:32, :] = slope[32:64]
+            slope_one[p - 2, 32:128, :] = inner_slope[p - 2]
+            slope_one[p - 2, 128:160, :] = slope[64:96]
+        hidden = jnp.concatenate([hidden[0:64], inner_hidden[p], hidden[64:128]], axis=0)
+        hidden = hidden.astype(F32)
         spread(taps_two, p, hidden, 192)
         if 3 <= p < 11:
             turn_levels(hidden[48:176].T[0:CH], p - 3, turned_two)
@@ -373,7 +404,7 @@
         begin(p)
     for t in range(12):
         if t < 7:
-            convolve(taps_one, fwd_one, total_one, t, 224)
+            convolve(taps_one, fwd_one, total_one, t, 128)
         if t < 6:
             begin(2 * t + 4)
             begin(2 * t + 5)
@@ -574,6 +605,19 @@
         east,
     )
 
+    inner_hidden, inner_slope = call(
+        inner_kernel,
+        "inner",
+        [shape(14, 96, LN), shape(10, 96, LN, dtype=F32)],
+        [pltpu.VMEM((8, 2, 96, TAPS), BF16), pltpu.VMEM((672, 2 * LN), F32)],
+        16,
+        1 << 32,
+        [VMEM] * 4,
+        own_grid,
+        side_grid,
+        middle,
+        fwd_one,
+    )
     activated, grad_one, masks, keep, send = call(
         lambda *refs: level_kernel(scale, *refs),
         "level",
@@ -585,10 +629,10 @@
             shape(4, 576, LN),
         ],
         [
-            pltpu.VMEM((8, 2, 224, TAPS), BF16),
+            pltpu.VMEM((8, 2, 128, TAPS), BF16),
             pltpu.VMEM((7, 2, 192, TAPS), BF16),
             pltpu.VMEM((6, 2, 160, TAPS), BF16),
-            pltpu.VMEM((7 * 224, 2 * LN), F32),
+            pltpu.VMEM((7 * 128, 2 * LN), F32),
             pltpu.VMEM((6 * 192, 2 * LN), F32),
             pltpu.VMEM((5 * 160, 2 * LN), F32),
             pltpu.VMEM((16, 128, LN), F32),
@@ -603,7 +647,7 @@
         ],
         40,
         1 << 34,
-        [VMEM] * 11,
+        [VMEM] * 13,
         own_grid,
         side_grid,
         own_cot,
@@ -615,6 +659,8 @@
         fwd_two,
         back_two,
         turned_one,
+        inner_hidden,
+        inner_slope,
     )
 
     part = (keep.astype(F32) + swap(send, 1).astype(F32)).astype(BF16)

time: 77.5 us -> 76.2 us (0.983)
  waiting for transfers between devices: 24 us -> 22.4 us
    ppermute x1, waiting for transfers between devices: 6.7 us -> 5.01 us  [local(): south = lax.ppermute(to_north, 'north', shift_by(1, 'north'))]
    pallas_call x11 -> x12, Pallas kernels: 18.6 us -> 19 us  [call(): pl.pallas_call(kernel, out_shape=outs, in_specs=specs, out_specs=[VMEM] *...]
  transfers between devices with their start and end apart: 14 -> 14, of which waited for: 12 -> 12; matrix products, arithmetic and copies ran while one was open for 0% -> 0% of each run, Pallas kernels for 5% -> 8%
where the time goes in v7:
time: 76.2 us; the launch traced here: 74.8 us
  starting transfers between devices  27.8 us (36%)
  waiting for transfers between devices  22.4 us (29%)
  Pallas kernels  19 us (25%)
  local copies, waits for them, and re-layouts  4.73 us (6%)
    pallas_call x12, Pallas kernels, call(): pl.pallas_call(kernel, out_shape=outs, in_specs=specs, out_specs=[VMEM] *...  19 us
    ppermute x10, starting transfers between devices, swap(): return lax.ppermute(value, BOTH, [(i, i ^ bits) for i in range(count)])  17.4 us
    ppermute x10, waiting for transfers between devices, swap(): return lax.ppermute(value, BOTH, [(i, i ^ bits) for i in range(count)])  15.4 us
    ppermute x1, waiting for transfers between devices, local(): south = lax.ppermute(to_north, 'north', shift_by(1, 'north'))  5.01 us
    unnamed x10, local copies, waits for them, and re-layouts  4.69 us
    ppermute x1, starting transfers between devices, local(): north = lax.ppermute(to_south, 'north', shift_by(-1, 'north'))  3.84 us
    ppermute x1, starting transfers between devices, local(): west = lax.ppermute(to_east, 'east', shift_by(1, 'east'))  3.35 us
    ppermute x1, starting transfers between devices, local(): east = lax.ppermute(to_west, 'east', shift_by(-1, 'east'))  3.09 us
  transfers between devices with their start and end apart: 14, of which 12 were waited for; matrix products, arithmetic and copies ran while one was open for 0% of the time, Pallas kernels for 8%

profile of v7, /device:TPU:2, one launch (start us, length us, event | category | flops | bytes accessed | tf_op | source)
XLA Modules:
  0.0 74.8 jit_solution(5959471726399649727)
XLA Ops:
  0.6 1.9 %strips.1 = (bf16[592,128]{1,0:T(8,128)(2,1)}, bf16[592,128]{1,0:T(8,128)(2,1)}) custom-call(s32[1,2]{1,0:T(1,128)} %bitcast.13, bf16[96,8,128]{2,1,0:T(8,128)(2,1)} %features.3, bf16[96,8,128]{2,1,0:T(8,128)(2,1)} %cotangent.3), custom_call_target="tpu_custom_call" | custom-call | flops 1048576 | bytes 1048576 | tf_op jit(solution)/shard_map/strips/pallas_call | solution.py:514
  2.5 3.3 %collective-permute-start = (bf16[592,128]{1,0:T(8,128)(2,1)}, bf16[592,128]{1,0:T(8,128)(2,1)S(1)}, u32[]{:S(2)}, u32[]{:S(2)}) collective-permute-start(bf16[592,128]{1,0:T(8,128)(2,1)} %get-tuple-element.44), channel_id=1, source_target_pairs={{0,16},{16,32},{32,48},{48,64},{64,80},{80,96},{96,112},{112,128},... | collective-permute-start | bytes 454664 | tf_op jit(solution)/shard_map/ppermute | solution.py:558
  5.9 3.1 %collective-permute-start.1 = (bf16[592,128]{1,0:T(8,128)(2,1)}, bf16[592,128]{1,0:T(8,128)(2,1)S(1)}, u32[]{:S(2)}, u32[]{:S(2)}) collective-permute-start(bf16[592,128]{1,0:T(8,128)(2,1)} %get-tuple-element.45), channel_id=1, source_target_pairs={{0,240},{16,0},{32,16},{48,32},{64,48},{80,64},{96,80},{112,96},{1... | collective-permute-start | bytes 454664 | tf_op jit(solution)/shard_map/ppermute | solution.py:559
  9.0 0.9 %copy-done = bf16[96,8,128]{2,1,0:T(8,128)(2,1)S(1)} copy-done((bf16[96,8,128]{2,1,0:T(8,128)(2,1)S(1)}, bf16[96,8,128]{2,1,0:T(8,128)(2,1)}, u32[]{:S(2)}) %copy-start) | copy-done | bytes 196632
  9.9 0.9 %copy-done.1 = bf16[96,8,128]{2,1,0:T(8,128)(2,1)S(1)} copy-done((bf16[96,8,128]{2,1,0:T(8,128)(2,1)S(1)}, bf16[96,8,128]{2,1,0:T(8,128)(2,1)}, u32[]{:S(2)}) %copy-start.1) | copy-done | bytes 196632
  10.8 0.7 copy-done.2
  11.5 1.1 %copy-done.3 = bf16[27,96,96]{2,1,0:T(8,128)(2,1)S(1)} copy-done((bf16[27,96,96]{2,1,0:T(8,128)(2,1)S(1)}, bf16[27,96,96]{2,1,0:T(8,128)(2,1)}, u32[]{:S(2)}) %copy-start.3) | copy-done | bytes 497688
  12.6 1.1 %copy-done.4 = bf16[27,96,96]{2,1,0:T(8,128)(2,1)S(1)} copy-done((bf16[27,96,96]{2,1,0:T(8,128)(2,1)S(1)}, bf16[27,96,96]{2,1,0:T(8,128)(2,1)}, u32[]{:S(2)}) %copy-start.4) | copy-done | bytes 497688
  13.7 1.8 %prepare.1 = (bf16[5,896,128]{2,1,0:T(8,128)(2,1)S(1)}, bf16[5,896,128]{2,1,0:T(8,128)(2,1)S(1)}, bf16[5,896,128]{2,1,0:T(8,128)(2,1)S(1)}, bf16[5,896,128]{2,1,...) custom-call(bf16[27,96,96]{2,1,0:T(8,128)(2,1)S(1)} %copy-done.3, ...), custom_call_target="tpu_custom_call" | custom-call | flops 8589934592 | bytes 1048576 | tf_op jit(solution)/shard_map/prepare/pallas_call | solution.py:514
  15.5 2.0 %collective-permute-done.1.east = bf16[592,128]{1,0:T(8,128)(2,1)S(1)} collective-permute-done((bf16[592,128]{1,0:T(8,128)(2,1)}, bf16[592,128]{1,0:T(8,128)(2,1)S(1)}, u32[]{:S(2)}, u32[]{:S(2)}) %collective-permute-start.1) | collective-permute-done | bytes 151584 | tf_op jit(solution)/shard_map/ppermute | solution.py:559
  17.9 3.8 %collective-permute-start.3 = (bf16[1104,128]{1,0:T(8,128)(2,1)S(1)}, bf16[1104,128]{1,0:T(8,128)(2,1)S(1)}, u32[]{:S(2)}, u32[]{:S(2)}) collective-permute-start(bf16[1104,128]{1,0:T(8,128)(2,1)S(1)} %get-tuple-element.53), channel_id=1, source_target_pairs={{0,15},{1,0},{2,1},{3,2},{4,3},{5,4},{6,5},{7,6},{8,7},{9,8},{10,9... | collective-permute-start | bytes 847880 | tf_op jit(solution)/shard_map/ppermute | solution.py:594
  21.9 1.7 %inner.1 = (bf16[14,96,128]{2,1,0:T(8,128)(2,1)S(1)}, f32[10,96,128]{2,1,0:T(8,128)S(1)}) custom-call(bf16[8,128,128]{2,1,0:T(8,128)(2,1)S(1)} %get-tuple-element.42.own_grid.refs_0_, bf16[8,128,128]{2,1,0:T(8,128)(2,1)S(1)} %get-tuple-element.46.side_grid.refs_1_, f32[3,128,128]{2,1,0:T(8,128)S(1)} %get-tuple-element.49.middle.refs_4_, ...), custom_call_target="tpu_custom_call" | custom-call | flops 4294967296 | bytes 1048576 | tf_op jit(solution)/shard_map/inner/pallas_call | solution.py:514
  23.6 5.0 %collective-permute-done.2.refs_5_ = bf16[1104,128]{1,0:T(8,128)(2,1)S(1)} collective-permute-done((bf16[1104,128]{1,0:T(8,128)(2,1)S(1)}, bf16[1104,128]{1,0:T(8,128)(2,1)S(1)}, u32[]{:S(2)}, u32[]{:S(2)}) %collective-permute-start.2) | collective-permute-done | bytes 282656 | tf_op jit(solution)/shard_map/ppermute | solution.py:593
  28.6 10.1 %level.1 = (bf16[96,8,128]{2,1,0:T(8,128)(2,1)}, bf16[10,160,128]{2,1,0:T(8,128)(2,1)S(1)}, f32[3,256,128]{2,1,0:T(8,128)S(1)}, bf16[4,576,128]{2,1,0:T(8,128)(2,1)S(1)}, bf16[4,576,128]{2,1,0:T(8,128)(2,1)S(1)}) custom-call(bf16[8,128,128]{2,1,0:T(8,128)(2,1)S(1)} %get-tuple-element.42.own_grid.refs_0_, ...), custom_call_target="tpu_custom_call" | custom-call | flops 17179869184 | bytes 1048576 | tf_op jit(solution)/shard_map/level/pallas_call | solution.py:514
  38.8 2.0 %collective-permute-done.4 = bf16[4,576,128]{2,1,0:T(8,128)(2,1)S(1)} collective-permute-done((bf16[4,576,128]{2,1,0:T(8,128)(2,1)S(1)}, bf16[4,576,128]{2,1,0:T(8,128)(2,1)S(1)}, u32[]{:S(2)}, u32[]{:S(2)}) %collective-permute-start.4) | collective-permute-done | bytes 589856 | tf_op jit(solution)/shard_map/ppermute | solution.py:537
  41.0 2.6 %collective-permute-start.7 = (bf16[576,128]{1,0:T(8,128)(2,1)S(1)}, bf16[576,128]{1,0:T(8,128)(2,1)S(1)}, u32[]{:S(2)}, u32[]{:S(2)}) collective-permute-start(bf16[576,128]{1,0:T(8,128)(2,1)S(1)} %get-tuple-element.80), channel_id=1, source_target_pairs={{0,204},{1,205},{2,206},{3,207},{4,200},{5,201},{6,202},{7,203},{8... | collective-permute-start | bytes 442376 | tf_op jit(solution)/shard_map/ppermute | solution.py:537
  44.1 1.6 %collective-permute-start.5 = (bf16[576,128]{1,0:T(8,128)(2,1)S(1)}, bf16[576,128]{1,0:T(8,128)(2,1)S(1)}, u32[]{:S(2)}, u32[]{:S(2)}) collective-permute-start(bf16[576,128]{1,0:T(8,128)(2,1)S(1)} %get-tuple-element.82), channel_id=1, source_target_pairs={{0,12},{1,13},{2,14},{3,15},{4,8},{5,9},{6,10},{7,11},{8,4},{9,5},... | collective-permute-start | bytes 442376 | tf_op jit(solution)/shard_map/ppermute | solution.py:537
  45.8 2.1 %final.1 = (bf16[96,8,128]{2,1,0:T(8,128)(2,1)}, f32[8,128]{1,0:T(8,128)S(1)}) custom-call(bf16[10,160,128]{2,1,0:T(8,128)(2,1)S(1)} %get-tuple-element.61.grad_one, f32[3,256,128]{2,1,0:T(8,128)S(1)} %get-tuple-element.62.masks, bf16[5,896,128]{2,1,0:T(8,128)(2,1)S(1)} %get-tuple-element.63.back_one), custom_call_target="tpu_custom_call" | custom-call | flops 4294967296 | bytes 1048576 | tf_op jit(solution)/shard_map/final/pallas_call | solution.py:514
  47.8 2.0 %collective-permute-done.7.a3 = bf16[576,128]{1,0:T(8,128)(2,1)S(1)} collective-permute-done((bf16[576,128]{1,0:T(8,128)(2,1)S(1)}, bf16[576,128]{1,0:T(8,128)(2,1)S(1)}, u32[]{:S(2)}, u32[]{:S(2)}) %collective-permute-start.7) | collective-permute-done | bytes 147488 | tf_op jit(solution)/shard_map/ppermute | solution.py:537
  49.9 1.3 %collective-permute-done.6.a2 = bf16[576,128]{1,0:T(8,128)(2,1)S(1)} collective-permute-done((bf16[576,128]{1,0:T(8,128)(2,1)S(1)}, bf16[576,128]{1,0:T(8,128)(2,1)S(1)}, u32[]{:S(2)}, u32[]{:S(2)}) %collective-permute-start.6) | collective-permute-done | bytes 147488 | tf_op jit(solution)/shard_map/ppermute | solution.py:537
  51.1 1.1 %collective-permute-done.5.a1 = bf16[576,128]{1,0:T(8,128)(2,1)S(1)} collective-permute-done((bf16[576,128]{1,0:T(8,128)(2,1)S(1)}, bf16[576,128]{1,0:T(8,128)(2,1)S(1)}, u32[]{:S(2)}, u32[]{:S(2)}) %collective-permute-start.5) | collective-permute-done | bytes 147488 | tf_op jit(solution)/shard_map/ppermute | solution.py:537
  52.3 1.1 %collective-permute-start.8 = (bf16[144,128]{1,0:T(8,128)(2,1)S(1)}, bf16[144,128]{1,0:T(8,128)(2,1)S(1)}, u32[]{:S(2)}, u32[]{:S(2)}) collective-permute-start(bf16[144,128]{1,0:T(8,128)(2,1)S(1)} %get-tuple-element.69), channel_id=1, source_target_pairs={{0,64},{1,65},{2,66},{3,67},{4,68},{5,69},{6,70},{7,71},{8,72},{9,... | collective-permute-start | bytes 110600 | tf_op jit(solution)/shard_map/ppermute | solution.py:537
  53.7 2.2 %collective-permute-start.10 = (bf16[144,128]{1,0:T(8,128)(2,1)S(1)}, bf16[144,128]{1,0:T(8,128)(2,1)S(1)}, u32[]{:S(2)}, u32[]{:S(2)}) collective-permute-start(bf16[144,128]{1,0:T(8,128)(2,1)S(1)} %get-tuple-element.71), channel_id=1, source_target_pairs={{0,68},{1,69},{2,70},{3,71},{4,64},{5,65},{6,66},{7,67},{8,76},{9,... | collective-permute-start | bytes 110600 | tf_op jit(solution)/shard_map/ppermute | solution.py:537
  56.3 1.1 %collective-permute-done.9.a2 = bf16[144,128]{1,0:T(8,128)(2,1)S(1)} collective-permute-done((bf16[144,128]{1,0:T(8,128)(2,1)S(1)}, bf16[144,128]{1,0:T(8,128)(2,1)S(1)}, u32[]{:S(2)}, u32[]{:S(2)}) %collective-permute-start.9) | collective-permute-done | bytes 36896 | tf_op jit(solution)/shard_map/ppermute | solution.py:537
  57.4 1.1 %collective-permute-done.10.a3 = bf16[144,128]{1,0:T(8,128)(2,1)S(1)} collective-permute-done((bf16[144,128]{1,0:T(8,128)(2,1)S(1)}, bf16[144,128]{1,0:T(8,128)(2,1)S(1)}, u32[]{:S(2)}, u32[]{:S(2)}) %collective-permute-start.10) | collective-permute-done | bytes 36896 | tf_op jit(solution)/shard_map/ppermute | solution.py:537
  58.7 4.3 %collective-permute-start.11 = (bf16[96,128]{1,0:T(8,128)(2,1)S(1)}, bf16[96,128]{1,0:T(8,128)(2,1)S(1)}, u32[]{:S(2)}, u32[]{:S(2)}) collective-permute-start(bf16[96,128]{1,0:T(8,128)(2,1)S(1)} %get-tuple-element.73), channel_id=1, source_target_pairs={{0,48},{1,49},{2,50},{3,51},{4,52},{5,53},{6,54},{7,55},{8,56},{9,... | collective-permute-start | bytes 73736 | tf_op jit(solution)/shard_map/ppermute | solution.py:537
  63.0 1.8 %collective-permute-done.11.got = bf16[96,128]{1,0:T(8,128)(2,1)S(1)} collective-permute-done((bf16[96,128]{1,0:T(8,128)(2,1)S(1)}, bf16[96,128]{1,0:T(8,128)(2,1)S(1)}, u32[]{:S(2)}, u32[]{:S(2)}) %collective-permute-start.11) | collective-permute-done | bytes 24608 | tf_op jit(solution)/shard_map/ppermute | solution.py:537
  64.8 3.8 %collective-permute-start.12 = (bf16[48,128]{1,0:T(8,128)(2,1)S(1)}, bf16[48,128]{1,0:T(8,128)(2,1)S(1)}, u32[]{:S(2)}, u32[]{:S(2)}) collective-permute-start(bf16[48,128]{1,0:T(8,128)(2,1)S(1)} %get-tuple-element.75), channel_id=1, source_target_pairs={{0,16},{1,17},{2,18},{3,19},{4,20},{5,21},{6,22},{7,23},{8,24},{9,... | collective-permute-start | bytes 36872 | tf_op jit(solution)/shard_map/ppermute | solution.py:537
  68.6 1.7 %collective-permute-done.12.got = bf16[48,128]{1,0:T(8,128)(2,1)S(1)} collective-permute-done((bf16[48,128]{1,0:T(8,128)(2,1)S(1)}, bf16[48,128]{1,0:T(8,128)(2,1)S(1)}, u32[]{:S(2)}, u32[]{:S(2)}) %collective-permute-start.12) | collective-permute-done | bytes 12320 | tf_op jit(solution)/shard_map/ppermute | solution.py:537
  70.3 0.9 %collective-permute-start.13 = (f32[24,128]{1,0:T(8,128)S(1)}, f32[24,128]{1,0:T(8,128)S(1)}, u32[]{:S(2)}, u32[]{:S(2)}) collective-permute-start(f32[24,128]{1,0:T(8,128)S(1)} %get-tuple-element.77), channel_id=1, source_target_pairs={{0,2},{1,3},{2,0},{3,1},{4,6},{5,7},{6,4},{7,5},{8,10},{9,11},{10,... | collective-permute-start | bytes 36872 | tf_op jit(solution)/shard_map/ppermute | solution.py:537
  71.2 2.8 %collective-permute-done.13.got = f32[24,128]{1,0:T(8,128)S(1)} collective-permute-done((f32[24,128]{1,0:T(8,128)S(1)}, f32[24,128]{1,0:T(8,128)S(1)}, u32[]{:S(2)}, u32[]{:S(2)}) %collective-permute-start.13) | collective-permute-done | bytes 12320 | tf_op jit(solution)/shard_map/ppermute | solution.py:537
  74.0 0.8 %finish.1 = (f32[8,128]{1,0:T(8,128)}, f32[8,128]{1,0:T(8,128)}) custom-call(f32[24,128]{1,0:T(8,128)S(1)} %get-tuple-element.76.held, f32[24,128]{1,0:T(8,128)S(1)} %collective-permute-done.13.got), custom_call_target="tpu_custom_call" | custom-call | flops 1048576 | bytes 1048576 | tf_op jit(solution)/shard_map/finish/pallas_call | solution.py:514
  (20 shorter events, 2.4 us)
Async XLA Ops:
  2.5 13.0 %collective-permute-start = (bf16[592,128]{1,0:T(8,128)(2,1)}, bf16[592,128]{1,0:T(8,128)(2,1)S(1)}, u32[]{:S(2)}, u32[]{:S(2)}) collective-permute-start(bf16[592,128]{1,0:T(8,128)(2,1)} %get-tuple-element.44), channel_id=1, source_target_pairs={{0,16},{16,32},{32,48},{48,64},{64,80},{80,96},{96,112},{112,128},... | collective-permute-start | bytes 454664 | tf_op jit(solution)/shard_map/ppermute | solution.py:558
  5.9 11.6 %collective-permute-start.1 = (bf16[592,128]{1,0:T(8,128)(2,1)}, bf16[592,128]{1,0:T(8,128)(2,1)S(1)}, u32[]{:S(2)}, u32[]{:S(2)}) collective-permute-start(bf16[592,128]{1,0:T(8,128)(2,1)} %get-tuple-element.45), channel_id=1, source_target_pairs={{0,240},{16,0},{32,16},{48,32},{64,48},{80,64},{96,80},{112,96},{1... | collective-permute-start | bytes 454664 | tf_op jit(solution)/shard_map/ppermute | solution.py:559
  9.0 0.9 %copy-start = (bf16[96,8,128]{2,1,0:T(8,128)(2,1)S(1)}, bf16[96,8,128]{2,1,0:T(8,128)(2,1)}, u32[]{:S(2)}) copy-start(bf16[96,8,128]{2,1,0:T(8,128)(2,1)} %features.3) | copy-start | bytes 589828
  9.9 0.9 %copy-start.1 = (bf16[96,8,128]{2,1,0:T(8,128)(2,1)S(1)}, bf16[96,8,128]{2,1,0:T(8,128)(2,1)}, u32[]{:S(2)}) copy-start(bf16[96,8,128]{2,1,0:T(8,128)(2,1)} %cotangent.3) | copy-start | bytes 589828
  10.8 0.7 copy-start.2
  11.5 1.1 %copy-start.3 = (bf16[27,96,96]{2,1,0:T(8,128)(2,1)S(1)}, bf16[27,96,96]{2,1,0:T(8,128)(2,1)}, u32[]{:S(2)}) copy-start(bf16[27,96,96]{2,1,0:T(8,128)(2,1)} %first.1) | copy-start | bytes 1492996
  12.6 1.1 %copy-start.4 = (bf16[27,96,96]{2,1,0:T(8,128)(2,1)S(1)}, bf16[27,96,96]{2,1,0:T(8,128)(2,1)}, u32[]{:S(2)}) copy-start(bf16[27,96,96]{2,1,0:T(8,128)(2,1)} %second.1) | copy-start | bytes 1492996
  17.8 10.8 %collective-permute-start.2 = (bf16[1104,128]{1,0:T(8,128)(2,1)S(1)}, bf16[1104,128]{1,0:T(8,128)(2,1)S(1)}, u32[]{:S(2)}, u32[]{:S(2)}) collective-permute-start(bf16[1104,128]{1,0:T(8,128)(2,1)S(1)} %get-tuple-element.52), channel_id=1, source_target_pairs={{0,1},{1,2},{2,3},{3,4},{4,5},{5,6},{6,7},{7,8},{8,9},{9,10},{10,1... | collective-permute-start | bytes 847880 | tf_op jit(solution)/shard_map/ppermute | solution.py:593
  17.9 10.8 %collective-permute-start.3 = (bf16[1104,128]{1,0:T(8,128)(2,1)S(1)}, bf16[1104,128]{1,0:T(8,128)(2,1)S(1)}, u32[]{:S(2)}, u32[]{:S(2)}) collective-permute-start(bf16[1104,128]{1,0:T(8,128)(2,1)S(1)} %get-tuple-element.53), channel_id=1, source_target_pairs={{0,15},{1,0},{2,1},{3,2},{4,3},{5,4},{6,5},{7,6},{8,7},{9,8},{10,9... | collective-permute-start | bytes 847880 | tf_op jit(solution)/shard_map/ppermute | solution.py:594
  38.7 2.0 %collective-permute-start.4 = (bf16[4,576,128]{2,1,0:T(8,128)(2,1)S(1)}, bf16[4,576,128]{2,1,0:T(8,128)(2,1)S(1)}, u32[]{:S(2)}, u32[]{:S(2)}) collective-permute-start(bf16[4,576,128]{2,1,0:T(8,128)(2,1)S(1)} %get-tuple-element.66), channel_id=1, source_target_pairs={{0,1},{1,0},{2,3},{3,2},{4,5},{5,4},{6,7},{7,6},{8,9},{9,8},{10,11... | collective-permute-start | bytes 1769480 | tf_op jit(solution)/shard_map/ppermute | solution.py:537
  41.0 8.9 %collective-permute-start.7 = (bf16[576,128]{1,0:T(8,128)(2,1)S(1)}, bf16[576,128]{1,0:T(8,128)(2,1)S(1)}, u32[]{:S(2)}, u32[]{:S(2)}) collective-permute-start(bf16[576,128]{1,0:T(8,128)(2,1)S(1)} %get-tuple-element.80), channel_id=1, source_target_pairs={{0,204},{1,205},{2,206},{3,207},{4,200},{5,201},{6,202},{7,203},{8... | collective-permute-start | bytes 442376 | tf_op jit(solution)/shard_map/ppermute | solution.py:537
  43.6 7.6 %collective-permute-start.6 = (bf16[576,128]{1,0:T(8,128)(2,1)S(1)}, bf16[576,128]{1,0:T(8,128)(2,1)S(1)}, u32[]{:S(2)}, u32[]{:S(2)}) collective-permute-start(bf16[576,128]{1,0:T(8,128)(2,1)S(1)} %get-tuple-element.81), channel_id=1, source_target_pairs={{0,192},{1,193},{2,194},{3,195},{4,196},{5,197},{6,198},{7,199},{8... | collective-permute-start | bytes 442376 | tf_op jit(solution)/shard_map/ppermute | solution.py:537
  44.1 8.1 %collective-permute-start.5 = (bf16[576,128]{1,0:T(8,128)(2,1)S(1)}, bf16[576,128]{1,0:T(8,128)(2,1)S(1)}, u32[]{:S(2)}, u32[]{:S(2)}) collective-permute-start(bf16[576,128]{1,0:T(8,128)(2,1)S(1)} %get-tuple-element.82), channel_id=1, source_target_pairs={{0,12},{1,13},{2,14},{3,15},{4,8},{5,9},{6,10},{7,11},{8,4},{9,5},... | collective-permute-start | bytes 442376 | tf_op jit(solution)/shard_map/ppermute | solution.py:537
  52.3 4.0 %collective-permute-start.8 = (bf16[144,128]{1,0:T(8,128)(2,1)S(1)}, bf16[144,128]{1,0:T(8,128)(2,1)S(1)}, u32[]{:S(2)}, u32[]{:S(2)}) collective-permute-start(bf16[144,128]{1,0:T(8,128)(2,1)S(1)} %get-tuple-element.69), channel_id=1, source_target_pairs={{0,64},{1,65},{2,66},{3,67},{4,68},{5,69},{6,70},{7,71},{8,72},{9,... | collective-permute-start | bytes 110600 | tf_op jit(solution)/shard_map/ppermute | solution.py:537
  53.3 4.1 %collective-permute-start.9 = (bf16[144,128]{1,0:T(8,128)(2,1)S(1)}, bf16[144,128]{1,0:T(8,128)(2,1)S(1)}, u32[]{:S(2)}, u32[]{:S(2)}) collective-permute-start(bf16[144,128]{1,0:T(8,128)(2,1)S(1)} %get-tuple-element.70), channel_id=1, source_target_pairs={{0,4},{1,5},{2,6},{3,7},{4,0},{5,1},{6,2},{7,3},{8,12},{9,13},{10,... | collective-permute-start | bytes 110600 | tf_op jit(solution)/shard_map/ppermute | solution.py:537
  53.7 4.9 %collective-permute-start.10 = (bf16[144,128]{1,0:T(8,128)(2,1)S(1)}, bf16[144,128]{1,0:T(8,128)(2,1)S(1)}, u32[]{:S(2)}, u32[]{:S(2)}) collective-permute-start(bf16[144,128]{1,0:T(8,128)(2,1)S(1)} %get-tuple-element.71), channel_id=1, source_target_pairs={{0,68},{1,69},{2,70},{3,71},{4,64},{5,65},{6,66},{7,67},{8,76},{9,... | collective-permute-start | bytes 110600 | tf_op jit(solution)/shard_map/ppermute | solution.py:537
  58.7 6.1 %collective-permute-start.11 = (bf16[96,128]{1,0:T(8,128)(2,1)S(1)}, bf16[96,128]{1,0:T(8,128)(2,1)S(1)}, u32[]{:S(2)}, u32[]{:S(2)}) collective-permute-start(bf16[96,128]{1,0:T(8,128)(2,1)S(1)} %get-tuple-element.73), channel_id=1, source_target_pairs={{0,48},{1,49},{2,50},{3,51},{4,52},{5,53},{6,54},{7,55},{8,56},{9,... | collective-permute-start | bytes 73736 | tf_op jit(solution)/shard_map/ppermute | solution.py:537
  64.8 5.5 %collective-permute-start.12 = (bf16[48,128]{1,0:T(8,128)(2,1)S(1)}, bf16[48,128]{1,0:T(8,128)(2,1)S(1)}, u32[]{:S(2)}, u32[]{:S(2)}) collective-permute-start(bf16[48,128]{1,0:T(8,128)(2,1)S(1)} %get-tuple-element.75), channel_id=1, source_target_pairs={{0,16},{1,17},{2,18},{3,19},{4,20},{5,21},{6,22},{7,23},{8,24},{9,... | collective-permute-start | bytes 36872 | tf_op jit(solution)/shard_map/ppermute | solution.py:537
  70.3 3.7 %collective-permute-start.13 = (f32[24,128]{1,0:T(8,128)S(1)}, f32[24,128]{1,0:T(8,128)S(1)}, u32[]{:S(2)}, u32[]{:S(2)}) collective-permute-start(f32[24,128]{1,0:T(8,128)S(1)} %get-tuple-element.77), channel_id=1, source_target_pairs={{0,2},{1,3},{2,0},{3,1},{4,6},{5,7},{6,4},{7,5},{8,10},{9,11},{10,... | collective-permute-start | bytes 36872 | tf_op jit(solution)/shard_map/ppermute | solution.py:537

commit v8 on v7

--- a/solution.py
+++ b/solution.py
@@ -102,19 +102,39 @@
         turned[c * CH : (c + 1) * CH, pl.ds(start, LN)] = moved.astype(BF16)
 
 
+def pack_weights(source, ahead, back):
+    for out in (ahead, back):
+        out[...] = jnp.zeros_like(out)
+
+    def body(plane, carry):
+        for k in range(9):
+            straight = source[9 * plane + k]
+            turned = jnp.pad(
+                source[26 - 9 * plane - k].astype(F32), ((0, LN - CH), (0, LN - CH))
+            ).T.astype(BF16)
+            if k in WHOLE:
+                row = WHOLE.index(k) * LN
+                ahead[plane + 1, row : row + CH, 0:CH] = straight
+                back[plane + 1, row : row + CH, :] = turned[0:CH]
+            else:
+                for q in range(3):
+                    row = (SPLIT.index(k) + q) * LN + CH
+                    ahead[plane + 1, row : row + 32, 0:CH] = straight[32 * q : 32 * q + 32]
+                    back[plane + 1, row : row + 32, :] = turned[32 * q : 32 * q + 32]
+        return carry
+
+    lax.fori_loop(0, 3, body, 0)
+
+
 def prepare_kernel(
-    first,
-    second,
+    weight,
     features,
     cotangent,
     occupied,
-    fwd_one,
-    fwd_two,
-    back_two,
-    back_one,
+    ahead,
+    back,
     turned_one,
     own_grid,
-    own_cot,
     feat,
     cot,
     own_mask,
@@ -124,28 +144,7 @@
     wide_feat[...] = features[...].astype(F32).reshape(CH * 8, LN)
     wide_cot[...] = cotangent[...].astype(F32).reshape(CH * 8, LN)
     own_mask[...] = mask_tile(occupied)
-    for out in (fwd_one, fwd_two, back_two, back_one):
-        out[...] = jnp.zeros_like(out)
-
-    def body(plane, carry):
-        for source, ahead, back in ((first, fwd_one, back_one), (second, fwd_two, back_two)):
-            for k in range(9):
-                straight = source[9 * plane + k]
-                turned = jnp.pad(
-                    source[26 - 9 * plane - k].astype(F32), ((0, LN - CH), (0, LN - CH))
-                ).T.astype(BF16)
-                if k in WHOLE:
-                    row = WHOLE.index(k) * LN
-                    ahead[plane + 1, row : row + CH, 0:CH] = straight
-                    back[plane + 1, row : row + CH, :] = turned[0:CH]
-                else:
-                    for q in range(3):
-                        row = (SPLIT.index(k) + q) * LN + CH
-                        ahead[plane + 1, row : row + 32, 0:CH] = straight[32 * q : 32 * q + 32]
-                        back[plane + 1, row : row + 32, :] = turned[32 * q : 32 * q + 32]
-        return carry
-
-    lax.fori_loop(0, 3, body, 0)
+    pack_weights(weight, ahead, back)
     mask = jnp.concatenate([own_mask[...].astype(F32)] * 6, axis=0)
     for x in range(8):
         plain = wide_feat[pl.ds(x, CH, stride=8), :]
@@ -153,9 +152,13 @@
         value = plain * mask
         turn_levels(value, x, turned_one)
         own_grid[x] = flip_pad(value).astype(BF16)
-        plain = wide_cot[pl.ds(x, CH, stride=8), :]
-        cot[x] = plain.astype(BF16)
-        own_cot[x] = flip_pad(plain).astype(BF16)
+        cot[x] = wide_cot[pl.ds(x, CH, stride=8), :].astype(BF16)
+
+
+def second_kernel(weight, cot, middle, ahead, back, own_cot):
+    pack_weights(weight, ahead, back)
+    for x in range(8):
+        own_cot[x] = flip_pad(cot[x]).astype(BF16)
 
 
 def rims_kernel(west, east, feat, cot, own_mask, to_south, to_north):
@@ -562,16 +565,15 @@
     tile = shape(8, LN, LN)
     image = shape(CH, 8, LN)
     planes = shape(8, CH, LN)
-    fwd_one, fwd_two, back_two, back_one, turned_one, own_grid, own_cot, feat, cot, own_mask = call(
+    fwd_one, back_one, turned_one, own_grid, feat, cot, own_mask = call(
         prepare_kernel,
         "prepare",
-        [weight] * 4 + [shape(288, 1024), tile, tile, planes, planes, shape(16, LN)],
+        [weight] * 2 + [shape(288, 1024), tile, planes, planes, shape(16, LN)],
         [wide, wide],
         12,
         1 << 33,
-        [VMEM] * 5,
+        [VMEM] * 4,
         weight_first,
-        weight_second,
         features,
         cotangent,
         occupied,
@@ -617,6 +619,18 @@
         side_grid,
         middle,
         fwd_one,
+    )
+    fwd_two, back_two, own_cot = call(
+        second_kernel,
+        "second",
+        [weight] * 2 + [tile],
+        [],
+        12,
+        1 << 31,
+        [VMEM] * 3,
+        weight_second,
+        cot,
+        middle,
     )
     activated, grad_one, masks, keep, send = call(
         lambda *refs: level_kernel(scale, *refs),

time: 76.2 us -> 76.4 us (level)
  local copies, waits for them, and re-layouts: 4.73 us -> 3.64 us
    ppermute x1, waiting for transfers between devices: 1.98 us -> 3.72 us  [local(): east = lax.ppermute(to_west, 'east', shift_by(-1, 'east'))]
    unnamed x10, local copies, waits for them, and re-layouts: 4.69 us -> 3.6 us
    ppermute x1, waiting for transfers between devices: 5.01 us -> 4.02 us  [local(): south = lax.ppermute(to_north, 'north', shift_by(1, 'north'))]
    pallas_call x12 -> x13, Pallas kernels: 19 us -> 19.3 us  [call(): pl.pallas_call(kernel, out_shape=outs, in_specs=specs, out_specs=[VMEM] *...]
where the time goes in v8:
time: 76.4 us; the launch traced here: 75 us
  starting transfers between devices  28.2 us (37%)
  waiting for transfers between devices  22.9 us (30%)
  Pallas kernels  19.3 us (25%)
  local copies, waits for them, and re-layouts  3.64 us (5%)
    pallas_call x13, Pallas kernels, call(): pl.pallas_call(kernel, out_shape=outs, in_specs=specs, out_specs=[VMEM] *...  19.3 us
    ppermute x10, starting transfers between devices, swap(): return lax.ppermute(value, BOTH, [(i, i ^ bits) for i in range(count)])  17.9 us
    ppermute x10, waiting for transfers between devices, swap(): return lax.ppermute(value, BOTH, [(i, i ^ bits) for i in range(count)])  15.1 us
    ppermute x1, waiting for transfers between devices, local(): south = lax.ppermute(to_north, 'north', shift_by(1, 'north'))  4.02 us
    ppermute x1, starting transfers between devices, local(): north = lax.ppermute(to_south, 'north', shift_by(-1, 'north'))  3.84 us
    ppermute x1, waiting for transfers between devices, local(): east = lax.ppermute(to_west, 'east', shift_by(-1, 'east'))  3.72 us
    unnamed x10, local copies, waits for them, and re-layouts  3.6 us
    ppermute x1, starting transfers between devices, local(): west = lax.ppermute(to_east, 'east', shift_by(1, 'east'))  3.35 us
  transfers between devices with their start and end apart: 14, of which 12 were waited for; matrix products, arithmetic and copies ran while one was open for 0% of the time, Pallas kernels for 8%

profile of v8, /device:TPU:2, one launch (start us, length us, event | category | flops | bytes accessed | tf_op | source)
XLA Modules:
  0.0 75.0 jit_solution(2489894234733292485)
XLA Ops:
  0.6 1.9 %strips.1 = (bf16[592,128]{1,0:T(8,128)(2,1)}, bf16[592,128]{1,0:T(8,128)(2,1)}) custom-call(s32[1,2]{1,0:T(1,128)} %bitcast.13, bf16[96,8,128]{2,1,0:T(8,128)(2,1)} %features.3, bf16[96,8,128]{2,1,0:T(8,128)(2,1)} %cotangent.3), custom_call_target="tpu_custom_call" | custom-call | flops 1048576 | bytes 1048576 | tf_op jit(solution)/shard_map/strips/pallas_call | solution.py:517
  2.5 3.3 %collective-permute-start = (bf16[592,128]{1,0:T(8,128)(2,1)}, bf16[592,128]{1,0:T(8,128)(2,1)S(1)}, u32[]{:S(2)}, u32[]{:S(2)}) collective-permute-start(bf16[592,128]{1,0:T(8,128)(2,1)} %get-tuple-element.44), channel_id=1, source_target_pairs={{0,16},{16,32},{32,48},{48,64},{64,80},{80,96},{96,112},{112,128},... | collective-permute-start | bytes 454664 | tf_op jit(solution)/shard_map/ppermute | solution.py:561
  5.9 3.1 %collective-permute-start.1 = (bf16[592,128]{1,0:T(8,128)(2,1)}, bf16[592,128]{1,0:T(8,128)(2,1)S(1)}, u32[]{:S(2)}, u32[]{:S(2)}) collective-permute-start(bf16[592,128]{1,0:T(8,128)(2,1)} %get-tuple-element.45), channel_id=1, source_target_pairs={{0,240},{16,0},{32,16},{48,32},{64,48},{80,64},{96,80},{112,96},{1... | collective-permute-start | bytes 454664 | tf_op jit(solution)/shard_map/ppermute | solution.py:562
  9.0 0.9 %copy-done = bf16[96,8,128]{2,1,0:T(8,128)(2,1)S(1)} copy-done((bf16[96,8,128]{2,1,0:T(8,128)(2,1)S(1)}, bf16[96,8,128]{2,1,0:T(8,128)(2,1)}, u32[]{:S(2)}) %copy-start) | copy-done | bytes 196632
  9.9 0.9 %copy-done.1 = bf16[96,8,128]{2,1,0:T(8,128)(2,1)S(1)} copy-done((bf16[96,8,128]{2,1,0:T(8,128)(2,1)S(1)}, bf16[96,8,128]{2,1,0:T(8,128)(2,1)}, u32[]{:S(2)}) %copy-start.1) | copy-done | bytes 196632
  10.8 0.7 copy-done.2
  11.5 1.1 %copy-done.3 = bf16[27,96,96]{2,1,0:T(8,128)(2,1)S(1)} copy-done((bf16[27,96,96]{2,1,0:T(8,128)(2,1)S(1)}, bf16[27,96,96]{2,1,0:T(8,128)(2,1)}, u32[]{:S(2)}) %copy-start.3) | copy-done | bytes 497688
  12.6 1.2 %prepare.1 = (bf16[5,896,128]{2,1,0:T(8,128)(2,1)S(1)}, bf16[5,896,128]{2,1,0:T(8,128)(2,1)S(1)}, bf16[288,1024]{1,0:T(8,128)(2,1)S(1)}, bf16[8,128,128]{2,1,0:T...) custom-call(bf16[27,96,96]{2,1,0:T(8,128)(2,1)S(1)} %copy-done.3, ...), custom_call_target="tpu_custom_call" | custom-call | flops 8589934592 | bytes 1048576 | tf_op jit(solution)/shard_map/prepare/pallas_call | solution.py:517
  13.8 3.7 %collective-permute-done.1.east = bf16[592,128]{1,0:T(8,128)(2,1)S(1)} collective-permute-done((bf16[592,128]{1,0:T(8,128)(2,1)}, bf16[592,128]{1,0:T(8,128)(2,1)S(1)}, u32[]{:S(2)}, u32[]{:S(2)}) %collective-permute-start.1) | collective-permute-done | bytes 151584 | tf_op jit(solution)/shard_map/ppermute | solution.py:562
  17.9 3.8 %collective-permute-start.3 = (bf16[1104,128]{1,0:T(8,128)(2,1)S(1)}, bf16[1104,128]{1,0:T(8,128)(2,1)S(1)}, u32[]{:S(2)}, u32[]{:S(2)}) collective-permute-start(bf16[1104,128]{1,0:T(8,128)(2,1)S(1)} %get-tuple-element.53), channel_id=1, source_target_pairs={{0,15},{1,0},{2,1},{3,2},{4,3},{5,4},{6,5},{7,6},{8,7},{9,8},{10,9... | collective-permute-start | bytes 847880 | tf_op jit(solution)/shard_map/ppermute | solution.py:596
  22.0 1.7 %inner.1 = (bf16[14,96,128]{2,1,0:T(8,128)(2,1)S(1)}, f32[10,96,128]{2,1,0:T(8,128)S(1)}) custom-call(bf16[8,128,128]{2,1,0:T(8,128)(2,1)S(1)} %get-tuple-element.42.own_grid.refs_0_, bf16[8,128,128]{2,1,0:T(8,128)(2,1)S(1)} %get-tuple-element.46.side_grid.refs_1_, f32[3,128,128]{2,1,0:T(8,128)S(1)} %get-tuple-element.48.middle.refs_4_, ...), custom_call_target="tpu_custom_call" | custom-call | flops 4294967296 | bytes 1048576 | tf_op jit(solution)/shard_map/inner/pallas_call | solution.py:517
  23.7 1.0 %second.1 = (bf16[5,896,128]{2,1,0:T(8,128)(2,1)S(1)}, bf16[5,896,128]{2,1,0:T(8,128)(2,1)S(1)}, bf16[8,128,128]{2,1,0:T(8,128)(2,1)S(1)}) custom-call(bf16[27,96,96]{2,1,0:T(8,128)(2,1)S(1)} %copy-done.4, bf16[8,96,128]{2,1,0:T(8,128)(2,1)S(1)} %get-tuple-element.47.cot, f32[3,128,128]{2,1,0:T(8,128)S(1)} %get-tuple-element.48.middle.refs_4_), custom_call_target="tpu_custom_call" | custom-call | flops 2147483648 | bytes 1048576 | tf_op jit(solution)/shard_map/second/pallas_call | solution.py:517
  24.6 4.0 %collective-permute-done.2.refs_5_ = bf16[1104,128]{1,0:T(8,128)(2,1)S(1)} collective-permute-done((bf16[1104,128]{1,0:T(8,128)(2,1)S(1)}, bf16[1104,128]{1,0:T(8,128)(2,1)S(1)}, u32[]{:S(2)}, u32[]{:S(2)}) %collective-permute-start.2) | collective-permute-done | bytes 282656 | tf_op jit(solution)/shard_map/ppermute | solution.py:595
  28.6 10.1 %level.1 = (bf16[96,8,128]{2,1,0:T(8,128)(2,1)}, bf16[10,160,128]{2,1,0:T(8,128)(2,1)S(1)}, f32[3,256,128]{2,1,0:T(8,128)S(1)}, bf16[4,576,128]{2,1,0:T(8,128)(2,1)S(1)}, bf16[4,576,128]{2,1,0:T(8,128)(2,1)S(1)}) custom-call(bf16[8,128,128]{2,1,0:T(8,128)(2,1)S(1)} %get-tuple-element.42.own_grid.refs_0_, ...), custom_call_target="tpu_custom_call" | custom-call | flops 17179869184 | bytes 1048576 | tf_op jit(solution)/shard_map/level/pallas_call | solution.py:517
  38.7 2.0 %collective-permute-done.4 = bf16[4,576,128]{2,1,0:T(8,128)(2,1)S(1)} collective-permute-done((bf16[4,576,128]{2,1,0:T(8,128)(2,1)S(1)}, bf16[4,576,128]{2,1,0:T(8,128)(2,1)S(1)}, u32[]{:S(2)}, u32[]{:S(2)}) %collective-permute-start.4) | collective-permute-done | bytes 589856 | tf_op jit(solution)/shard_map/ppermute | solution.py:540
  41.0 2.8 %collective-permute-start.7 = (bf16[576,128]{1,0:T(8,128)(2,1)S(1)}, bf16[576,128]{1,0:T(8,128)(2,1)S(1)}, u32[]{:S(2)}, u32[]{:S(2)}) collective-permute-start(bf16[576,128]{1,0:T(8,128)(2,1)S(1)} %get-tuple-element.80), channel_id=1, source_target_pairs={{0,204},{1,205},{2,206},{3,207},{4,200},{5,201},{6,202},{7,203},{8... | collective-permute-start | bytes 442376 | tf_op jit(solution)/shard_map/ppermute | solution.py:540
  44.3 1.7 %collective-permute-start.5 = (bf16[576,128]{1,0:T(8,128)(2,1)S(1)}, bf16[576,128]{1,0:T(8,128)(2,1)S(1)}, u32[]{:S(2)}, u32[]{:S(2)}) collective-permute-start(bf16[576,128]{1,0:T(8,128)(2,1)S(1)} %get-tuple-element.82), channel_id=1, source_target_pairs={{0,12},{1,13},{2,14},{3,15},{4,8},{5,9},{6,10},{7,11},{8,4},{9,5},... | collective-permute-start | bytes 442376 | tf_op jit(solution)/shard_map/ppermute | solution.py:540
  46.0 2.1 %final.1 = (bf16[96,8,128]{2,1,0:T(8,128)(2,1)}, f32[8,128]{1,0:T(8,128)S(1)}) custom-call(bf16[10,160,128]{2,1,0:T(8,128)(2,1)S(1)} %get-tuple-element.61.grad_one, f32[3,256,128]{2,1,0:T(8,128)S(1)} %get-tuple-element.62.masks, bf16[5,896,128]{2,1,0:T(8,128)(2,1)S(1)} %get-tuple-element.63.back_one), custom_call_target="tpu_custom_call" | custom-call | flops 4294967296 | bytes 1048576 | tf_op jit(solution)/shard_map/final/pallas_call | solution.py:517
  48.0 2.0 %collective-permute-done.7.a3 = bf16[576,128]{1,0:T(8,128)(2,1)S(1)} collective-permute-done((bf16[576,128]{1,0:T(8,128)(2,1)S(1)}, bf16[576,128]{1,0:T(8,128)(2,1)S(1)}, u32[]{:S(2)}, u32[]{:S(2)}) %collective-permute-start.7) | collective-permute-done | bytes 147488 | tf_op jit(solution)/shard_map/ppermute | solution.py:540
  50.1 1.3 %collective-permute-done.6.a2 = bf16[576,128]{1,0:T(8,128)(2,1)S(1)} collective-permute-done((bf16[576,128]{1,0:T(8,128)(2,1)S(1)}, bf16[576,128]{1,0:T(8,128)(2,1)S(1)}, u32[]{:S(2)}, u32[]{:S(2)}) %collective-permute-start.6) | collective-permute-done | bytes 147488 | tf_op jit(solution)/shard_map/ppermute | solution.py:540
  51.3 1.1 %collective-permute-done.5.a1 = bf16[576,128]{1,0:T(8,128)(2,1)S(1)} collective-permute-done((bf16[576,128]{1,0:T(8,128)(2,1)S(1)}, bf16[576,128]{1,0:T(8,128)(2,1)S(1)}, u32[]{:S(2)}, u32[]{:S(2)}) %collective-permute-start.5) | collective-permute-done | bytes 147488 | tf_op jit(solution)/shard_map/ppermute | solution.py:540
  52.5 0.8 %collective-permute-start.8 = (bf16[144,128]{1,0:T(8,128)(2,1)S(1)}, bf16[144,128]{1,0:T(8,128)(2,1)S(1)}, u32[]{:S(2)}, u32[]{:S(2)}) collective-permute-start(bf16[144,128]{1,0:T(8,128)(2,1)S(1)} %get-tuple-element.69), channel_id=1, source_target_pairs={{0,64},{1,65},{2,66},{3,67},{4,68},{5,69},{6,70},{7,71},{8,72},{9,... | collective-permute-start | bytes 110600 | tf_op jit(solution)/shard_map/ppermute | solution.py:540
  53.7 2.4 %collective-permute-start.10 = (bf16[144,128]{1,0:T(8,128)(2,1)S(1)}, bf16[144,128]{1,0:T(8,128)(2,1)S(1)}, u32[]{:S(2)}, u32[]{:S(2)}) collective-permute-start(bf16[144,128]{1,0:T(8,128)(2,1)S(1)} %get-tuple-element.71), channel_id=1, source_target_pairs={{0,68},{1,69},{2,70},{3,71},{4,64},{5,65},{6,66},{7,67},{8,76},{9,... | collective-permute-start | bytes 110600 | tf_op jit(solution)/shard_map/ppermute | solution.py:540
  56.1 0.7 collective-permute-done.8.a1
  57.4 1.1 %collective-permute-done.10.a3 = bf16[144,128]{1,0:T(8,128)(2,1)S(1)} collective-permute-done((bf16[144,128]{1,0:T(8,128)(2,1)S(1)}, bf16[144,128]{1,0:T(8,128)(2,1)S(1)}, u32[]{:S(2)}, u32[]{:S(2)}) %collective-permute-start.10) | collective-permute-done | bytes 36896 | tf_op jit(solution)/shard_map/ppermute | solution.py:540
  58.6 4.6 %collective-permute-start.11 = (bf16[96,128]{1,0:T(8,128)(2,1)S(1)}, bf16[96,128]{1,0:T(8,128)(2,1)S(1)}, u32[]{:S(2)}, u32[]{:S(2)}) collective-permute-start(bf16[96,128]{1,0:T(8,128)(2,1)S(1)} %get-tuple-element.73), channel_id=1, source_target_pairs={{0,48},{1,49},{2,50},{3,51},{4,52},{5,53},{6,54},{7,55},{8,56},{9,... | collective-permute-start | bytes 73736 | tf_op jit(solution)/shard_map/ppermute | solution.py:540
  63.2 1.8 %collective-permute-done.11.got = bf16[96,128]{1,0:T(8,128)(2,1)S(1)} collective-permute-done((bf16[96,128]{1,0:T(8,128)(2,1)S(1)}, bf16[96,128]{1,0:T(8,128)(2,1)S(1)}, u32[]{:S(2)}, u32[]{:S(2)}) %collective-permute-start.11) | collective-permute-done | bytes 24608 | tf_op jit(solution)/shard_map/ppermute | solution.py:540
  65.0 3.8 %collective-permute-start.12 = (bf16[48,128]{1,0:T(8,128)(2,1)S(1)}, bf16[48,128]{1,0:T(8,128)(2,1)S(1)}, u32[]{:S(2)}, u32[]{:S(2)}) collective-permute-start(bf16[48,128]{1,0:T(8,128)(2,1)S(1)} %get-tuple-element.75), channel_id=1, source_target_pairs={{0,16},{1,17},{2,18},{3,19},{4,20},{5,21},{6,22},{7,23},{8,24},{9,... | collective-permute-start | bytes 36872 | tf_op jit(solution)/shard_map/ppermute | solution.py:540
  68.9 1.7 %collective-permute-done.12.got = bf16[48,128]{1,0:T(8,128)(2,1)S(1)} collective-permute-done((bf16[48,128]{1,0:T(8,128)(2,1)S(1)}, bf16[48,128]{1,0:T(8,128)(2,1)S(1)}, u32[]{:S(2)}, u32[]{:S(2)}) %collective-permute-start.12) | collective-permute-done | bytes 12320 | tf_op jit(solution)/shard_map/ppermute | solution.py:540
  70.5 0.9 %collective-permute-start.13 = (f32[24,128]{1,0:T(8,128)S(1)}, f32[24,128]{1,0:T(8,128)S(1)}, u32[]{:S(2)}, u32[]{:S(2)}) collective-permute-start(f32[24,128]{1,0:T(8,128)S(1)} %get-tuple-element.77), channel_id=1, source_target_pairs={{0,2},{1,3},{2,0},{3,1},{4,6},{5,7},{6,4},{7,5},{8,10},{9,11},{10,... | collective-permute-start | bytes 36872 | tf_op jit(solution)/shard_map/ppermute | solution.py:540
  71.4 2.8 %collective-permute-done.13.got = f32[24,128]{1,0:T(8,128)S(1)} collective-permute-done((f32[24,128]{1,0:T(8,128)S(1)}, f32[24,128]{1,0:T(8,128)S(1)}, u32[]{:S(2)}, u32[]{:S(2)}) %collective-permute-start.13) | collective-permute-done | bytes 12320 | tf_op jit(solution)/shard_map/ppermute | solution.py:540
  74.2 0.8 %finish.1 = (f32[8,128]{1,0:T(8,128)}, f32[8,128]{1,0:T(8,128)}) custom-call(f32[24,128]{1,0:T(8,128)S(1)} %get-tuple-element.76.held, f32[24,128]{1,0:T(8,128)S(1)} %collective-permute-done.13.got), custom_call_target="tpu_custom_call" | custom-call | flops 1048576 | bytes 1048576 | tf_op jit(solution)/shard_map/finish/pallas_call | solution.py:517
  (21 shorter events, 2.5 us)
Async XLA Ops:
  2.5 11.2 %collective-permute-start = (bf16[592,128]{1,0:T(8,128)(2,1)}, bf16[592,128]{1,0:T(8,128)(2,1)S(1)}, u32[]{:S(2)}, u32[]{:S(2)}) collective-permute-start(bf16[592,128]{1,0:T(8,128)(2,1)} %get-tuple-element.44), channel_id=1, source_target_pairs={{0,16},{16,32},{32,48},{48,64},{64,80},{80,96},{96,112},{112,128},... | collective-permute-start | bytes 454664 | tf_op jit(solution)/shard_map/ppermute | solution.py:561
  5.9 11.6 %collective-permute-start.1 = (bf16[592,128]{1,0:T(8,128)(2,1)}, bf16[592,128]{1,0:T(8,128)(2,1)S(1)}, u32[]{:S(2)}, u32[]{:S(2)}) collective-permute-start(bf16[592,128]{1,0:T(8,128)(2,1)} %get-tuple-element.45), channel_id=1, source_target_pairs={{0,240},{16,0},{32,16},{48,32},{64,48},{80,64},{96,80},{112,96},{1... | collective-permute-start | bytes 454664 | tf_op jit(solution)/shard_map/ppermute | solution.py:562
  9.0 0.9 %copy-start = (bf16[96,8,128]{2,1,0:T(8,128)(2,1)S(1)}, bf16[96,8,128]{2,1,0:T(8,128)(2,1)}, u32[]{:S(2)}) copy-start(bf16[96,8,128]{2,1,0:T(8,128)(2,1)} %features.3) | copy-start | bytes 589828
  9.9 0.9 %copy-start.1 = (bf16[96,8,128]{2,1,0:T(8,128)(2,1)S(1)}, bf16[96,8,128]{2,1,0:T(8,128)(2,1)}, u32[]{:S(2)}) copy-start(bf16[96,8,128]{2,1,0:T(8,128)(2,1)} %cotangent.3) | copy-start | bytes 589828
  10.8 0.7 copy-start.2
  11.5 1.1 %copy-start.3 = (bf16[27,96,96]{2,1,0:T(8,128)(2,1)S(1)}, bf16[27,96,96]{2,1,0:T(8,128)(2,1)}, u32[]{:S(2)}) copy-start(bf16[27,96,96]{2,1,0:T(8,128)(2,1)} %weight.2) | copy-start | bytes 1492996
  17.8 10.8 %collective-permute-start.2 = (bf16[1104,128]{1,0:T(8,128)(2,1)S(1)}, bf16[1104,128]{1,0:T(8,128)(2,1)S(1)}, u32[]{:S(2)}, u32[]{:S(2)}) collective-permute-start(bf16[1104,128]{1,0:T(8,128)(2,1)S(1)} %get-tuple-element.52), channel_id=1, source_target_pairs={{0,1},{1,2},{2,3},{3,4},{4,5},{5,6},{6,7},{7,8},{8,9},{9,10},{10,1... | collective-permute-start | bytes 847880 | tf_op jit(solution)/shard_map/ppermute | solution.py:595
  17.9 10.8 %collective-permute-start.3 = (bf16[1104,128]{1,0:T(8,128)(2,1)S(1)}, bf16[1104,128]{1,0:T(8,128)(2,1)S(1)}, u32[]{:S(2)}, u32[]{:S(2)}) collective-permute-start(bf16[1104,128]{1,0:T(8,128)(2,1)S(1)} %get-tuple-element.53), channel_id=1, source_target_pairs={{0,15},{1,0},{2,1},{3,2},{4,3},{5,4},{6,5},{7,6},{8,7},{9,8},{10,9... | collective-permute-start | bytes 847880 | tf_op jit(solution)/shard_map/ppermute | solution.py:596
  21.9 1.7 %copy-start.4 = (bf16[27,96,96]{2,1,0:T(8,128)(2,1)S(1)}, bf16[27,96,96]{2,1,0:T(8,128)(2,1)}, u32[]{:S(2)}) copy-start(bf16[27,96,96]{2,1,0:T(8,128)(2,1)} %weight.3) | copy-start | bytes 1492996
  38.7 2.0 %collective-permute-start.4 = (bf16[4,576,128]{2,1,0:T(8,128)(2,1)S(1)}, bf16[4,576,128]{2,1,0:T(8,128)(2,1)S(1)}, u32[]{:S(2)}, u32[]{:S(2)}) collective-permute-start(bf16[4,576,128]{2,1,0:T(8,128)(2,1)S(1)} %get-tuple-element.66), channel_id=1, source_target_pairs={{0,1},{1,0},{2,3},{3,2},{4,5},{5,4},{6,7},{7,6},{8,9},{9,8},{10,11... | collective-permute-start | bytes 1769480 | tf_op jit(solution)/shard_map/ppermute | solution.py:540
  41.0 9.1 %collective-permute-start.7 = (bf16[576,128]{1,0:T(8,128)(2,1)S(1)}, bf16[576,128]{1,0:T(8,128)(2,1)S(1)}, u32[]{:S(2)}, u32[]{:S(2)}) collective-permute-start(bf16[576,128]{1,0:T(8,128)(2,1)S(1)} %get-tuple-element.80), channel_id=1, source_target_pairs={{0,204},{1,205},{2,206},{3,207},{4,200},{5,201},{6,202},{7,203},{8... | collective-permute-start | bytes 442376 | tf_op jit(solution)/shard_map/ppermute | solution.py:540
  43.8 7.6 %collective-permute-start.6 = (bf16[576,128]{1,0:T(8,128)(2,1)S(1)}, bf16[576,128]{1,0:T(8,128)(2,1)S(1)}, u32[]{:S(2)}, u32[]{:S(2)}) collective-permute-start(bf16[576,128]{1,0:T(8,128)(2,1)S(1)} %get-tuple-element.81), channel_id=1, source_target_pairs={{0,192},{1,193},{2,194},{3,195},{4,196},{5,197},{6,198},{7,199},{8... | collective-permute-start | bytes 442376 | tf_op jit(solution)/shard_map/ppermute | solution.py:540
  44.3 8.1 %collective-permute-start.5 = (bf16[576,128]{1,0:T(8,128)(2,1)S(1)}, bf16[576,128]{1,0:T(8,128)(2,1)S(1)}, u32[]{:S(2)}, u32[]{:S(2)}) collective-permute-start(bf16[576,128]{1,0:T(8,128)(2,1)S(1)} %get-tuple-element.82), channel_id=1, source_target_pairs={{0,12},{1,13},{2,14},{3,15},{4,8},{5,9},{6,10},{7,11},{8,4},{9,5},... | collective-permute-start | bytes 442376 | tf_op jit(solution)/shard_map/ppermute | solution.py:540
  52.5 4.3 %collective-permute-start.8 = (bf16[144,128]{1,0:T(8,128)(2,1)S(1)}, bf16[144,128]{1,0:T(8,128)(2,1)S(1)}, u32[]{:S(2)}, u32[]{:S(2)}) collective-permute-start(bf16[144,128]{1,0:T(8,128)(2,1)S(1)} %get-tuple-element.69), channel_id=1, source_target_pairs={{0,64},{1,65},{2,66},{3,67},{4,68},{5,69},{6,70},{7,71},{8,72},{9,... | collective-permute-start | bytes 110600 | tf_op jit(solution)/shard_map/ppermute | solution.py:540
  53.3 4.1 %collective-permute-start.9 = (bf16[144,128]{1,0:T(8,128)(2,1)S(1)}, bf16[144,128]{1,0:T(8,128)(2,1)S(1)}, u32[]{:S(2)}, u32[]{:S(2)}) collective-permute-start(bf16[144,128]{1,0:T(8,128)(2,1)S(1)} %get-tuple-element.70), channel_id=1, source_target_pairs={{0,4},{1,5},{2,6},{3,7},{4,0},{5,1},{6,2},{7,3},{8,12},{9,13},{10,... | collective-permute-start | bytes 110600 | tf_op jit(solution)/shard_map/ppermute | solution.py:540
  53.7 4.9 %collective-permute-start.10 = (bf16[144,128]{1,0:T(8,128)(2,1)S(1)}, bf16[144,128]{1,0:T(8,128)(2,1)S(1)}, u32[]{:S(2)}, u32[]{:S(2)}) collective-permute-start(bf16[144,128]{1,0:T(8,128)(2,1)S(1)} %get-tuple-element.71), channel_id=1, source_target_pairs={{0,68},{1,69},{2,70},{3,71},{4,64},{5,65},{6,66},{7,67},{8,76},{9,... | collective-permute-start | bytes 110600 | tf_op jit(solution)/shard_map/ppermute | solution.py:540
  58.6 6.4 %collective-permute-start.11 = (bf16[96,128]{1,0:T(8,128)(2,1)S(1)}, bf16[96,128]{1,0:T(8,128)(2,1)S(1)}, u32[]{:S(2)}, u32[]{:S(2)}) collective-permute-start(bf16[96,128]{1,0:T(8,128)(2,1)S(1)} %get-tuple-element.73), channel_id=1, source_target_pairs={{0,48},{1,49},{2,50},{3,51},{4,52},{5,53},{6,54},{7,55},{8,56},{9,... | collective-permute-start | bytes 73736 | tf_op jit(solution)/shard_map/ppermute | solution.py:540
  65.0 5.5 %collective-permute-start.12 = (bf16[48,128]{1,0:T(8,128)(2,1)S(1)}, bf16[48,128]{1,0:T(8,128)(2,1)S(1)}, u32[]{:S(2)}, u32[]{:S(2)}) collective-permute-start(bf16[48,128]{1,0:T(8,128)(2,1)S(1)} %get-tuple-element.75), channel_id=1, source_target_pairs={{0,16},{1,17},{2,18},{3,19},{4,20},{5,21},{6,22},{7,23},{8,24},{9,... | collective-permute-start | bytes 36872 | tf_op jit(solution)/shard_map/ppermute | solution.py:540
  70.5 3.7 %collective-permute-start.13 = (f32[24,128]{1,0:T(8,128)S(1)}, f32[24,128]{1,0:T(8,128)S(1)}, u32[]{:S(2)}, u32[]{:S(2)}) collective-permute-start(f32[24,128]{1,0:T(8,128)S(1)} %get-tuple-element.77), channel_id=1, source_target_pairs={{0,2},{1,3},{2,0},{3,1},{4,6},{5,7},{6,4},{7,5},{8,10},{9,11},{10,... | collective-permute-start | bytes 36872 | tf_op jit(solution)/shard_map/ppermute | solution.py:540

commit v9 on v8

--- a/solution.py
+++ b/solution.py
@@ -55,6 +55,52 @@
 def mask_tile(occupied):
     levels = occupied[...].astype(F32)
     return jnp.where((lanes(16) & 15) < 8, levels[:, 0:1], levels[:, 1:2]).astype(BF16)
+
+
+def cuts(rows, parts):
+    tiles = rows // 16
+    bounds = [16 * (tiles * k // parts) for k in range(parts + 1)]
+    return list(zip(bounds, bounds[1:]))
+
+
+def divide(whole, parts):
+    for (low, high), part in zip(cuts(whole.shape[0], len(parts)), parts):
+        part[...] = whole[low:high, :]
+
+
+def unite(parts, whole):
+    for (low, high), part in zip(cuts(whole.shape[0], len(parts)), parts):
+        whole[low:high, :] = part[...]
+
+
+def strips_parts(occupied, features, cotangent, *refs):
+    to_west, to_east = refs[8:10]
+    strips_kernel(occupied, features, cotangent, to_west, to_east, *refs[10:])
+    divide(to_west, refs[0:4])
+    divide(to_east, refs[4:8])
+
+
+def rims_parts(*refs):
+    west, east, to_south, to_north = refs[19:23]
+    unite(refs[0:4], west)
+    unite(refs[4:8], east)
+    rims_kernel(west, east, *refs[8:11], to_south, to_north)
+    divide(to_south, refs[11:15])
+    divide(to_north, refs[15:19])
+
+
+def sides_parts(own_mask, *refs):
+    west, east = refs[11:13]
+    unite(refs[0:4], west)
+    unite(refs[4:8], east)
+    sides_kernel(own_mask, west, east, *refs[8:11])
+
+
+def level_parts(scale, *refs):
+    south, north = refs[-2:]
+    unite(refs[5:9], south)
+    unite(refs[9:13], north)
+    level_kernel(scale, *refs[0:5], south, north, *refs[13:-2])
 
 
 def strips_kernel(
@@ -466,10 +512,14 @@
     feature_grad[...] = rows[...].reshape(CH, 8, LN).astype(BF16)
 
 
-def gather_kernel(a0, a1, a2, a3, token, *outs):
+def gather_kernel(own, *refs):
+    others, outs = refs[0:6], refs[7:11]
     for k, out in enumerate(outs):
-        piece = slice(144 * k, 144 * k + 144)
-        out[...] = sum(ref[piece, :].astype(F32) for ref in (a0, a1, a2, a3)).astype(BF16)
+        total = own[144 * k : 144 * k + 144, :].astype(F32)
+        start = 144 * (k % 2)
+        for ref in others[k // 2 :: 2]:
+            total = total + ref[start : start + 144, :].astype(F32)
+        out[...] = total.astype(BF16)
 
 
 def unpack_kernel(a0, a1, a2, a3, hold, give):
@@ -546,11 +596,15 @@
     wide = pltpu.VMEM((CH * 8, LN), F32)
     near = pltpu.VMEM((CH, 8, LN), BF16)
 
-    to_west, to_east = call(
-        strips_kernel,
+    strip_parts = [shape(high - low, LN) for low, high in cuts(STRIP, 4)]
+    rim_parts = [shape(high - low, LN) for low, high in cuts(RIM, 4)]
+    strip = pltpu.VMEM((STRIP, LN), BF16)
+    rim = pltpu.VMEM((RIM, LN), BF16)
+    moving = call(
+        strips_parts,
         "strips",
-        [shape(STRIP, LN), shape(STRIP, LN)],
-        [near, near, pltpu.VMEM((1, 2), jnp.int32), wide, wide, pltpu.SemaphoreType.DMA((3,))],
+        strip_parts * 2,
+        [strip, strip, near, near, pltpu.VMEM((1, 2), jnp.int32), wide, wide, pltpu.SemaphoreType.DMA((3,))],
         60,
         1 << 20,
         [pl.BlockSpec(memory_space=pltpu.HBM)] * 3,
@@ -558,8 +612,10 @@
         features,
         cotangent,
     )
-    west = lax.ppermute(to_east, "east", shift_by(1, "east"))
-    east = lax.ppermute(to_west, "east", shift_by(-1, "east"))
+    west, east = [], []
+    for k in range(4):
+        west.append(lax.ppermute(moving[4 + k], "east", shift_by(1, "east")))
+        east.append(lax.ppermute(moving[k], "east", shift_by(-1, "east")))
 
     weight = shape(5, TAPS, LN)
     tile = shape(8, LN, LN)
@@ -578,33 +634,35 @@
         cotangent,
         occupied,
     )
-    to_south, to_north = call(
-        rims_kernel,
+    moving = call(
+        rims_parts,
         "rims",
-        [shape(RIM, LN), shape(RIM, LN)],
-        [],
+        rim_parts * 2,
+        [strip, strip, rim, rim],
         8,
         1 << 20,
-        [VMEM] * 5,
-        west,
-        east,
+        [VMEM] * 11,
+        *west,
+        *east,
         feat,
         cot,
         own_mask,
     )
-    south = lax.ppermute(to_north, "north", shift_by(1, "north"))
-    north = lax.ppermute(to_south, "north", shift_by(-1, "north"))
+    south, north = [], []
+    for k in range(4):
+        south.append(lax.ppermute(moving[4 + k], "north", shift_by(1, "north")))
+        north.append(lax.ppermute(moving[k], "north", shift_by(-1, "north")))
     side_grid, side_cot, middle = call(
-        sides_kernel,
+        sides_parts,
         "sides",
         [tile, shape(4, LN, LN), shape(3, LN, LN, dtype=F32)],
-        [],
+        [strip, strip],
         8,
         1 << 31,
-        [VMEM] * 3,
+        [VMEM] * 9,
         own_mask,
-        west,
-        east,
+        *west,
+        *east,
     )
 
     inner_hidden, inner_slope = call(
@@ -633,7 +691,7 @@
         middle,
     )
     activated, grad_one, masks, keep, send = call(
-        lambda *refs: level_kernel(scale, *refs),
+        lambda *refs: level_parts(scale, *refs),
         "level",
         [
             image,
@@ -658,17 +716,19 @@
             pltpu.VMEM((2592 + 16, LN), F32),
             pltpu.VMEM((256 * 24, LN), F32),
             wide,
+            rim,
+            rim,
         ],
         40,
         1 << 34,
-        [VMEM] * 13,
+        [VMEM] * 19,
         own_grid,
         side_grid,
         own_cot,
         side_cot,
         middle,
-        south,
-        north,
+        *south,
+        *north,
         fwd_one,
         fwd_two,
         back_two,
@@ -678,7 +738,12 @@
     )
 
     part = (keep.astype(F32) + swap(send, 1).astype(F32)).astype(BF16)
-    others = [swap(part[k], bits) for k, bits in ((2, 12), (1, 192), (3, 204))]
+    halves = {
+        (k, half): swap(part[k, 288 * half : 288 * half + 288], bits)
+        for half in range(2)
+        for k, bits in ((2, 12), (1, 192), (3, 204))
+    }
+    others = [halves[k, half] for k in (2, 1, 3) for half in range(2)]
     feature_grad, token = call(
         final_kernel,
         "final",
@@ -698,7 +763,7 @@
         [],
         8,
         1 << 20,
-        [VMEM] * 5,
+        [VMEM] * 8,
         part[0],
         *others,
         token,

time: 76.4 us -> 96.4 us (1.26)
  starting transfers between devices: 28.2 us -> 51.4 us
  waiting for transfers between devices: 22.9 us -> 20.2 us
    ppermute x4 -> x16, starting transfers between devices: 10.4 us -> 28.6 us  [the longest x4 11.7 us: local(): west.append(lax.ppermute(moving[4 + k], 'east', shift_by(1, 'east')))]
    ppermute x4 -> x16, waiting for transfers between devices: 7.74 us -> 1.49 us  [the longest x4 1.45 us: local(): south.append(lax.ppermute(moving[4 + k], 'north', shift_by(1, 'north')))]
    ppermute x10 -> x13, starting transfers between devices: 17.9 us -> 22.8 us  [swap(): return lax.ppermute(value, BOTH, [(i, i ^ bits) for i in range(count)])]
    ppermute x10 -> x13, waiting for transfers between devices: 15.1 us -> 18.8 us  [swap(): return lax.ppermute(value, BOTH, [(i, i ^ bits) for i in range(count)])]
  transfers between devices with their start and end apart: 14 -> 29, of which waited for: 12 -> 12; matrix products, arithmetic and copies ran while one was open for 0% -> 0% of each run, Pallas kernels for 8% -> 6%
where the time goes in v9:
time: 96.4 us; the launch traced here: 95.6 us
  starting transfers between devices  51.4 us (53%)
  waiting for transfers between devices  20.2 us (21%)
  Pallas kernels  19.3 us (20%)
  local copies, waits for them, and re-layouts  3.65 us (4%)
    ppermute x13, starting transfers between devices, swap(): return lax.ppermute(value, BOTH, [(i, i ^ bits) for i in range(count)])  22.8 us
    pallas_call x13, Pallas kernels, call(): pl.pallas_call(kernel, out_shape=outs, in_specs=specs, out_specs=[VMEM] *...  19.3 us
    ppermute x13, waiting for transfers between devices, swap(): return lax.ppermute(value, BOTH, [(i, i ^ bits) for i in range(count)])  18.8 us
    ppermute x4, starting transfers between devices, local(): west.append(lax.ppermute(moving[4 + k], 'east', shift_by(1, 'east')))  11.7 us
    ppermute x4, starting transfers between devices, local(): north.append(lax.ppermute(moving[k], 'north', shift_by(-1, 'north')))  8.82 us
    ppermute x4, starting transfers between devices, local(): east.append(lax.ppermute(moving[k], 'east', shift_by(-1, 'east')))  6.86 us
    unnamed x10, local copies, waits for them, and re-layouts  3.6 us
  transfers between devices with their start and end apart: 29, of which 12 were waited for; matrix products, arithmetic and copies ran while one was open for 0% of the time, Pallas kernels for 6%

profile of v9, /device:TPU:2, one launch (start us, length us, event | category | flops | bytes accessed | tf_op | source)
XLA Modules:
  0.0 95.6 jit_solution(9756159756967670613)
XLA Ops:
  0.6 1.8 %strips.1 = (bf16[144,128]{1,0:T(8,128)(2,1)}, bf16[144,128]{1,0:T(8,128)(2,1)}, bf16[144,128]{1,0:T(8,128)(2,1)}, bf16[160,128]{1,0:T(8,128)(2,1)}, bf16[144,12...) custom-call(s32[1,2]{1,0:T(1,128)} %bitcast.19, ...), custom_call_target="tpu_custom_call" | custom-call | flops 1048576 | bytes 1048576 | tf_op jit(solution)/shard_map/strips/pallas_call | solution.py:567
  2.5 3.3 %collective-permute-start = (bf16[144,128]{1,0:T(8,128)(2,1)}, bf16[144,128]{1,0:T(8,128)(2,1)S(1)}, u32[]{:S(2)}, u32[]{:S(2)}) collective-permute-start(bf16[144,128]{1,0:T(8,128)(2,1)} %get-tuple-element.56), channel_id=1, source_target_pairs={{0,16},{16,32},{32,48},{48,64},{64,80},{80,96},{96,112},{112,128},... | collective-permute-start | bytes 110600 | tf_op jit(solution)/shard_map/ppermute | solution.py:617
  5.8 4.5 %collective-permute-start.1 = (bf16[144,128]{1,0:T(8,128)(2,1)}, bf16[144,128]{1,0:T(8,128)(2,1)S(1)}, u32[]{:S(2)}, u32[]{:S(2)}) collective-permute-start(bf16[144,128]{1,0:T(8,128)(2,1)} %get-tuple-element.57), channel_id=1, source_target_pairs={{0,16},{16,32},{32,48},{48,64},{64,80},{80,96},{96,112},{112,128},... | collective-permute-start | bytes 110600 | tf_op jit(solution)/shard_map/ppermute | solution.py:617
  10.3 1.5 %collective-permute-start.2 = (bf16[144,128]{1,0:T(8,128)(2,1)}, bf16[144,128]{1,0:T(8,128)(2,1)S(1)}, u32[]{:S(2)}, u32[]{:S(2)}) collective-permute-start(bf16[144,128]{1,0:T(8,128)(2,1)} %get-tuple-element.58), channel_id=1, source_target_pairs={{0,16},{16,32},{32,48},{48,64},{64,80},{80,96},{96,112},{112,128},... | collective-permute-start | bytes 110600 | tf_op jit(solution)/shard_map/ppermute | solution.py:617
  11.8 3.6 %collective-permute-start.4 = (bf16[144,128]{1,0:T(8,128)(2,1)}, bf16[144,128]{1,0:T(8,128)(2,1)S(1)}, u32[]{:S(2)}, u32[]{:S(2)}) collective-permute-start(bf16[144,128]{1,0:T(8,128)(2,1)} %get-tuple-element.60), channel_id=1, source_target_pairs={{0,240},{16,0},{32,16},{48,32},{64,48},{80,64},{96,80},{112,96},{1... | collective-permute-start | bytes 110600 | tf_op jit(solution)/shard_map/ppermute | solution.py:618
  16.0 2.4 %collective-permute-start.3 = (bf16[160,128]{1,0:T(8,128)(2,1)}, bf16[160,128]{1,0:T(8,128)(2,1)S(1)}, u32[]{:S(2)}, u32[]{:S(2)}) collective-permute-start(bf16[160,128]{1,0:T(8,128)(2,1)} %get-tuple-element.59), channel_id=1, source_target_pairs={{0,16},{16,32},{32,48},{48,64},{64,80},{80,96},{96,112},{112,128},... | collective-permute-start | bytes 122888 | tf_op jit(solution)/shard_map/ppermute | solution.py:617
  18.4 2.7 %collective-permute-start.7 = (bf16[160,128]{1,0:T(8,128)(2,1)}, bf16[160,128]{1,0:T(8,128)(2,1)S(1)}, u32[]{:S(2)}, u32[]{:S(2)}) collective-permute-start(bf16[160,128]{1,0:T(8,128)(2,1)} %get-tuple-element.63), channel_id=1, source_target_pairs={{0,240},{16,0},{32,16},{48,32},{64,48},{80,64},{96,80},{112,96},{1... | collective-permute-start | bytes 122888 | tf_op jit(solution)/shard_map/ppermute | solution.py:618
  23.5 1.1 %copy-done.3 = bf16[27,96,96]{2,1,0:T(8,128)(2,1)S(1)} copy-done((bf16[27,96,96]{2,1,0:T(8,128)(2,1)S(1)}, bf16[27,96,96]{2,1,0:T(8,128)(2,1)}, u32[]{:S(2)}) %copy-start.3) | copy-done | bytes 497688
  24.6 1.2 %prepare.1 = (bf16[5,896,128]{2,1,0:T(8,128)(2,1)S(1)}, bf16[5,896,128]{2,1,0:T(8,128)(2,1)S(1)}, bf16[288,1024]{1,0:T(8,128)(2,1)S(1)}, bf16[8,128,128]{2,1,0:T...) custom-call(bf16[27,96,96]{2,1,0:T(8,128)(2,1)S(1)} %copy-done.3, ...), custom_call_target="tpu_custom_call" | custom-call | flops 8589934592 | bytes 1048576 | tf_op jit(solution)/shard_map/prepare/pallas_call | solution.py:567
  26.3 1.1 %collective-permute-start.9 = (bf16[272,128]{1,0:T(8,128)(2,1)S(1)}, bf16[272,128]{1,0:T(8,128)(2,1)S(1)}, u32[]{:S(2)}, u32[]{:S(2)}) collective-permute-start(bf16[272,128]{1,0:T(8,128)(2,1)S(1)} %get-tuple-element.71), channel_id=1, source_target_pairs={{0,1},{1,2},{2,3},{3,4},{4,5},{5,6},{6,7},{7,8},{8,9},{9,10},{10,1... | collective-permute-start | bytes 208904 | tf_op jit(solution)/shard_map/ppermute | solution.py:653
  27.5 3.8 %collective-permute-start.12 = (bf16[272,128]{1,0:T(8,128)(2,1)S(1)}, bf16[272,128]{1,0:T(8,128)(2,1)S(1)}, u32[]{:S(2)}, u32[]{:S(2)}) collective-permute-start(bf16[272,128]{1,0:T(8,128)(2,1)S(1)} %get-tuple-element.74), channel_id=1, source_target_pairs={{0,15},{1,0},{2,1},{3,2},{4,3},{5,4},{6,5},{7,6},{8,7},{9,8},{10,9... | collective-permute-start | bytes 208904 | tf_op jit(solution)/shard_map/ppermute | solution.py:654
  31.6 1.7 %inner.1 = (bf16[14,96,128]{2,1,0:T(8,128)(2,1)S(1)}, f32[10,96,128]{2,1,0:T(8,128)S(1)}) custom-call(bf16[8,128,128]{2,1,0:T(8,128)(2,1)S(1)} %get-tuple-element.54.own_grid.refs_0_, bf16[8,128,128]{2,1,0:T(8,128)(2,1)S(1)} %get-tuple-element.64.side_grid.refs_1_, f32[3,128,128]{2,1,0:T(8,128)S(1)} %get-tuple-element.66.middle.refs_4_, ...), custom_call_target="tpu_custom_call" | custom-call | flops 4294967296 | bytes 1048576 | tf_op jit(solution)/shard_map/inner/pallas_call | solution.py:567
  33.3 1.2 %collective-permute-start.14 = (bf16[272,128]{1,0:T(8,128)(2,1)S(1)}, bf16[272,128]{1,0:T(8,128)(2,1)S(1)}, u32[]{:S(2)}, u32[]{:S(2)}) collective-permute-start(bf16[272,128]{1,0:T(8,128)(2,1)S(1)} %get-tuple-element.76), channel_id=1, source_target_pairs={{0,15},{1,0},{2,1},{3,2},{4,3},{5,4},{6,5},{7,6},{8,7},{9,8},{10,9... | collective-permute-start | bytes 208904 | tf_op jit(solution)/shard_map/ppermute | solution.py:654
  34.4 3.9 %collective-permute-start.15 = (bf16[288,128]{1,0:T(8,128)(2,1)S(1)}, bf16[288,128]{1,0:T(8,128)(2,1)S(1)}, u32[]{:S(2)}, u32[]{:S(2)}) collective-permute-start(bf16[288,128]{1,0:T(8,128)(2,1)S(1)} %get-tuple-element.77), channel_id=1, source_target_pairs={{0,15},{1,0},{2,1},{3,2},{4,3},{5,4},{6,5},{7,6},{8,7},{9,8},{10,9... | collective-permute-start | bytes 221192 | tf_op jit(solution)/shard_map/ppermute | solution.py:654
  38.3 1.0 %second.1 = (bf16[5,896,128]{2,1,0:T(8,128)(2,1)S(1)}, bf16[5,896,128]{2,1,0:T(8,128)(2,1)S(1)}, bf16[8,128,128]{2,1,0:T(8,128)(2,1)S(1)}) custom-call(bf16[27,96,96]{2,1,0:T(8,128)(2,1)S(1)} %copy-done.4, bf16[8,96,128]{2,1,0:T(8,128)(2,1)S(1)} %get-tuple-element.65.cot.refs_9_, f32[3,128,128]{2,1,0:T(8,128)S(1)} %get-tuple-element.66.middle.refs_4_), custom_call_target="tpu_custom_call" | custom-call | flops 2147483648 | bytes 1048576 | tf_op jit(solution)/shard_map/second/pallas_call | solution.py:567
  39.3 1.4 %collective-permute-done.11.refs_8_ = bf16[288,128]{1,0:T(8,128)(2,1)S(1)} collective-permute-done((bf16[288,128]{1,0:T(8,128)(2,1)S(1)}, bf16[288,128]{1,0:T(8,128)(2,1)S(1)}, u32[]{:S(2)}, u32[]{:S(2)}) %collective-permute-start.11) | collective-permute-done | bytes 73760 | tf_op jit(solution)/shard_map/ppermute | solution.py:653
  40.7 10.1 %level.1 = (bf16[96,8,128]{2,1,0:T(8,128)(2,1)}, bf16[10,160,128]{2,1,0:T(8,128)(2,1)S(1)}, f32[3,256,128]{2,1,0:T(8,128)S(1)}, bf16[4,576,128]{2,1,0:T(8,128)(2,1)S(1)}, bf16[4,576,128]{2,1,0:T(8,128)(2,1)S(1)}) custom-call(bf16[8,128,128]{2,1,0:T(8,128)(2,1)S(1)} %get-tuple-element.54.own_grid.refs_0_, ...), custom_call_target="tpu_custom_call" | custom-call | flops 17179869184 | bytes 1048576 | tf_op jit(solution)/shard_map/level/pallas_call | solution.py:567
  50.8 2.0 %collective-permute-done.16 = bf16[4,576,128]{2,1,0:T(8,128)(2,1)S(1)} collective-permute-done((bf16[4,576,128]{2,1,0:T(8,128)(2,1)S(1)}, bf16[4,576,128]{2,1,0:T(8,128)(2,1)S(1)}, u32[]{:S(2)}, u32[]{:S(2)}) %collective-permute-start.16) | collective-permute-done | bytes 589856 | tf_op jit(solution)/shard_map/ppermute | solution.py:590
  53.0 1.4 %collective-permute-start.22 = (bf16[288,128]{1,0:T(8,128)(2,1)S(1)}, bf16[288,128]{1,0:T(8,128)(2,1)S(1)}, u32[]{:S(2)}, u32[]{:S(2)}) collective-permute-start(bf16[288,128]{1,0:T(8,128)(2,1)S(1)} %get-tuple-element.104), channel_id=1, source_target_pairs={{0,204},{1,205},{2,206},{3,207},{4,200},{5,201},{6,202},{7,203},{8... | collective-permute-start | bytes 221192 | tf_op jit(solution)/shard_map/ppermute | solution.py:590
  54.5 2.1 %final.1 = (bf16[96,8,128]{2,1,0:T(8,128)(2,1)}, f32[8,128]{1,0:T(8,128)S(1)}) custom-call(bf16[10,160,128]{2,1,0:T(8,128)(2,1)S(1)} %get-tuple-element.85.grad_one, f32[3,256,128]{2,1,0:T(8,128)S(1)} %get-tuple-element.86.masks, bf16[5,896,128]{2,1,0:T(8,128)(2,1)S(1)} %get-tuple-element.87.back_one), custom_call_target="tpu_custom_call" | custom-call | flops 4294967296 | bytes 1048576 | tf_op jit(solution)/shard_map/final/pallas_call | solution.py:567
  56.5 2.8 %collective-permute-start.21 = (bf16[288,128]{1,0:T(8,128)(2,1)S(1)}, bf16[288,128]{1,0:T(8,128)(2,1)S(1)}, u32[]{:S(2)}, u32[]{:S(2)}) collective-permute-start(bf16[288,128]{1,0:T(8,128)(2,1)S(1)} %get-tuple-element.105), channel_id=1, source_target_pairs={{0,204},{1,205},{2,206},{3,207},{4,200},{5,201},{6,202},{7,203},{8... | collective-permute-start | bytes 221192 | tf_op jit(solution)/shard_map/ppermute | solution.py:590
  59.3 1.5 %collective-permute-start.20 = (bf16[288,128]{1,0:T(8,128)(2,1)S(1)}, bf16[288,128]{1,0:T(8,128)(2,1)S(1)}, u32[]{:S(2)}, u32[]{:S(2)}) collective-permute-start(bf16[288,128]{1,0:T(8,128)(2,1)S(1)} %get-tuple-element.106), channel_id=1, source_target_pairs={{0,192},{1,193},{2,194},{3,195},{4,196},{5,197},{6,198},{7,199},{8... | collective-permute-start | bytes 221192 | tf_op jit(solution)/shard_map/ppermute | solution.py:590
  61.8 2.8 %collective-permute-start.17 = (bf16[288,128]{1,0:T(8,128)(2,1)S(1)}, bf16[288,128]{1,0:T(8,128)(2,1)S(1)}, u32[]{:S(2)}, u32[]{:S(2)}) collective-permute-start(bf16[288,128]{1,0:T(8,128)(2,1)S(1)} %get-tuple-element.109), channel_id=1, source_target_pairs={{0,12},{1,13},{2,14},{3,15},{4,8},{5,9},{6,10},{7,11},{8,4},{9,5},... | collective-permute-start | bytes 221192 | tf_op jit(solution)/shard_map/ppermute | solution.py:590
  67.8 6.3 %collective-permute-start.23 = (bf16[144,128]{1,0:T(8,128)(2,1)S(1)}, bf16[144,128]{1,0:T(8,128)(2,1)S(1)}, u32[]{:S(2)}, u32[]{:S(2)}) collective-permute-start(bf16[144,128]{1,0:T(8,128)(2,1)S(1)} %get-tuple-element.93), channel_id=1, source_target_pairs={{0,64},{1,65},{2,66},{3,67},{4,68},{5,69},{6,70},{7,71},{8,72},{9,... | collective-permute-start | bytes 110600 | tf_op jit(solution)/shard_map/ppermute | solution.py:590
  74.1 1.6 %collective-permute-start.25 = (bf16[144,128]{1,0:T(8,128)(2,1)S(1)}, bf16[144,128]{1,0:T(8,128)(2,1)S(1)}, u32[]{:S(2)}, u32[]{:S(2)}) collective-permute-start(bf16[144,128]{1,0:T(8,128)(2,1)S(1)} %get-tuple-element.95), channel_id=1, source_target_pairs={{0,68},{1,69},{2,70},{3,71},{4,64},{5,65},{6,66},{7,67},{8,76},{9,... | collective-permute-start | bytes 110600 | tf_op jit(solution)/shard_map/ppermute | solution.py:590
  76.2 1.8 %collective-permute-done.24.a2 = bf16[144,128]{1,0:T(8,128)(2,1)S(1)} collective-permute-done((bf16[144,128]{1,0:T(8,128)(2,1)S(1)}, bf16[144,128]{1,0:T(8,128)(2,1)S(1)}, u32[]{:S(2)}, u32[]{:S(2)}) %collective-permute-start.24) | collective-permute-done | bytes 36896 | tf_op jit(solution)/shard_map/ppermute | solution.py:590
  79.0 1.0 %collective-permute-start.26 = (bf16[96,128]{1,0:T(8,128)(2,1)S(1)}, bf16[96,128]{1,0:T(8,128)(2,1)S(1)}, u32[]{:S(2)}, u32[]{:S(2)}) collective-permute-start(bf16[96,128]{1,0:T(8,128)(2,1)S(1)} %get-tuple-element.97), channel_id=1, source_target_pairs={{0,48},{1,49},{2,50},{3,51},{4,52},{5,53},{6,54},{7,55},{8,56},{9,... | collective-permute-start | bytes 73736 | tf_op jit(solution)/shard_map/ppermute | solution.py:590
  80.1 5.0 %collective-permute-done.26.got = bf16[96,128]{1,0:T(8,128)(2,1)S(1)} collective-permute-done((bf16[96,128]{1,0:T(8,128)(2,1)S(1)}, bf16[96,128]{1,0:T(8,128)(2,1)S(1)}, u32[]{:S(2)}, u32[]{:S(2)}) %collective-permute-start.26) | collective-permute-done | bytes 24608 | tf_op jit(solution)/shard_map/ppermute | solution.py:590
  85.0 1.0 %collective-permute-start.27 = (bf16[48,128]{1,0:T(8,128)(2,1)S(1)}, bf16[48,128]{1,0:T(8,128)(2,1)S(1)}, u32[]{:S(2)}, u32[]{:S(2)}) collective-permute-start(bf16[48,128]{1,0:T(8,128)(2,1)S(1)} %get-tuple-element.99), channel_id=1, source_target_pairs={{0,16},{1,17},{2,18},{3,19},{4,20},{5,21},{6,22},{7,23},{8,24},{9,... | collective-permute-start | bytes 36872 | tf_op jit(solution)/shard_map/ppermute | solution.py:590
  86.0 3.7 %collective-permute-done.27.got = bf16[48,128]{1,0:T(8,128)(2,1)S(1)} collective-permute-done((bf16[48,128]{1,0:T(8,128)(2,1)S(1)}, bf16[48,128]{1,0:T(8,128)(2,1)S(1)}, u32[]{:S(2)}, u32[]{:S(2)}) %collective-permute-start.27) | collective-permute-done | bytes 12320 | tf_op jit(solution)/shard_map/ppermute | solution.py:590
  89.7 3.5 %collective-permute-start.28 = (f32[24,128]{1,0:T(8,128)S(1)}, f32[24,128]{1,0:T(8,128)S(1)}, u32[]{:S(2)}, u32[]{:S(2)}) collective-permute-start(f32[24,128]{1,0:T(8,128)S(1)} %get-tuple-element.101), channel_id=1, source_target_pairs={{0,2},{1,3},{2,0},{3,1},{4,6},{5,7},{6,4},{7,5},{8,10},{9,11},{10,... | collective-permute-start | bytes 36872 | tf_op jit(solution)/shard_map/ppermute | solution.py:590
  93.2 1.7 %collective-permute-done.28.got = f32[24,128]{1,0:T(8,128)S(1)} collective-permute-done((f32[24,128]{1,0:T(8,128)S(1)}, f32[24,128]{1,0:T(8,128)S(1)}, u32[]{:S(2)}, u32[]{:S(2)}) %collective-permute-start.28) | collective-permute-done | bytes 12320 | tf_op jit(solution)/shard_map/ppermute | solution.py:590
  (52 shorter events, 10.7 us)
Async XLA Ops:
  2.5 12.9 %collective-permute-start = (bf16[144,128]{1,0:T(8,128)(2,1)}, bf16[144,128]{1,0:T(8,128)(2,1)S(1)}, u32[]{:S(2)}, u32[]{:S(2)}) collective-permute-start(bf16[144,128]{1,0:T(8,128)(2,1)} %get-tuple-element.56), channel_id=1, source_target_pairs={{0,16},{16,32},{32,48},{48,64},{64,80},{80,96},{96,112},{112,128},... | collective-permute-start | bytes 110600 | tf_op jit(solution)/shard_map/ppermute | solution.py:617
  5.8 10.2 %collective-permute-start.1 = (bf16[144,128]{1,0:T(8,128)(2,1)}, bf16[144,128]{1,0:T(8,128)(2,1)S(1)}, u32[]{:S(2)}, u32[]{:S(2)}) collective-permute-start(bf16[144,128]{1,0:T(8,128)(2,1)} %get-tuple-element.57), channel_id=1, source_target_pairs={{0,16},{16,32},{32,48},{48,64},{64,80},{80,96},{96,112},{112,128},... | collective-permute-start | bytes 110600 | tf_op jit(solution)/shard_map/ppermute | solution.py:617
  10.3 8.1 %collective-permute-start.2 = (bf16[144,128]{1,0:T(8,128)(2,1)}, bf16[144,128]{1,0:T(8,128)(2,1)S(1)}, u32[]{:S(2)}, u32[]{:S(2)}) collective-permute-start(bf16[144,128]{1,0:T(8,128)(2,1)} %get-tuple-element.58), channel_id=1, source_target_pairs={{0,16},{16,32},{32,48},{48,64},{64,80},{80,96},{96,112},{112,128},... | collective-permute-start | bytes 110600 | tf_op jit(solution)/shard_map/ppermute | solution.py:617
  11.8 14.0 %collective-permute-start.4 = (bf16[144,128]{1,0:T(8,128)(2,1)}, bf16[144,128]{1,0:T(8,128)(2,1)S(1)}, u32[]{:S(2)}, u32[]{:S(2)}) collective-permute-start(bf16[144,128]{1,0:T(8,128)(2,1)} %get-tuple-element.60), channel_id=1, source_target_pairs={{0,240},{16,0},{32,16},{48,32},{64,48},{80,64},{96,80},{112,96},{1... | collective-permute-start | bytes 110600 | tf_op jit(solution)/shard_map/ppermute | solution.py:618
  15.3 10.5 %collective-permute-start.5 = (bf16[144,128]{1,0:T(8,128)(2,1)}, bf16[144,128]{1,0:T(8,128)(2,1)S(1)}, u32[]{:S(2)}, u32[]{:S(2)}) collective-permute-start(bf16[144,128]{1,0:T(8,128)(2,1)} %get-tuple-element.61), channel_id=1, source_target_pairs={{0,240},{16,0},{32,16},{48,32},{64,48},{80,64},{96,80},{112,96},{1... | collective-permute-start | bytes 110600 | tf_op jit(solution)/shard_map/ppermute | solution.py:618
  15.4 10.4 %collective-permute-start.6 = (bf16[144,128]{1,0:T(8,128)(2,1)}, bf16[144,128]{1,0:T(8,128)(2,1)S(1)}, u32[]{:S(2)}, u32[]{:S(2)}) collective-permute-start(bf16[144,128]{1,0:T(8,128)(2,1)} %get-tuple-element.62), channel_id=1, source_target_pairs={{0,240},{16,0},{32,16},{48,32},{64,48},{80,64},{96,80},{112,96},{1... | collective-permute-start | bytes 110600 | tf_op jit(solution)/shard_map/ppermute | solution.py:618
  16.0 9.8 %collective-permute-start.3 = (bf16[160,128]{1,0:T(8,128)(2,1)}, bf16[160,128]{1,0:T(8,128)(2,1)S(1)}, u32[]{:S(2)}, u32[]{:S(2)}) collective-permute-start(bf16[160,128]{1,0:T(8,128)(2,1)} %get-tuple-element.59), channel_id=1, source_target_pairs={{0,16},{16,32},{32,48},{48,64},{64,80},{80,96},{96,112},{112,128},... | collective-permute-start | bytes 122888 | tf_op jit(solution)/shard_map/ppermute | solution.py:617
  18.4 7.5 %collective-permute-start.7 = (bf16[160,128]{1,0:T(8,128)(2,1)}, bf16[160,128]{1,0:T(8,128)(2,1)S(1)}, u32[]{:S(2)}, u32[]{:S(2)}) collective-permute-start(bf16[160,128]{1,0:T(8,128)(2,1)} %get-tuple-element.63), channel_id=1, source_target_pairs={{0,240},{16,0},{32,16},{48,32},{64,48},{80,64},{96,80},{112,96},{1... | collective-permute-start | bytes 122888 | tf_op jit(solution)/shard_map/ppermute | solution.py:618
  21.0 0.9 copy-start
  23.5 1.1 %copy-start.3 = (bf16[27,96,96]{2,1,0:T(8,128)(2,1)S(1)}, bf16[27,96,96]{2,1,0:T(8,128)(2,1)}, u32[]{:S(2)}) copy-start(bf16[27,96,96]{2,1,0:T(8,128)(2,1)} %weight.2) | copy-start | bytes 1492996
  26.2 7.0 %collective-permute-start.8 = (bf16[272,128]{1,0:T(8,128)(2,1)S(1)}, bf16[272,128]{1,0:T(8,128)(2,1)S(1)}, u32[]{:S(2)}, u32[]{:S(2)}) collective-permute-start(bf16[272,128]{1,0:T(8,128)(2,1)S(1)} %get-tuple-element.70), channel_id=1, source_target_pairs={{0,1},{1,2},{2,3},{3,4},{4,5},{5,6},{6,7},{7,8},{8,9},{9,10},{10,1... | collective-permute-start | bytes 208904 | tf_op jit(solution)/shard_map/ppermute | solution.py:653
  26.3 8.1 %collective-permute-start.9 = (bf16[272,128]{1,0:T(8,128)(2,1)S(1)}, bf16[272,128]{1,0:T(8,128)(2,1)S(1)}, u32[]{:S(2)}, u32[]{:S(2)}) collective-permute-start(bf16[272,128]{1,0:T(8,128)(2,1)S(1)} %get-tuple-element.71), channel_id=1, source_target_pairs={{0,1},{1,2},{2,3},{3,4},{4,5},{5,6},{6,7},{7,8},{8,9},{9,10},{10,1... | collective-permute-start | bytes 208904 | tf_op jit(solution)/shard_map/ppermute | solution.py:653
  27.4 7.0 %collective-permute-start.10 = (bf16[272,128]{1,0:T(8,128)(2,1)S(1)}, bf16[272,128]{1,0:T(8,128)(2,1)S(1)}, u32[]{:S(2)}, u32[]{:S(2)}) collective-permute-start(bf16[272,128]{1,0:T(8,128)(2,1)S(1)} %get-tuple-element.72), channel_id=1, source_target_pairs={{0,1},{1,2},{2,3},{3,4},{4,5},{5,6},{6,7},{7,8},{8,9},{9,10},{10,1... | collective-permute-start | bytes 208904 | tf_op jit(solution)/shard_map/ppermute | solution.py:653
  27.5 11.7 %collective-permute-start.12 = (bf16[272,128]{1,0:T(8,128)(2,1)S(1)}, bf16[272,128]{1,0:T(8,128)(2,1)S(1)}, u32[]{:S(2)}, u32[]{:S(2)}) collective-permute-start(bf16[272,128]{1,0:T(8,128)(2,1)S(1)} %get-tuple-element.74), channel_id=1, source_target_pairs={{0,15},{1,0},{2,1},{3,2},{4,3},{5,4},{6,5},{7,6},{8,7},{9,8},{10,9... | collective-permute-start | bytes 208904 | tf_op jit(solution)/shard_map/ppermute | solution.py:654
  31.3 8.0 %collective-permute-start.13 = (bf16[272,128]{1,0:T(8,128)(2,1)S(1)}, bf16[272,128]{1,0:T(8,128)(2,1)S(1)}, u32[]{:S(2)}, u32[]{:S(2)}) collective-permute-start(bf16[272,128]{1,0:T(8,128)(2,1)S(1)} %get-tuple-element.75), channel_id=1, source_target_pairs={{0,15},{1,0},{2,1},{3,2},{4,3},{5,4},{6,5},{7,6},{8,7},{9,8},{10,9... | collective-permute-start | bytes 208904 | tf_op jit(solution)/shard_map/ppermute | solution.py:654
  31.6 6.7 %copy-start.4 = (bf16[27,96,96]{2,1,0:T(8,128)(2,1)S(1)}, bf16[27,96,96]{2,1,0:T(8,128)(2,1)}, u32[]{:S(2)}) copy-start(bf16[27,96,96]{2,1,0:T(8,128)(2,1)} %weight.3) | copy-start | bytes 1492996
  33.3 6.0 %collective-permute-start.14 = (bf16[272,128]{1,0:T(8,128)(2,1)S(1)}, bf16[272,128]{1,0:T(8,128)(2,1)S(1)}, u32[]{:S(2)}, u32[]{:S(2)}) collective-permute-start(bf16[272,128]{1,0:T(8,128)(2,1)S(1)} %get-tuple-element.76), channel_id=1, source_target_pairs={{0,15},{1,0},{2,1},{3,2},{4,3},{5,4},{6,5},{7,6},{8,7},{9,8},{10,9... | collective-permute-start | bytes 208904 | tf_op jit(solution)/shard_map/ppermute | solution.py:654
  34.4 6.3 %collective-permute-start.11 = (bf16[288,128]{1,0:T(8,128)(2,1)S(1)}, bf16[288,128]{1,0:T(8,128)(2,1)S(1)}, u32[]{:S(2)}, u32[]{:S(2)}) collective-permute-start(bf16[288,128]{1,0:T(8,128)(2,1)S(1)} %get-tuple-element.73), channel_id=1, source_target_pairs={{0,1},{1,2},{2,3},{3,4},{4,5},{5,6},{6,7},{7,8},{8,9},{9,10},{10,1... | collective-permute-start | bytes 221192 | tf_op jit(solution)/shard_map/ppermute | solution.py:653
  34.4 6.3 %collective-permute-start.15 = (bf16[288,128]{1,0:T(8,128)(2,1)S(1)}, bf16[288,128]{1,0:T(8,128)(2,1)S(1)}, u32[]{:S(2)}, u32[]{:S(2)}) collective-permute-start(bf16[288,128]{1,0:T(8,128)(2,1)S(1)} %get-tuple-element.77), channel_id=1, source_target_pairs={{0,15},{1,0},{2,1},{3,2},{4,3},{5,4},{6,5},{7,6},{8,7},{9,8},{10,9... | collective-permute-start | bytes 221192 | tf_op jit(solution)/shard_map/ppermute | solution.py:654
  50.8 2.0 %collective-permute-start.16 = (bf16[4,576,128]{2,1,0:T(8,128)(2,1)S(1)}, bf16[4,576,128]{2,1,0:T(8,128)(2,1)S(1)}, u32[]{:S(2)}, u32[]{:S(2)}) collective-permute-start(bf16[4,576,128]{2,1,0:T(8,128)(2,1)S(1)} %get-tuple-element.90), channel_id=1, source_target_pairs={{0,1},{1,0},{2,3},{3,2},{4,5},{5,4},{6,7},{7,6},{8,9},{9,8},{10,11... | collective-permute-start | bytes 1769480 | tf_op jit(solution)/shard_map/ppermute | solution.py:590
  53.0 8.7 %collective-permute-start.22 = (bf16[288,128]{1,0:T(8,128)(2,1)S(1)}, bf16[288,128]{1,0:T(8,128)(2,1)S(1)}, u32[]{:S(2)}, u32[]{:S(2)}) collective-permute-start(bf16[288,128]{1,0:T(8,128)(2,1)S(1)} %get-tuple-element.104), channel_id=1, source_target_pairs={{0,204},{1,205},{2,206},{3,207},{4,200},{5,201},{6,202},{7,203},{8... | collective-permute-start | bytes 221192 | tf_op jit(solution)/shard_map/ppermute | solution.py:590
  56.5 8.1 %collective-permute-start.21 = (bf16[288,128]{1,0:T(8,128)(2,1)S(1)}, bf16[288,128]{1,0:T(8,128)(2,1)S(1)}, u32[]{:S(2)}, u32[]{:S(2)}) collective-permute-start(bf16[288,128]{1,0:T(8,128)(2,1)S(1)} %get-tuple-element.105), channel_id=1, source_target_pairs={{0,204},{1,205},{2,206},{3,207},{4,200},{5,201},{6,202},{7,203},{8... | collective-permute-start | bytes 221192 | tf_op jit(solution)/shard_map/ppermute | solution.py:590
  59.3 5.9 %collective-permute-start.20 = (bf16[288,128]{1,0:T(8,128)(2,1)S(1)}, bf16[288,128]{1,0:T(8,128)(2,1)S(1)}, u32[]{:S(2)}, u32[]{:S(2)}) collective-permute-start(bf16[288,128]{1,0:T(8,128)(2,1)S(1)} %get-tuple-element.106), channel_id=1, source_target_pairs={{0,192},{1,193},{2,194},{3,195},{4,196},{5,197},{6,198},{7,199},{8... | collective-permute-start | bytes 221192 | tf_op jit(solution)/shard_map/ppermute | solution.py:590
  60.8 5.2 %collective-permute-start.19 = (bf16[288,128]{1,0:T(8,128)(2,1)S(1)}, bf16[288,128]{1,0:T(8,128)(2,1)S(1)}, u32[]{:S(2)}, u32[]{:S(2)}) collective-permute-start(bf16[288,128]{1,0:T(8,128)(2,1)S(1)} %get-tuple-element.107), channel_id=1, source_target_pairs={{0,192},{1,193},{2,194},{3,195},{4,196},{5,197},{6,198},{7,199},{8... | collective-permute-start | bytes 221192 | tf_op jit(solution)/shard_map/ppermute | solution.py:590
  61.4 5.6 %collective-permute-start.18 = (bf16[288,128]{1,0:T(8,128)(2,1)S(1)}, bf16[288,128]{1,0:T(8,128)(2,1)S(1)}, u32[]{:S(2)}, u32[]{:S(2)}) collective-permute-start(bf16[288,128]{1,0:T(8,128)(2,1)S(1)} %get-tuple-element.108), channel_id=1, source_target_pairs={{0,12},{1,13},{2,14},{3,15},{4,8},{5,9},{6,10},{7,11},{8,4},{9,5},... | collective-permute-start | bytes 221192 | tf_op jit(solution)/shard_map/ppermute | solution.py:590
  61.8 5.9 %collective-permute-start.17 = (bf16[288,128]{1,0:T(8,128)(2,1)S(1)}, bf16[288,128]{1,0:T(8,128)(2,1)S(1)}, u32[]{:S(2)}, u32[]{:S(2)}) collective-permute-start(bf16[288,128]{1,0:T(8,128)(2,1)S(1)} %get-tuple-element.109), channel_id=1, source_target_pairs={{0,12},{1,13},{2,14},{3,15},{4,8},{5,9},{6,10},{7,11},{8,4},{9,5},... | collective-permute-start | bytes 221192 | tf_op jit(solution)/shard_map/ppermute | solution.py:590
  67.8 8.4 %collective-permute-start.23 = (bf16[144,128]{1,0:T(8,128)(2,1)S(1)}, bf16[144,128]{1,0:T(8,128)(2,1)S(1)}, u32[]{:S(2)}, u32[]{:S(2)}) collective-permute-start(bf16[144,128]{1,0:T(8,128)(2,1)S(1)} %get-tuple-element.93), channel_id=1, source_target_pairs={{0,64},{1,65},{2,66},{3,67},{4,68},{5,69},{6,70},{7,71},{8,72},{9,... | collective-permute-start | bytes 110600 | tf_op jit(solution)/shard_map/ppermute | solution.py:590
  74.1 4.0 %collective-permute-start.24 = (bf16[144,128]{1,0:T(8,128)(2,1)S(1)}, bf16[144,128]{1,0:T(8,128)(2,1)S(1)}, u32[]{:S(2)}, u32[]{:S(2)}) collective-permute-start(bf16[144,128]{1,0:T(8,128)(2,1)S(1)} %get-tuple-element.94), channel_id=1, source_target_pairs={{0,4},{1,5},{2,6},{3,7},{4,0},{5,1},{6,2},{7,3},{8,12},{9,13},{10,... | collective-permute-start | bytes 110600 | tf_op jit(solution)/shard_map/ppermute | solution.py:590
  74.1 4.9 %collective-permute-start.25 = (bf16[144,128]{1,0:T(8,128)(2,1)S(1)}, bf16[144,128]{1,0:T(8,128)(2,1)S(1)}, u32[]{:S(2)}, u32[]{:S(2)}) collective-permute-start(bf16[144,128]{1,0:T(8,128)(2,1)S(1)} %get-tuple-element.95), channel_id=1, source_target_pairs={{0,68},{1,69},{2,70},{3,71},{4,64},{5,65},{6,66},{7,67},{8,76},{9,... | collective-permute-start | bytes 110600 | tf_op jit(solution)/shard_map/ppermute | solution.py:590
  79.0 6.0 %collective-permute-start.26 = (bf16[96,128]{1,0:T(8,128)(2,1)S(1)}, bf16[96,128]{1,0:T(8,128)(2,1)S(1)}, u32[]{:S(2)}, u32[]{:S(2)}) collective-permute-start(bf16[96,128]{1,0:T(8,128)(2,1)S(1)} %get-tuple-element.97), channel_id=1, source_target_pairs={{0,48},{1,49},{2,50},{3,51},{4,52},{5,53},{6,54},{7,55},{8,56},{9,... | collective-permute-start | bytes 73736 | tf_op jit(solution)/shard_map/ppermute | solution.py:590
  85.0 4.7 %collective-permute-start.27 = (bf16[48,128]{1,0:T(8,128)(2,1)S(1)}, bf16[48,128]{1,0:T(8,128)(2,1)S(1)}, u32[]{:S(2)}, u32[]{:S(2)}) collective-permute-start(bf16[48,128]{1,0:T(8,128)(2,1)S(1)} %get-tuple-element.99), channel_id=1, source_target_pairs={{0,16},{1,17},{2,18},{3,19},{4,20},{5,21},{6,22},{7,23},{8,24},{9,... | collective-permute-start | bytes 36872 | tf_op jit(solution)/shard_map/ppermute | solution.py:590
  89.7 5.1 %collective-permute-start.28 = (f32[24,128]{1,0:T(8,128)S(1)}, f32[24,128]{1,0:T(8,128)S(1)}, u32[]{:S(2)}, u32[]{:S(2)}) collective-permute-start(f32[24,128]{1,0:T(8,128)S(1)} %get-tuple-element.101), channel_id=1, source_target_pairs={{0,2},{1,3},{2,0},{3,1},{4,6},{5,7},{6,4},{7,5},{8,10},{9,11},{10,... | collective-permute-start | bytes 36872 | tf_op jit(solution)/shard_map/ppermute | solution.py:590
  (2 other events, 1.6 us)
